TPU v7x, 128 devices: a whole 4x4x4 slice. The times are simulated.
128 devices in a mesh: ctx: 16 (over y_lo, x, core), tp: 8 (over y_hi, z).
Axes of the slice: x: 4, y: 4 (y_hi: 2, y_lo: 2; y = y_hi * 2 + y_lo), z: 4, core: 2. Of those that a mesh axis runs over, the one named last changes fastest.
Arguments:
- tokens: bfloat16 [16384, 4096], P('ctx', 'tp'), may hold values from -6 to 6
- in_weight: bfloat16 [4096, 3, 4096], P('tp', None, 'ctx'), may hold values from -0.09375 to 0.09375
- short_filter: float32 [3, 3, 4096], replicated, may hold values from -3 to 3
- filter_residues: float32 [4096, 16], replicated, may hold values from -1.8 to 1.8
- filter_rates: float32 [4096, 16], replicated, may hold values from 3.0517578e-05 to 0.1
- skip_gain: float32 [4096], replicated, may hold values from -3 to 3
Outputs:
- gated: bfloat16 [16384, 4096], P('ctx', 'tp')
All inputs are finite; a program needn't handle non-finite values.
Results may differ from a plain program's by a relative error of at most 0.034.
Values may be sent and summed in bfloat16 or wider, within the bound.
No kernel may reach another device: no remote copies, remote signals or barrier semaphores. Data moves between devices by JAX's collectives and lax.ppermute only.
A program may use at most 192 MiB of HBM per device.

v0:
```python
import math

import jax
import jax.numpy as jnp
from jax import lax
from jax.sharding import PartitionSpec as P

D = 4096


HIGH = lax.Precision.HIGHEST


def angle_table(first_len, second_len, period):
    product = lax.broadcasted_iota(jnp.int32, (first_len, second_len), 0) * lax.broadcasted_iota(
        jnp.int32, (first_len, second_len), 1
    )
    phase = (product % period).astype(jnp.float32) * (2.0 * math.pi / period)
    return (jnp.cos(phase), jnp.sin(phase))


def right_mul(values, table):
    return jnp.einsum("gkm,mj->gkj", values, table, precision=HIGH)


def spectrum(field, tables):
    cos_low, sin_low, cos_turn, sin_turn, cos_two, sin_two = tables
    first_re = jnp.einsum("kn,gnm->gkm", cos_low, field, precision=HIGH)
    first_im = -jnp.einsum("kn,gnm->gkm", sin_low, field, precision=HIGH)
    turned_re = first_re * cos_turn + first_im * sin_turn
    turned_im = first_im * cos_turn - first_re * sin_turn
    spec_re = right_mul(turned_re, cos_two) + right_mul(turned_im, sin_two)
    spec_im = right_mul(turned_im, cos_two) - right_mul(turned_re, sin_two)
    return (spec_re, spec_im)


def inverse(spec_re, spec_im, tables, period):
    cos_low, sin_low, cos_turn, sin_turn, cos_two, sin_two = tables
    back_re = right_mul(spec_re, cos_two) - right_mul(spec_im, sin_two)
    back_im = right_mul(spec_im, cos_two) + right_mul(spec_re, sin_two)
    turn_re = back_re * cos_turn - back_im * sin_turn
    turn_im = back_im * cos_turn + back_re * sin_turn
    field = jnp.einsum("kn,gkm->gnm", cos_low, turn_re, precision=HIGH) - jnp.einsum(
        "kn,gkm->gnm", sin_low, turn_im, precision=HIGH
    )
    return field / period


def delayed(values, steps, seq_len):
    return jnp.pad(values, ((0, 0), (0, 0), (steps, 0)))[:, :, :seq_len]


def on_device(tokens, in_weight, short_filter, filter_residues, filter_rates, skip_gain):
    n_ctx = lax.axis_size("ctx")
    n_tp = lax.axis_size("tp")
    group_size = D // (n_ctx * n_tp)
    full_weight = lax.all_gather(in_weight, "ctx", axis=2, tiled=True)
    summed = lax.psum_scatter(
        jnp.einsum("ri,igc->rgc", tokens, full_weight, preferred_element_type=jnp.float32).astype(
            jnp.bfloat16
        ),
        "tp",
        scatter_dimension=0,
        tiled=True,
    )
    arrived = lax.all_to_all(summed, ("ctx", "tp"), split_axis=2, concat_axis=0, tiled=True)
    fields = jnp.transpose(arrived, (1, 2, 0))
    channel_start = (lax.axis_index("ctx") * n_tp + lax.axis_index("tp")) * group_size
    seq_len = fields.shape[2]
    streams = fields.astype(jnp.float32)
    tap_weights = lax.dynamic_slice_in_dim(short_filter, channel_start, group_size, 2)
    featured = tap_weights[0][:, :, None] * streams
    featured = featured + tap_weights[1][:, :, None] * delayed(streams, 1, seq_len)
    featured = featured + tap_weights[2][:, :, None] * delayed(streams, 2, seq_len)
    product = featured[1] * featured[2]
    residues = lax.dynamic_slice_in_dim(filter_residues, channel_start, group_size, 0)
    rates = lax.dynamic_slice_in_dim(filter_rates, channel_start, group_size, 0)
    gains = lax.dynamic_slice_in_dim(skip_gain, channel_start, group_size, 0)
    lag_steps = jnp.arange(seq_len).astype(jnp.float32)
    response = jnp.sum(
        (residues * jnp.sqrt(rates))[:, :, None]
        * jnp.exp(-rates[:, :, None] * lag_steps[None, None, :]),
        axis=1,
    )
    fold_rows = 128
    half_fold = fold_rows // 2
    period = 2 * seq_len
    columns_count = period // fold_rows
    cos_one, sin_one = angle_table(fold_rows, half_fold, fold_rows)
    cos_turn, sin_turn = angle_table(fold_rows, columns_count, period)
    cos_two, sin_two = angle_table(columns_count, columns_count, columns_count)
    tables = (cos_one, sin_one, cos_turn, sin_turn, cos_two, sin_two)
    stacked = jnp.concatenate([product, response], axis=0).reshape(
        2 * group_size, half_fold, columns_count
    )
    spec_re, spec_im = spectrum(stacked, tables)
    data_re, filter_re = (spec_re[:group_size], spec_re[group_size:])
    data_im, filter_im = (spec_im[:group_size], spec_im[group_size:])
    joint_re = data_re * filter_re - data_im * filter_im
    joint_im = data_re * filter_im + data_im * filter_re
    convolution = inverse(joint_re, joint_im, tables, period).reshape(group_size, seq_len)
    convolved = convolution + gains[:, None] * product
    gated_local = (featured[0] * convolved).astype(jnp.bfloat16)
    spread_back = lax.all_to_all(
        gated_local, ("ctx", "tp"), split_axis=1, concat_axis=0, tiled=True
    )
    own_block = lax.all_to_all(spread_back, "tp", split_axis=0, concat_axis=1, tiled=True)
    return own_block.T


def solution(mesh):
    placed = (P("ctx", "tp"), P("tp", None, "ctx"), P(), P(), P(), P())
    return jax.shard_map(
        on_device, mesh=mesh, in_specs=placed, out_specs=P("ctx", "tp"), check_vma=False
    )
```

profile of v0, /device:TPU:1, one launch (start us, length us, event | category | flops | bytes accessed | tf_op | source)
XLA Modules:
  0.0 651.0 jit_solution(2935074125548245033)
XLA Ops:
  6.5 0.0 copy-start
  6.5 0.0 all-gather.2.cloned.1.call-start
  6.5 0.7 all-gather.2.cloned.1.call-update
  7.3 0.0 reduce-scatter.2.cloned.1.call-start
  7.3 84.8 %all-gather.2.cloned.1.call-done = bf16[512,3,4096]{2,0,1:T(8,128)(2,1)} async-done(((bf16[512,3,256]{2,0,1:T(8,128)(2,1)}), bf16[512,3,4096]{2,0,1:T(8,128)(2,1)}) %all-gather.2.cloned.1.call-update) | async-done | bytes 12582928 | tf_op jit(solution)/shard_map/all_gather | solution.py:57
  92.1 0.0 copy-done
  92.1 21.0 %convolution_convert_fusion = bf16[1024,3,4096]{2,0,1:T(8,128)(2,1)} fusion(bf16[512,3,4096]{2,0,1:T(8,128)(2,1)} %all-gather.2.cloned.1.call-done, bf16[1024,512]{1,0:T(8,128)(2,1)S(1)} %copy-done), kind=kOutput, calls=%fused_computation.1 | convolution fusion | flops 12897484800 | bytes 38797312 | tf_op jit(solution)/shard_map/ri,igc->rgc/dot_general | solution.py:59
  113.1 0.0 reduce-scatter.2.cloned.1.call-update
  113.1 262.9 %reduce-scatter.2.cloned.1.call-done = bf16[128,3,4096]{2,0,1:T(8,128)(2,1)} async-done(((bf16[1024,3,4096]{2,0,1:T(8,128)(2,1)}), bf16[128,3,4096]{2,0,1:T(8,128)(2,1)}) %reduce-scatter.2.cloned.1.call-update) | async-done | bytes 3145744 | tf_op jit(solution)/shard_map/reduce_scatter | solution.py:58
  376.0 7.2 %copy.57 = bf16[128,3,4096]{0,1,2:T(4,128)(2,1)} copy(bf16[128,3,4096]{2,0,1:T(8,128)(2,1)} %reduce-scatter.2.cloned.1.call-done) | data formatting | bytes 6291456 | tf_op jit(solution)/shard_map/reduce_scatter | solution.py:58
  383.2 9.2 %all-to-all-start = ((bf16[128,3,4096]{0,1,2:T(4,128)(2,1)}), bf16[128,3,4096]{0,1,2:T(4,128)(2,1)}, u32[]{:S(2)}, u32[]{:S(2)}) async-start(bf16[128,3,4096]{0,1,2:T(4,128)(2,1)} %copy.57), calls=%async_computation.1 | async-start | bytes 8388608 | tf_op jit(solution)/shard_map/all_to_all | solution.py:66
  392.4 0.8 sqrt_multiply_fusion
  393.2 0.1 copy.61
  393.3 0.1 copy.60
  393.4 11.5 %multiply_reduce_fusion = f32[32,16384]{1,0:T(8,128)} fusion(f32[16384]{0:T(1024)S(1)} %iota_convert_fusion, f32[32,16]{1,0:T(8,128)S(1)} %copy.61, f32[32,16]{1,0:T(8,128)S(1)} %copy.60), kind=kLoop, calls=%fused_computation | loop fusion | flops 24641536 | bytes 2166784 | tf_op jit(solution)/shard_map/reduce_sum | solution.py:80
  404.9 2.2 copy.79
  407.1 0.5 fusion.60
  407.6 0.1 copy.67
  407.8 0.3 copy.66
  408.0 0.8 dynamic_slice.15
  408.8 0.8 dynamic-slice_bitcast_fusion.2
  409.6 33.7 %all-to-all-done = bf16[128,3,4096]{0,1,2:T(4,128)(2,1)} async-done(((bf16[128,3,4096]{0,1,2:T(4,128)(2,1)}), bf16[128,3,4096]{0,1,2:T(4,128)(2,1)}, u32[]{:S(2)}, u32[]{:S(2)}) %all-to-all-start) | async-done | bytes 3145760 | tf_op jit(solution)/shard_map/all_to_all | solution.py:66
  443.3 2.6 copy.58
  446.0 0.6 bitcast_bitcast_fusion
  446.5 3.5 fusion.4
  450.0 0.3 slice_multiply_fusion
  450.4 0.0 copy-start.2
  450.4 0.6 copy.78
  451.0 0.2 constant_dynamic-update-slice_fusion.1
  451.2 0.5 copy-done.2
  451.7 0.1 constant_dynamic-update-slice_fusion
  451.8 13.6 %fusion.69 = f32[64,256,128]{2,1,0:T(8,128)S(1)} fusion(f32[64,64,256]{2,1,0:T(8,128)S(1)} %constant_dynamic-update-slice_fusion), kind=kOutput, calls=%fused_computation.87 | convolution fusion | flops 1610727424 | bytes 12582912 | tf_op jit(solution)/shard_map/kn,gnm->gkm/dot_general | solution.py:28
  465.5 13.4 %fusion.66 = f32[64,256,128]{2,1,0:T(8,128)S(1)} fusion(f32[64,64,256]{2,1,0:T(8,128)S(1)} %constant_dynamic-update-slice_fusion), kind=kOutput, calls=%fused_computation.84 | convolution fusion | flops 1610727424 | bytes 12582912 | tf_op jit(solution)/shard_map/kn,gnm->gkm/dot_general | solution.py:29
  478.9 17.6 %fusion.19 = f32[64,128,256]{2,1,0:T(8,128)} fusion(f32[64,256,128]{2,1,0:T(8,128)S(1)} %fusion.69, f32[64,256,128]{2,1,0:T(8,128)S(1)} %fusion.66, f32[128,256]{0,1:T(8,128)S(1)} %get-tuple-element.14, f32[128,256]{0,1:T(8,128)S(1)} %get-tuple-element.15), kind=kOutput, calls=%fused_computation.41 | convolution fusion | flops 6451757056 | bytes 25427968 | tf_op jit(solution)/shard_map/gkm,mj->gkj/dot_general | solution.py:23
  496.5 17.9 %fusion.23 = f32[64,128,256]{2,1,0:T(8,128)} fusion(f32[64,256,128]{2,1,0:T(8,128)S(1)} %fusion.69, f32[64,256,128]{2,1,0:T(8,128)S(1)} %fusion.66, f32[128,256]{0,1:T(8,128)S(1)} %get-tuple-element.14, f32[128,256]{0,1:T(8,128)S(1)} %get-tuple-element.15), kind=kOutput, calls=%fused_computation.42 | convolution fusion | flops 6451757056 | bytes 25427968 | tf_op jit(solution)/shard_map/gkm,mj->gkj/dot_general | solution.py:23
  514.4 1.7 copy.77
  516.1 20.2 %convolution_subtract_fusion = f32[64,128,256]{2,1,0:T(8,128)} fusion(f32[64,128,256]{2,1,0:T(8,128)} %fusion.19, f32[64,256,128]{2,1,0:T(8,128)S(1)} %fusion.69, f32[64,256,128]{2,1,0:T(8,128)S(1)} %fusion.66, f32[128,256]{0,1:T(8,128)S(1)} %get-tuple-element.14, f32[128,256]{0,1:T(8,128)S(1)} %get-tuple-element.15), kind=kOutput, calls=%fused_computation.26 | convolution fusion | flops 6453854208 | bytes 33816576 | tf_op jit(solution)/shard_map/gkm,mj->gkj/dot_general | solution.py:23
  536.3 20.0 %convolution_add_fusion = f32[64,128,256]{2,1,0:T(8,128)} fusion(f32[64,128,256]{2,1,0:T(8,128)} %fusion.23, f32[64,256,128]{2,1,0:T(8,128)S(1)} %fusion.69, f32[64,256,128]{2,1,0:T(8,128)S(1)} %fusion.66, f32[128,256]{0,1:T(8,128)S(1)} %get-tuple-element.14, f32[128,256]{0,1:T(8,128)S(1)} %get-tuple-element.15), kind=kOutput, calls=%fused_computation.27 | convolution fusion | flops 6453854208 | bytes 33816576 | tf_op jit(solution)/shard_map/gkm,mj->gkj/dot_general | solution.py:23
  556.3 6.7 %multiply_add_fusion = (f32[32,128,256]{2,1,0:T(8,128)S(1)}, f32[32,128,256]{2,1,0:T(8,128)S(1)}) fusion(f32[64,128,256]{2,1,0:T(8,128)} %convolution_subtract_fusion, f32[64,128,256]{2,1,0:T(8,128)} %convolution_add_fusion), kind=kLoop, calls=%fused_computation.24 | loop fusion | flops 6291456 | bytes 25165824 | tf_op jit(solution)/shard_map/add | solution.py:100
  563.0 4.6 fusion.37
  567.6 4.6 fusion.35
  572.2 5.2 convolution_subtract_fusion.1
  577.4 4.6 convolution_add_fusion.1
  582.1 3.1 fusion.6
  585.2 4.7 multiply_bitcast_fusion
  589.9 0.0 copy-start.3
  589.9 2.8 reshape.67
  592.7 0.0 copy-start.4
  592.7 0.0 copy-start.5
  592.7 0.0 copy-done.3
  592.7 0.4 copy.80
  593.1 1.2 copy-done.4
  594.3 0.6 copy-done.5
  594.9 0.0 copy-start.1
  594.9 3.4 fusion.14
  598.3 24.2 %all_to_all.41 = bf16[32,128,128]{2,0,1:T(8,128)(2,1)S(1)} all-to-all(bf16[32,128,128]{2,0,1:T(8,128)(2,1)S(1)} %fusion.14), channel_id=1, replica_groups=mesh['ctx'=16,'tp'=8] {'ctx','tp'}, dimensions={1} | all-to-all | bytes 2097152 | tf_op jit(solution)/shard_map/all_to_all | solution.py:104
  622.5 20.2 %all_to_all.42 = bf16[8,512,128]{2,1,0:T(8,128)(2,1)S(1)} all-to-all(bf16[8,512,128]{2,1,0:T(8,128)(2,1)S(1)} %bitcast.104), channel_id=1, replica_groups=mesh['ctx'=16,'tp'=8] {'tp'}, dimensions={0} | all-to-all | bytes 2097152 | tf_op jit(solution)/shard_map/all_to_all | solution.py:107
  642.7 1.3 copy.71
  644.0 0.0 copy-done.1
  (1 shorter events, 0.0 us)
Async XLA Ops:
  6.5 85.6 %copy-start = (bf16[1024,512]{1,0:T(8,128)(2,1)S(1)}, bf16[1024,512]{1,0:T(8,128)(2,1)}, u32[]{:S(2)}) copy-start(bf16[1024,512]{1,0:T(8,128)(2,1)} %param.6) | copy-start | bytes 3145732
  6.5 85.6 %all-gather.2.cloned.1.call-start = ((), (), s32[]{:S(2)}) async-start(), calls=%async_computation.4 | async-start | bytes 13369344 | tf_op jit(solution)/shard_map/all_gather | solution.py:57
  7.3 368.8 %reduce-scatter.2.cloned.1.call-start = ((), (), s32[]{:S(2)}) async-start(), calls=%async_computation.5 | async-start | bytes 28311552 | tf_op jit(solution)/shard_map/reduce_scatter | solution.py:58
  383.2 60.1 %all-to-all-start = ((bf16[128,3,4096]{0,1,2:T(4,128)(2,1)}), bf16[128,3,4096]{0,1,2:T(4,128)(2,1)}, u32[]{:S(2)}, u32[]{:S(2)}) async-start(bf16[128,3,4096]{0,1,2:T(4,128)(2,1)} %copy.57), calls=%async_computation.1 | async-start | bytes 8388608 | tf_op jit(solution)/shard_map/all_to_all | solution.py:66
  450.4 1.3 copy-start.2
  589.9 2.8 copy-start.3
  592.7 1.6 copy-start.4
  592.7 2.2 copy-start.5
  594.9 49.1 %copy-start.1 = (bf16[1024,512]{1,0:T(8,128)(2,1)S(1)}, bf16[1024,512]{1,0:T(8,128)(2,1)}, u32[]{:S(2)}) copy-start(bf16[1024,512]{1,0:T(8,128)(2,1)} %param.6) | copy-start | bytes 3145732
Sparse Core Ops, SparseCore 0:
  9.0 83.0 all-gather.1
  113.2 262.7 reduce-scatter.1
where the time goes:
time: 656 us; the launch traced here: 651 us
  waiting for transfers between devices  382 us (58%)
  matrix products  151 us (23%)
  blocking collectives  44.4 us (7%)
  other arithmetic  27.3 us (4%)
  local copies, waits for them, and re-layouts  23.5 us (4%)
  between operations  13.8 us (2%)
  starting transfers between devices  9.28 us (1%)
    reduce_scatter x1, waiting for transfers between devices, on_device(): lax.psum_scatter(jnp.einsum('ri,igc->rgc', tokens, full_weight, preferred...  263 us
    dot_general x8, matrix products, right_mul(): return jnp.einsum('gkm,mj->gkj', values, table, precision=HIGH)  94.7 us
    all_gather x1, waiting for transfers between devices, on_device(): full_weight = lax.all_gather(in_weight, 'ctx', axis=2, tiled=True)  84.8 us
    all_to_all x1, waiting for transfers between devices, on_device(): lax.all_to_all(summed, ('ctx', 'tp'), split_axis=2, concat_axis=0, tiled=...  33.7 us
    all_to_all x1, blocking collectives, on_device(): lax.all_to_all(gated_local, ('ctx', 'tp'), split_axis=1, concat_axis=0, t...  24.2 us
    dot_general x1, matrix products, on_device(): jnp.einsum('ri,igc->rgc', tokens, full_weight, preferred_element_type=jnp...  21 us
    all_to_all x1, blocking collectives, on_device(): lax.all_to_all(spread_back, 'tp', split_axis=0, concat_axis=1, tiled=True)  20.2 us
    dot_general x1, matrix products, spectrum(): first_re = jnp.einsum('kn,gnm->gkm', cos_low, field, precision=HIGH)  13.6 us
  transfers between devices with their start and end apart: 3, of which 3 were waited for; matrix products, arithmetic and copies ran while one was open for 3% of the time, Pallas kernels for 0%

commit v1 on v0

v1 whole, which is shorter than its diff:
```python
import functools

import jax
import jax.numpy as jnp
from jax import lax
from jax.experimental import pallas as pl
from jax.experimental.pallas import tpu as pltpu
from jax.sharding import PartitionSpec as P

D = 4096
MODES = 16
BLOCK = 512
SEG = 8
HALO = 16
SIZES = (2, 4, 2, 2, 4)
LANES = 128
CHUNKS = 2
F32 = jnp.float32


def route(move):
    pairs = []
    for yl in range(2):
        for x in range(4):
            for c in range(2):
                for yh in range(2):
                    for z in range(4):
                        to = move(yl, x, c, yh, z)
                        if to is None:
                            continue
                        a, b, e, f, g = to
                        pairs.append(
                            (
                                ((yl * 4 + x) * 2 + c) * 8 + yh * 4 + z,
                                (((a % 2) * 4 + b % 4) * 2 + e % 2) * 8 + (f % 2) * 4 + g % 4,
                            )
                        )
    return pairs


def send(value, move):
    return lax.ppermute(value, ("ctx", "tp"), route(move))


def along_z(value, step):
    return send(value, lambda yl, x, c, yh, z: (yl, x, c, yh, z + step))


def along_x(value, step):
    return send(value, lambda yl, x, c, yh, z: (yl, x + step, c, yh, z))


def other_core(value):
    return send(value, lambda yl, x, c, yh, z: (yl, x, c + 1, yh, z))


def other_yhi(value):
    return send(value, lambda yl, x, c, yh, z: (yl, x, c, yh + 1, z))


def other_ylo(value):
    return send(value, lambda yl, x, c, yh, z: (yl + 1, x, c, yh, z))


def transposed_piece(piece, p):
    return send(piece, lambda yl, x, c, yh, z: (yl, z + p, c, yh, x))


Y_A = {0: 1, 2: 0, 1: 3, 3: 2}
Y_B = {0: 0, 2: 1, 1: 2, 3: 3}


def along_y(value, table):
    def move(yl, x, c, yh, z):
        to = table[2 * yh + yl]
        return (to % 2, x, c, to // 2, z)

    return send(value, move)


def shift_down(value, steps):
    rows = lax.broadcasted_iota(jnp.int32, value.shape, 0)
    return jnp.where(rows >= steps, pltpu.roll(value, steps, 0), 0.0)


def project_kernel(rows, *refs):
    where, *refs = refs
    toks, refs = refs[:8], refs[8:]
    weights, refs = refs[:8], refs[8:]
    prm, y_ref, x1_ref, u_ref, lhs, wts, proj, sem_t, sem_w = refs
    seg_len = rows // SEG
    copies = []
    for s in range(8):
        for p in range(4):
            slot = where[s * 4 + p]
            copies.append(
                pltpu.make_async_copy(
                    toks[s].at[:, pl.ds(p * LANES, LANES)],
                    lhs.at[:, pl.ds(pl.multiple_of(slot * LANES, LANES), LANES)],
                    sem_t.at[s * 4 + p],
                )
            )
    width = 3 * LANES
    for k in range(4):
        for o in range(2):
            at = where[32 + o] * width
            copies.append(
                pltpu.make_async_copy(
                    weights[o * 4 + k],
                    wts.at[pl.ds(k * 1024, 1024), pl.ds(pl.multiple_of(at, LANES), width)],
                    sem_w.at[k * 2 + o],
                )
            )
    for copy in copies:
        copy.start()
    for copy in copies:
        copy.wait()

    tile = (rows + HALO) // 5

    def matmul(m, carry):
        at = pl.ds(pl.multiple_of(m * tile, 16), tile)
        out = jnp.dot(lhs[at, :], wts[...], preferred_element_type=F32)
        out = out.astype(jnp.bfloat16).astype(F32)
        for n in range(6):
            proj[n, at, :] = out[:, n * LANES:(n + 1) * LANES]
        return carry

    lax.fori_loop(0, 5, matmul, 0)

    for q in range(2):
        lanes = pl.ds(q * LANES, LANES)
        bcast = lambda r: jnp.broadcast_to(prm[pl.ds(r, 1), lanes], (SEG, LANES))
        decay = [bcast(k) for k in range(MODES)]
        amp = [bcast(MODES + k) for k in range(MODES)]
        taps = [[bcast(2 * MODES + 3 * j + g) for g in range(3)] for j in range(3)]
        gain = bcast(2 * MODES + 9)

        def load(g, at):
            return proj[q * 3 + g, pl.ds(at, SEG, stride=seg_len), :]

        def step(i, carry):
            before, last, states = carry
            now = [load(g, HALO + i) for g in range(3)]
            feat = [
                taps[0][g] * now[g] + taps[1][g] * last[g] + taps[2][g] * before[g]
                for g in range(3)
            ]
            product = feat[1] * feat[2]
            states = [decay[k] * states[k] + product for k in range(MODES)]
            terms = [amp[k] * states[k] for k in range(MODES)] + [gain * product]
            while len(terms) > 1:
                terms = [a + b for a, b in zip(terms[::2], terms[1::2])] + (
                    [terms[-1]] if len(terms) % 2 else []
                )
            at = pl.ds(pl.multiple_of(i * SEG, SEG), SEG)
            y_ref[at, lanes] = terms[0]
            x1_ref[at, lanes] = feat[0]
            return (last, now, states)

        zero = jnp.zeros((SEG, LANES), F32)
        first = ([load(g, HALO - 2) for g in range(3)], [load(g, HALO - 1) for g in range(3)])
        _, _, states = lax.fori_loop(0, seg_len, step, (*first, [zero] * MODES))
        for k in range(MODES):
            rate = prm[pl.ds(48 + k, 1), lanes]
            u = states[k]
            for n in (1, 2, 4):
                u = u + jnp.exp(-rate * (float(n) * seg_len)) * shift_down(u, n)
            u_ref[pl.ds(k * SEG, SEG), lanes] = u


def project(where, toks, weights, prm, rows):
    any_spec = pl.BlockSpec(memory_space=pl.ANY)
    vmem = pl.BlockSpec(memory_space=pltpu.VMEM)
    wide = 2 * LANES
    return pl.pallas_call(
        functools.partial(project_kernel, rows),
        out_shape=[
            jax.ShapeDtypeStruct((rows, wide), F32),
            jax.ShapeDtypeStruct((rows, wide), F32),
            jax.ShapeDtypeStruct((MODES * SEG, wide), F32),
        ],
        in_specs=[pl.BlockSpec(memory_space=pltpu.SMEM)] + [any_spec] * 16 + [vmem],
        out_specs=[vmem] * 3,
        scratch_shapes=[
            pltpu.VMEM((rows + HALO, D), jnp.bfloat16),
            pltpu.VMEM((D, 6 * LANES), jnp.bfloat16),
            pltpu.VMEM((6, rows + HALO, LANES), F32),
            pltpu.SemaphoreType.DMA((32,)),
            pltpu.SemaphoreType.DMA((8,)),
        ],
        compiler_params=pltpu.CompilerParams(vmem_limit_bytes=34 << 20),
        cost_estimate=pl.CostEstimate(
            flops=2 * rows * D * 6 * LANES, bytes_accessed=18 << 20, transcendentals=0
        ),
    )(where, *toks, *weights, prm)


def gate_kernel(rows, y0, y1, x0, x1, u0, u1, state_ref, prm0, prm1, out_ref, wide):
    seg_len = rows // SEG
    seg = lax.broadcasted_iota(jnp.int32, (SEG, LANES), 0).astype(F32) * seg_len
    for j, (y, x, u, prm) in enumerate(((y0, x0, u0, prm0), (y1, x1, u1, prm1))):
        for q in range(2):
            lanes = pl.ds(q * LANES, LANES)
            to = pl.ds(q * 2 * LANES + j * LANES, LANES)
            decay, carried = [], []
            for k in range(MODES):
                d = jnp.broadcast_to(prm[pl.ds(k, 1), lanes], (SEG, LANES))
                rate = prm[pl.ds(48 + k, 1), lanes]
                start = shift_down(u[pl.ds(k * SEG, SEG), lanes], 1)
                start = start + jnp.exp(-rate * seg) * state_ref[pl.ds(k, 1), to]
                decay.append(d)
                carried.append(prm[pl.ds(MODES + k, 1), lanes] * d * start)

            def step(i, carried):
                terms = list(carried)
                while len(terms) > 1:
                    terms = [a + b for a, b in zip(terms[::2], terms[1::2])]
                at = pl.ds(pl.multiple_of(i * SEG, SEG), SEG)
                wide[q * 2 + j, pl.ds(i, SEG, stride=seg_len), :] = x[at, lanes] * (
                    y[at, lanes] + terms[0]
                )
                return [c * d for c, d in zip(carried, decay)]

            lax.fori_loop(0, seg_len, step, carried)
    for n in range(BLOCK // LANES):
        out_ref[:, n * LANES:(n + 1) * LANES] = wide[n].astype(out_ref.dtype)


def gate(ys, xs, us, state, prms, rows):
    vmem = pl.BlockSpec(memory_space=pltpu.VMEM)
    return pl.pallas_call(
        functools.partial(gate_kernel, rows),
        out_shape=jax.ShapeDtypeStruct((rows, BLOCK), jnp.bfloat16),
        in_specs=[vmem] * 9,
        out_specs=vmem,
        scratch_shapes=[pltpu.VMEM((BLOCK // LANES, rows, LANES), F32)],
        compiler_params=pltpu.CompilerParams(vmem_limit_bytes=20 << 20),
    )(*ys, *xs, *us, state, *prms)


def earlier_state(total, rate, rows, x, core, y_lo):
    def fade(n):
        return jnp.exp(-rate * n.astype(F32) if hasattr(n, "astype") else -rate * float(n))

    peer = other_core(total)
    first, second = jnp.where(core == 0, total, peer), jnp.where(core == 0, peer, total)
    chip = fade(rows) * first + second
    behind = [along_x(chip, m) for m in (1, 2, 3)]
    upto = jnp.zeros_like(chip)
    for m in (1, 2, 3):
        upto = upto + jnp.where(x >= m, fade(2 * rows * (m - 1)), 0.0) * behind[m - 1]
    plane = jnp.zeros_like(chip)
    for m, value in enumerate([chip] + behind):
        of = (x - m) % 4
        plane = plane + fade(2 * rows * (3 - of)) * value
    lower = other_ylo(plane)
    start = upto + jnp.where(y_lo == 1, fade(2 * rows * x), 0.0) * lower
    return jnp.where(core == 0, start, fade(rows) * start + peer)


def on_device(tokens, in_weight, short_filter, filter_residues, filter_rates, skip_gain):
    rows = tokens.shape[0]
    ctx, tp = lax.axis_index("ctx"), lax.axis_index("tp")
    y_lo, x, core = ctx // 8, (ctx // 2) % 4, ctx % 2
    y_hi, z = tp // 4, tp % 4

    ordered = in_weight.reshape(BLOCK, 3, CHUNKS, LANES).transpose(0, 2, 1, 3).reshape(BLOCK, -1)
    quarter = BLOCK // 4
    pieces = [transposed_piece(ordered[p * quarter:(p + 1) * quarter], p) for p in range(4)]
    turned = jnp.concatenate(pieces, axis=0)
    from_a, from_b = along_y(turned, Y_A), along_y(turned, Y_B)

    def next_ctx(yl, x, c, yh, z):
        n = (yl * 4 + x) * 2 + c + 1
        return None if n == 16 else (n // 8, (n // 2) % 4, n % 2, yh, z)

    halo = send(tokens[rows - HALO:], next_ctx)
    own = jnp.concatenate([halo, tokens], axis=0)
    mine, theirs = [own], [other_yhi(own)]
    mine += [along_z(own, 1), along_z(own, -1)]
    theirs += [along_z(theirs[0], 1), along_z(theirs[0], -1)]
    mine.append(along_z(mine[1], 1))
    theirs.append(along_z(theirs[2], -1))
    toks = mine + theirs

    slots = []
    for dy in range(2):
        of_y = (y_hi + dy) % 2
        half = jnp.where(of_y == y_lo, 1, 0)
        for dz in (0, -1, 1, 2):
            of_z = (z + dz) % 4
            for p in range(4):
                ring = (of_z + p - x) % 4
                k = jnp.where(ring == 3, 1, jnp.where(ring == 1, 2, jnp.where(ring == 2, 3, 0)))
                slots.append((k * 2 + half) * 4 + p)
    where = jnp.stack(slots + [core, 1 - core]).astype(jnp.int32)

    base = tp * BLOCK
    rates = lax.dynamic_slice_in_dim(filter_rates, base, BLOCK, 0).T
    amps = lax.dynamic_slice_in_dim(filter_residues, base, BLOCK, 0).T * jnp.sqrt(rates)
    taps = lax.dynamic_slice_in_dim(short_filter, base, BLOCK, 2).reshape(9, BLOCK)
    gains = lax.dynamic_slice_in_dim(skip_gain, base, BLOCK, 0)[None]
    prm = jnp.concatenate(
        [jnp.exp(-rates), amps, taps, gains, jnp.zeros((6, BLOCK), F32), rates], axis=0
    )

    width = 3 * LANES
    ys, xs, us, prms = [], [], [], []
    for j in range(CHUNKS):
        cut = slice(j * width, (j + 1) * width)
        held = jnp.concatenate([from_a[:, cut], from_b[:, cut]], axis=0)
        up, down = along_x(held, 1), along_x(held, -1)
        far = along_x(up, 1) if j == 0 else along_x(down, -1)
        ring = [held, up, down, far]
        weights = ring + [other_core(w) for w in ring]
        prm_j = jnp.concatenate(
            [prm[:, c * 2 * LANES + j * LANES:c * 2 * LANES + (j + 1) * LANES] for c in range(2)],
            axis=1,
        )
        y, x1, u = project(where, toks, weights, prm_j, rows)
        ys.append(y)
        xs.append(x1)
        us.append(u)
        prms.append(prm_j)

    ends = [u.reshape(MODES, SEG, 2 * LANES)[:, SEG - 1] for u in us]
    total = jnp.concatenate(
        [ends[j][:, c * LANES:(c + 1) * LANES] for c in range(2) for j in range(CHUNKS)], axis=1
    )
    state = earlier_state(total, rates, rows, x, core, y_lo)
    return gate(ys, xs, us, state, prms, rows)


def solution(mesh):
    placed = (P("ctx", "tp"), P("tp", None, "ctx"), P(), P(), P(), P())
    return jax.shard_map(
        on_device, mesh=mesh, in_specs=placed, out_specs=P("ctx", "tp"), check_vma=False
    )
```

time: 656 us -> 197 us (0.30)
  waiting for transfers between devices: 382 us -> 78.7 us
  matrix products: 151 us -> 0 us
  Pallas kernels: 0 us -> 45.9 us
  blocking collectives: 44.4 us -> 0 us
  starting transfers between devices: 9.28 us -> 49.4 us
  other arithmetic: 27.3 us -> 5.26 us
  between operations: 13.8 us -> 0.39 us
  local copies, waits for them, and re-layouts: 23.5 us -> 14.7 us
    reduce_scatter x1 -> x0, waiting for transfers between devices: 263 us -> none  [on_device(): lax.psum_scatter(jnp.einsum('ri,igc->rgc', tokens, full_weight, preferred...]
    dot_general x13 -> x0, matrix products: 151 us -> none  [the longest x8 94.7 us: right_mul(): return jnp.einsum('gkm,mj->gkj', values, table, precision=HIGH)]
    all_gather x1 -> x0, waiting for transfers between devices: 84.8 us -> none  [on_device(): full_weight = lax.all_gather(in_weight, 'ctx', axis=2, tiled=True)]
    ppermute x0 -> x33, waiting for transfers between devices: none -> 78.7 us  [send(): return lax.ppermute(value, ('ctx', 'tp'), route(move))]
    ppermute x0 -> x33, starting transfers between devices: none -> 49.4 us  [send(): return lax.ppermute(value, ('ctx', 'tp'), route(move))]
    pallas_call x0 -> x3, Pallas kernels: none -> 45.9 us  [the longest x2 40.1 us: project(): pl.pallas_call(functools.partial(project_kernel, rows), out_shape=[jax.Sh...]
    all_to_all x2 -> x0, blocking collectives: 44.4 us -> none  [the longest x1 24.2 us: on_device(): lax.all_to_all(gated_local, ('ctx', 'tp'), split_axis=1, concat_axis=0, t...]
    all_to_all x1 -> x0, waiting for transfers between devices: 33.7 us -> none  [on_device(): lax.all_to_all(summed, ('ctx', 'tp'), split_axis=2, concat_axis=0, tiled=...]
  transfers between devices with their start and end apart: 3 -> 33, of which waited for: 3 -> 14; matrix products, arithmetic and copies ran while one was open for 3% -> 1% of each run, Pallas kernels for 0% -> 11%
where the time goes in v1:
time: 197 us; the launch traced here: 194 us
  waiting for transfers between devices  78.7 us (40%)
  starting transfers between devices  49.4 us (25%)
  Pallas kernels  45.9 us (23%)
  local copies, waits for them, and re-layouts  14.7 us (7%)
  other arithmetic  5.26 us (3%)
    ppermute x33, waiting for transfers between devices, send(): return lax.ppermute(value, ('ctx', 'tp'), route(move))  78.7 us
    ppermute x33, starting transfers between devices, send(): return lax.ppermute(value, ('ctx', 'tp'), route(move))  49.4 us
    pallas_call x2, Pallas kernels, project(): pl.pallas_call(functools.partial(project_kernel, rows), out_shape=[jax.Sh...  40.1 us
    unnamed x43, local copies, waits for them, and re-layouts  12.6 us
    pallas_call x1, Pallas kernels, gate(): pl.pallas_call(functools.partial(gate_kernel, rows), out_shape=jax.ShapeD...  5.81 us
  transfers between devices with their start and end apart: 33, of which 14 were waited for; matrix products, arithmetic and copies ran while one was open for 1% of the time, Pallas kernels for 11%

profile of v1, /device:TPU:1, one launch (start us, length us, event | category | flops | bytes accessed | tf_op | source)
XLA Modules:
  0.0 194.4 jit_solution(14820248168247382639)
XLA Ops:
  0.0 1.5 copy.14
  1.5 0.2 fusion.2
  1.7 0.1 copy.16
  1.8 0.7 collective-permute-start.8
  2.5 0.1 copy.18
  2.7 5.0 %collective-permute-start.9 = (bf16[128,768]{1,0:T(8,128)(2,1)S(1)}, bf16[128,768]{1,0:T(8,128)(2,1)S(1)}, u32[]{:S(2)}, u32[]{:S(2)}) collective-permute-start(bf16[128,768]{1,0:T(8,128)(2,1)S(1)} %copy.18), channel_id=1, source_target_pairs={{0,16},{1,32},{2,48},{3,0},{4,20},{5,36},{6,52},{7,4},{8,24},{9,40... | collective-permute-start | bytes 589832 | tf_op jit(solution)/shard_map/ppermute | solution.py:42
  7.6 0.1 copy.20
  7.8 4.3 %collective-permute-start.10 = (bf16[128,768]{1,0:T(8,128)(2,1)S(1)}, bf16[128,768]{1,0:T(8,128)(2,1)S(1)}, u32[]{:S(2)}, u32[]{:S(2)}) collective-permute-start(bf16[128,768]{1,0:T(8,128)(2,1)S(1)} %copy.20), channel_id=1, source_target_pairs={{0,32},{1,48},{2,0},{3,16},{4,36},{5,52},{6,4},{7,20},{8,40},{9,56... | collective-permute-start | bytes 589832 | tf_op jit(solution)/shard_map/ppermute | solution.py:42
  12.3 1.9 collective-permute-start.11
  14.3 8.5 %collective-permute-done.10 = bf16[128,768]{1,0:T(8,128)(2,1)S(1)} collective-permute-done((bf16[128,768]{1,0:T(8,128)(2,1)S(1)}, bf16[128,768]{1,0:T(8,128)(2,1)S(1)}, u32[]{:S(2)}, u32[]{:S(2)}) %collective-permute-start.10) | collective-permute-done | bytes 196640 | tf_op jit(solution)/shard_map/ppermute | solution.py:42
  22.9 0.7 collective-permute-start.13
  23.6 3.9 %collective-permute-start.12 = (bf16[512,768]{1,0:T(8,128)(2,1)S(1)}, bf16[512,768]{1,0:T(8,128)(2,1)S(1)}, u32[]{:S(2)}, u32[]{:S(2)}) collective-permute-start(bf16[512,768]{1,0:T(8,128)(2,1)S(1)} %constant_dynamic-update-slice_fusion.2), channel_id=1, source_target_pairs={{0,64},{1,65},{2,66},{3,67},{4,0},{5,1},{6,2},{7,3},{8,72},{9,73},... | collective-permute-start | bytes 2359304 | tf_op jit(solution)/shard_map/ppermute | solution.py:42
  27.5 3.4 %collective-permute-start = (bf16[16,512]{1,0:T(8,128)(2,1)S(1)}, bf16[16,512]{1,0:T(8,128)(2,1)S(1)}, u32[]{:S(2)}, u32[]{:S(2)}) collective-permute-start(bf16[16,512]{1,0:T(8,128)(2,1)S(1)} %slice.69), channel_id=1, source_target_pairs={{0,8},{1,9},{2,10},{3,11},{4,12},{5,13},{6,14},{7,15},{8,16},{9,17... | collective-permute-start | bytes 49160 | tf_op jit(solution)/shard_map/ppermute | solution.py:42
  30.8 0.8 collective-permute-done
  31.8 1.4 collective-permute-start.1
  33.1 1.6 collective-permute-start.2
  34.7 0.3 collective-permute-start.4
  35.1 9.9 %collective-permute-done.12 = bf16[512,768]{1,0:T(8,128)(2,1)S(1)} collective-permute-done((bf16[512,768]{1,0:T(8,128)(2,1)S(1)}, bf16[512,768]{1,0:T(8,128)(2,1)S(1)}, u32[]{:S(2)}, u32[]{:S(2)}) %collective-permute-start.12) | collective-permute-done | bytes 786464 | tf_op jit(solution)/shard_map/ppermute | solution.py:42
  45.2 3.0 %collective-permute-start.15 = (bf16[1024,384]{1,0:T(8,128)(2,1)S(1)}, bf16[1024,384]{1,0:T(8,128)(2,1)}, u32[]{:S(2)}, u32[]{:S(2)}) collective-permute-start(bf16[1024,384]{1,0:T(8,128)(2,1)S(1)} %pad_maximum_fusion.refs_9_), channel_id=1, source_target_pairs={{0,48},{1,49},{2,50},{3,51},{4,52},{5,53},{6,54},{7,55},{8,56},{9,... | collective-permute-start | bytes 2359304 | tf_op jit(solution)/shard_map/ppermute | solution.py:42
  48.4 10.0 %collective-permute-done.1.refs_2_ = bf16[1040,512]{1,0:T(8,128)(2,1)} collective-permute-done((bf16[1040,512]{1,0:T(8,128)(2,1)S(1)}, bf16[1040,512]{1,0:T(8,128)(2,1)}, u32[]{:S(2)}, u32[]{:S(2)}) %collective-permute-start.1) | collective-permute-done | bytes 1064992 | tf_op jit(solution)/shard_map/ppermute | solution.py:42
  58.4 3.2 %collective-permute-start.21 = (bf16[1024,384]{1,0:T(8,128)(2,1)S(1)}, bf16[1024,384]{1,0:T(8,128)(2,1)}, u32[]{:S(2)}, u32[]{:S(2)}) collective-permute-start(bf16[1024,384]{1,0:T(8,128)(2,1)S(1)} %pad_maximum_fusion.1.refs_9_), channel_id=1, source_target_pairs={{0,16},{1,17},{2,18},{3,19},{4,20},{5,21},{6,22},{7,23},{8,24},{9,... | collective-permute-start | bytes 2359304 | tf_op jit(solution)/shard_map/ppermute | solution.py:42
  61.6 1.0 copy-done.13
  62.6 5.3 %collective-permute-done.4.refs_5_ = bf16[1040,512]{1,0:T(8,128)(2,1)} collective-permute-done((bf16[1040,512]{1,0:T(8,128)(2,1)S(1)}, bf16[1040,512]{1,0:T(8,128)(2,1)}, u32[]{:S(2)}, u32[]{:S(2)}) %collective-permute-start.4) | collective-permute-done | bytes 1064992 | tf_op jit(solution)/shard_map/ppermute | solution.py:42
  67.9 1.2 collective-permute-start.6
  69.1 0.3 collective-permute-start.3
  69.4 10.6 %collective-permute-done.21.refs_10_ = bf16[1024,384]{1,0:T(8,128)(2,1)} collective-permute-done((bf16[1024,384]{1,0:T(8,128)(2,1)S(1)}, bf16[1024,384]{1,0:T(8,128)(2,1)}, u32[]{:S(2)}, u32[]{:S(2)}) %collective-permute-start.21) | collective-permute-done | bytes 786464 | tf_op jit(solution)/shard_map/ppermute | solution.py:42
  80.1 3.6 %collective-permute-start.24 = (bf16[1024,384]{1,0:T(8,128)(2,1)S(1)}, bf16[1024,384]{1,0:T(8,128)(2,1)}, u32[]{:S(2)}, u32[]{:S(2)}) collective-permute-start(bf16[1024,384]{1,0:T(8,128)(2,1)S(1)} %pad_maximum_fusion.1.refs_9_), channel_id=1, source_target_pairs={{0,8},{1,9},{2,10},{3,11},{4,12},{5,13},{6,14},{7,15},{8,0},{9,1},... | collective-permute-start | bytes 2359304 | tf_op jit(solution)/shard_map/ppermute | solution.py:42
  83.6 1.5 collective-permute-start.23
  85.1 6.5 %collective-permute-done.6.refs_7_ = bf16[1040,512]{1,0:T(8,128)(2,1)S(1)} collective-permute-done((bf16[1040,512]{1,0:T(8,128)(2,1)}, bf16[1040,512]{1,0:T(8,128)(2,1)S(1)}, u32[]{:S(2)}, u32[]{:S(2)}) %collective-permute-start.6) | collective-permute-done | bytes 1064992 | tf_op jit(solution)/shard_map/ppermute | solution.py:42
  91.6 1.8 collective-permute-start.7
  93.3 3.4 %collective-permute-start.26 = (bf16[1024,384]{1,0:T(8,128)(2,1)}, bf16[1024,384]{1,0:T(8,128)(2,1)}, u32[]{:S(2)}, u32[]{:S(2)}) collective-permute-start(bf16[1024,384]{1,0:T(8,128)(2,1)} %collective-permute-done.22.refs_11_), channel_id=1, source_target_pairs={{0,8},{1,9},{2,10},{3,11},{4,12},{5,13},{6,14},{7,15},{8,0},{9,1},... | collective-permute-start | bytes 2359304 | tf_op jit(solution)/shard_map/ppermute | solution.py:42
  96.7 19.3 %collective-permute-done.5.refs_6_ = bf16[1040,512]{1,0:T(8,128)(2,1)} collective-permute-done((bf16[1040,512]{1,0:T(8,128)(2,1)}, bf16[1040,512]{1,0:T(8,128)(2,1)}, u32[]{:S(2)}, u32[]{:S(2)}) %collective-permute-start.5) | collective-permute-done | bytes 1064992 | tf_op jit(solution)/shard_map/ppermute | solution.py:42
  116.0 3.4 %collective-permute-start.25 = (bf16[1024,384]{1,0:T(8,128)(2,1)}, bf16[1024,384]{1,0:T(8,128)(2,1)}, u32[]{:S(2)}, u32[]{:S(2)}) collective-permute-start(bf16[1024,384]{1,0:T(8,128)(2,1)} %collective-permute-done.21.refs_10_), channel_id=1, source_target_pairs={{0,8},{1,9},{2,10},{3,11},{4,12},{5,13},{6,14},{7,15},{8,0},{9,1},... | collective-permute-start | bytes 2359304 | tf_op jit(solution)/shard_map/ppermute | solution.py:42
  119.4 0.8 dynamic_slice.15
  120.2 0.8 bitcast_multiply_fusion
  121.2 0.6 collective-permute-start.17
  121.8 0.2 collective-permute-start.18
  122.0 0.3 collective-permute-start.19
  122.3 0.3 collective-permute-start.20
  122.7 1.1 copy-done.6
  123.9 1.2 copy-done.12
  125.1 1.2 copy-done.14
  126.3 1.2 copy-done.16
  127.6 20.5 %shard_map.65 = (f32[1024,256]{1,0:T(8,128)S(1)}, f32[1024,256]{1,0:T(8,128)S(1)}, f32[128,256]{1,0:T(8,128)S(1)}) custom-call(s32[34]{0:T(128)S(1)} %stack.139.refs_0_, bf16[1040,512]{1,0:T(8,128)(2,1)S(1)} %copy-done.12, bf16[1040,512]{1,0:T(8,128)(2,1)} %collective-permute-done.1.refs_2_, bf16[1040,512]{1,0:T(8,128)(2,1)S(1)} %copy-done.14, ...), custom_call_target="tpu_custom_call" | custom-call | flops 6442450944 | bytes 18874368 | tf_op jit(solution)/shard_map/pallas_call | solution.py:176
  148.1 0.6 copy-done.7
  148.8 19.6 %shard_map.64 = (f32[1024,256]{1,0:T(8,128)S(1)}, f32[1024,256]{1,0:T(8,128)S(1)}, f32[128,256]{1,0:T(8,128)S(1)}) custom-call(s32[34]{0:T(128)S(1)} %stack.139.refs_0_, bf16[1040,512]{1,0:T(8,128)(2,1)S(1)} %copy-done.12, bf16[1040,512]{1,0:T(8,128)(2,1)} %collective-permute-done.1.refs_2_, bf16[1040,512]{1,0:T(8,128)(2,1)S(1)} %copy-done.14, ...), custom_call_target="tpu_custom_call" | custom-call | flops 6442450944 | bytes 18874368 | tf_op jit(solution)/shard_map/pallas_call | solution.py:176
  168.4 1.0 copy-done.1
  169.4 0.6 copy-done.9
  170.1 0.6 pad_maximum_fusion.4
  170.7 0.4 collective-permute-start.28
  171.1 1.2 collective-permute-done.28
  172.3 1.4 select_add_fusion
  173.7 1.8 collective-permute-start.31
  175.5 0.9 collective-permute-start.29
  176.4 0.4 collective-permute-done.31
  176.8 3.4 %collective-permute-done.30 = f32[16,512]{1,0:T(8,128)} collective-permute-done((f32[16,512]{1,0:T(8,128)}, f32[16,512]{1,0:T(8,128)}, u32[]{:S(2)}, u32[]{:S(2)}) %collective-permute-start.30) | collective-permute-done | bytes 32800 | tf_op jit(solution)/shard_map/ppermute | solution.py:42
  180.2 1.4 multiply_add_fusion
  181.6 0.6 collective-permute-start.32
  182.2 2.5 %collective-permute-done.32 = f32[16,512]{1,0:T(8,128)} collective-permute-done((f32[16,512]{1,0:T(8,128)}, f32[16,512]{1,0:T(8,128)}, u32[]{:S(2)}, u32[]{:S(2)}) %collective-permute-start.32) | collective-permute-done | bytes 32800 | tf_op jit(solution)/shard_map/ppermute | solution.py:42
  184.7 0.9 add_select_fusion.state_ref
  185.6 1.2 copy-done.2
  186.8 0.9 copy-done.8
  187.7 0.9 copy-done.10
  188.6 5.8 %shard_map.66 = bf16[1024,512]{1,0:T(8,128)(2,1)} custom-call(f32[1024,256]{1,0:T(8,128)S(1)} %get-tuple-element.11.y0, f32[1024,256]{1,0:T(8,128)S(1)} %get-tuple-element.12.y1, f32[1024,256]{1,0:T(8,128)S(1)} %copy-done.2, f32[1024,256]{1,0:T(8,128)S(1)} %get-tuple-element.14.x1, f32[128,256]{1,0:T(8,128)S(1)} %copy-done.10, f32[128,256]{1,0:T(8,128)S(1)} %copy-done.8, ...), custom_call_target="tpu_custom_call" | custom-call | tf_op jit(solution)/shard_map/pallas_call | solution.py:232
  (82 shorter events, 1.5 us)
Async XLA Ops:
  0.0 119.4 %copy-start = (f32[3,3,4096]{2,1,0:T(4,128)S(1)}, f32[3,3,4096]{2,1,0:T(4,128)}, u32[]{:S(2)}) copy-start(f32[3,3,4096]{2,1,0:T(4,128)} %param.8) | copy-start | bytes 442372
  1.8 12.4 %collective-permute-start.8 = (bf16[128,768]{1,0:T(8,128)(2,1)S(1)}, bf16[128,768]{1,0:T(8,128)(2,1)S(1)}, u32[]{:S(2)}, u32[]{:S(2)}) collective-permute-start(bf16[128,768]{1,0:T(8,128)(2,1)S(1)} %copy.16), channel_id=1, source_target_pairs={{0,0},{1,16},{2,32},{3,48},{4,4},{5,20},{6,36},{7,52},{8,8},{9,24}... | collective-permute-start | bytes 589832 | tf_op jit(solution)/shard_map/ppermute | solution.py:42
  2.7 11.6 %collective-permute-start.9 = (bf16[128,768]{1,0:T(8,128)(2,1)S(1)}, bf16[128,768]{1,0:T(8,128)(2,1)S(1)}, u32[]{:S(2)}, u32[]{:S(2)}) collective-permute-start(bf16[128,768]{1,0:T(8,128)(2,1)S(1)} %copy.18), channel_id=1, source_target_pairs={{0,16},{1,32},{2,48},{3,0},{4,20},{5,36},{6,52},{7,4},{8,24},{9,40... | collective-permute-start | bytes 589832 | tf_op jit(solution)/shard_map/ppermute | solution.py:42
  7.8 15.0 %collective-permute-start.10 = (bf16[128,768]{1,0:T(8,128)(2,1)S(1)}, bf16[128,768]{1,0:T(8,128)(2,1)S(1)}, u32[]{:S(2)}, u32[]{:S(2)}) collective-permute-start(bf16[128,768]{1,0:T(8,128)(2,1)S(1)} %copy.20), channel_id=1, source_target_pairs={{0,32},{1,48},{2,0},{3,16},{4,36},{5,52},{6,4},{7,20},{8,40},{9,56... | collective-permute-start | bytes 589832 | tf_op jit(solution)/shard_map/ppermute | solution.py:42
  12.1 15.3 %copy-start.17 = (bf16[1024,512]{1,0:T(8,128)(2,1)S(1)}, bf16[1024,512]{1,0:T(8,128)(2,1)}, u32[]{:S(2)}) copy-start(bf16[1024,512]{1,0:T(8,128)(2,1)} %param.6) | copy-start | bytes 3145732
  12.3 10.6 %collective-permute-start.11 = (bf16[128,768]{1,0:T(8,128)(2,1)S(1)}, bf16[128,768]{1,0:T(8,128)(2,1)S(1)}, u32[]{:S(2)}, u32[]{:S(2)}) collective-permute-start(bf16[128,768]{1,0:T(8,128)(2,1)S(1)} %copy.22), channel_id=1, source_target_pairs={{0,48},{1,0},{2,16},{3,32},{4,52},{5,4},{6,20},{7,36},{8,56},{9,8}... | collective-permute-start | bytes 589832 | tf_op jit(solution)/shard_map/ppermute | solution.py:42
  22.9 12.1 %collective-permute-start.13 = (bf16[512,768]{1,0:T(8,128)(2,1)S(1)}, bf16[512,768]{1,0:T(8,128)(2,1)S(1)}, u32[]{:S(2)}, u32[]{:S(2)}) collective-permute-start(bf16[512,768]{1,0:T(8,128)(2,1)S(1)} %constant_dynamic-update-slice_fusion.2), channel_id=1, source_target_pairs={{0,0},{1,1},{2,2},{3,3},{4,64},{5,65},{6,66},{7,67},{8,8},{9,9},{1... | collective-permute-start | bytes 2359304 | tf_op jit(solution)/shard_map/ppermute | solution.py:42
  23.6 21.4 %collective-permute-start.12 = (bf16[512,768]{1,0:T(8,128)(2,1)S(1)}, bf16[512,768]{1,0:T(8,128)(2,1)S(1)}, u32[]{:S(2)}, u32[]{:S(2)}) collective-permute-start(bf16[512,768]{1,0:T(8,128)(2,1)S(1)} %constant_dynamic-update-slice_fusion.2), channel_id=1, source_target_pairs={{0,64},{1,65},{2,66},{3,67},{4,0},{5,1},{6,2},{7,3},{8,72},{9,73},... | collective-permute-start | bytes 2359304 | tf_op jit(solution)/shard_map/ppermute | solution.py:42
  27.5 4.2 %collective-permute-start = (bf16[16,512]{1,0:T(8,128)(2,1)S(1)}, bf16[16,512]{1,0:T(8,128)(2,1)S(1)}, u32[]{:S(2)}, u32[]{:S(2)}) collective-permute-start(bf16[16,512]{1,0:T(8,128)(2,1)S(1)} %slice.69), channel_id=1, source_target_pairs={{0,8},{1,9},{2,10},{3,11},{4,12},{5,13},{6,14},{7,15},{8,16},{9,17... | collective-permute-start | bytes 49160 | tf_op jit(solution)/shard_map/ppermute | solution.py:42
  31.8 13.3 %copy-start.11 = (bf16[1040,512]{1,0:T(8,128)(2,1)}, bf16[1040,512]{1,0:T(8,128)(2,1)S(1)}, u32[]{:S(2)}) copy-start(bf16[1040,512]{1,0:T(8,128)(2,1)S(1)} %constant_dynamic-update-slice_fusion.refs_1_) | copy-start | bytes 3194884
  31.8 26.6 %collective-permute-start.1 = (bf16[1040,512]{1,0:T(8,128)(2,1)S(1)}, bf16[1040,512]{1,0:T(8,128)(2,1)}, u32[]{:S(2)}, u32[]{:S(2)}) collective-permute-start(bf16[1040,512]{1,0:T(8,128)(2,1)S(1)} %constant_dynamic-update-slice_fusion.refs_1_), channel_id=1, source_target_pairs={{0,1},{1,2},{2,3},{3,0},{4,5},{5,6},{6,7},{7,4},{8,9},{9,10},{10,1... | collective-permute-start | bytes 3194888 | tf_op jit(solution)/shard_map/ppermute | solution.py:42
  33.1 28.4 %collective-permute-start.2 = (bf16[1040,512]{1,0:T(8,128)(2,1)S(1)}, bf16[1040,512]{1,0:T(8,128)(2,1)S(1)}, u32[]{:S(2)}, u32[]{:S(2)}) collective-permute-start(bf16[1040,512]{1,0:T(8,128)(2,1)S(1)} %constant_dynamic-update-slice_fusion.refs_1_), channel_id=1, source_target_pairs={{0,3},{1,0},{2,1},{3,2},{4,7},{5,4},{6,5},{7,6},{8,11},{9,8},{10,9... | collective-permute-start | bytes 3194888 | tf_op jit(solution)/shard_map/ppermute | solution.py:42
  34.7 33.2 %collective-permute-start.4 = (bf16[1040,512]{1,0:T(8,128)(2,1)S(1)}, bf16[1040,512]{1,0:T(8,128)(2,1)}, u32[]{:S(2)}, u32[]{:S(2)}) collective-permute-start(bf16[1040,512]{1,0:T(8,128)(2,1)S(1)} %constant_dynamic-update-slice_fusion.refs_1_), channel_id=1, source_target_pairs={{0,4},{1,5},{2,6},{3,7},{4,0},{5,1},{6,2},{7,3},{8,12},{9,13},{10,... | collective-permute-start | bytes 3194888 | tf_op jit(solution)/shard_map/ppermute | solution.py:42
  45.2 76.1 %copy-start.3 = (bf16[1024,384]{1,0:T(8,128)(2,1)}, bf16[1024,384]{1,0:T(8,128)(2,1)S(1)}, u32[]{:S(2)}) copy-start(bf16[1024,384]{1,0:T(8,128)(2,1)S(1)} %pad_maximum_fusion.refs_9_) | copy-start | bytes 2359300
  45.2 23.9 %collective-permute-start.14 = (bf16[1024,384]{1,0:T(8,128)(2,1)S(1)}, bf16[1024,384]{1,0:T(8,128)(2,1)}, u32[]{:S(2)}, u32[]{:S(2)}) collective-permute-start(bf16[1024,384]{1,0:T(8,128)(2,1)S(1)} %pad_maximum_fusion.refs_9_), channel_id=1, source_target_pairs={{0,16},{1,17},{2,18},{3,19},{4,20},{5,21},{6,22},{7,23},{8,24},{9,... | collective-permute-start | bytes 2359304 | tf_op jit(solution)/shard_map/ppermute | solution.py:42
  45.2 24.1 %collective-permute-start.15 = (bf16[1024,384]{1,0:T(8,128)(2,1)S(1)}, bf16[1024,384]{1,0:T(8,128)(2,1)}, u32[]{:S(2)}, u32[]{:S(2)}) collective-permute-start(bf16[1024,384]{1,0:T(8,128)(2,1)S(1)} %pad_maximum_fusion.refs_9_), channel_id=1, source_target_pairs={{0,48},{1,49},{2,50},{3,51},{4,52},{5,53},{6,54},{7,55},{8,56},{9,... | collective-permute-start | bytes 2359304 | tf_op jit(solution)/shard_map/ppermute | solution.py:42
  48.3 72.8 %copy-start.5 = (bf16[1024,384]{1,0:T(8,128)(2,1)}, bf16[1024,384]{1,0:T(8,128)(2,1)S(1)}, u32[]{:S(2)}) copy-start(bf16[1024,384]{1,0:T(8,128)(2,1)S(1)} %pad_maximum_fusion.1.refs_9_) | copy-start | bytes 2359300
  58.4 21.7 %collective-permute-start.21 = (bf16[1024,384]{1,0:T(8,128)(2,1)S(1)}, bf16[1024,384]{1,0:T(8,128)(2,1)}, u32[]{:S(2)}, u32[]{:S(2)}) collective-permute-start(bf16[1024,384]{1,0:T(8,128)(2,1)S(1)} %pad_maximum_fusion.1.refs_9_), channel_id=1, source_target_pairs={{0,16},{1,17},{2,18},{3,19},{4,20},{5,21},{6,22},{7,23},{8,24},{9,... | collective-permute-start | bytes 2359304 | tf_op jit(solution)/shard_map/ppermute | solution.py:42
  61.6 1.0 copy-start.13
  62.6 21.1 %collective-permute-start.22 = (bf16[1024,384]{1,0:T(8,128)(2,1)S(1)}, bf16[1024,384]{1,0:T(8,128)(2,1)}, u32[]{:S(2)}, u32[]{:S(2)}) collective-permute-start(bf16[1024,384]{1,0:T(8,128)(2,1)S(1)} %pad_maximum_fusion.1.refs_9_), channel_id=1, source_target_pairs={{0,48},{1,49},{2,50},{3,51},{4,52},{5,53},{6,54},{7,55},{8,56},{9,... | collective-permute-start | bytes 2359304 | tf_op jit(solution)/shard_map/ppermute | solution.py:42
  67.9 23.7 %collective-permute-start.6 = (bf16[1040,512]{1,0:T(8,128)(2,1)}, bf16[1040,512]{1,0:T(8,128)(2,1)S(1)}, u32[]{:S(2)}, u32[]{:S(2)}) collective-permute-start(bf16[1040,512]{1,0:T(8,128)(2,1)} %collective-permute-done.4.refs_5_), channel_id=1, source_target_pairs={{0,3},{1,0},{2,1},{3,2},{4,7},{5,4},{6,5},{7,6},{8,11},{9,8},{10,9... | collective-permute-start | bytes 3194888 | tf_op jit(solution)/shard_map/ppermute | solution.py:42
  69.1 27.6 %collective-permute-start.3 = (bf16[1040,512]{1,0:T(8,128)(2,1)}, bf16[1040,512]{1,0:T(8,128)(2,1)}, u32[]{:S(2)}, u32[]{:S(2)}) collective-permute-start(bf16[1040,512]{1,0:T(8,128)(2,1)} %collective-permute-done.1.refs_2_), channel_id=1, source_target_pairs={{0,1},{1,2},{2,3},{3,0},{4,5},{5,6},{6,7},{7,4},{8,9},{9,10},{10,1... | collective-permute-start | bytes 3194888 | tf_op jit(solution)/shard_map/ppermute | solution.py:42
  69.4 46.6 %collective-permute-start.5 = (bf16[1040,512]{1,0:T(8,128)(2,1)}, bf16[1040,512]{1,0:T(8,128)(2,1)}, u32[]{:S(2)}, u32[]{:S(2)}) collective-permute-start(bf16[1040,512]{1,0:T(8,128)(2,1)} %collective-permute-done.4.refs_5_), channel_id=1, source_target_pairs={{0,1},{1,2},{2,3},{3,0},{4,5},{5,6},{6,7},{7,4},{8,9},{9,10},{10,1... | collective-permute-start | bytes 3194888 | tf_op jit(solution)/shard_map/ppermute | solution.py:42
  80.1 13.3 %collective-permute-start.24 = (bf16[1024,384]{1,0:T(8,128)(2,1)S(1)}, bf16[1024,384]{1,0:T(8,128)(2,1)}, u32[]{:S(2)}, u32[]{:S(2)}) collective-permute-start(bf16[1024,384]{1,0:T(8,128)(2,1)S(1)} %pad_maximum_fusion.1.refs_9_), channel_id=1, source_target_pairs={{0,8},{1,9},{2,10},{3,11},{4,12},{5,13},{6,14},{7,15},{8,0},{9,1},... | collective-permute-start | bytes 2359304 | tf_op jit(solution)/shard_map/ppermute | solution.py:42
  83.6 35.7 %collective-permute-start.23 = (bf16[1024,384]{1,0:T(8,128)(2,1)}, bf16[1024,384]{1,0:T(8,128)(2,1)}, u32[]{:S(2)}, u32[]{:S(2)}) collective-permute-start(bf16[1024,384]{1,0:T(8,128)(2,1)} %collective-permute-done.22.refs_11_), channel_id=1, source_target_pairs={{0,48},{1,49},{2,50},{3,51},{4,52},{5,53},{6,54},{7,55},{8,56},{9,... | collective-permute-start | bytes 2359304 | tf_op jit(solution)/shard_map/ppermute | solution.py:42
  91.6 29.6 %copy-start.15 = (bf16[1040,512]{1,0:T(8,128)(2,1)}, bf16[1040,512]{1,0:T(8,128)(2,1)S(1)}, u32[]{:S(2)}) copy-start(bf16[1040,512]{1,0:T(8,128)(2,1)S(1)} %collective-permute-done.6.refs_7_) | copy-start | bytes 3194884
  91.6 30.8 %collective-permute-start.7 = (bf16[1040,512]{1,0:T(8,128)(2,1)S(1)}, bf16[1040,512]{1,0:T(8,128)(2,1)}, u32[]{:S(2)}, u32[]{:S(2)}) collective-permute-start(bf16[1040,512]{1,0:T(8,128)(2,1)S(1)} %collective-permute-done.6.refs_7_), channel_id=1, source_target_pairs={{0,3},{1,0},{2,1},{3,2},{4,7},{5,4},{6,5},{7,6},{8,11},{9,8},{10,9... | collective-permute-start | bytes 3194888 | tf_op jit(solution)/shard_map/ppermute | solution.py:42
  93.3 28.6 %collective-permute-start.26 = (bf16[1024,384]{1,0:T(8,128)(2,1)}, bf16[1024,384]{1,0:T(8,128)(2,1)}, u32[]{:S(2)}, u32[]{:S(2)}) collective-permute-start(bf16[1024,384]{1,0:T(8,128)(2,1)} %collective-permute-done.22.refs_11_), channel_id=1, source_target_pairs={{0,8},{1,9},{2,10},{3,11},{4,12},{5,13},{6,14},{7,15},{8,0},{9,1},... | collective-permute-start | bytes 2359304 | tf_op jit(solution)/shard_map/ppermute | solution.py:42
  96.7 24.5 %collective-permute-start.16 = (bf16[1024,384]{1,0:T(8,128)(2,1)}, bf16[1024,384]{1,0:T(8,128)(2,1)}, u32[]{:S(2)}, u32[]{:S(2)}) collective-permute-start(bf16[1024,384]{1,0:T(8,128)(2,1)} %collective-permute-done.14.refs_10_), channel_id=1, source_target_pairs={{0,16},{1,17},{2,18},{3,19},{4,20},{5,21},{6,22},{7,23},{8,24},{9,... | collective-permute-start | bytes 2359304 | tf_op jit(solution)/shard_map/ppermute | solution.py:42
  116.0 5.8 %collective-permute-start.25 = (bf16[1024,384]{1,0:T(8,128)(2,1)}, bf16[1024,384]{1,0:T(8,128)(2,1)}, u32[]{:S(2)}, u32[]{:S(2)}) collective-permute-start(bf16[1024,384]{1,0:T(8,128)(2,1)} %collective-permute-done.21.refs_10_), channel_id=1, source_target_pairs={{0,8},{1,9},{2,10},{3,11},{4,12},{5,13},{6,14},{7,15},{8,0},{9,1},... | collective-permute-start | bytes 2359304 | tf_op jit(solution)/shard_map/ppermute | solution.py:42
  119.3 3.4 %collective-permute-start.27 = (bf16[1024,384]{1,0:T(8,128)(2,1)}, bf16[1024,384]{1,0:T(8,128)(2,1)}, u32[]{:S(2)}, u32[]{:S(2)}) collective-permute-start(bf16[1024,384]{1,0:T(8,128)(2,1)} %collective-permute-done.23.refs_12_), channel_id=1, source_target_pairs={{0,8},{1,9},{2,10},{3,11},{4,12},{5,13},{6,14},{7,15},{8,0},{9,1},... | collective-permute-start | bytes 2359304 | tf_op jit(solution)/shard_map/ppermute | solution.py:42
  121.2 27.5 %collective-permute-start.17 = (bf16[1024,384]{1,0:T(8,128)(2,1)S(1)}, bf16[1024,384]{1,0:T(8,128)(2,1)S(1)}, u32[]{:S(2)}, u32[]{:S(2)}) collective-permute-start(bf16[1024,384]{1,0:T(8,128)(2,1)S(1)} %pad_maximum_fusion.refs_9_), channel_id=1, source_target_pairs={{0,8},{1,9},{2,10},{3,11},{4,12},{5,13},{6,14},{7,15},{8,0},{9,1},... | collective-permute-start | bytes 2359304 | tf_op jit(solution)/shard_map/ppermute | solution.py:42
  121.8 26.9 %collective-permute-start.18 = (bf16[1024,384]{1,0:T(8,128)(2,1)}, bf16[1024,384]{1,0:T(8,128)(2,1)S(1)}, u32[]{:S(2)}, u32[]{:S(2)}) collective-permute-start(bf16[1024,384]{1,0:T(8,128)(2,1)} %collective-permute-done.14.refs_10_), channel_id=1, source_target_pairs={{0,8},{1,9},{2,10},{3,11},{4,12},{5,13},{6,14},{7,15},{8,0},{9,1},... | collective-permute-start | bytes 2359304 | tf_op jit(solution)/shard_map/ppermute | solution.py:42
  122.0 26.8 %collective-permute-start.19 = (bf16[1024,384]{1,0:T(8,128)(2,1)}, bf16[1024,384]{1,0:T(8,128)(2,1)S(1)}, u32[]{:S(2)}, u32[]{:S(2)}) collective-permute-start(bf16[1024,384]{1,0:T(8,128)(2,1)} %collective-permute-done.15.refs_11_), channel_id=1, source_target_pairs={{0,8},{1,9},{2,10},{3,11},{4,12},{5,13},{6,14},{7,15},{8,0},{9,1},... | collective-permute-start | bytes 2359304 | tf_op jit(solution)/shard_map/ppermute | solution.py:42
  122.3 26.4 %collective-permute-start.20 = (bf16[1024,384]{1,0:T(8,128)(2,1)}, bf16[1024,384]{1,0:T(8,128)(2,1)S(1)}, u32[]{:S(2)}, u32[]{:S(2)}) collective-permute-start(bf16[1024,384]{1,0:T(8,128)(2,1)} %collective-permute-done.16.refs_12_), channel_id=1, source_target_pairs={{0,8},{1,9},{2,10},{3,11},{4,12},{5,13},{6,14},{7,15},{8,0},{9,1},... | collective-permute-start | bytes 2359304 | tf_op jit(solution)/shard_map/ppermute | solution.py:42
  122.7 1.1 copy-start.6
  123.9 1.2 copy-start.12
  125.1 1.2 copy-start.14
  126.3 1.2 copy-start.16
  127.6 21.2 %copy-start.4 = (bf16[1024,384]{1,0:T(8,128)(2,1)S(1)}, bf16[1024,384]{1,0:T(8,128)(2,1)}, u32[]{:S(2)}) copy-start(bf16[1024,384]{1,0:T(8,128)(2,1)} %copy-done.3) | copy-start | bytes 2359300
  148.1 0.7 copy-start.7
  168.4 1.0 copy-start.1
  169.4 0.7 copy-start.9
  170.7 1.6 collective-permute-start.28
  173.7 3.1 %collective-permute-start.31 = (f32[16,512]{1,0:T(8,128)}, f32[16,512]{1,0:T(8,128)S(1)}, u32[]{:S(2)}, u32[]{:S(2)}) collective-permute-start(f32[16,512]{1,0:T(8,128)} %select_add_fusion), channel_id=1, source_target_pairs={{0,48},{1,49},{2,50},{3,51},{4,52},{5,53},{6,54},{7,55},{8,56},{9,... | collective-permute-start | bytes 98312 | tf_op jit(solution)/shard_map/ppermute | solution.py:42
  175.4 4.7 %collective-permute-start.30 = (f32[16,512]{1,0:T(8,128)}, f32[16,512]{1,0:T(8,128)}, u32[]{:S(2)}, u32[]{:S(2)}) collective-permute-start(f32[16,512]{1,0:T(8,128)} %select_add_fusion), channel_id=1, source_target_pairs={{0,32},{1,33},{2,34},{3,35},{4,36},{5,37},{6,38},{7,39},{8,40},{9,... | collective-permute-start | bytes 98312 | tf_op jit(solution)/shard_map/ppermute | solution.py:42
  175.5 4.6 %collective-permute-start.29 = (f32[16,512]{1,0:T(8,128)}, f32[16,512]{1,0:T(8,128)}, u32[]{:S(2)}, u32[]{:S(2)}) collective-permute-start(f32[16,512]{1,0:T(8,128)} %select_add_fusion), channel_id=1, source_target_pairs={{0,16},{1,17},{2,18},{3,19},{4,20},{5,21},{6,22},{7,23},{8,24},{9,... | collective-permute-start | bytes 98312 | tf_op jit(solution)/shard_map/ppermute | solution.py:42
  181.6 3.1 %collective-permute-start.32 = (f32[16,512]{1,0:T(8,128)}, f32[16,512]{1,0:T(8,128)}, u32[]{:S(2)}, u32[]{:S(2)}) collective-permute-start(f32[16,512]{1,0:T(8,128)} %multiply_add_fusion), channel_id=1, source_target_pairs={{0,64},{1,65},{2,66},{3,67},{4,68},{5,69},{6,70},{7,71},{8,72},{9,... | collective-permute-start | bytes 98312 | tf_op jit(solution)/shard_map/ppermute | solution.py:42
  185.5 1.2 copy-start.2
  186.8 0.9 copy-start.8
  187.7 0.9 copy-start.10

commit v2 on v1

v2 whole, which is shorter than its diff:
```python
import functools

import jax
import jax.numpy as jnp
from jax import lax
from jax.experimental import pallas as pl
from jax.experimental.pallas import tpu as pltpu
from jax.sharding import PartitionSpec as P

D = 4096
MODES = 16
BLOCK = 512
SEG = 8
HALO = 16
SIZES = (2, 4, 2, 2, 4)
LANES = 128
F32 = jnp.float32


def route(move):
    pairs = []
    for yl in range(2):
        for x in range(4):
            for c in range(2):
                for yh in range(2):
                    for z in range(4):
                        to = move(yl, x, c, yh, z)
                        if to is None:
                            continue
                        a, b, e, f, g = to
                        pairs.append(
                            (
                                ((yl * 4 + x) * 2 + c) * 8 + yh * 4 + z,
                                (((a % 2) * 4 + b % 4) * 2 + e % 2) * 8 + (f % 2) * 4 + g % 4,
                            )
                        )
    return pairs


def send(value, move):
    return lax.ppermute(value, ("ctx", "tp"), route(move))


def along_z(value, step):
    return send(value, lambda yl, x, c, yh, z: (yl, x, c, yh, z + step))


def along_x(value, step):
    return send(value, lambda yl, x, c, yh, z: (yl, x + step, c, yh, z))


def other_core(value):
    return send(value, lambda yl, x, c, yh, z: (yl, x, c + 1, yh, z))


def other_yhi(value):
    return send(value, lambda yl, x, c, yh, z: (yl, x, c, yh + 1, z))


def other_ylo(value):
    return send(value, lambda yl, x, c, yh, z: (yl + 1, x, c, yh, z))


def other_ylo_and_core(value):
    return send(value, lambda yl, x, c, yh, z: (yl + 1, x, c + 1, yh, z))


def transposed(value):
    return send(value, lambda yl, x, c, yh, z: (yh, x + z, c, yl, x))


together = lax.optimization_barrier


def shift_down(value, steps):
    rows = lax.broadcasted_iota(jnp.int32, value.shape, 0)
    return jnp.where(rows >= steps, pltpu.roll(value, steps, 0), 0.0)


def project_kernel(rows, *refs):
    where, *refs = refs
    toks, refs = refs[:8], refs[8:]
    weights, refs = refs[:8], refs[8:]
    prm, y_ref, x1_ref, u_ref, end_ref, lhs, wts, proj, sem_t, sem_w = refs
    seg_len = rows // SEG
    width = 3 * LANES
    copies = []
    for s in range(8):
        copies.append(
            pltpu.make_async_copy(toks[s], lhs.at[:, pl.ds(s * BLOCK, BLOCK)], sem_t.at[s])
        )
    for k in range(8):
        at = pl.multiple_of(where[k] * BLOCK, BLOCK)
        copies.append(pltpu.make_async_copy(weights[k], wts.at[pl.ds(at, BLOCK), :], sem_w.at[k]))
    for copy in copies:
        copy.start()
    for copy in copies:
        copy.wait()

    tile = (rows + HALO) // 5

    def matmul(m, carry):
        at = pl.ds(pl.multiple_of(m * tile, 16), tile)
        out = jnp.dot(lhs[at, :], wts[...], preferred_element_type=F32)
        out = out.astype(jnp.bfloat16).astype(F32)
        for n in range(6):
            proj[n, at, :] = out[:, n * LANES:(n + 1) * LANES]
        return carry

    lax.fori_loop(0, 5, matmul, 0)

    for q in range(2):
        lanes = pl.ds(q * LANES, LANES)
        bcast = lambda r: jnp.broadcast_to(prm[pl.ds(r, 1), lanes], (SEG, LANES))
        decay = [bcast(k) for k in range(MODES)]
        amp = [bcast(MODES + k) for k in range(MODES)]
        taps = [[bcast(2 * MODES + 3 * j + g) for g in range(3)] for j in range(3)]
        gain = bcast(2 * MODES + 9)

        def load(g, at):
            return proj[2 * g + q, pl.ds(at, SEG, stride=seg_len), :]

        def step(i, carry):
            before, last, states = carry
            now = [load(g, HALO + i) for g in range(3)]
            feat = [
                taps[0][g] * now[g] + taps[1][g] * last[g] + taps[2][g] * before[g]
                for g in range(3)
            ]
            product = feat[1] * feat[2]
            states = [decay[k] * states[k] + product for k in range(MODES)]
            terms = [amp[k] * states[k] for k in range(MODES)] + [gain * product]
            while len(terms) > 1:
                terms = [a + b for a, b in zip(terms[::2], terms[1::2])] + (
                    [terms[-1]] if len(terms) % 2 else []
                )
            at = pl.ds(pl.multiple_of(i * SEG, SEG), SEG)
            y_ref[at, lanes] = terms[0]
            x1_ref[at, lanes] = feat[0]
            return (last, now, states)

        zero = jnp.zeros((SEG, LANES), F32)
        first = ([load(g, HALO - 2) for g in range(3)], [load(g, HALO - 1) for g in range(3)])
        _, _, states = lax.fori_loop(0, seg_len, step, (*first, [zero] * MODES), unroll=4)
        for k in range(MODES):
            rate = prm[pl.ds(48 + k, 1), lanes]
            u = states[k]
            for n in (1, 2, 4):
                u = u + jnp.exp(-rate * (float(n) * seg_len)) * shift_down(u, n)
            u_ref[pl.ds(k * SEG, SEG), lanes] = u
            end_ref[pl.ds(k, 1), lanes] = u[SEG - 1:]


def project(where, toks, weights, prm, rows):
    any_spec = pl.BlockSpec(memory_space=pl.ANY)
    vmem = pl.BlockSpec(memory_space=pltpu.VMEM)
    wide = 2 * LANES
    return pl.pallas_call(
        functools.partial(project_kernel, rows),
        out_shape=[
            jax.ShapeDtypeStruct((rows, wide), F32),
            jax.ShapeDtypeStruct((rows, wide), F32),
            jax.ShapeDtypeStruct((MODES * SEG, wide), F32),
            jax.ShapeDtypeStruct((MODES, wide), F32),
        ],
        in_specs=[pl.BlockSpec(memory_space=pltpu.SMEM)] + [any_spec] * 16 + [vmem],
        out_specs=[vmem] * 4,
        scratch_shapes=[
            pltpu.VMEM((rows + HALO, D), jnp.bfloat16),
            pltpu.VMEM((D, 6 * LANES), jnp.bfloat16),
            pltpu.VMEM((6, rows + HALO, LANES), F32),
            pltpu.SemaphoreType.DMA((8,)),
            pltpu.SemaphoreType.DMA((8,)),
        ],
        compiler_params=pltpu.CompilerParams(vmem_limit_bytes=34 << 20),
        cost_estimate=pl.CostEstimate(
            flops=2 * rows * D * 6 * LANES, bytes_accessed=18 << 20, transcendentals=0
        ),
    )(where, *toks, *weights, prm)


def gate_kernel(rows, core_ref, y0, y1, x0, x1, u0, u1, p0, p1, near, sent, same, cross, fades,
                out_ref, ybuf, xbuf, wide, sem):
    seg_len = rows // SEG
    core = core_ref[0]
    copies = []
    for o, (y, x) in enumerate(((y0, x0), (y1, x1))):
        copies.append(
            (
                pltpu.make_async_copy(y, ybuf.at[o], sem.at[2 * o]),
                pltpu.make_async_copy(x, xbuf.at[o], sem.at[2 * o + 1]),
            )
        )
        for copy in copies[o]:
            copy.start()
    seg = lax.broadcasted_iota(jnp.int32, (SEG, LANES), 0).astype(F32) * seg_len
    for o, (u, prm) in enumerate(((u0, p0), (u1, p1))):
        base = lax.rem(core + o, 2) * (2 * LANES)
        for q in range(2):
            lanes = pl.ds(q * LANES, LANES)
            to = pl.ds(pl.multiple_of(base + q * LANES, LANES), LANES)
            shard, straight, across = (
                fades[pl.ds(n * MODES, MODES), to] for n in range(3)
            )
            state = (
                shard * near[:, to] + sent[:, to] + straight * same[:, to] + across * cross[:, to]
            )
            decay, carried = [], []
            for k in range(MODES):
                d = jnp.broadcast_to(prm[pl.ds(k, 1), lanes], (SEG, LANES))
                rate = prm[pl.ds(48 + k, 1), lanes]
                start = shift_down(u[pl.ds(k * SEG, SEG), lanes], 1)
                start = start + jnp.exp(-rate * seg) * state[k:k + 1]
                decay.append(d)
                carried.append(prm[pl.ds(MODES + k, 1), lanes] * d * start)
            if q == 0:
                for copy in copies[o]:
                    copy.wait()

            def step(i, carried):
                terms = list(carried)
                while len(terms) > 1:
                    terms = [a + b for a, b in zip(terms[::2], terms[1::2])]
                at = pl.ds(pl.multiple_of(i * SEG, SEG), SEG)
                wide[pl.ds(i, SEG, stride=seg_len), :] = xbuf[o, at, lanes] * (
                    ybuf[o, at, lanes] + terms[0]
                )
                return [c * d for c, d in zip(carried, decay)]

            lax.fori_loop(0, seg_len, step, carried, unroll=4)
            out_ref[:, to] = wide[...].astype(out_ref.dtype)


def gate(core, ys, xs, us, prms, state, rows):
    vmem = pl.BlockSpec(memory_space=pltpu.VMEM)
    anywhere = pl.BlockSpec(memory_space=pl.ANY)
    wide = 2 * LANES
    return pl.pallas_call(
        functools.partial(gate_kernel, rows),
        out_shape=jax.ShapeDtypeStruct((rows, BLOCK), jnp.bfloat16),
        in_specs=[pl.BlockSpec(memory_space=pltpu.SMEM)] + [anywhere] * 4 + [vmem] * 9,
        out_specs=vmem,
        scratch_shapes=[
            pltpu.VMEM((2, rows, wide), F32),
            pltpu.VMEM((2, rows, wide), F32),
            pltpu.VMEM((rows, LANES), F32),
            pltpu.SemaphoreType.DMA((4,)),
        ],
        compiler_params=pltpu.CompilerParams(vmem_limit_bytes=20 << 20),
    )(core, *ys, *xs, *us, *prms, *state)


def on_device(tokens, in_weight, short_filter, filter_residues, filter_rates, skip_gain):
    rows = tokens.shape[0]
    ctx, tp = lax.axis_index("ctx"), lax.axis_index("tp")
    y_lo, x, core = ctx // 8, (ctx // 2) % 4, ctx % 2
    y_hi, z = tp // 4, tp % 4
    wide = 2 * LANES

    base = tp * BLOCK
    rates = lax.dynamic_slice_in_dim(filter_rates, base, BLOCK, 0).T
    amps = lax.dynamic_slice_in_dim(filter_residues, base, BLOCK, 0).T * jnp.sqrt(rates)
    taps = lax.dynamic_slice_in_dim(short_filter, base, BLOCK, 2).reshape(9, BLOCK)
    gains = lax.dynamic_slice_in_dim(skip_gain, base, BLOCK, 0)[None]
    prm = jnp.concatenate(
        [jnp.exp(-rates), amps, taps, gains, jnp.zeros((6, BLOCK), F32), rates], axis=0
    )
    prms = [lax.dynamic_slice_in_dim(prm, (core + o) % 2 * wide, wide, 1) for o in range(2)]

    def fade(steps):
        return jnp.exp(-rates * jnp.asarray(steps).astype(F32))

    shard = fade(rows)
    behind = [jnp.where(x >= m, fade(2 * rows * (m - 1)), 0.0) for m in (1, 2, 3)]
    plane = [fade(2 * rows * (3 - (x - m) % 4)) for m in range(4)]
    chip = fade(2 * rows)
    lower = jnp.where(y_lo == 1, fade(2 * rows * x), 0.0)
    straight = lower * shard
    across = lower * jnp.where(core == 0, 1.0, shard * shard)
    fades = jnp.concatenate([shard, straight, across], axis=0)
    behind, plane = jnp.stack(behind), jnp.stack(plane)

    slots = []
    for of_y in (y_lo, 1 - y_lo):
        for ring in (0, -1, 1, 2):
            of_z = (x + ring - z) % 4
            step = (of_z - z) % 4
            place = jnp.where(step == 3, 1, jnp.where(step == 1, 2, jnp.where(step == 2, 3, 0)))
            slots.append(jnp.where(of_y == y_hi, 0, 4) + place)
    where = jnp.stack(slots + [core]).astype(jnp.int32)
    core_at = jnp.stack([core]).astype(jnp.int32)

    def next_ctx(yl, x, c, yh, z):
        n = (yl * 4 + x) * 2 + c + 1
        return None if n == 16 else (n // 8, (n // 2) % 4, n % 2, yh, z)

    halo = send(tokens[rows - HALO:], next_ctx)
    b = transposed(in_weight.reshape(BLOCK, 3 * wide))
    t = jnp.concatenate([halo, tokens], axis=0)
    t, b, where, core_at, fades, behind, plane, chip, *prms = together(
        (t, b, where, core_at, fades, behind, plane, chip, *prms)
    )
    tp_, tm, ty = along_z(t, 1), along_z(t, -1), other_yhi(t)
    bp, bm = along_x(b, 1), along_x(b, -1)
    t, b, tp_, tm, ty, bp, bm = together((t, b, tp_, tm, ty, bp, bm))
    typ, tym = along_z(ty, 1), along_z(ty, -1)
    bf, a = along_x(bp, 1), other_ylo(b)
    cb = other_core(b)
    t, b, tp_, tm, ty, bp, bm, typ, tym, bf, a, cb = together(
        (t, b, tp_, tm, ty, bp, bm, typ, tym, bf, a, cb)
    )
    tf, tyf = along_z(tp_, 1), along_z(tym, -1)
    ap, am, af = along_x(a, 1), along_x(a, -1), other_ylo(bf)
    b, bp, bm, bf, a, ap, am, af, tf, tyf = together((b, bp, bm, bf, a, ap, am, af, tf, tyf))
    toks = [t, tp_, tm, tf, ty, typ, tym, tyf]
    mine = [b, bp, bm, bf, a, ap, am, af]
    theirs = [cb] + [other_core(w) for w in mine[1:]]

    ys, xs, us, ends = [], [], [], []
    for o, weights in enumerate((mine, theirs)):
        y, x1, u, end = project(where, toks, weights, prms[o], rows)
        ys.append(y)
        xs.append(x1)
        us.append(u)
        ends.append(end)

    total = jnp.concatenate(
        [jnp.where(core == 0, ends[0], ends[1]), jnp.where(core == 0, ends[1], ends[0])], axis=1
    )
    came = [total] + [along_x(total, m) for m in (1, 2, 3)]
    near = behind[0] * came[1] + behind[1] * came[2] + behind[2] * came[3]
    whole = plane[0] * came[0] + plane[1] * came[1] + plane[2] * came[2] + plane[3] * came[3]
    sent = other_core(jnp.where(core == 0, chip * near + total, near))
    state = [near, sent, other_ylo(whole), other_ylo_and_core(whole), fades]
    return gate(core_at, ys, xs, us, prms, state, rows)


def solution(mesh):
    placed = (P("ctx", "tp"), P("tp", None, "ctx"), P(), P(), P(), P())
    return jax.shard_map(
        on_device, mesh=mesh, in_specs=placed, out_specs=P("ctx", "tp"), check_vma=False
    )
```

time: 197 us -> 165 us (0.84); the launches traced: 194 us -> 165 us
  waiting for transfers between devices: 78.7 us -> 65.5 us
  Pallas kernels: 45.9 us -> 34.3 us
  local copies, waits for them, and re-layouts: 14.7 us -> 4.08 us
  starting transfers between devices: 49.4 us -> 58.7 us
  other arithmetic: 5.26 us -> 1.72 us
    ppermute x33 -> x30, waiting for transfers between devices: 78.7 us -> 65.5 us  [send(): return lax.ppermute(value, ('ctx', 'tp'), route(move))]
    unnamed x43 -> x5, local copies, waits for them, and re-layouts: 12.6 us -> 1.42 us
    pallas_call x2, Pallas kernels: 40.1 us -> 29.7 us  [project(): pl.pallas_call(functools.partial(project_kernel, rows), out_shape=[jax.Sh...]
    ppermute x33 -> x30, starting transfers between devices: 49.4 us -> 58.7 us  [send(): return lax.ppermute(value, ('ctx', 'tp'), route(move))]
    add x2 -> x0, other arithmetic: 2.82 us -> none  [the longest x1 1.43 us: earlier_state(): plane = plane + fade(2 * rows * (3 - of)) * value]
  transfers between devices with their start and end apart: 33 -> 30, of which waited for: 14 -> 15; matrix products, arithmetic and copies ran while one was open for 1% -> 3% of each run, Pallas kernels for 11% -> 9%
where the time goes in v2:
time: 165 us
  waiting for transfers between devices  65.5 us (40%)
  starting transfers between devices  58.7 us (36%)
  Pallas kernels  34.3 us (21%)
  local copies, waits for them, and re-layouts  4.08 us (2%)
  other arithmetic  1.72 us (1%)
    ppermute x30, waiting for transfers between devices, send(): return lax.ppermute(value, ('ctx', 'tp'), route(move))  65.5 us
    ppermute x30, starting transfers between devices, send(): return lax.ppermute(value, ('ctx', 'tp'), route(move))  58.7 us
    pallas_call x2, Pallas kernels, project(): pl.pallas_call(functools.partial(project_kernel, rows), out_shape=[jax.Sh...  29.7 us
    pallas_call x1, Pallas kernels, gate(): pl.pallas_call(functools.partial(gate_kernel, rows), out_shape=jax.ShapeD...  4.57 us
  transfers between devices with their start and end apart: 30, of which 15 were waited for; matrix products, arithmetic and copies ran while one was open for 3% of the time, Pallas kernels for 9%

profile of v2, /device:TPU:1, one launch (start us, length us, event | category | flops | bytes accessed | tf_op | source)
XLA Modules:
  0.0 165.1 jit_solution(13456466935357441064)
XLA Ops:
  0.0 1.4 slice.24
  1.4 4.5 %collective-permute-start = (bf16[16,512]{1,0:T(8,128)(2,1)}, bf16[16,512]{1,0:T(8,128)(2,1)}, u32[]{:S(2)}, u32[]{:S(2)}) collective-permute-start(bf16[16,512]{1,0:T(8,128)(2,1)} %slice.24), channel_id=1, source_target_pairs={{0,8},{1,9},{2,10},{3,11},{4,12},{5,13},{6,14},{7,15},{8,16},{9,17... | collective-permute-start | bytes 49160 | tf_op jit(solution)/shard_map/ppermute | solution.py:41
  5.9 1.4 copy.8
  7.3 0.3 copy.9
  7.6 0.7 collective-permute-start.1
  8.4 0.8 bitcast_multiply_fusion.7
  9.2 0.0 copy-start.1
  9.2 0.1 negate_exponential_fusion
  9.4 0.9 dynamic_slice.21
  10.6 0.1 stack.67.refs_0_
  10.6 0.0 collective-permute-done
  10.7 0.8 pad_maximum_fusion.refs_1_
  11.5 0.0 collective-permute-done.1.refs_9_
  11.5 21.2 %collective-permute-start.2 = (bf16[1040,512]{1,0:T(8,128)(2,1)S(1)}, bf16[1040,512]{1,0:T(8,128)(2,1)S(1)}, u32[]{:S(2)}, u32[]{:S(2)}) collective-permute-start(bf16[1040,512]{1,0:T(8,128)(2,1)S(1)} %pad_maximum_fusion.refs_1_), channel_id=1, source_target_pairs={{0,1},{1,2},{2,3},{3,0},{4,5},{5,6},{6,7},{7,4},{8,9},{9,10},{10,1... | collective-permute-start | bytes 3194888 | tf_op jit(solution)/shard_map/ppermute | solution.py:41
  32.6 3.3 %collective-permute-start.3 = (bf16[1040,512]{1,0:T(8,128)(2,1)S(1)}, bf16[1040,512]{1,0:T(8,128)(2,1)S(1)}, u32[]{:S(2)}, u32[]{:S(2)}) collective-permute-start(bf16[1040,512]{1,0:T(8,128)(2,1)S(1)} %pad_maximum_fusion.refs_1_), channel_id=1, source_target_pairs={{0,3},{1,0},{2,1},{3,2},{4,7},{5,4},{6,5},{7,6},{8,11},{9,8},{10,9... | collective-permute-start | bytes 3194888 | tf_op jit(solution)/shard_map/ppermute | solution.py:41
  36.0 3.8 %collective-permute-start.4 = (bf16[1040,512]{1,0:T(8,128)(2,1)S(1)}, bf16[1040,512]{1,0:T(8,128)(2,1)S(1)}, u32[]{:S(2)}, u32[]{:S(2)}) collective-permute-start(bf16[1040,512]{1,0:T(8,128)(2,1)S(1)} %pad_maximum_fusion.refs_1_), channel_id=1, source_target_pairs={{0,4},{1,5},{2,6},{3,7},{4,0},{5,1},{6,2},{7,3},{8,12},{9,13},{10,... | collective-permute-start | bytes 3194888 | tf_op jit(solution)/shard_map/ppermute | solution.py:41
  39.8 0.0 collective-permute-start.5
  39.8 2.7 %collective-permute-start.6 = (bf16[512,768]{1,0:T(8,128)(2,1)S(1)}, bf16[512,768]{1,0:T(8,128)(2,1)S(1)}, u32[]{:S(2)}, u32[]{:S(2)}) collective-permute-start(bf16[512,768]{1,0:T(8,128)(2,1)S(1)} %collective-permute-done.1.refs_9_), channel_id=1, source_target_pairs={{0,48},{1,49},{2,50},{3,51},{4,52},{5,53},{6,54},{7,55},{8,56},{9,... | collective-permute-start | bytes 2359304 | tf_op jit(solution)/shard_map/ppermute | solution.py:41
  42.4 16.6 %collective-permute-done.5.refs_10_ = bf16[512,768]{1,0:T(8,128)(2,1)S(1)} collective-permute-done((bf16[512,768]{1,0:T(8,128)(2,1)S(1)}, bf16[512,768]{1,0:T(8,128)(2,1)S(1)}, u32[]{:S(2)}, u32[]{:S(2)}) %collective-permute-start.5) | collective-permute-done | bytes 786464 | tf_op jit(solution)/shard_map/ppermute | solution.py:41
  59.1 0.4 collective-permute-done.2.refs_2_
  59.5 0.0 collective-permute-done.3.refs_3_
  59.5 3.5 %collective-permute-done.4.refs_5_ = bf16[1040,512]{1,0:T(8,128)(2,1)S(1)} collective-permute-done((bf16[1040,512]{1,0:T(8,128)(2,1)S(1)}, bf16[1040,512]{1,0:T(8,128)(2,1)S(1)}, u32[]{:S(2)}, u32[]{:S(2)}) %collective-permute-start.4) | collective-permute-done | bytes 1064992 | tf_op jit(solution)/shard_map/ppermute | solution.py:41
  63.0 2.7 %collective-permute-start.8 = (bf16[1040,512]{1,0:T(8,128)(2,1)S(1)}, bf16[1040,512]{1,0:T(8,128)(2,1)S(1)}, u32[]{:S(2)}, u32[]{:S(2)}) collective-permute-start(bf16[1040,512]{1,0:T(8,128)(2,1)S(1)} %collective-permute-done.4.refs_5_), channel_id=1, source_target_pairs={{0,3},{1,0},{2,1},{3,2},{4,7},{5,4},{6,5},{7,6},{8,11},{9,8},{10,9... | collective-permute-start | bytes 3194888 | tf_op jit(solution)/shard_map/ppermute | solution.py:41
  65.7 0.0 collective-permute-start.9
  65.7 0.8 collective-permute-start.10
  66.5 2.4 %collective-permute-start.11 = (bf16[512,768]{1,0:T(8,128)(2,1)S(1)}, bf16[512,768]{1,0:T(8,128)(2,1)S(1)}, u32[]{:S(2)}, u32[]{:S(2)}) collective-permute-start(bf16[512,768]{1,0:T(8,128)(2,1)S(1)} %collective-permute-done.1.refs_9_), channel_id=1, source_target_pairs={{0,8},{1,9},{2,10},{3,11},{4,12},{5,13},{6,14},{7,15},{8,0},{9,1},... | collective-permute-start | bytes 2359304 | tf_op jit(solution)/shard_map/ppermute | solution.py:41
  68.9 15.2 %collective-permute-done.9.refs_12_ = bf16[512,768]{1,0:T(8,128)(2,1)S(1)} collective-permute-done((bf16[512,768]{1,0:T(8,128)(2,1)S(1)}, bf16[512,768]{1,0:T(8,128)(2,1)S(1)}, u32[]{:S(2)}, u32[]{:S(2)}) %collective-permute-start.9) | collective-permute-done | bytes 786464 | tf_op jit(solution)/shard_map/ppermute | solution.py:41
  84.1 3.8 %collective-permute-done.7.refs_6_ = bf16[1040,512]{1,0:T(8,128)(2,1)S(1)} collective-permute-done((bf16[1040,512]{1,0:T(8,128)(2,1)S(1)}, bf16[1040,512]{1,0:T(8,128)(2,1)S(1)}, u32[]{:S(2)}, u32[]{:S(2)}) %collective-permute-start.7) | collective-permute-done | bytes 1064992 | tf_op jit(solution)/shard_map/ppermute | solution.py:41
  88.0 0.0 collective-permute-done.8.refs_7_
  88.0 0.0 collective-permute-start.15
  88.0 2.7 %collective-permute-start.16 = (bf16[1040,512]{1,0:T(8,128)(2,1)S(1)}, bf16[1040,512]{1,0:T(8,128)(2,1)S(1)}, u32[]{:S(2)}, u32[]{:S(2)}) collective-permute-start(bf16[1040,512]{1,0:T(8,128)(2,1)S(1)} %collective-permute-done.8.refs_7_), channel_id=1, source_target_pairs={{0,3},{1,0},{2,1},{3,2},{4,7},{5,4},{6,5},{7,6},{8,11},{9,8},{10,9... | collective-permute-start | bytes 3194888 | tf_op jit(solution)/shard_map/ppermute | solution.py:41
  90.7 0.1 collective-permute-start.12
  90.8 2.6 %collective-permute-start.13 = (bf16[512,768]{1,0:T(8,128)(2,1)S(1)}, bf16[512,768]{1,0:T(8,128)(2,1)S(1)}, u32[]{:S(2)}, u32[]{:S(2)}) collective-permute-start(bf16[512,768]{1,0:T(8,128)(2,1)S(1)} %collective-permute-done.10.refs_13_), channel_id=1, source_target_pairs={{0,48},{1,49},{2,50},{3,51},{4,52},{5,53},{6,54},{7,55},{8,56},{9,... | collective-permute-start | bytes 2359304 | tf_op jit(solution)/shard_map/ppermute | solution.py:41
  93.3 0.8 collective-permute-start.14
  94.1 14.1 %collective-permute-done.12.refs_14_ = bf16[512,768]{1,0:T(8,128)(2,1)S(1)} collective-permute-done((bf16[512,768]{1,0:T(8,128)(2,1)S(1)}, bf16[512,768]{1,0:T(8,128)(2,1)S(1)}, u32[]{:S(2)}, u32[]{:S(2)}) %collective-permute-start.12) | collective-permute-done | bytes 786464 | tf_op jit(solution)/shard_map/ppermute | solution.py:41
  108.2 0.0 collective-permute-done.13.refs_15_
  108.2 0.9 collective-permute-done.14.refs_16_
  109.1 2.9 %collective-permute-done.15.refs_4_ = bf16[1040,512]{1,0:T(8,128)(2,1)S(1)} collective-permute-done((bf16[1040,512]{1,0:T(8,128)(2,1)S(1)}, bf16[1040,512]{1,0:T(8,128)(2,1)S(1)}, u32[]{:S(2)}, u32[]{:S(2)}) %collective-permute-start.15) | collective-permute-done | bytes 1064992 | tf_op jit(solution)/shard_map/ppermute | solution.py:41
  112.1 0.0 collective-permute-done.16.refs_8_
  112.1 3.1 %collective-permute-start.17 = (bf16[512,768]{1,0:T(8,128)(2,1)S(1)}, bf16[512,768]{1,0:T(8,128)(2,1)S(1)}, u32[]{:S(2)}, u32[]{:S(2)}) collective-permute-start(bf16[512,768]{1,0:T(8,128)(2,1)S(1)} %collective-permute-done.5.refs_10_), channel_id=1, source_target_pairs={{0,8},{1,9},{2,10},{3,11},{4,12},{5,13},{6,14},{7,15},{8,0},{9,1},... | collective-permute-start | bytes 2359304 | tf_op jit(solution)/shard_map/ppermute | solution.py:41
  115.1 0.0 collective-permute-start.18
  115.1 0.5 collective-permute-start.19
  115.6 0.0 collective-permute-start.20
  115.6 0.5 collective-permute-start.21
  116.2 0.9 collective-permute-done.17.refs_10_
  117.0 0.4 collective-permute-start.22
  117.4 0.8 collective-permute-done.18.refs_11_
  118.2 0.4 collective-permute-start.23
  118.5 14.9 %shard_map.64 = (f32[1024,256]{1,0:T(8,128)S(1)}, f32[1024,256]{1,0:T(8,128)S(1)}, f32[128,256]{1,0:T(8,128)S(1)}, f32[16,256]{1,0:T(8,128)S(1)}) custom-call(s32[9]{0:T(128)S(1)} %stack.67.refs_0_, bf16[1040,512]{1,0:T(8,128)(2,1)S(1)} %pad_maximum_fusion.refs_1_, bf16[1040,512]{1,0:T(8,128)(2,1)S(1)} %collective-permute-done.2.refs_2_, ...), custom_call_target="tpu_custom_call" | custom-call | flops 6442450944 | bytes 18874368 | tf_op jit(solution)/shard_map/pallas_call | solution.py:158
  133.4 0.0 collective-permute-done.19.refs_12_
  133.4 0.0 collective-permute-done.22.refs_15_
  133.4 0.0 collective-permute-done.23.refs_16_
  133.5 14.9 %shard_map.65 = (f32[1024,256]{1,0:T(8,128)S(1)}, f32[1024,256]{1,0:T(8,128)S(1)}, f32[128,256]{1,0:T(8,128)S(1)}, f32[16,256]{1,0:T(8,128)S(1)}) custom-call(s32[9]{0:T(128)S(1)} %stack.67.refs_0_, bf16[1040,512]{1,0:T(8,128)(2,1)S(1)} %pad_maximum_fusion.refs_1_, bf16[1040,512]{1,0:T(8,128)(2,1)S(1)} %collective-permute-done.2.refs_2_, ...), custom_call_target="tpu_custom_call" | custom-call | flops 6442450944 | bytes 18874368 | tf_op jit(solution)/shard_map/pallas_call | solution.py:158
  148.4 0.1 collective-permute-start.26
  148.5 1.8 %collective-permute-start.25 = (f32[16,512]{1,0:T(8,128)S(1)}, f32[16,512]{1,0:T(8,128)S(1)}, u32[]{:S(2)}, u32[]{:S(2)}) collective-permute-start(f32[16,512]{1,0:T(8,128)S(1)} %pad_maximum_fusion.4), channel_id=1, source_target_pairs={{0,32},{1,33},{2,34},{3,35},{4,36},{5,37},{6,38},{7,39},{8,40},{9,... | collective-permute-start | bytes 98312 | tf_op jit(solution)/shard_map/ppermute | solution.py:41
  150.3 0.9 collective-permute-done.26
  151.2 1.6 collective-permute-done.25
  152.8 1.5 collective-permute-done.24
  154.3 1.9 %collective-permute-start.27 = (f32[16,512]{1,0:T(8,128)S(1)}, f32[16,512]{1,0:T(8,128)S(1)}, u32[]{:S(2)}, u32[]{:S(2)}) collective-permute-start(f32[16,512]{1,0:T(8,128)S(1)} %get-tuple-element.99), channel_id=1, source_target_pairs={{0,8},{1,9},{2,10},{3,11},{4,12},{5,13},{6,14},{7,15},{8,0},{9,1},... | collective-permute-start | bytes 98312 | tf_op jit(solution)/shard_map/ppermute | solution.py:41
  156.3 0.7 collective-permute-start.28
  157.0 1.0 collective-permute-start.29
  158.0 1.1 collective-permute-done.28.same
  159.0 1.3 collective-permute-done.29.cross
  160.3 4.6 %shard_map.66 = bf16[1024,512]{1,0:T(8,128)(2,1)} custom-call(s32[1]{0:T(128)} %bitcast.9.core_ref, f32[1024,256]{1,0:T(8,128)S(1)} %get-tuple-element.85.y0, f32[1024,256]{1,0:T(8,128)S(1)} %get-tuple-element.88.y1, f32[1024,256]{1,0:T(8,128)S(1)} %get-tuple-element.89.x0, f32[1024,256]{1,0:T(8,128)S(1)} %get-tuple-element.90.x1, ...), custom_call_target="tpu_custom_call" | custom-call | tf_op jit(solution)/shard_map/pallas_call | solution.py:238
  (22 shorter events, 0.2 us)
Async XLA Ops:
  0.0 9.3 %copy-start = (f32[3,3,4096]{2,1,0:T(4,128)S(1)}, f32[3,3,4096]{2,1,0:T(4,128)}, u32[]{:S(2)}) copy-start(f32[3,3,4096]{2,1,0:T(4,128)} %param.8) | copy-start | bytes 442372
  1.4 9.3 %collective-permute-start = (bf16[16,512]{1,0:T(8,128)(2,1)}, bf16[16,512]{1,0:T(8,128)(2,1)}, u32[]{:S(2)}, u32[]{:S(2)}) collective-permute-start(bf16[16,512]{1,0:T(8,128)(2,1)} %slice.24), channel_id=1, source_target_pairs={{0,8},{1,9},{2,10},{3,11},{4,12},{5,13},{6,14},{7,15},{8,16},{9,17... | collective-permute-start | bytes 49160 | tf_op jit(solution)/shard_map/ppermute | solution.py:41
  7.6 3.9 %collective-permute-start.1 = (bf16[512,768]{1,0:T(8,128)(2,1)S(1)}, bf16[512,768]{1,0:T(8,128)(2,1)S(1)}, u32[]{:S(2)}, u32[]{:S(2)}) collective-permute-start(bf16[512,768]{1,0:T(8,128)(2,1)S(1)} %copy.9), channel_id=1, source_target_pairs={{0,0},{1,16},{2,32},{3,48},{4,64},{5,80},{6,96},{7,112},{8,8},{9,2... | collective-permute-start | bytes 2359304 | tf_op jit(solution)/shard_map/ppermute | solution.py:41
  9.2 1.4 copy-start.1
  11.5 48.0 %collective-permute-start.2 = (bf16[1040,512]{1,0:T(8,128)(2,1)S(1)}, bf16[1040,512]{1,0:T(8,128)(2,1)S(1)}, u32[]{:S(2)}, u32[]{:S(2)}) collective-permute-start(bf16[1040,512]{1,0:T(8,128)(2,1)S(1)} %pad_maximum_fusion.refs_1_), channel_id=1, source_target_pairs={{0,1},{1,2},{2,3},{3,0},{4,5},{5,6},{6,7},{7,4},{8,9},{9,10},{10,1... | collective-permute-start | bytes 3194888 | tf_op jit(solution)/shard_map/ppermute | solution.py:41
  32.6 26.9 %collective-permute-start.3 = (bf16[1040,512]{1,0:T(8,128)(2,1)S(1)}, bf16[1040,512]{1,0:T(8,128)(2,1)S(1)}, u32[]{:S(2)}, u32[]{:S(2)}) collective-permute-start(bf16[1040,512]{1,0:T(8,128)(2,1)S(1)} %pad_maximum_fusion.refs_1_), channel_id=1, source_target_pairs={{0,3},{1,0},{2,1},{3,2},{4,7},{5,4},{6,5},{7,6},{8,11},{9,8},{10,9... | collective-permute-start | bytes 3194888 | tf_op jit(solution)/shard_map/ppermute | solution.py:41
  36.0 27.0 %collective-permute-start.4 = (bf16[1040,512]{1,0:T(8,128)(2,1)S(1)}, bf16[1040,512]{1,0:T(8,128)(2,1)S(1)}, u32[]{:S(2)}, u32[]{:S(2)}) collective-permute-start(bf16[1040,512]{1,0:T(8,128)(2,1)S(1)} %pad_maximum_fusion.refs_1_), channel_id=1, source_target_pairs={{0,4},{1,5},{2,6},{3,7},{4,0},{5,1},{6,2},{7,3},{8,12},{9,13},{10,... | collective-permute-start | bytes 3194888 | tf_op jit(solution)/shard_map/ppermute | solution.py:41
  39.8 19.3 %collective-permute-start.5 = (bf16[512,768]{1,0:T(8,128)(2,1)S(1)}, bf16[512,768]{1,0:T(8,128)(2,1)S(1)}, u32[]{:S(2)}, u32[]{:S(2)}) collective-permute-start(bf16[512,768]{1,0:T(8,128)(2,1)S(1)} %collective-permute-done.1.refs_9_), channel_id=1, source_target_pairs={{0,16},{1,17},{2,18},{3,19},{4,20},{5,21},{6,22},{7,23},{8,24},{9,... | collective-permute-start | bytes 2359304 | tf_op jit(solution)/shard_map/ppermute | solution.py:41
  39.8 19.3 %collective-permute-start.6 = (bf16[512,768]{1,0:T(8,128)(2,1)S(1)}, bf16[512,768]{1,0:T(8,128)(2,1)S(1)}, u32[]{:S(2)}, u32[]{:S(2)}) collective-permute-start(bf16[512,768]{1,0:T(8,128)(2,1)S(1)} %collective-permute-done.1.refs_9_), channel_id=1, source_target_pairs={{0,48},{1,49},{2,50},{3,51},{4,52},{5,53},{6,54},{7,55},{8,56},{9,... | collective-permute-start | bytes 2359304 | tf_op jit(solution)/shard_map/ppermute | solution.py:41
  63.0 25.0 %collective-permute-start.7 = (bf16[1040,512]{1,0:T(8,128)(2,1)S(1)}, bf16[1040,512]{1,0:T(8,128)(2,1)S(1)}, u32[]{:S(2)}, u32[]{:S(2)}) collective-permute-start(bf16[1040,512]{1,0:T(8,128)(2,1)S(1)} %collective-permute-done.4.refs_5_), channel_id=1, source_target_pairs={{0,1},{1,2},{2,3},{3,0},{4,5},{5,6},{6,7},{7,4},{8,9},{9,10},{10,1... | collective-permute-start | bytes 3194888 | tf_op jit(solution)/shard_map/ppermute | solution.py:41
  63.0 25.0 %collective-permute-start.8 = (bf16[1040,512]{1,0:T(8,128)(2,1)S(1)}, bf16[1040,512]{1,0:T(8,128)(2,1)S(1)}, u32[]{:S(2)}, u32[]{:S(2)}) collective-permute-start(bf16[1040,512]{1,0:T(8,128)(2,1)S(1)} %collective-permute-done.4.refs_5_), channel_id=1, source_target_pairs={{0,3},{1,0},{2,1},{3,2},{4,7},{5,4},{6,5},{7,6},{8,11},{9,8},{10,9... | collective-permute-start | bytes 3194888 | tf_op jit(solution)/shard_map/ppermute | solution.py:41
  65.7 18.5 %collective-permute-start.9 = (bf16[512,768]{1,0:T(8,128)(2,1)S(1)}, bf16[512,768]{1,0:T(8,128)(2,1)S(1)}, u32[]{:S(2)}, u32[]{:S(2)}) collective-permute-start(bf16[512,768]{1,0:T(8,128)(2,1)S(1)} %collective-permute-done.5.refs_10_), channel_id=1, source_target_pairs={{0,16},{1,17},{2,18},{3,19},{4,20},{5,21},{6,22},{7,23},{8,24},{9,... | collective-permute-start | bytes 2359304 | tf_op jit(solution)/shard_map/ppermute | solution.py:41
  65.7 18.5 %collective-permute-start.10 = (bf16[512,768]{1,0:T(8,128)(2,1)S(1)}, bf16[512,768]{1,0:T(8,128)(2,1)S(1)}, u32[]{:S(2)}, u32[]{:S(2)}) collective-permute-start(bf16[512,768]{1,0:T(8,128)(2,1)S(1)} %collective-permute-done.1.refs_9_), channel_id=1, source_target_pairs={{0,64},{1,65},{2,66},{3,67},{4,68},{5,69},{6,70},{7,71},{8,72},{9,... | collective-permute-start | bytes 2359304 | tf_op jit(solution)/shard_map/ppermute | solution.py:41
  66.5 17.6 %collective-permute-start.11 = (bf16[512,768]{1,0:T(8,128)(2,1)S(1)}, bf16[512,768]{1,0:T(8,128)(2,1)S(1)}, u32[]{:S(2)}, u32[]{:S(2)}) collective-permute-start(bf16[512,768]{1,0:T(8,128)(2,1)S(1)} %collective-permute-done.1.refs_9_), channel_id=1, source_target_pairs={{0,8},{1,9},{2,10},{3,11},{4,12},{5,13},{6,14},{7,15},{8,0},{9,1},... | collective-permute-start | bytes 2359304 | tf_op jit(solution)/shard_map/ppermute | solution.py:41
  88.0 24.1 %collective-permute-start.15 = (bf16[1040,512]{1,0:T(8,128)(2,1)S(1)}, bf16[1040,512]{1,0:T(8,128)(2,1)S(1)}, u32[]{:S(2)}, u32[]{:S(2)}) collective-permute-start(bf16[1040,512]{1,0:T(8,128)(2,1)S(1)} %collective-permute-done.2.refs_2_), channel_id=1, source_target_pairs={{0,1},{1,2},{2,3},{3,0},{4,5},{5,6},{6,7},{7,4},{8,9},{9,10},{10,1... | collective-permute-start | bytes 3194888 | tf_op jit(solution)/shard_map/ppermute | solution.py:41
  88.0 24.1 %collective-permute-start.16 = (bf16[1040,512]{1,0:T(8,128)(2,1)S(1)}, bf16[1040,512]{1,0:T(8,128)(2,1)S(1)}, u32[]{:S(2)}, u32[]{:S(2)}) collective-permute-start(bf16[1040,512]{1,0:T(8,128)(2,1)S(1)} %collective-permute-done.8.refs_7_), channel_id=1, source_target_pairs={{0,3},{1,0},{2,1},{3,2},{4,7},{5,4},{6,5},{7,6},{8,11},{9,8},{10,9... | collective-permute-start | bytes 3194888 | tf_op jit(solution)/shard_map/ppermute | solution.py:41
  90.7 17.5 %collective-permute-start.12 = (bf16[512,768]{1,0:T(8,128)(2,1)S(1)}, bf16[512,768]{1,0:T(8,128)(2,1)S(1)}, u32[]{:S(2)}, u32[]{:S(2)}) collective-permute-start(bf16[512,768]{1,0:T(8,128)(2,1)S(1)} %collective-permute-done.10.refs_13_), channel_id=1, source_target_pairs={{0,16},{1,17},{2,18},{3,19},{4,20},{5,21},{6,22},{7,23},{8,24},{9,... | collective-permute-start | bytes 2359304 | tf_op jit(solution)/shard_map/ppermute | solution.py:41
  90.8 17.4 %collective-permute-start.13 = (bf16[512,768]{1,0:T(8,128)(2,1)S(1)}, bf16[512,768]{1,0:T(8,128)(2,1)S(1)}, u32[]{:S(2)}, u32[]{:S(2)}) collective-permute-start(bf16[512,768]{1,0:T(8,128)(2,1)S(1)} %collective-permute-done.10.refs_13_), channel_id=1, source_target_pairs={{0,48},{1,49},{2,50},{3,51},{4,52},{5,53},{6,54},{7,55},{8,56},{9,... | collective-permute-start | bytes 2359304 | tf_op jit(solution)/shard_map/ppermute | solution.py:41
  93.3 15.8 %collective-permute-start.14 = (bf16[512,768]{1,0:T(8,128)(2,1)S(1)}, bf16[512,768]{1,0:T(8,128)(2,1)S(1)}, u32[]{:S(2)}, u32[]{:S(2)}) collective-permute-start(bf16[512,768]{1,0:T(8,128)(2,1)S(1)} %collective-permute-done.9.refs_12_), channel_id=1, source_target_pairs={{0,64},{1,65},{2,66},{3,67},{4,68},{5,69},{6,70},{7,71},{8,72},{9,... | collective-permute-start | bytes 2359304 | tf_op jit(solution)/shard_map/ppermute | solution.py:41
  112.1 5.0 %collective-permute-start.17 = (bf16[512,768]{1,0:T(8,128)(2,1)S(1)}, bf16[512,768]{1,0:T(8,128)(2,1)S(1)}, u32[]{:S(2)}, u32[]{:S(2)}) collective-permute-start(bf16[512,768]{1,0:T(8,128)(2,1)S(1)} %collective-permute-done.5.refs_10_), channel_id=1, source_target_pairs={{0,8},{1,9},{2,10},{3,11},{4,12},{5,13},{6,14},{7,15},{8,0},{9,1},... | collective-permute-start | bytes 2359304 | tf_op jit(solution)/shard_map/ppermute | solution.py:41
  115.1 3.0 %collective-permute-start.18 = (bf16[512,768]{1,0:T(8,128)(2,1)S(1)}, bf16[512,768]{1,0:T(8,128)(2,1)S(1)}, u32[]{:S(2)}, u32[]{:S(2)}) collective-permute-start(bf16[512,768]{1,0:T(8,128)(2,1)S(1)} %collective-permute-done.6.refs_11_), channel_id=1, source_target_pairs={{0,8},{1,9},{2,10},{3,11},{4,12},{5,13},{6,14},{7,15},{8,0},{9,1},... | collective-permute-start | bytes 2359304 | tf_op jit(solution)/shard_map/ppermute | solution.py:41
  115.1 18.3 %collective-permute-start.19 = (bf16[512,768]{1,0:T(8,128)(2,1)S(1)}, bf16[512,768]{1,0:T(8,128)(2,1)S(1)}, u32[]{:S(2)}, u32[]{:S(2)}) collective-permute-start(bf16[512,768]{1,0:T(8,128)(2,1)S(1)} %collective-permute-done.9.refs_12_), channel_id=1, source_target_pairs={{0,8},{1,9},{2,10},{3,11},{4,12},{5,13},{6,14},{7,15},{8,0},{9,1},... | collective-permute-start | bytes 2359304 | tf_op jit(solution)/shard_map/ppermute | solution.py:41
  115.6 17.8 %collective-permute-start.20 = (bf16[512,768]{1,0:T(8,128)(2,1)S(1)}, bf16[512,768]{1,0:T(8,128)(2,1)S(1)}, u32[]{:S(2)}, u32[]{:S(2)}) collective-permute-start(bf16[512,768]{1,0:T(8,128)(2,1)S(1)} %collective-permute-done.10.refs_13_), channel_id=1, source_target_pairs={{0,8},{1,9},{2,10},{3,11},{4,12},{5,13},{6,14},{7,15},{8,0},{9,1},... | collective-permute-start | bytes 2359304 | tf_op jit(solution)/shard_map/ppermute | solution.py:41
  115.6 17.8 %collective-permute-start.21 = (bf16[512,768]{1,0:T(8,128)(2,1)S(1)}, bf16[512,768]{1,0:T(8,128)(2,1)S(1)}, u32[]{:S(2)}, u32[]{:S(2)}) collective-permute-start(bf16[512,768]{1,0:T(8,128)(2,1)S(1)} %collective-permute-done.12.refs_14_), channel_id=1, source_target_pairs={{0,8},{1,9},{2,10},{3,11},{4,12},{5,13},{6,14},{7,15},{8,0},{9,1},... | collective-permute-start | bytes 2359304 | tf_op jit(solution)/shard_map/ppermute | solution.py:41
  117.0 16.4 %collective-permute-start.22 = (bf16[512,768]{1,0:T(8,128)(2,1)S(1)}, bf16[512,768]{1,0:T(8,128)(2,1)S(1)}, u32[]{:S(2)}, u32[]{:S(2)}) collective-permute-start(bf16[512,768]{1,0:T(8,128)(2,1)S(1)} %collective-permute-done.13.refs_15_), channel_id=1, source_target_pairs={{0,8},{1,9},{2,10},{3,11},{4,12},{5,13},{6,14},{7,15},{8,0},{9,1},... | collective-permute-start | bytes 2359304 | tf_op jit(solution)/shard_map/ppermute | solution.py:41
  118.2 15.3 %collective-permute-start.23 = (bf16[512,768]{1,0:T(8,128)(2,1)S(1)}, bf16[512,768]{1,0:T(8,128)(2,1)S(1)}, u32[]{:S(2)}, u32[]{:S(2)}) collective-permute-start(bf16[512,768]{1,0:T(8,128)(2,1)S(1)} %collective-permute-done.14.refs_16_), channel_id=1, source_target_pairs={{0,8},{1,9},{2,10},{3,11},{4,12},{5,13},{6,14},{7,15},{8,0},{9,1},... | collective-permute-start | bytes 2359304 | tf_op jit(solution)/shard_map/ppermute | solution.py:41
  148.4 2.8 %collective-permute-start.26 = (f32[16,512]{1,0:T(8,128)S(1)}, f32[16,512]{1,0:T(8,128)S(1)}, u32[]{:S(2)}, u32[]{:S(2)}) collective-permute-start(f32[16,512]{1,0:T(8,128)S(1)} %pad_maximum_fusion.4), channel_id=1, source_target_pairs={{0,48},{1,49},{2,50},{3,51},{4,52},{5,53},{6,54},{7,55},{8,56},{9,... | collective-permute-start | bytes 98312 | tf_op jit(solution)/shard_map/ppermute | solution.py:41
  148.5 4.3 %collective-permute-start.25 = (f32[16,512]{1,0:T(8,128)S(1)}, f32[16,512]{1,0:T(8,128)S(1)}, u32[]{:S(2)}, u32[]{:S(2)}) collective-permute-start(f32[16,512]{1,0:T(8,128)S(1)} %pad_maximum_fusion.4), channel_id=1, source_target_pairs={{0,32},{1,33},{2,34},{3,35},{4,36},{5,37},{6,38},{7,39},{8,40},{9,... | collective-permute-start | bytes 98312 | tf_op jit(solution)/shard_map/ppermute | solution.py:41
  150.3 4.0 %collective-permute-start.24 = (f32[16,512]{1,0:T(8,128)S(1)}, f32[16,512]{1,0:T(8,128)S(1)}, u32[]{:S(2)}, u32[]{:S(2)}) collective-permute-start(f32[16,512]{1,0:T(8,128)S(1)} %pad_maximum_fusion.4), channel_id=1, source_target_pairs={{0,16},{1,17},{2,18},{3,19},{4,20},{5,21},{6,22},{7,23},{8,24},{9,... | collective-permute-start | bytes 98312 | tf_op jit(solution)/shard_map/ppermute | solution.py:41
  154.3 3.7 %collective-permute-start.27 = (f32[16,512]{1,0:T(8,128)S(1)}, f32[16,512]{1,0:T(8,128)S(1)}, u32[]{:S(2)}, u32[]{:S(2)}) collective-permute-start(f32[16,512]{1,0:T(8,128)S(1)} %get-tuple-element.99), channel_id=1, source_target_pairs={{0,8},{1,9},{2,10},{3,11},{4,12},{5,13},{6,14},{7,15},{8,0},{9,1},... | collective-permute-start | bytes 98312 | tf_op jit(solution)/shard_map/ppermute | solution.py:41
  156.3 2.8 %collective-permute-start.28 = (f32[16,512]{1,0:T(8,128)S(1)}, f32[16,512]{1,0:T(8,128)S(1)}, u32[]{:S(2)}, u32[]{:S(2)}) collective-permute-start(f32[16,512]{1,0:T(8,128)S(1)} %get-tuple-element.103), channel_id=1, source_target_pairs={{0,64},{1,65},{2,66},{3,67},{4,68},{5,69},{6,70},{7,71},{8,72},{9,... | collective-permute-start | bytes 98312 | tf_op jit(solution)/shard_map/ppermute | solution.py:41
  157.0 3.4 %collective-permute-start.29 = (f32[16,512]{1,0:T(8,128)S(1)}, f32[16,512]{1,0:T(8,128)S(1)}, u32[]{:S(2)}, u32[]{:S(2)}) collective-permute-start(f32[16,512]{1,0:T(8,128)S(1)} %get-tuple-element.103), channel_id=1, source_target_pairs={{0,72},{1,73},{2,74},{3,75},{4,76},{5,77},{6,78},{7,79},{8,64},{9,... | collective-permute-start | bytes 98312 | tf_op jit(solution)/shard_map/ppermute | solution.py:41

commit v3 on v2

--- a/solution.py
+++ b/solution.py
@@ -77,37 +77,122 @@
     return jnp.where(rows >= steps, pltpu.roll(value, steps, 0), 0.0)
 
 
-def project_kernel(rows, *refs):
-    where, *refs = refs
-    toks, refs = refs[:8], refs[8:]
+def row_tiles(rows, body):
+    tile = (rows + HALO) // 5
+
+    def step(m, carry):
+        body(pl.ds(pl.multiple_of(m * tile, 16), tile))
+        return carry
+
+    lax.fori_loop(0, 5, step, 0)
+
+
+def copy_rows(rows, target, source):
+    def body(at):
+        target[at, :] = source[at, :]
+
+    row_tiles(rows, body)
+
+
+def first_half(rows, where, lhs, weights, acc):
+    def clear(at):
+        acc[at, :] = jnp.zeros((at.size, acc.shape[1]), F32)
+
+    row_tiles(rows, clear)
+    for k in range(4):
+        slot = where[k]
+
+        @pl.when(lax.rem(slot, 4) != 3)
+        def _(k=k, slot=slot):
+            def body(at):
+                acc[at, :] += jnp.dot(lhs[slot, at, :], weights[k][...], preferred_element_type=F32)
+
+            row_tiles(rows, body)
+
+
+def begin_kernel(rows, where, *refs):
+    toks, weights, (lhs, acc) = refs[:6], refs[6:10], refs[10:]
+    for n, s in enumerate((0, 1, 2, 4, 5, 6)):
+        copy_rows(rows, lhs.at[s], toks[n])
+    first_half(rows, where, lhs, weights, acc)
+
+
+def also_kernel(rows, where, *refs):
+    lhs, weights, acc = refs[0], refs[1:5], refs[5]
+    first_half(rows, where, lhs, weights, acc)
+
+
+def begin(where, toks, weights, rows):
+    vmem = pl.BlockSpec(memory_space=pltpu.VMEM)
+    tall, width = rows + HALO, weights[0].shape[1]
+    return pl.pallas_call(
+        functools.partial(begin_kernel, rows),
+        out_shape=[
+            jax.ShapeDtypeStruct((8, tall, BLOCK), jnp.bfloat16),
+            jax.ShapeDtypeStruct((tall, width), F32),
+        ],
+        in_specs=[pl.BlockSpec(memory_space=pltpu.SMEM)] + [vmem] * 10,
+        out_specs=[vmem] * 2,
+        compiler_params=pltpu.CompilerParams(vmem_limit_bytes=26 << 20),
+        cost_estimate=pl.CostEstimate(
+            flops=2 * tall * 3 * BLOCK * width, bytes_accessed=12 << 20, transcendentals=0
+        ),
+    )(where, *toks, *weights)
+
+
+def also(where, lhs, weights, rows):
+    vmem = pl.BlockSpec(memory_space=pltpu.VMEM)
+    tall, width = rows + HALO, weights[0].shape[1]
+    return pl.pallas_call(
+        functools.partial(also_kernel, rows),
+        out_shape=jax.ShapeDtypeStruct((tall, width), F32),
+        in_specs=[pl.BlockSpec(memory_space=pltpu.SMEM)] + [vmem] * 5,
+        out_specs=vmem,
+        compiler_params=pltpu.CompilerParams(vmem_limit_bytes=26 << 20),
+        cost_estimate=pl.CostEstimate(
+            flops=2 * tall * 3 * BLOCK * width, bytes_accessed=12 << 20, transcendentals=0
+        ),
+    )(where, lhs, *weights)
+
+
+def project_kernel(rows, where, *refs):
+    lhs, near, far, part, *refs = refs
     weights, refs = refs[:8], refs[8:]
-    prm, y_ref, x1_ref, u_ref, end_ref, lhs, wts, proj, sem_t, sem_w = refs
+    prm, y_ref, x1_ref, u_ref, end_ref, last, acc, proj = refs
     seg_len = rows // SEG
-    width = 3 * LANES
-    copies = []
-    for s in range(8):
-        copies.append(
-            pltpu.make_async_copy(toks[s], lhs.at[:, pl.ds(s * BLOCK, BLOCK)], sem_t.at[s])
-        )
-    for k in range(8):
-        at = pl.multiple_of(where[k] * BLOCK, BLOCK)
-        copies.append(pltpu.make_async_copy(weights[k], wts.at[pl.ds(at, BLOCK), :], sem_w.at[k]))
-    for copy in copies:
-        copy.start()
-    for copy in copies:
-        copy.wait()
-
-    tile = (rows + HALO) // 5
-
-    def matmul(m, carry):
-        at = pl.ds(pl.multiple_of(m * tile, 16), tile)
-        out = jnp.dot(lhs[at, :], wts[...], preferred_element_type=F32)
+    for k in range(4):
+        slot = where[4 + k]
+
+        @pl.when(lax.rem(slot, 4) != 3)
+        def _(k=k, slot=slot):
+            copy_rows(rows, last.at[k], lhs.at[slot])
+
+        for s, ref in ((3, near), (7, far)):
+
+            @pl.when(slot == s)
+            def _(k=k, ref=ref):
+                copy_rows(rows, last.at[k], ref)
+
+            @pl.when(where[k] == s)
+            def _(k=k, ref=ref):
+                def body(at):
+                    acc[at, :] = part[at, :] + jnp.dot(
+                        ref[at, :], weights[k][...], preferred_element_type=F32
+                    )
+
+                row_tiles(rows, body)
+
+    def finish(at):
+        out = acc[at, :]
+        for k in range(4):
+            out = out + jnp.dot(
+                last[k, at, :], weights[4 + k][...], preferred_element_type=F32
+            )
         out = out.astype(jnp.bfloat16).astype(F32)
         for n in range(6):
             proj[n, at, :] = out[:, n * LANES:(n + 1) * LANES]
-        return carry
-
-    lax.fori_loop(0, 5, matmul, 0)
+
+    row_tiles(rows, finish)
 
     for q in range(2):
         lanes = pl.ds(q * LANES, LANES)
@@ -151,10 +236,9 @@
             end_ref[pl.ds(k, 1), lanes] = u[SEG - 1:]
 
 
-def project(where, toks, weights, prm, rows):
-    any_spec = pl.BlockSpec(memory_space=pl.ANY)
+def project(where, lhs, near, far, part, weights, prm, rows):
     vmem = pl.BlockSpec(memory_space=pltpu.VMEM)
-    wide = 2 * LANES
+    wide, tall = 2 * LANES, rows + HALO
     return pl.pallas_call(
         functools.partial(project_kernel, rows),
         out_shape=[
@@ -163,20 +247,18 @@
             jax.ShapeDtypeStruct((MODES * SEG, wide), F32),
             jax.ShapeDtypeStruct((MODES, wide), F32),
         ],
-        in_specs=[pl.BlockSpec(memory_space=pltpu.SMEM)] + [any_spec] * 16 + [vmem],
+        in_specs=[pl.BlockSpec(memory_space=pltpu.SMEM)] + [vmem] * 13,
         out_specs=[vmem] * 4,
         scratch_shapes=[
-            pltpu.VMEM((rows + HALO, D), jnp.bfloat16),
-            pltpu.VMEM((D, 6 * LANES), jnp.bfloat16),
-            pltpu.VMEM((6, rows + HALO, LANES), F32),
-            pltpu.SemaphoreType.DMA((8,)),
-            pltpu.SemaphoreType.DMA((8,)),
+            pltpu.VMEM((4, tall, BLOCK), jnp.bfloat16),
+            pltpu.VMEM((tall, 3 * wide), F32),
+            pltpu.VMEM((6, tall, LANES), F32),
         ],
-        compiler_params=pltpu.CompilerParams(vmem_limit_bytes=34 << 20),
+        compiler_params=pltpu.CompilerParams(vmem_limit_bytes=26 << 20),
         cost_estimate=pl.CostEstimate(
-            flops=2 * rows * D * 6 * LANES, bytes_accessed=18 << 20, transcendentals=0
+            flops=2 * tall * 5 * BLOCK * 3 * wide, bytes_accessed=12 << 20, transcendentals=0
         ),
-    )(where, *toks, *weights, prm)
+    )(where, lhs, near, far, part, *weights, prm)
 
 
 def gate_kernel(rows, core_ref, y0, y1, x0, x1, u0, u1, p0, p1, near, sent, same, cross, fades,
@@ -294,9 +376,9 @@
         n = (yl * 4 + x) * 2 + c + 1
         return None if n == 16 else (n // 8, (n // 2) % 4, n % 2, yh, z)
 
-    halo = send(tokens[rows - HALO:], next_ctx)
-    b = transposed(in_weight.reshape(BLOCK, 3 * wide))
-    t = jnp.concatenate([halo, tokens], axis=0)
+    w, tail = together((in_weight.reshape(BLOCK, 3 * wide), tokens[rows - HALO:]))
+    b = transposed(w)
+    t = jnp.concatenate([send(tail, next_ctx), tokens], axis=0)
     t, b, where, core_at, fades, behind, plane, chip, *prms = together(
         (t, b, where, core_at, fades, behind, plane, chip, *prms)
     )
@@ -304,21 +386,28 @@
     bp, bm = along_x(b, 1), along_x(b, -1)
     t, b, tp_, tm, ty, bp, bm = together((t, b, tp_, tm, ty, bp, bm))
     typ, tym = along_z(ty, 1), along_z(ty, -1)
+    cb, cbp, cbm = other_core(b), other_core(bp), other_core(bm)
+    b, bp, cb, cbp, cbm = together((b, bp, cb, cbp, cbm))
     bf, a = along_x(bp, 1), other_ylo(b)
-    cb = other_core(b)
-    t, b, tp_, tm, ty, bp, bm, typ, tym, bf, a, cb = together(
-        (t, b, tp_, tm, ty, bp, bm, typ, tym, bf, a, cb)
+    t, b, tp_, tm, ty, bp, bm, typ, tym, bf, a, cb, cbp, cbm = together(
+        (t, b, tp_, tm, ty, bp, bm, typ, tym, bf, a, cb, cbp, cbm)
     )
     tf, tyf = along_z(tp_, 1), along_z(tym, -1)
-    ap, am, af = along_x(a, 1), along_x(a, -1), other_ylo(bf)
-    b, bp, bm, bf, a, ap, am, af, tf, tyf = together((b, bp, bm, bf, a, ap, am, af, tf, tyf))
-    toks = [t, tp_, tm, tf, ty, typ, tym, tyf]
+    ap = along_x(a, 1)
+    cbf, ca = other_core(bf), other_core(a)
+    bf, a, cbf, ca = together((bf, a, cbf, ca))
+    am, af = along_x(a, -1), other_ylo(bf)
+    lhs, part = begin(where, [t, tp_, tm, ty, typ, tym], [b, bp, bm, bf], rows)
+    part_too = also(where, lhs, [cb, cbp, cbm, cbf], rows)
+    lhs, part, part_too, ap, am, af, tf, tyf = together(
+        (lhs, part, part_too, ap, am, af, tf, tyf)
+    )
     mine = [b, bp, bm, bf, a, ap, am, af]
-    theirs = [cb] + [other_core(w) for w in mine[1:]]
+    theirs = [cb, cbp, cbm, cbf, ca] + [other_core(w) for w in (ap, am, af)]
 
     ys, xs, us, ends = [], [], [], []
-    for o, weights in enumerate((mine, theirs)):
-        y, x1, u, end = project(where, toks, weights, prms[o], rows)
+    for o, (weights, done) in enumerate(((mine, part), (theirs, part_too))):
+        y, x1, u, end = project(where, lhs, tf, tyf, done, weights, prms[o], rows)
         ys.append(y)
         xs.append(x1)
         us.append(u)

time: 165 us -> 161 us (0.976)
  waiting for transfers between devices: 65.5 us -> 57.7 us
  Pallas kernels: 34.3 us -> 41.3 us
  starting transfers between devices: 58.7 us -> 55.6 us
    pallas_call x0 -> x2, Pallas kernels: none -> 12.3 us  [the longest x1 6.42 us: begin(): pl.pallas_call(functools.partial(begin_kernel, rows), out_shape=[jax.Shap...]
    ppermute x30, waiting for transfers between devices: 65.5 us -> 57.7 us  [send(): return lax.ppermute(value, ('ctx', 'tp'), route(move))]
    pallas_call x2, Pallas kernels: 29.7 us -> 24.4 us  [project(): pl.pallas_call(functools.partial(project_kernel, rows), out_shape=[jax.Sh...]
    ppermute x30, starting transfers between devices: 58.7 us -> 55.6 us  [send(): return lax.ppermute(value, ('ctx', 'tp'), route(move))]
  transfers between devices with their start and end apart: 30 -> 30, of which waited for: 15 -> 13; matrix products, arithmetic and copies ran while one was open for 3% -> 2% of each run, Pallas kernels for 9% -> 15%
where the time goes in v3:
time: 161 us; the launch traced here: 160 us
  waiting for transfers between devices  57.7 us (36%)
  starting transfers between devices  55.6 us (35%)
  Pallas kernels  41.3 us (26%)
  local copies, waits for them, and re-layouts  3.33 us (2%)
  other arithmetic  1.72 us (1%)
    ppermute x30, waiting for transfers between devices, send(): return lax.ppermute(value, ('ctx', 'tp'), route(move))  57.7 us
    ppermute x30, starting transfers between devices, send(): return lax.ppermute(value, ('ctx', 'tp'), route(move))  55.6 us
    pallas_call x2, Pallas kernels, project(): pl.pallas_call(functools.partial(project_kernel, rows), out_shape=[jax.Sh...  24.4 us
    pallas_call x1, Pallas kernels, begin(): pl.pallas_call(functools.partial(begin_kernel, rows), out_shape=[jax.Shap...  6.42 us
    pallas_call x1, Pallas kernels, also(): pl.pallas_call(functools.partial(also_kernel, rows), out_shape=jax.ShapeD...  5.9 us
    pallas_call x1, Pallas kernels, gate(): pl.pallas_call(functools.partial(gate_kernel, rows), out_shape=jax.ShapeD...  4.57 us
  transfers between devices with their start and end apart: 30, of which 13 were waited for; matrix products, arithmetic and copies ran while one was open for 2% of the time, Pallas kernels for 15%

profile of v3, /device:TPU:1, one launch (start us, length us, event | category | flops | bytes accessed | tf_op | source)
XLA Modules:
  0.0 160.4 jit_solution(11275127654060905326)
XLA Ops:
  0.0 1.5 copy.8
  1.5 0.6 slice.24
  2.1 4.5 %collective-permute-start = (bf16[16,512]{1,0:T(8,128)(2,1)}, bf16[16,512]{1,0:T(8,128)(2,1)}, u32[]{:S(2)}, u32[]{:S(2)}) collective-permute-start(bf16[16,512]{1,0:T(8,128)(2,1)} %slice.24), channel_id=1, source_target_pairs={{0,8},{1,9},{2,10},{3,11},{4,12},{5,13},{6,14},{7,15},{8,16},{9,17... | collective-permute-start | bytes 49160 | tf_op jit(solution)/shard_map/ppermute | solution.py:41
  6.6 0.3 copy.9
  6.9 0.7 collective-permute-start.1
  7.8 0.8 bitcast_multiply_fusion.7
  8.6 0.1 negate_exponential_fusion
  8.7 0.8 dynamic_slice.21
  9.8 0.1 stack.67.where
  9.9 0.0 collective-permute-done
  9.9 0.8 pad_maximum_fusion.refs_0_
  10.7 0.0 collective-permute-done.1.refs_6_.refs_4_
  10.7 21.3 %collective-permute-start.2 = (bf16[1040,512]{1,0:T(8,128)(2,1)S(1)}, bf16[1040,512]{1,0:T(8,128)(2,1)S(1)}, u32[]{:S(2)}, u32[]{:S(2)}) collective-permute-start(bf16[1040,512]{1,0:T(8,128)(2,1)S(1)} %pad_maximum_fusion.refs_0_), channel_id=1, source_target_pairs={{0,1},{1,2},{2,3},{3,0},{4,5},{5,6},{6,7},{7,4},{8,9},{9,10},{10,1... | collective-permute-start | bytes 3194888 | tf_op jit(solution)/shard_map/ppermute | solution.py:41
  32.0 3.3 %collective-permute-start.3 = (bf16[1040,512]{1,0:T(8,128)(2,1)S(1)}, bf16[1040,512]{1,0:T(8,128)(2,1)S(1)}, u32[]{:S(2)}, u32[]{:S(2)}) collective-permute-start(bf16[1040,512]{1,0:T(8,128)(2,1)S(1)} %pad_maximum_fusion.refs_0_), channel_id=1, source_target_pairs={{0,3},{1,0},{2,1},{3,2},{4,7},{5,4},{6,5},{7,6},{8,11},{9,8},{10,9... | collective-permute-start | bytes 3194888 | tf_op jit(solution)/shard_map/ppermute | solution.py:41
  35.3 3.8 %collective-permute-start.4 = (bf16[1040,512]{1,0:T(8,128)(2,1)S(1)}, bf16[1040,512]{1,0:T(8,128)(2,1)S(1)}, u32[]{:S(2)}, u32[]{:S(2)}) collective-permute-start(bf16[1040,512]{1,0:T(8,128)(2,1)S(1)} %pad_maximum_fusion.refs_0_), channel_id=1, source_target_pairs={{0,4},{1,5},{2,6},{3,7},{4,0},{5,1},{6,2},{7,3},{8,12},{9,13},{10,... | collective-permute-start | bytes 3194888 | tf_op jit(solution)/shard_map/ppermute | solution.py:41
  39.1 0.0 collective-permute-start.5
  39.1 2.7 %collective-permute-start.6 = (bf16[512,768]{1,0:T(8,128)(2,1)S(1)}, bf16[512,768]{1,0:T(8,128)(2,1)S(1)}, u32[]{:S(2)}, u32[]{:S(2)}) collective-permute-start(bf16[512,768]{1,0:T(8,128)(2,1)S(1)} %collective-permute-done.1.refs_6_.refs_4_), channel_id=1, source_target_pairs={{0,48},{1,49},{2,50},{3,51},{4,52},{5,53},{6,54},{7,55},{8,56},{9,... | collective-permute-start | bytes 2359304 | tf_op jit(solution)/shard_map/ppermute | solution.py:41
  41.8 16.6 %collective-permute-done.5.refs_7_.refs_5_ = bf16[512,768]{1,0:T(8,128)(2,1)S(1)} collective-permute-done((bf16[512,768]{1,0:T(8,128)(2,1)S(1)}, bf16[512,768]{1,0:T(8,128)(2,1)S(1)}, u32[]{:S(2)}, u32[]{:S(2)}) %collective-permute-start.5) | collective-permute-done | bytes 786464 | tf_op jit(solution)/shard_map/ppermute | solution.py:41
  58.4 0.0 collective-permute-done.6.refs_8_.refs_6_
  58.4 0.4 collective-permute-done.2.refs_1_
  58.9 0.0 collective-permute-done.3.refs_2_
  58.9 3.5 %collective-permute-done.4.refs_3_ = bf16[1040,512]{1,0:T(8,128)(2,1)S(1)} collective-permute-done((bf16[1040,512]{1,0:T(8,128)(2,1)S(1)}, bf16[1040,512]{1,0:T(8,128)(2,1)S(1)}, u32[]{:S(2)}, u32[]{:S(2)}) %collective-permute-start.4) | collective-permute-done | bytes 1064992 | tf_op jit(solution)/shard_map/ppermute | solution.py:41
  62.4 1.2 collective-permute-start.7
  63.6 0.0 collective-permute-start.8
  63.6 0.5 collective-permute-start.9
  64.1 2.7 %collective-permute-start.11 = (bf16[1040,512]{1,0:T(8,128)(2,1)S(1)}, bf16[1040,512]{1,0:T(8,128)(2,1)S(1)}, u32[]{:S(2)}, u32[]{:S(2)}) collective-permute-start(bf16[1040,512]{1,0:T(8,128)(2,1)S(1)} %collective-permute-done.4.refs_3_), channel_id=1, source_target_pairs={{0,3},{1,0},{2,1},{3,2},{4,7},{5,4},{6,5},{7,6},{8,11},{9,8},{10,9... | collective-permute-start | bytes 3194888 | tf_op jit(solution)/shard_map/ppermute | solution.py:41
  66.8 0.0 collective-permute-done.7.refs_1_.refs_4_
  66.8 1.0 collective-permute-done.9.refs_3_.refs_6_
  67.8 0.0 collective-permute-start.12
  67.8 0.9 collective-permute-start.13
  68.6 21.8 %collective-permute-done.10.refs_4_ = bf16[1040,512]{1,0:T(8,128)(2,1)S(1)} collective-permute-done((bf16[1040,512]{1,0:T(8,128)(2,1)S(1)}, bf16[1040,512]{1,0:T(8,128)(2,1)S(1)}, u32[]{:S(2)}, u32[]{:S(2)}) %collective-permute-start.10) | collective-permute-done | bytes 1064992 | tf_op jit(solution)/shard_map/ppermute | solution.py:41
  90.5 0.9 collective-permute-start.14
  91.3 0.1 collective-permute-start.15
  91.4 2.7 %collective-permute-start.20 = (bf16[1040,512]{1,0:T(8,128)(2,1)S(1)}, bf16[1040,512]{1,0:T(8,128)(2,1)S(1)}, u32[]{:S(2)}, u32[]{:S(2)}) collective-permute-start(bf16[1040,512]{1,0:T(8,128)(2,1)S(1)} %collective-permute-done.11.refs_5_), channel_id=1, source_target_pairs={{0,3},{1,0},{2,1},{3,2},{4,7},{5,4},{6,5},{7,6},{8,11},{9,8},{10,9... | collective-permute-start | bytes 3194888 | tf_op jit(solution)/shard_map/ppermute | solution.py:41
  94.1 0.0 collective-permute-start.16
  94.1 0.0 collective-permute-done.14.refs_4_.refs_7_
  94.1 0.3 collective-permute-done.15.refs_8_
  94.4 2.4 %collective-permute-start.17 = (bf16[512,768]{1,0:T(8,128)(2,1)S(1)}, bf16[512,768]{1,0:T(8,128)(2,1)S(1)}, u32[]{:S(2)}, u32[]{:S(2)}) collective-permute-start(bf16[512,768]{1,0:T(8,128)(2,1)S(1)} %collective-permute-done.13.refs_8_), channel_id=1, source_target_pairs={{0,48},{1,49},{2,50},{3,51},{4,52},{5,53},{6,54},{7,55},{8,56},{9,... | collective-permute-start | bytes 2359304 | tf_op jit(solution)/shard_map/ppermute | solution.py:41
  96.8 0.9 collective-permute-start.18
  97.7 6.4 %shard_map.64 = (bf16[8,1040,512]{2,1,0:T(8,128)(2,1)S(1)}, f32[1040,768]{1,0:T(8,128)S(1)}) custom-call(s32[9]{0:T(128)S(1)} %stack.67.where, bf16[1040,512]{1,0:T(8,128)(2,1)S(1)} %pad_maximum_fusion.refs_0_, bf16[1040,512]{1,0:T(8,128)(2,1)S(1)} %collective-permute-done.2.refs_1_, bf16[1040,512]{1,0:T(8,128)(2,1)S(1)} %collective-permute-done.3.refs_2_, ...), custom_call_target="tpu_custom_call" | custom-call | flops 2453667840 | bytes 12582912 | tf_op jit(solution)/shard_map/pallas_call | solution.py:128
  104.1 5.9 %shard_map.65.refs_3_ = f32[1040,768]{1,0:T(8,128)S(1)} custom-call(s32[9]{0:T(128)S(1)} %stack.67.where, bf16[8,1040,512]{2,1,0:T(8,128)(2,1)S(1)} %get-tuple-element.102.refs_0_, bf16[512,768]{1,0:T(8,128)(2,1)S(1)} %collective-permute-done.7.refs_1_.refs_4_, bf16[512,768]{1,0:T(8,128)(2,1)S(1)} %collective-permute-done.8.refs_2_.refs_5_, ...), custom_call_target="tpu_custom_call" | custom-call | flops 2453667840 | bytes 12582912 | tf_op jit(solution)/shard_map/pallas_call | solution.py:146
  110.0 3.4 %collective-permute-done.16.refs_9_ = bf16[512,768]{1,0:T(8,128)(2,1)S(1)} collective-permute-done((bf16[512,768]{1,0:T(8,128)(2,1)S(1)}, bf16[512,768]{1,0:T(8,128)(2,1)S(1)}, u32[]{:S(2)}, u32[]{:S(2)}) %collective-permute-start.16) | collective-permute-done | bytes 786464 | tf_op jit(solution)/shard_map/ppermute | solution.py:41
  113.4 3.9 %collective-permute-done.19.refs_1_ = bf16[1040,512]{1,0:T(8,128)(2,1)S(1)} collective-permute-done((bf16[1040,512]{1,0:T(8,128)(2,1)S(1)}, bf16[1040,512]{1,0:T(8,128)(2,1)S(1)}, u32[]{:S(2)}, u32[]{:S(2)}) %collective-permute-start.19) | collective-permute-done | bytes 1064992 | tf_op jit(solution)/shard_map/ppermute | solution.py:41
  117.3 0.0 collective-permute-done.20.refs_2_
  117.3 0.0 collective-permute-done.17.refs_10_
  117.3 0.0 collective-permute-done.18.refs_11_
  117.3 1.3 collective-permute-start.21
  118.7 0.1 collective-permute-start.22
  118.7 0.4 collective-permute-start.23
  119.2 12.3 %shard_map.66 = (f32[1024,256]{1,0:T(8,128)S(1)}, f32[1024,256]{1,0:T(8,128)S(1)}, f32[128,256]{1,0:T(8,128)S(1)}, f32[16,256]{1,0:T(8,128)S(1)}) custom-call(s32[9]{0:T(128)S(1)} %stack.67.where, bf16[8,1040,512]{2,1,0:T(8,128)(2,1)S(1)} %get-tuple-element.102.refs_0_, bf16[1040,512]{1,0:T(8,128)(2,1)S(1)} %collective-permute-done.19.refs_1_, ...), custom_call_target="tpu_custom_call" | custom-call | flops 4089446400 | bytes 12582912 | tf_op jit(solution)/shard_map/pallas_call | solution.py:242
  131.5 0.0 collective-permute-done.21.refs_9_
  131.5 12.1 %shard_map.67 = (f32[1024,256]{1,0:T(8,128)S(1)}, f32[1024,256]{1,0:T(8,128)S(1)}, f32[128,256]{1,0:T(8,128)S(1)}, f32[16,256]{1,0:T(8,128)S(1)}) custom-call(s32[9]{0:T(128)S(1)} %stack.67.where, bf16[8,1040,512]{2,1,0:T(8,128)(2,1)S(1)} %get-tuple-element.102.refs_0_, bf16[1040,512]{1,0:T(8,128)(2,1)S(1)} %collective-permute-done.19.refs_1_, ...), custom_call_target="tpu_custom_call" | custom-call | flops 4089446400 | bytes 12582912 | tf_op jit(solution)/shard_map/pallas_call | solution.py:242
  143.6 0.7 collective-permute-start.26
  144.3 1.0 collective-permute-start.25
  145.3 0.8 collective-permute-start.24
  146.1 0.4 collective-permute-done.26
  146.5 2.1 %collective-permute-done.25 = f32[16,512]{1,0:T(8,128)S(1)} collective-permute-done((f32[16,512]{1,0:T(8,128)S(1)}, f32[16,512]{1,0:T(8,128)S(1)}, u32[]{:S(2)}, u32[]{:S(2)}) %collective-permute-start.25) | collective-permute-done | bytes 32800 | tf_op jit(solution)/shard_map/ppermute | solution.py:41
  148.6 1.1 collective-permute-done.24
  149.8 1.1 collective-permute-start.27
  150.9 1.4 collective-permute-start.28
  152.3 0.3 collective-permute-start.29
  152.6 1.1 collective-permute-done.28.same
  153.7 2.0 %collective-permute-done.29.cross = f32[16,512]{1,0:T(8,128)S(1)} collective-permute-done((f32[16,512]{1,0:T(8,128)S(1)}, f32[16,512]{1,0:T(8,128)S(1)}, u32[]{:S(2)}, u32[]{:S(2)}) %collective-permute-start.29) | collective-permute-done | bytes 32800 | tf_op jit(solution)/shard_map/ppermute | solution.py:41
  155.7 4.6 %shard_map.68 = bf16[1024,512]{1,0:T(8,128)(2,1)} custom-call(s32[1]{0:T(128)} %bitcast.9.core_ref, f32[1024,256]{1,0:T(8,128)S(1)} %get-tuple-element.110.y0, f32[1024,256]{1,0:T(8,128)S(1)} %get-tuple-element.114.y1, f32[1024,256]{1,0:T(8,128)S(1)} %get-tuple-element.115.x0, f32[1024,256]{1,0:T(8,128)S(1)} %get-tuple-element.116.x1, ...), custom_call_target="tpu_custom_call" | custom-call | tf_op jit(solution)/shard_map/pallas_call | solution.py:320
  (24 shorter events, 0.2 us)
Async XLA Ops:
  0.0 8.6 %copy-start = (f32[3,3,4096]{2,1,0:T(4,128)S(1)}, f32[3,3,4096]{2,1,0:T(4,128)}, u32[]{:S(2)}) copy-start(f32[3,3,4096]{2,1,0:T(4,128)} %param.8) | copy-start | bytes 442372
  0.0 1.5 copy-start.1
  2.1 7.8 %collective-permute-start = (bf16[16,512]{1,0:T(8,128)(2,1)}, bf16[16,512]{1,0:T(8,128)(2,1)}, u32[]{:S(2)}, u32[]{:S(2)}) collective-permute-start(bf16[16,512]{1,0:T(8,128)(2,1)} %slice.24), channel_id=1, source_target_pairs={{0,8},{1,9},{2,10},{3,11},{4,12},{5,13},{6,14},{7,15},{8,16},{9,17... | collective-permute-start | bytes 49160 | tf_op jit(solution)/shard_map/ppermute | solution.py:41
  6.9 3.8 %collective-permute-start.1 = (bf16[512,768]{1,0:T(8,128)(2,1)S(1)}, bf16[512,768]{1,0:T(8,128)(2,1)S(1)}, u32[]{:S(2)}, u32[]{:S(2)}) collective-permute-start(bf16[512,768]{1,0:T(8,128)(2,1)S(1)} %copy.9), channel_id=1, source_target_pairs={{0,0},{1,16},{2,32},{3,48},{4,64},{5,80},{6,96},{7,112},{8,8},{9,2... | collective-permute-start | bytes 2359304 | tf_op jit(solution)/shard_map/ppermute | solution.py:41
  10.7 48.2 %collective-permute-start.2 = (bf16[1040,512]{1,0:T(8,128)(2,1)S(1)}, bf16[1040,512]{1,0:T(8,128)(2,1)S(1)}, u32[]{:S(2)}, u32[]{:S(2)}) collective-permute-start(bf16[1040,512]{1,0:T(8,128)(2,1)S(1)} %pad_maximum_fusion.refs_0_), channel_id=1, source_target_pairs={{0,1},{1,2},{2,3},{3,0},{4,5},{5,6},{6,7},{7,4},{8,9},{9,10},{10,1... | collective-permute-start | bytes 3194888 | tf_op jit(solution)/shard_map/ppermute | solution.py:41
  32.0 26.9 %collective-permute-start.3 = (bf16[1040,512]{1,0:T(8,128)(2,1)S(1)}, bf16[1040,512]{1,0:T(8,128)(2,1)S(1)}, u32[]{:S(2)}, u32[]{:S(2)}) collective-permute-start(bf16[1040,512]{1,0:T(8,128)(2,1)S(1)} %pad_maximum_fusion.refs_0_), channel_id=1, source_target_pairs={{0,3},{1,0},{2,1},{3,2},{4,7},{5,4},{6,5},{7,6},{8,11},{9,8},{10,9... | collective-permute-start | bytes 3194888 | tf_op jit(solution)/shard_map/ppermute | solution.py:41
  35.3 27.0 %collective-permute-start.4 = (bf16[1040,512]{1,0:T(8,128)(2,1)S(1)}, bf16[1040,512]{1,0:T(8,128)(2,1)S(1)}, u32[]{:S(2)}, u32[]{:S(2)}) collective-permute-start(bf16[1040,512]{1,0:T(8,128)(2,1)S(1)} %pad_maximum_fusion.refs_0_), channel_id=1, source_target_pairs={{0,4},{1,5},{2,6},{3,7},{4,0},{5,1},{6,2},{7,3},{8,12},{9,13},{10,... | collective-permute-start | bytes 3194888 | tf_op jit(solution)/shard_map/ppermute | solution.py:41
  39.1 19.3 %collective-permute-start.5 = (bf16[512,768]{1,0:T(8,128)(2,1)S(1)}, bf16[512,768]{1,0:T(8,128)(2,1)S(1)}, u32[]{:S(2)}, u32[]{:S(2)}) collective-permute-start(bf16[512,768]{1,0:T(8,128)(2,1)S(1)} %collective-permute-done.1.refs_6_.refs_4_), channel_id=1, source_target_pairs={{0,16},{1,17},{2,18},{3,19},{4,20},{5,21},{6,22},{7,23},{8,24},{9,... | collective-permute-start | bytes 2359304 | tf_op jit(solution)/shard_map/ppermute | solution.py:41
  39.1 19.3 %collective-permute-start.6 = (bf16[512,768]{1,0:T(8,128)(2,1)S(1)}, bf16[512,768]{1,0:T(8,128)(2,1)S(1)}, u32[]{:S(2)}, u32[]{:S(2)}) collective-permute-start(bf16[512,768]{1,0:T(8,128)(2,1)S(1)} %collective-permute-done.1.refs_6_.refs_4_), channel_id=1, source_target_pairs={{0,48},{1,49},{2,50},{3,51},{4,52},{5,53},{6,54},{7,55},{8,56},{9,... | collective-permute-start | bytes 2359304 | tf_op jit(solution)/shard_map/ppermute | solution.py:41
  62.4 4.4 %collective-permute-start.7 = (bf16[512,768]{1,0:T(8,128)(2,1)S(1)}, bf16[512,768]{1,0:T(8,128)(2,1)S(1)}, u32[]{:S(2)}, u32[]{:S(2)}) collective-permute-start(bf16[512,768]{1,0:T(8,128)(2,1)S(1)} %collective-permute-done.1.refs_6_.refs_4_), channel_id=1, source_target_pairs={{0,8},{1,9},{2,10},{3,11},{4,12},{5,13},{6,14},{7,15},{8,0},{9,1},... | collective-permute-start | bytes 2359304 | tf_op jit(solution)/shard_map/ppermute | solution.py:41
  63.6 3.2 %collective-permute-start.8 = (bf16[512,768]{1,0:T(8,128)(2,1)S(1)}, bf16[512,768]{1,0:T(8,128)(2,1)S(1)}, u32[]{:S(2)}, u32[]{:S(2)}) collective-permute-start(bf16[512,768]{1,0:T(8,128)(2,1)S(1)} %collective-permute-done.5.refs_7_.refs_5_), channel_id=1, source_target_pairs={{0,8},{1,9},{2,10},{3,11},{4,12},{5,13},{6,14},{7,15},{8,0},{9,1},... | collective-permute-start | bytes 2359304 | tf_op jit(solution)/shard_map/ppermute | solution.py:41
  63.6 4.2 %collective-permute-start.9 = (bf16[512,768]{1,0:T(8,128)(2,1)S(1)}, bf16[512,768]{1,0:T(8,128)(2,1)S(1)}, u32[]{:S(2)}, u32[]{:S(2)}) collective-permute-start(bf16[512,768]{1,0:T(8,128)(2,1)S(1)} %collective-permute-done.6.refs_8_.refs_6_), channel_id=1, source_target_pairs={{0,8},{1,9},{2,10},{3,11},{4,12},{5,13},{6,14},{7,15},{8,0},{9,1},... | collective-permute-start | bytes 2359304 | tf_op jit(solution)/shard_map/ppermute | solution.py:41
  64.1 26.4 %collective-permute-start.10 = (bf16[1040,512]{1,0:T(8,128)(2,1)S(1)}, bf16[1040,512]{1,0:T(8,128)(2,1)S(1)}, u32[]{:S(2)}, u32[]{:S(2)}) collective-permute-start(bf16[1040,512]{1,0:T(8,128)(2,1)S(1)} %collective-permute-done.4.refs_3_), channel_id=1, source_target_pairs={{0,1},{1,2},{2,3},{3,0},{4,5},{5,6},{6,7},{7,4},{8,9},{9,10},{10,1... | collective-permute-start | bytes 3194888 | tf_op jit(solution)/shard_map/ppermute | solution.py:41
  64.1 26.4 %collective-permute-start.11 = (bf16[1040,512]{1,0:T(8,128)(2,1)S(1)}, bf16[1040,512]{1,0:T(8,128)(2,1)S(1)}, u32[]{:S(2)}, u32[]{:S(2)}) collective-permute-start(bf16[1040,512]{1,0:T(8,128)(2,1)S(1)} %collective-permute-done.4.refs_3_), channel_id=1, source_target_pairs={{0,3},{1,0},{2,1},{3,2},{4,7},{5,4},{6,5},{7,6},{8,11},{9,8},{10,9... | collective-permute-start | bytes 3194888 | tf_op jit(solution)/shard_map/ppermute | solution.py:41
  67.8 22.7 %collective-permute-start.12 = (bf16[512,768]{1,0:T(8,128)(2,1)S(1)}, bf16[512,768]{1,0:T(8,128)(2,1)S(1)}, u32[]{:S(2)}, u32[]{:S(2)}) collective-permute-start(bf16[512,768]{1,0:T(8,128)(2,1)S(1)} %collective-permute-done.5.refs_7_.refs_5_), channel_id=1, source_target_pairs={{0,16},{1,17},{2,18},{3,19},{4,20},{5,21},{6,22},{7,23},{8,24},{9,... | collective-permute-start | bytes 2359304 | tf_op jit(solution)/shard_map/ppermute | solution.py:41
  67.8 22.7 %collective-permute-start.13 = (bf16[512,768]{1,0:T(8,128)(2,1)S(1)}, bf16[512,768]{1,0:T(8,128)(2,1)S(1)}, u32[]{:S(2)}, u32[]{:S(2)}) collective-permute-start(bf16[512,768]{1,0:T(8,128)(2,1)S(1)} %collective-permute-done.1.refs_6_.refs_4_), channel_id=1, source_target_pairs={{0,64},{1,65},{2,66},{3,67},{4,68},{5,69},{6,70},{7,71},{8,72},{9,... | collective-permute-start | bytes 2359304 | tf_op jit(solution)/shard_map/ppermute | solution.py:41
  90.5 3.6 %collective-permute-start.14 = (bf16[512,768]{1,0:T(8,128)(2,1)S(1)}, bf16[512,768]{1,0:T(8,128)(2,1)S(1)}, u32[]{:S(2)}, u32[]{:S(2)}) collective-permute-start(bf16[512,768]{1,0:T(8,128)(2,1)S(1)} %collective-permute-done.12.refs_9_.refs_7_), channel_id=1, source_target_pairs={{0,8},{1,9},{2,10},{3,11},{4,12},{5,13},{6,14},{7,15},{8,0},{9,1},... | collective-permute-start | bytes 2359304 | tf_op jit(solution)/shard_map/ppermute | solution.py:41
  91.3 3.0 %collective-permute-start.15 = (bf16[512,768]{1,0:T(8,128)(2,1)S(1)}, bf16[512,768]{1,0:T(8,128)(2,1)S(1)}, u32[]{:S(2)}, u32[]{:S(2)}) collective-permute-start(bf16[512,768]{1,0:T(8,128)(2,1)S(1)} %collective-permute-done.13.refs_8_), channel_id=1, source_target_pairs={{0,8},{1,9},{2,10},{3,11},{4,12},{5,13},{6,14},{7,15},{8,0},{9,1},... | collective-permute-start | bytes 2359304 | tf_op jit(solution)/shard_map/ppermute | solution.py:41
  91.4 25.9 %collective-permute-start.19 = (bf16[1040,512]{1,0:T(8,128)(2,1)S(1)}, bf16[1040,512]{1,0:T(8,128)(2,1)S(1)}, u32[]{:S(2)}, u32[]{:S(2)}) collective-permute-start(bf16[1040,512]{1,0:T(8,128)(2,1)S(1)} %collective-permute-done.2.refs_1_), channel_id=1, source_target_pairs={{0,1},{1,2},{2,3},{3,0},{4,5},{5,6},{6,7},{7,4},{8,9},{9,10},{10,1... | collective-permute-start | bytes 3194888 | tf_op jit(solution)/shard_map/ppermute | solution.py:41
  91.4 25.9 %collective-permute-start.20 = (bf16[1040,512]{1,0:T(8,128)(2,1)S(1)}, bf16[1040,512]{1,0:T(8,128)(2,1)S(1)}, u32[]{:S(2)}, u32[]{:S(2)}) collective-permute-start(bf16[1040,512]{1,0:T(8,128)(2,1)S(1)} %collective-permute-done.11.refs_5_), channel_id=1, source_target_pairs={{0,3},{1,0},{2,1},{3,2},{4,7},{5,4},{6,5},{7,6},{8,11},{9,8},{10,9... | collective-permute-start | bytes 3194888 | tf_op jit(solution)/shard_map/ppermute | solution.py:41
  94.1 19.3 %collective-permute-start.16 = (bf16[512,768]{1,0:T(8,128)(2,1)S(1)}, bf16[512,768]{1,0:T(8,128)(2,1)S(1)}, u32[]{:S(2)}, u32[]{:S(2)}) collective-permute-start(bf16[512,768]{1,0:T(8,128)(2,1)S(1)} %collective-permute-done.13.refs_8_), channel_id=1, source_target_pairs={{0,16},{1,17},{2,18},{3,19},{4,20},{5,21},{6,22},{7,23},{8,24},{9,... | collective-permute-start | bytes 2359304 | tf_op jit(solution)/shard_map/ppermute | solution.py:41
  94.4 22.9 %collective-permute-start.17 = (bf16[512,768]{1,0:T(8,128)(2,1)S(1)}, bf16[512,768]{1,0:T(8,128)(2,1)S(1)}, u32[]{:S(2)}, u32[]{:S(2)}) collective-permute-start(bf16[512,768]{1,0:T(8,128)(2,1)S(1)} %collective-permute-done.13.refs_8_), channel_id=1, source_target_pairs={{0,48},{1,49},{2,50},{3,51},{4,52},{5,53},{6,54},{7,55},{8,56},{9,... | collective-permute-start | bytes 2359304 | tf_op jit(solution)/shard_map/ppermute | solution.py:41
  96.8 20.5 %collective-permute-start.18 = (bf16[512,768]{1,0:T(8,128)(2,1)S(1)}, bf16[512,768]{1,0:T(8,128)(2,1)S(1)}, u32[]{:S(2)}, u32[]{:S(2)}) collective-permute-start(bf16[512,768]{1,0:T(8,128)(2,1)S(1)} %collective-permute-done.12.refs_9_.refs_7_), channel_id=1, source_target_pairs={{0,64},{1,65},{2,66},{3,67},{4,68},{5,69},{6,70},{7,71},{8,72},{9,... | collective-permute-start | bytes 2359304 | tf_op jit(solution)/shard_map/ppermute | solution.py:41
  117.3 14.1 %collective-permute-start.21 = (bf16[512,768]{1,0:T(8,128)(2,1)S(1)}, bf16[512,768]{1,0:T(8,128)(2,1)S(1)}, u32[]{:S(2)}, u32[]{:S(2)}) collective-permute-start(bf16[512,768]{1,0:T(8,128)(2,1)S(1)} %collective-permute-done.16.refs_9_), channel_id=1, source_target_pairs={{0,8},{1,9},{2,10},{3,11},{4,12},{5,13},{6,14},{7,15},{8,0},{9,1},... | collective-permute-start | bytes 2359304 | tf_op jit(solution)/shard_map/ppermute | solution.py:41
  118.7 12.8 %collective-permute-start.22 = (bf16[512,768]{1,0:T(8,128)(2,1)S(1)}, bf16[512,768]{1,0:T(8,128)(2,1)S(1)}, u32[]{:S(2)}, u32[]{:S(2)}) collective-permute-start(bf16[512,768]{1,0:T(8,128)(2,1)S(1)} %collective-permute-done.17.refs_10_), channel_id=1, source_target_pairs={{0,8},{1,9},{2,10},{3,11},{4,12},{5,13},{6,14},{7,15},{8,0},{9,1},... | collective-permute-start | bytes 2359304 | tf_op jit(solution)/shard_map/ppermute | solution.py:41
  118.7 12.7 %collective-permute-start.23 = (bf16[512,768]{1,0:T(8,128)(2,1)S(1)}, bf16[512,768]{1,0:T(8,128)(2,1)S(1)}, u32[]{:S(2)}, u32[]{:S(2)}) collective-permute-start(bf16[512,768]{1,0:T(8,128)(2,1)S(1)} %collective-permute-done.18.refs_11_), channel_id=1, source_target_pairs={{0,8},{1,9},{2,10},{3,11},{4,12},{5,13},{6,14},{7,15},{8,0},{9,1},... | collective-permute-start | bytes 2359304 | tf_op jit(solution)/shard_map/ppermute | solution.py:41
  143.6 2.8 %collective-permute-start.26 = (f32[16,512]{1,0:T(8,128)S(1)}, f32[16,512]{1,0:T(8,128)S(1)}, u32[]{:S(2)}, u32[]{:S(2)}) collective-permute-start(f32[16,512]{1,0:T(8,128)S(1)} %pad_maximum_fusion.4), channel_id=1, source_target_pairs={{0,48},{1,49},{2,50},{3,51},{4,52},{5,53},{6,54},{7,55},{8,56},{9,... | collective-permute-start | bytes 98312 | tf_op jit(solution)/shard_map/ppermute | solution.py:41
  144.3 4.3 %collective-permute-start.25 = (f32[16,512]{1,0:T(8,128)S(1)}, f32[16,512]{1,0:T(8,128)S(1)}, u32[]{:S(2)}, u32[]{:S(2)}) collective-permute-start(f32[16,512]{1,0:T(8,128)S(1)} %pad_maximum_fusion.4), channel_id=1, source_target_pairs={{0,32},{1,33},{2,34},{3,35},{4,36},{5,37},{6,38},{7,39},{8,40},{9,... | collective-permute-start | bytes 98312 | tf_op jit(solution)/shard_map/ppermute | solution.py:41
  145.3 4.4 %collective-permute-start.24 = (f32[16,512]{1,0:T(8,128)S(1)}, f32[16,512]{1,0:T(8,128)S(1)}, u32[]{:S(2)}, u32[]{:S(2)}) collective-permute-start(f32[16,512]{1,0:T(8,128)S(1)} %pad_maximum_fusion.4), channel_id=1, source_target_pairs={{0,16},{1,17},{2,18},{3,19},{4,20},{5,21},{6,22},{7,23},{8,24},{9,... | collective-permute-start | bytes 98312 | tf_op jit(solution)/shard_map/ppermute | solution.py:41
  149.8 2.9 %collective-permute-start.27 = (f32[16,512]{1,0:T(8,128)S(1)}, f32[16,512]{1,0:T(8,128)S(1)}, u32[]{:S(2)}, u32[]{:S(2)}) collective-permute-start(f32[16,512]{1,0:T(8,128)S(1)} %get-tuple-element.125), channel_id=1, source_target_pairs={{0,8},{1,9},{2,10},{3,11},{4,12},{5,13},{6,14},{7,15},{8,0},{9,1},... | collective-permute-start | bytes 98312 | tf_op jit(solution)/shard_map/ppermute | solution.py:41
  150.9 2.8 %collective-permute-start.28 = (f32[16,512]{1,0:T(8,128)S(1)}, f32[16,512]{1,0:T(8,128)S(1)}, u32[]{:S(2)}, u32[]{:S(2)}) collective-permute-start(f32[16,512]{1,0:T(8,128)S(1)} %get-tuple-element.129), channel_id=1, source_target_pairs={{0,64},{1,65},{2,66},{3,67},{4,68},{5,69},{6,70},{7,71},{8,72},{9,... | collective-permute-start | bytes 98312 | tf_op jit(solution)/shard_map/ppermute | solution.py:41
  152.3 3.4 %collective-permute-start.29 = (f32[16,512]{1,0:T(8,128)S(1)}, f32[16,512]{1,0:T(8,128)S(1)}, u32[]{:S(2)}, u32[]{:S(2)}) collective-permute-start(f32[16,512]{1,0:T(8,128)S(1)} %get-tuple-element.129), channel_id=1, source_target_pairs={{0,72},{1,73},{2,74},{3,75},{4,76},{5,77},{6,78},{7,79},{8,64},{9,... | collective-permute-start | bytes 98312 | tf_op jit(solution)/shard_map/ppermute | solution.py:41

commit v4 on v3

--- a/solution.py
+++ b/solution.py
@@ -155,52 +155,61 @@
     )(where, lhs, *weights)
 
 
-def project_kernel(rows, where, *refs):
-    lhs, near, far, part, *refs = refs
-    weights, refs = refs[:8], refs[8:]
-    prm, y_ref, x1_ref, u_ref, end_ref, last, acc, proj = refs
-    seg_len = rows // SEG
+def more_kernel(rows, where, *refs):
+    lhs, part, weights, acc = refs[0], refs[1], refs[2:6], refs[6]
+    copy_rows(rows, acc, part)
     for k in range(4):
         slot = where[4 + k]
 
         @pl.when(lax.rem(slot, 4) != 3)
         def _(k=k, slot=slot):
-            copy_rows(rows, last.at[k], lhs.at[slot])
-
+            def body(at):
+                acc[at, :] += jnp.dot(lhs[slot, at, :], weights[k][...], preferred_element_type=F32)
+
+            row_tiles(rows, body)
+
+
+def more(where, lhs, part, weights, rows):
+    vmem = pl.BlockSpec(memory_space=pltpu.VMEM)
+    tall, width = rows + HALO, weights[0].shape[1]
+    return pl.pallas_call(
+        functools.partial(more_kernel, rows),
+        out_shape=jax.ShapeDtypeStruct((tall, width), F32),
+        in_specs=[pl.BlockSpec(memory_space=pltpu.SMEM)] + [vmem] * 6,
+        out_specs=vmem,
+        compiler_params=pltpu.CompilerParams(vmem_limit_bytes=26 << 20),
+        cost_estimate=pl.CostEstimate(
+            flops=2 * tall * 3 * BLOCK * width, bytes_accessed=12 << 20, transcendentals=0
+        ),
+    )(where, lhs, part, *weights)
+
+
+def project_kernel(rows, where, *refs):
+    near, far, part, *refs = refs
+    weights, refs = refs[:8], refs[8:]
+    prm, prod_ref, x1_ref, u_ref, end_ref, acc, proj = refs
+    seg_len = rows // SEG
+    for k in range(8):
         for s, ref in ((3, near), (7, far)):
-
-            @pl.when(slot == s)
-            def _(k=k, ref=ref):
-                copy_rows(rows, last.at[k], ref)
 
             @pl.when(where[k] == s)
             def _(k=k, ref=ref):
                 def body(at):
-                    acc[at, :] = part[at, :] + jnp.dot(
-                        ref[at, :], weights[k][...], preferred_element_type=F32
-                    )
+                    out = jnp.dot(ref[at, :], weights[k][...], preferred_element_type=F32)
+                    if k < 4:
+                        acc[at, :] = part[at, :] + out
+                        return
+                    out = (acc[at, :] + out).astype(jnp.bfloat16).astype(F32)
+                    for n in range(6):
+                        proj[n, at, :] = out[:, n * LANES:(n + 1) * LANES]
 
                 row_tiles(rows, body)
-
-    def finish(at):
-        out = acc[at, :]
-        for k in range(4):
-            out = out + jnp.dot(
-                last[k, at, :], weights[4 + k][...], preferred_element_type=F32
-            )
-        out = out.astype(jnp.bfloat16).astype(F32)
-        for n in range(6):
-            proj[n, at, :] = out[:, n * LANES:(n + 1) * LANES]
-
-    row_tiles(rows, finish)
 
     for q in range(2):
         lanes = pl.ds(q * LANES, LANES)
         bcast = lambda r: jnp.broadcast_to(prm[pl.ds(r, 1), lanes], (SEG, LANES))
         decay = [bcast(k) for k in range(MODES)]
-        amp = [bcast(MODES + k) for k in range(MODES)]
         taps = [[bcast(2 * MODES + 3 * j + g) for g in range(3)] for j in range(3)]
-        gain = bcast(2 * MODES + 9)
 
         def load(g, at):
             return proj[2 * g + q, pl.ds(at, SEG, stride=seg_len), :]
@@ -213,16 +222,10 @@
                 for g in range(3)
             ]
             product = feat[1] * feat[2]
-            states = [decay[k] * states[k] + product for k in range(MODES)]
-            terms = [amp[k] * states[k] for k in range(MODES)] + [gain * product]
-            while len(terms) > 1:
-                terms = [a + b for a, b in zip(terms[::2], terms[1::2])] + (
-                    [terms[-1]] if len(terms) % 2 else []
-                )
             at = pl.ds(pl.multiple_of(i * SEG, SEG), SEG)
-            y_ref[at, lanes] = terms[0]
+            prod_ref[at, lanes] = product
             x1_ref[at, lanes] = feat[0]
-            return (last, now, states)
+            return (last, now, [decay[k] * states[k] + product for k in range(MODES)])
 
         zero = jnp.zeros((SEG, LANES), F32)
         first = ([load(g, HALO - 2) for g in range(3)], [load(g, HALO - 1) for g in range(3)])
@@ -236,7 +239,7 @@
             end_ref[pl.ds(k, 1), lanes] = u[SEG - 1:]
 
 
-def project(where, lhs, near, far, part, weights, prm, rows):
+def project(where, near, far, part, weights, prm, rows):
     vmem = pl.BlockSpec(memory_space=pltpu.VMEM)
     wide, tall = 2 * LANES, rows + HALO
     return pl.pallas_call(
@@ -247,21 +250,59 @@
             jax.ShapeDtypeStruct((MODES * SEG, wide), F32),
             jax.ShapeDtypeStruct((MODES, wide), F32),
         ],
-        in_specs=[pl.BlockSpec(memory_space=pltpu.SMEM)] + [vmem] * 13,
+        in_specs=[pl.BlockSpec(memory_space=pltpu.SMEM)] + [vmem] * 12,
         out_specs=[vmem] * 4,
         scratch_shapes=[
-            pltpu.VMEM((4, tall, BLOCK), jnp.bfloat16),
             pltpu.VMEM((tall, 3 * wide), F32),
             pltpu.VMEM((6, tall, LANES), F32),
         ],
         compiler_params=pltpu.CompilerParams(vmem_limit_bytes=26 << 20),
         cost_estimate=pl.CostEstimate(
-            flops=2 * tall * 5 * BLOCK * 3 * wide, bytes_accessed=12 << 20, transcendentals=0
+            flops=2 * tall * 4 * BLOCK * 3 * wide, bytes_accessed=12 << 20, transcendentals=0
         ),
-    )(where, lhs, near, far, part, *weights, prm)
-
-
-def gate_kernel(rows, core_ref, y0, y1, x0, x1, u0, u1, p0, p1, near, sent, same, cross, fades,
+    )(where, near, far, part, *weights, prm)
+
+
+def read_kernel(rows, prod_ref, u_ref, prm, y_ref):
+    seg_len = rows // SEG
+    for q in range(2):
+        lanes = pl.ds(q * LANES, LANES)
+        bcast = lambda r: jnp.broadcast_to(prm[pl.ds(r, 1), lanes], (SEG, LANES))
+        decay = [bcast(k) for k in range(MODES)]
+        amp = [bcast(MODES + k) for k in range(MODES)]
+        gain = bcast(2 * MODES + 9)
+
+        def step(i, states):
+            at = pl.ds(pl.multiple_of(i * SEG, SEG), SEG)
+            product = prod_ref[at, lanes]
+            states = [decay[k] * states[k] + product for k in range(MODES)]
+            terms = [amp[k] * states[k] for k in range(MODES)] + [gain * product]
+            while len(terms) > 1:
+                terms = [a + b for a, b in zip(terms[::2], terms[1::2])] + (
+                    [terms[-1]] if len(terms) % 2 else []
+                )
+            y_ref[at, lanes] = terms[0]
+            return states
+
+        start = [shift_down(u_ref[pl.ds(k * SEG, SEG), lanes], 1) for k in range(MODES)]
+        lax.fori_loop(0, seg_len, step, start, unroll=4)
+
+
+def read(prod, u, prm, rows):
+    vmem = pl.BlockSpec(memory_space=pltpu.VMEM)
+    return pl.pallas_call(
+        functools.partial(read_kernel, rows),
+        out_shape=jax.ShapeDtypeStruct(prod.shape, F32),
+        in_specs=[vmem] * 3,
+        out_specs=vmem,
+        compiler_params=pltpu.CompilerParams(vmem_limit_bytes=12 << 20),
+        cost_estimate=pl.CostEstimate(
+            flops=4 * MODES * prod.size, bytes_accessed=12 << 20, transcendentals=0
+        ),
+    )(prod, u, prm)
+
+
+def gate_kernel(rows, core_ref, y0, y1, x0, x1, p0, p1, near, sent, same, cross, fades,
                 out_ref, ybuf, xbuf, wide, sem):
     seg_len = rows // SEG
     core = core_ref[0]
@@ -276,7 +317,7 @@
         for copy in copies[o]:
             copy.start()
     seg = lax.broadcasted_iota(jnp.int32, (SEG, LANES), 0).astype(F32) * seg_len
-    for o, (u, prm) in enumerate(((u0, p0), (u1, p1))):
+    for o, prm in enumerate((p0, p1)):
         base = lax.rem(core + o, 2) * (2 * LANES)
         for q in range(2):
             lanes = pl.ds(q * LANES, LANES)
@@ -291,8 +332,7 @@
             for k in range(MODES):
                 d = jnp.broadcast_to(prm[pl.ds(k, 1), lanes], (SEG, LANES))
                 rate = prm[pl.ds(48 + k, 1), lanes]
-                start = shift_down(u[pl.ds(k * SEG, SEG), lanes], 1)
-                start = start + jnp.exp(-rate * seg) * state[k:k + 1]
+                start = jnp.exp(-rate * seg) * state[k:k + 1]
                 decay.append(d)
                 carried.append(prm[pl.ds(MODES + k, 1), lanes] * d * start)
             if q == 0:
@@ -313,14 +353,14 @@
             out_ref[:, to] = wide[...].astype(out_ref.dtype)
 
 
-def gate(core, ys, xs, us, prms, state, rows):
+def gate(core, ys, xs, prms, state, rows):
     vmem = pl.BlockSpec(memory_space=pltpu.VMEM)
     anywhere = pl.BlockSpec(memory_space=pl.ANY)
     wide = 2 * LANES
     return pl.pallas_call(
         functools.partial(gate_kernel, rows),
         out_shape=jax.ShapeDtypeStruct((rows, BLOCK), jnp.bfloat16),
-        in_specs=[pl.BlockSpec(memory_space=pltpu.SMEM)] + [anywhere] * 4 + [vmem] * 9,
+        in_specs=[pl.BlockSpec(memory_space=pltpu.SMEM)] + [anywhere] * 4 + [vmem] * 7,
         out_specs=vmem,
         scratch_shapes=[
             pltpu.VMEM((2, rows, wide), F32),
@@ -329,7 +369,7 @@
             pltpu.SemaphoreType.DMA((4,)),
         ],
         compiler_params=pltpu.CompilerParams(vmem_limit_bytes=20 << 20),
-    )(core, *ys, *xs, *us, *prms, *state)
+    )(core, *ys, *xs, *prms, *state)
 
 
 def on_device(tokens, in_weight, short_filter, filter_residues, filter_rates, skip_gain):
@@ -382,33 +422,33 @@
     t, b, where, core_at, fades, behind, plane, chip, *prms = together(
         (t, b, where, core_at, fades, behind, plane, chip, *prms)
     )
-    tp_, tm, ty = along_z(t, 1), along_z(t, -1), other_yhi(t)
+    ty = other_yhi(t)
+    tp_, tm = along_z(t, 1), along_z(t, -1)
     bp, bm = along_x(b, 1), along_x(b, -1)
     t, b, tp_, tm, ty, bp, bm = together((t, b, tp_, tm, ty, bp, bm))
     typ, tym = along_z(ty, 1), along_z(ty, -1)
     cb, cbp, cbm = other_core(b), other_core(bp), other_core(bm)
     b, bp, cb, cbp, cbm = together((b, bp, cb, cbp, cbm))
     bf, a = along_x(bp, 1), other_ylo(b)
-    t, b, tp_, tm, ty, bp, bm, typ, tym, bf, a, cb, cbp, cbm = together(
-        (t, b, tp_, tm, ty, bp, bm, typ, tym, bf, a, cb, cbp, cbm)
-    )
+    bf, a = together((bf, a))
+    ap, am, af = along_x(a, 1), along_x(a, -1), other_ylo(bf)
+    t, tp_, tm, ty, typ, tym, bf, a = together((t, tp_, tm, ty, typ, tym, bf, a))
     tf, tyf = along_z(tp_, 1), along_z(tym, -1)
-    ap = along_x(a, 1)
     cbf, ca = other_core(bf), other_core(a)
-    bf, a, cbf, ca = together((bf, a, cbf, ca))
-    am, af = along_x(a, -1), other_ylo(bf)
     lhs, part = begin(where, [t, tp_, tm, ty, typ, tym], [b, bp, bm, bf], rows)
     part_too = also(where, lhs, [cb, cbp, cbm, cbf], rows)
-    lhs, part, part_too, ap, am, af, tf, tyf = together(
-        (lhs, part, part_too, ap, am, af, tf, tyf)
-    )
+    ap, am, af, part_too = together((ap, am, af, part_too))
+    cap, cam, caf = other_core(ap), other_core(am), other_core(af)
     mine = [b, bp, bm, bf, a, ap, am, af]
-    theirs = [cb, cbp, cbm, cbf, ca] + [other_core(w) for w in (ap, am, af)]
-
-    ys, xs, us, ends = [], [], [], []
+    theirs = [cb, cbp, cbm, cbf, ca, cap, cam, caf]
+    part = more(where, lhs, part, mine[4:], rows)
+    part_too = more(where, lhs, part_too, theirs[4:], rows)
+    tf, tyf, part, part_too = together((tf, tyf, part, part_too))
+
+    products, xs, us, ends = [], [], [], []
     for o, (weights, done) in enumerate(((mine, part), (theirs, part_too))):
-        y, x1, u, end = project(where, lhs, tf, tyf, done, weights, prms[o], rows)
-        ys.append(y)
+        product, x1, u, end = project(where, tf, tyf, done, weights, prms[o], rows)
+        products.append(product)
         xs.append(x1)
         us.append(u)
         ends.append(end)
@@ -416,12 +456,17 @@
     total = jnp.concatenate(
         [jnp.where(core == 0, ends[0], ends[1]), jnp.where(core == 0, ends[1], ends[0])], axis=1
     )
+    total, products[0] = together((total, products[0]))
     came = [total] + [along_x(total, m) for m in (1, 2, 3)]
+    y0 = read(products[0], us[0], prms[0], rows)
+    came, products[1], y0 = together((came, products[1], y0))
+    total = came[0]
     near = behind[0] * came[1] + behind[1] * came[2] + behind[2] * came[3]
     whole = plane[0] * came[0] + plane[1] * came[1] + plane[2] * came[2] + plane[3] * came[3]
     sent = other_core(jnp.where(core == 0, chip * near + total, near))
-    state = [near, sent, other_ylo(whole), other_ylo_and_core(whole), fades]
-    return gate(core_at, ys, xs, us, prms, state, rows)
+    same, cross = other_ylo(whole), other_ylo_and_core(whole)
+    y1 = read(products[1], us[1], prms[1], rows)
+    return gate(core_at, [y0, y1], xs, prms, [near, sent, same, cross, fades], rows)
 
 
 def solution(mesh):

time: 161 us -> 169 us (1.050)
  Pallas kernels: 41.3 us -> 51.7 us
  starting transfers between devices: 55.6 us -> 51.2 us
  local copies, waits for them, and re-layouts: 3.33 us -> 6.2 us
  waiting for transfers between devices: 57.7 us -> 55.8 us
    pallas_call x0 -> x4, Pallas kernels: none -> 17.1 us  [the longest x2 12 us: more(): pl.pallas_call(functools.partial(more_kernel, rows), out_shape=jax.ShapeD...]
    pallas_call x2, Pallas kernels: 24.4 us -> 17.7 us  [project(): pl.pallas_call(functools.partial(project_kernel, rows), out_shape=[jax.Sh...]
    ppermute x30, starting transfers between devices: 55.6 us -> 51.2 us  [send(): return lax.ppermute(value, ('ctx', 'tp'), route(move))]
    unnamed x5 -> x43, local copies, waits for them, and re-layouts: 1.52 us -> 4.17 us
    ppermute x30, waiting for transfers between devices: 57.7 us -> 55.8 us  [send(): return lax.ppermute(value, ('ctx', 'tp'), route(move))]
  transfers between devices with their start and end apart: 30 -> 30, of which waited for: 13 -> 11; matrix products, arithmetic and copies ran while one was open for 2% -> 2% of each run, Pallas kernels for 15% -> 17%
where the time goes in v4:
time: 169 us
  waiting for transfers between devices  55.8 us (33%)
  Pallas kernels  51.7 us (31%)
  starting transfers between devices  51.2 us (30%)
  local copies, waits for them, and re-layouts  6.2 us (4%)
  other arithmetic  2.94 us (2%)
    ppermute x30, waiting for transfers between devices, send(): return lax.ppermute(value, ('ctx', 'tp'), route(move))  55.8 us
    ppermute x30, starting transfers between devices, send(): return lax.ppermute(value, ('ctx', 'tp'), route(move))  51.2 us
    pallas_call x2, Pallas kernels, project(): pl.pallas_call(functools.partial(project_kernel, rows), out_shape=[jax.Sh...  17.7 us
    pallas_call x2, Pallas kernels, more(): pl.pallas_call(functools.partial(more_kernel, rows), out_shape=jax.ShapeD...  12 us
    pallas_call x1, Pallas kernels, begin(): pl.pallas_call(functools.partial(begin_kernel, rows), out_shape=[jax.Shap...  6.42 us
    pallas_call x1, Pallas kernels, also(): pl.pallas_call(functools.partial(also_kernel, rows), out_shape=jax.ShapeD...  5.9 us
    pallas_call x2, Pallas kernels, read(): pl.pallas_call(functools.partial(read_kernel, rows), out_shape=jax.ShapeD...  5.09 us
    pallas_call x1, Pallas kernels, gate(): pl.pallas_call(functools.partial(gate_kernel, rows), out_shape=jax.ShapeD...  4.56 us
  transfers between devices with their start and end apart: 30, of which 11 were waited for; matrix products, arithmetic and copies ran while one was open for 2% of the time, Pallas kernels for 17%

profile of v4, /device:TPU:1, one launch (start us, length us, event | category | flops | bytes accessed | tf_op | source)
XLA Modules:
  0.0 168.5 jit_solution(187872793954256928)
XLA Ops:
  0.0 0.8 slice.24
  0.8 1.4 copy.8
  2.2 4.5 %collective-permute-start = (bf16[16,512]{1,0:T(8,128)(2,1)S(1)}, bf16[16,512]{1,0:T(8,128)(2,1)S(1)}, u32[]{:S(2)}, u32[]{:S(2)}) collective-permute-start(bf16[16,512]{1,0:T(8,128)(2,1)S(1)} %slice.24), channel_id=1, source_target_pairs={{0,8},{1,9},{2,10},{3,11},{4,12},{5,13},{6,14},{7,15},{8,16},{9,17... | collective-permute-start | bytes 49160 | tf_op jit(solution)/shard_map/ppermute | solution.py:41
  6.7 0.3 copy.9
  7.0 0.7 collective-permute-start.1
  7.8 0.8 bitcast_multiply_fusion.7
  8.6 0.0 copy-start.18
  8.6 0.1 negate_exponential_fusion
  8.8 0.8 dynamic_slice.21
  9.7 0.6 pad_maximum_fusion.2.fades
  10.4 0.7 pad_maximum_fusion.1
  11.0 0.7 pad_maximum_fusion.3
  11.7 0.1 stack.67.where
  11.8 0.1 pad_maximum_fusion.refs_0_
  11.8 0.0 collective-permute-done.1.refs_6_.refs_3_
  11.9 18.4 %collective-permute-start.4 = (bf16[1040,512]{1,0:T(8,128)(2,1)S(1)}, bf16[1040,512]{1,0:T(8,128)(2,1)S(1)}, u32[]{:S(2)}, u32[]{:S(2)}) collective-permute-start(bf16[1040,512]{1,0:T(8,128)(2,1)S(1)} %pad_maximum_fusion.refs_0_), channel_id=1, source_target_pairs={{0,4},{1,5},{2,6},{3,7},{4,0},{5,1},{6,2},{7,3},{8,12},{9,13},{10,... | collective-permute-start | bytes 3194888 | tf_op jit(solution)/shard_map/ppermute | solution.py:41
  30.2 8.3 %collective-permute-start.3 = (bf16[1040,512]{1,0:T(8,128)(2,1)S(1)}, bf16[1040,512]{1,0:T(8,128)(2,1)S(1)}, u32[]{:S(2)}, u32[]{:S(2)}) collective-permute-start(bf16[1040,512]{1,0:T(8,128)(2,1)S(1)} %pad_maximum_fusion.refs_0_), channel_id=1, source_target_pairs={{0,3},{1,0},{2,1},{3,2},{4,7},{5,4},{6,5},{7,6},{8,11},{9,8},{10,9... | collective-permute-start | bytes 3194888 | tf_op jit(solution)/shard_map/ppermute | solution.py:41
  38.5 0.0 collective-permute-start.2
  38.5 0.3 collective-permute-start.6
  38.8 1.2 collective-permute-start.5
  40.0 17.2 %collective-permute-done.6.refs_8_.refs_5_ = bf16[512,768]{1,0:T(8,128)(2,1)S(1)} collective-permute-done((bf16[512,768]{1,0:T(8,128)(2,1)S(1)}, bf16[512,768]{1,0:T(8,128)(2,1)S(1)}, u32[]{:S(2)}, u32[]{:S(2)}) %collective-permute-start.6) | collective-permute-done | bytes 786464 | tf_op jit(solution)/shard_map/ppermute | solution.py:41
  57.2 0.6 collective-permute-done.5.refs_7_.refs_4_
  57.7 0.0 collective-permute-done.4.refs_3_
  57.7 3.5 %collective-permute-done.3.refs_2_ = bf16[1040,512]{1,0:T(8,128)(2,1)S(1)} collective-permute-done((bf16[1040,512]{1,0:T(8,128)(2,1)S(1)}, bf16[1040,512]{1,0:T(8,128)(2,1)S(1)}, u32[]{:S(2)}, u32[]{:S(2)}) %collective-permute-start.3) | collective-permute-done | bytes 1064992 | tf_op jit(solution)/shard_map/ppermute | solution.py:41
  61.2 3.1 %collective-permute-done.2.refs_1_ = bf16[1040,512]{1,0:T(8,128)(2,1)S(1)} collective-permute-done((bf16[1040,512]{1,0:T(8,128)(2,1)S(1)}, bf16[1040,512]{1,0:T(8,128)(2,1)S(1)}, u32[]{:S(2)}, u32[]{:S(2)}) %collective-permute-start.2) | collective-permute-done | bytes 1064992 | tf_op jit(solution)/shard_map/ppermute | solution.py:41
  64.3 1.3 collective-permute-start.9
  65.6 0.0 collective-permute-start.10
  65.7 0.5 collective-permute-start.11
  66.2 0.0 collective-permute-start.8
  66.2 1.5 collective-permute-start.7
  67.6 1.1 collective-permute-done.10.refs_2_.refs_4_
  68.7 1.1 collective-permute-done.11.refs_3_.refs_5_
  69.8 0.2 collective-permute-start.12
  70.0 19.8 %collective-permute-done.12.refs_9_.refs_6_ = bf16[512,768]{1,0:T(8,128)(2,1)S(1)} collective-permute-done((bf16[512,768]{1,0:T(8,128)(2,1)S(1)}, bf16[512,768]{1,0:T(8,128)(2,1)S(1)}, u32[]{:S(2)}, u32[]{:S(2)}) %collective-permute-start.12) | collective-permute-done | bytes 786464 | tf_op jit(solution)/shard_map/ppermute | solution.py:41
  89.8 1.5 collective-permute-done.8.refs_5_
  91.3 0.9 collective-permute-done.7.refs_4_
  92.2 1.1 collective-permute-start.19
  93.3 0.3 collective-permute-start.17
  93.6 1.2 collective-permute-start.16
  94.8 0.6 collective-permute-start.20
  95.3 6.4 %shard_map.64 = (bf16[8,1040,512]{2,1,0:T(8,128)(2,1)S(1)}, f32[1040,768]{1,0:T(8,128)S(1)}) custom-call(s32[9]{0:T(128)S(1)} %stack.67.where, bf16[1040,512]{1,0:T(8,128)(2,1)S(1)} %pad_maximum_fusion.refs_0_, bf16[1040,512]{1,0:T(8,128)(2,1)S(1)} %collective-permute-done.2.refs_1_, bf16[1040,512]{1,0:T(8,128)(2,1)S(1)} %collective-permute-done.3.refs_2_, ...), custom_call_target="tpu_custom_call" | custom-call | flops 2453667840 | bytes 12582912 | tf_op jit(solution)/shard_map/pallas_call | solution.py:128
  101.8 5.9 %collective-permute-done.18.refs_5_.refs_10_ = bf16[512,768]{1,0:T(8,128)(2,1)S(1)} collective-permute-done((bf16[512,768]{1,0:T(8,128)(2,1)S(1)}, bf16[512,768]{1,0:T(8,128)(2,1)S(1)}, u32[]{:S(2)}, u32[]{:S(2)}) %collective-permute-start.18) | collective-permute-done | bytes 786464 | tf_op jit(solution)/shard_map/ppermute | solution.py:41
  107.6 2.7 %collective-permute-start.15 = (bf16[1040,512]{1,0:T(8,128)(2,1)S(1)}, bf16[1040,512]{1,0:T(8,128)(2,1)}, u32[]{:S(2)}, u32[]{:S(2)}) collective-permute-start(bf16[1040,512]{1,0:T(8,128)(2,1)S(1)} %collective-permute-done.8.refs_5_), channel_id=1, source_target_pairs={{0,3},{1,0},{2,1},{3,2},{4,7},{5,4},{6,5},{7,6},{8,11},{9,8},{10,9... | collective-permute-start | bytes 3194888 | tf_op jit(solution)/shard_map/ppermute | solution.py:41
  110.3 5.9 %shard_map.65.refs_1_ = f32[1040,768]{1,0:T(8,128)S(1)} custom-call(s32[9]{0:T(128)S(1)} %stack.67.where, bf16[8,1040,512]{2,1,0:T(8,128)(2,1)S(1)} %get-tuple-element.89.refs_0_, bf16[512,768]{1,0:T(8,128)(2,1)S(1)} %collective-permute-done.9.refs_1_.refs_3_, bf16[512,768]{1,0:T(8,128)(2,1)S(1)} %collective-permute-done.10.refs_2_.refs_4_, ...), custom_call_target="tpu_custom_call" | custom-call | flops 2453667840 | bytes 12582912 | tf_op jit(solution)/shard_map/pallas_call | solution.py:146
  116.2 2.8 %collective-permute-start.21 = (bf16[512,768]{1,0:T(8,128)(2,1)S(1)}, bf16[512,768]{1,0:T(8,128)(2,1)S(1)}, u32[]{:S(2)}, u32[]{:S(2)}) collective-permute-start(bf16[512,768]{1,0:T(8,128)(2,1)S(1)} %collective-permute-done.16.refs_3_.refs_8_), channel_id=1, source_target_pairs={{0,8},{1,9},{2,10},{3,11},{4,12},{5,13},{6,14},{7,15},{8,0},{9,1},... | collective-permute-start | bytes 2359304 | tf_op jit(solution)/shard_map/ppermute | solution.py:41
  119.0 0.1 collective-permute-start.22
  119.1 0.9 copy-done.9
  120.0 0.4 collective-permute-start.23
  120.5 6.1 %shard_map.66.refs_2_ = f32[1040,768]{1,0:T(8,128)S(1)} custom-call(s32[9]{0:T(128)S(1)} %stack.67.where, bf16[8,1040,512]{2,1,0:T(8,128)(2,1)S(1)} %get-tuple-element.89.refs_0_, f32[1040,768]{1,0:T(8,128)S(1)} %get-tuple-element.90.refs_1_, bf16[512,768]{1,0:T(8,128)(2,1)S(1)} %collective-permute-done.13.refs_2_.refs_7_, ...), custom_call_target="tpu_custom_call" | custom-call | flops 2453667840 | bytes 12582912 | tf_op jit(solution)/shard_map/pallas_call | solution.py:175
  126.6 0.9 copy-done.11
  127.5 5.9 %shard_map.67.refs_2_ = f32[1040,768]{1,0:T(8,128)S(1)} custom-call(s32[9]{0:T(128)S(1)} %stack.67.where, bf16[8,1040,512]{2,1,0:T(8,128)(2,1)S(1)} %get-tuple-element.89.refs_0_, f32[1040,768]{1,0:T(8,128)S(1)} %shard_map.65.refs_1_, bf16[512,768]{1,0:T(8,128)(2,1)S(1)} %copy-done.10, bf16[512,768]{1,0:T(8,128)(2,1)S(1)} %collective-permute-done.21.refs_3_.refs_8_, ...), custom_call_target="tpu_custom_call" | custom-call | flops 2453667840 | bytes 12582912 | tf_op jit(solution)/shard_map/pallas_call | solution.py:175
  133.4 0.9 copy-done.13
  134.4 8.9 %shard_map.68 = (f32[1024,256]{1,0:T(8,128)S(1)}, f32[1024,256]{1,0:T(8,128)S(1)}, f32[128,256]{1,0:T(8,128)S(1)}, f32[16,256]{1,0:T(8,128)S(1)}) custom-call(s32[9]{0:T(128)S(1)} %stack.67.where, bf16[1040,512]{1,0:T(8,128)(2,1)} %collective-permute-done.14.refs_0_, bf16[1040,512]{1,0:T(8,128)(2,1)} %collective-permute-done.15.refs_1_, ...), custom_call_target="tpu_custom_call" | custom-call | flops 3271557120 | bytes 12582912 | tf_op jit(solution)/shard_map/pallas_call | solution.py:245
  143.3 8.8 %shard_map.69 = (f32[1024,256]{1,0:T(8,128)S(1)}, f32[1024,256]{1,0:T(8,128)S(1)}, f32[128,256]{1,0:T(8,128)S(1)}, f32[16,256]{1,0:T(8,128)S(1)}) custom-call(s32[9]{0:T(128)S(1)} %stack.67.where, bf16[1040,512]{1,0:T(8,128)(2,1)} %collective-permute-done.14.refs_0_, bf16[1040,512]{1,0:T(8,128)(2,1)} %collective-permute-done.15.refs_1_, ...), custom_call_target="tpu_custom_call" | custom-call | flops 3271557120 | bytes 12582912 | tf_op jit(solution)/shard_map/pallas_call | solution.py:245
  152.1 1.2 collective-permute-start.26
  153.3 0.7 collective-permute-start.24
  154.0 2.5 %shard_map.70.y0 = f32[1024,256]{1,0:T(8,128)S(1)} custom-call(f32[1024,256]{1,0:T(8,128)S(1)} %get-tuple-element.110.prod_ref, f32[128,256]{1,0:T(8,128)S(1)} %get-tuple-element.111.u_ref, f32[64,256]{1,0:T(8,128)S(1)} %get-tuple-element.102.refs_11_.prm.p0), custom_call_target="tpu_custom_call" | custom-call | flops 16777216 | bytes 12582912 | tf_op jit(solution)/shard_map/pallas_call | solution.py:293
  156.6 1.1 collective-permute-done.25
  157.7 0.0 collective-permute-done.24
  157.8 2.0 %collective-permute-start.27 = (f32[16,512]{1,0:T(8,128)S(1)}, f32[16,512]{1,0:T(8,128)S(1)}, u32[]{:S(2)}, u32[]{:S(2)}) collective-permute-start(f32[16,512]{1,0:T(8,128)S(1)} %get-tuple-element.125), channel_id=1, source_target_pairs={{0,8},{1,9},{2,10},{3,11},{4,12},{5,13},{6,14},{7,15},{8,0},{9,1},... | collective-permute-start | bytes 98312 | tf_op jit(solution)/shard_map/ppermute | solution.py:41
  159.8 0.5 collective-permute-start.29
  160.3 0.9 collective-permute-start.28
  161.2 2.5 %shard_map.71.y1 = f32[1024,256]{1,0:T(8,128)S(1)} custom-call(f32[1024,256]{1,0:T(8,128)S(1)} %get-tuple-element.113.prod_ref, f32[128,256]{1,0:T(8,128)S(1)} %get-tuple-element.114.u_ref, f32[64,256]{1,0:T(8,128)S(1)} %get-tuple-element.105.refs_11_.prm.p1), custom_call_target="tpu_custom_call" | custom-call | flops 16777216 | bytes 12582912 | tf_op jit(solution)/shard_map/pallas_call | solution.py:293
  163.8 4.6 %shard_map.72 = bf16[1024,512]{1,0:T(8,128)(2,1)} custom-call(s32[1]{0:T(128)} %bitcast.9.core_ref, f32[1024,256]{1,0:T(8,128)S(1)} %shard_map.70.y0, f32[1024,256]{1,0:T(8,128)S(1)} %shard_map.71.y1, f32[1024,256]{1,0:T(8,128)S(1)} %get-tuple-element.115.x0, f32[1024,256]{1,0:T(8,128)S(1)} %get-tuple-element.116.x1, ...), custom_call_target="tpu_custom_call" | custom-call | tf_op jit(solution)/shard_map/pallas_call | solution.py:360
  (66 shorter events, 0.2 us)
Async XLA Ops:
  0.0 8.7 %copy-start = (f32[3,3,4096]{2,1,0:T(4,128)S(1)}, f32[3,3,4096]{2,1,0:T(4,128)}, u32[]{:S(2)}) copy-start(f32[3,3,4096]{2,1,0:T(4,128)} %param.8) | copy-start | bytes 442372
  2.2 9.6 %collective-permute-start = (bf16[16,512]{1,0:T(8,128)(2,1)S(1)}, bf16[16,512]{1,0:T(8,128)(2,1)S(1)}, u32[]{:S(2)}, u32[]{:S(2)}) collective-permute-start(bf16[16,512]{1,0:T(8,128)(2,1)S(1)} %slice.24), channel_id=1, source_target_pairs={{0,8},{1,9},{2,10},{3,11},{4,12},{5,13},{6,14},{7,15},{8,16},{9,17... | collective-permute-start | bytes 49160 | tf_op jit(solution)/shard_map/ppermute | solution.py:41
  7.0 4.9 %collective-permute-start.1 = (bf16[512,768]{1,0:T(8,128)(2,1)S(1)}, bf16[512,768]{1,0:T(8,128)(2,1)S(1)}, u32[]{:S(2)}, u32[]{:S(2)}) collective-permute-start(bf16[512,768]{1,0:T(8,128)(2,1)S(1)} %copy.9), channel_id=1, source_target_pairs={{0,0},{1,16},{2,32},{3,48},{4,64},{5,80},{6,96},{7,112},{8,8},{9,2... | collective-permute-start | bytes 2359304 | tf_op jit(solution)/shard_map/ppermute | solution.py:41
  8.6 3.1 %copy-start.18 = (bf16[1024,512]{1,0:T(8,128)(2,1)S(1)}, bf16[1024,512]{1,0:T(8,128)(2,1)}, u32[]{:S(2)}) copy-start(bf16[1024,512]{1,0:T(8,128)(2,1)} %param.6) | copy-start | bytes 3145732
  11.9 45.9 %collective-permute-start.4 = (bf16[1040,512]{1,0:T(8,128)(2,1)S(1)}, bf16[1040,512]{1,0:T(8,128)(2,1)S(1)}, u32[]{:S(2)}, u32[]{:S(2)}) collective-permute-start(bf16[1040,512]{1,0:T(8,128)(2,1)S(1)} %pad_maximum_fusion.refs_0_), channel_id=1, source_target_pairs={{0,4},{1,5},{2,6},{3,7},{4,0},{5,1},{6,2},{7,3},{8,12},{9,13},{10,... | collective-permute-start | bytes 3194888 | tf_op jit(solution)/shard_map/ppermute | solution.py:41
  30.2 31.0 %collective-permute-start.3 = (bf16[1040,512]{1,0:T(8,128)(2,1)S(1)}, bf16[1040,512]{1,0:T(8,128)(2,1)S(1)}, u32[]{:S(2)}, u32[]{:S(2)}) collective-permute-start(bf16[1040,512]{1,0:T(8,128)(2,1)S(1)} %pad_maximum_fusion.refs_0_), channel_id=1, source_target_pairs={{0,3},{1,0},{2,1},{3,2},{4,7},{5,4},{6,5},{7,6},{8,11},{9,8},{10,9... | collective-permute-start | bytes 3194888 | tf_op jit(solution)/shard_map/ppermute | solution.py:41
  38.5 25.8 %collective-permute-start.2 = (bf16[1040,512]{1,0:T(8,128)(2,1)S(1)}, bf16[1040,512]{1,0:T(8,128)(2,1)S(1)}, u32[]{:S(2)}, u32[]{:S(2)}) collective-permute-start(bf16[1040,512]{1,0:T(8,128)(2,1)S(1)} %pad_maximum_fusion.refs_0_), channel_id=1, source_target_pairs={{0,1},{1,2},{2,3},{3,0},{4,5},{5,6},{6,7},{7,4},{8,9},{9,10},{10,1... | collective-permute-start | bytes 3194888 | tf_op jit(solution)/shard_map/ppermute | solution.py:41
  38.5 18.6 %collective-permute-start.6 = (bf16[512,768]{1,0:T(8,128)(2,1)S(1)}, bf16[512,768]{1,0:T(8,128)(2,1)S(1)}, u32[]{:S(2)}, u32[]{:S(2)}) collective-permute-start(bf16[512,768]{1,0:T(8,128)(2,1)S(1)} %collective-permute-done.1.refs_6_.refs_3_), channel_id=1, source_target_pairs={{0,48},{1,49},{2,50},{3,51},{4,52},{5,53},{6,54},{7,55},{8,56},{9,... | collective-permute-start | bytes 2359304 | tf_op jit(solution)/shard_map/ppermute | solution.py:41
  38.8 19.0 %collective-permute-start.5 = (bf16[512,768]{1,0:T(8,128)(2,1)S(1)}, bf16[512,768]{1,0:T(8,128)(2,1)S(1)}, u32[]{:S(2)}, u32[]{:S(2)}) collective-permute-start(bf16[512,768]{1,0:T(8,128)(2,1)S(1)} %collective-permute-done.1.refs_6_.refs_3_), channel_id=1, source_target_pairs={{0,16},{1,17},{2,18},{3,19},{4,20},{5,21},{6,22},{7,23},{8,24},{9,... | collective-permute-start | bytes 2359304 | tf_op jit(solution)/shard_map/ppermute | solution.py:41
  64.3 3.3 %collective-permute-start.9 = (bf16[512,768]{1,0:T(8,128)(2,1)S(1)}, bf16[512,768]{1,0:T(8,128)(2,1)S(1)}, u32[]{:S(2)}, u32[]{:S(2)}) collective-permute-start(bf16[512,768]{1,0:T(8,128)(2,1)S(1)} %collective-permute-done.1.refs_6_.refs_3_), channel_id=1, source_target_pairs={{0,8},{1,9},{2,10},{3,11},{4,12},{5,13},{6,14},{7,15},{8,0},{9,1},... | collective-permute-start | bytes 2359304 | tf_op jit(solution)/shard_map/ppermute | solution.py:41
  65.6 3.0 %collective-permute-start.10 = (bf16[512,768]{1,0:T(8,128)(2,1)S(1)}, bf16[512,768]{1,0:T(8,128)(2,1)S(1)}, u32[]{:S(2)}, u32[]{:S(2)}) collective-permute-start(bf16[512,768]{1,0:T(8,128)(2,1)S(1)} %collective-permute-done.5.refs_7_.refs_4_), channel_id=1, source_target_pairs={{0,8},{1,9},{2,10},{3,11},{4,12},{5,13},{6,14},{7,15},{8,0},{9,1},... | collective-permute-start | bytes 2359304 | tf_op jit(solution)/shard_map/ppermute | solution.py:41
  65.7 4.2 %collective-permute-start.11 = (bf16[512,768]{1,0:T(8,128)(2,1)S(1)}, bf16[512,768]{1,0:T(8,128)(2,1)S(1)}, u32[]{:S(2)}, u32[]{:S(2)}) collective-permute-start(bf16[512,768]{1,0:T(8,128)(2,1)S(1)} %collective-permute-done.6.refs_8_.refs_5_), channel_id=1, source_target_pairs={{0,8},{1,9},{2,10},{3,11},{4,12},{5,13},{6,14},{7,15},{8,0},{9,1},... | collective-permute-start | bytes 2359304 | tf_op jit(solution)/shard_map/ppermute | solution.py:41
  66.2 25.1 %collective-permute-start.8 = (bf16[1040,512]{1,0:T(8,128)(2,1)S(1)}, bf16[1040,512]{1,0:T(8,128)(2,1)S(1)}, u32[]{:S(2)}, u32[]{:S(2)}) collective-permute-start(bf16[1040,512]{1,0:T(8,128)(2,1)S(1)} %collective-permute-done.4.refs_3_), channel_id=1, source_target_pairs={{0,3},{1,0},{2,1},{3,2},{4,7},{5,4},{6,5},{7,6},{8,11},{9,8},{10,9... | collective-permute-start | bytes 3194888 | tf_op jit(solution)/shard_map/ppermute | solution.py:41
  66.2 26.0 %collective-permute-start.7 = (bf16[1040,512]{1,0:T(8,128)(2,1)S(1)}, bf16[1040,512]{1,0:T(8,128)(2,1)S(1)}, u32[]{:S(2)}, u32[]{:S(2)}) collective-permute-start(bf16[1040,512]{1,0:T(8,128)(2,1)S(1)} %collective-permute-done.4.refs_3_), channel_id=1, source_target_pairs={{0,1},{1,2},{2,3},{3,0},{4,5},{5,6},{6,7},{7,4},{8,9},{9,10},{10,1... | collective-permute-start | bytes 3194888 | tf_op jit(solution)/shard_map/ppermute | solution.py:41
  69.8 40.5 %copy-start.1 = (bf16[512,768]{1,0:T(8,128)(2,1)}, bf16[512,768]{1,0:T(8,128)(2,1)S(1)}, u32[]{:S(2)}) copy-start(bf16[512,768]{1,0:T(8,128)(2,1)S(1)} %collective-permute-done.11.refs_3_.refs_5_) | copy-start | bytes 2359300
  69.8 20.0 %collective-permute-start.12 = (bf16[512,768]{1,0:T(8,128)(2,1)S(1)}, bf16[512,768]{1,0:T(8,128)(2,1)S(1)}, u32[]{:S(2)}, u32[]{:S(2)}) collective-permute-start(bf16[512,768]{1,0:T(8,128)(2,1)S(1)} %collective-permute-done.5.refs_7_.refs_4_), channel_id=1, source_target_pairs={{0,16},{1,17},{2,18},{3,19},{4,20},{5,21},{6,22},{7,23},{8,24},{9,... | collective-permute-start | bytes 2359304 | tf_op jit(solution)/shard_map/ppermute | solution.py:41
  70.0 19.8 %collective-permute-start.13 = (bf16[512,768]{1,0:T(8,128)(2,1)S(1)}, bf16[512,768]{1,0:T(8,128)(2,1)S(1)}, u32[]{:S(2)}, u32[]{:S(2)}) collective-permute-start(bf16[512,768]{1,0:T(8,128)(2,1)S(1)} %collective-permute-done.1.refs_6_.refs_3_), channel_id=1, source_target_pairs={{0,64},{1,65},{2,66},{3,67},{4,68},{5,69},{6,70},{7,71},{8,72},{9,... | collective-permute-start | bytes 2359304 | tf_op jit(solution)/shard_map/ppermute | solution.py:41
  89.8 30.7 %copy-start.3 = (bf16[512,768]{1,0:T(8,128)(2,1)}, bf16[512,768]{1,0:T(8,128)(2,1)S(1)}, u32[]{:S(2)}) copy-start(bf16[512,768]{1,0:T(8,128)(2,1)S(1)} %collective-permute-done.13.refs_2_.refs_7_) | copy-start | bytes 2359300
  89.8 17.8 %collective-permute-start.18 = (bf16[512,768]{1,0:T(8,128)(2,1)S(1)}, bf16[512,768]{1,0:T(8,128)(2,1)S(1)}, u32[]{:S(2)}, u32[]{:S(2)}) collective-permute-start(bf16[512,768]{1,0:T(8,128)(2,1)S(1)} %collective-permute-done.12.refs_9_.refs_6_), channel_id=1, source_target_pairs={{0,64},{1,65},{2,66},{3,67},{4,68},{5,69},{6,70},{7,71},{8,72},{9,... | collective-permute-start | bytes 2359304 | tf_op jit(solution)/shard_map/ppermute | solution.py:41
  92.2 15.4 %collective-permute-start.19 = (bf16[512,768]{1,0:T(8,128)(2,1)S(1)}, bf16[512,768]{1,0:T(8,128)(2,1)S(1)}, u32[]{:S(2)}, u32[]{:S(2)}) collective-permute-start(bf16[512,768]{1,0:T(8,128)(2,1)S(1)} %collective-permute-done.12.refs_9_.refs_6_), channel_id=1, source_target_pairs={{0,8},{1,9},{2,10},{3,11},{4,12},{5,13},{6,14},{7,15},{8,0},{9,1},... | collective-permute-start | bytes 2359304 | tf_op jit(solution)/shard_map/ppermute | solution.py:41
  93.3 22.9 %collective-permute-start.17 = (bf16[512,768]{1,0:T(8,128)(2,1)S(1)}, bf16[512,768]{1,0:T(8,128)(2,1)S(1)}, u32[]{:S(2)}, u32[]{:S(2)}) collective-permute-start(bf16[512,768]{1,0:T(8,128)(2,1)S(1)} %collective-permute-done.13.refs_2_.refs_7_), channel_id=1, source_target_pairs={{0,48},{1,49},{2,50},{3,51},{4,52},{5,53},{6,54},{7,55},{8,56},{9,... | collective-permute-start | bytes 2359304 | tf_op jit(solution)/shard_map/ppermute | solution.py:41
  93.6 22.7 %collective-permute-start.16 = (bf16[512,768]{1,0:T(8,128)(2,1)S(1)}, bf16[512,768]{1,0:T(8,128)(2,1)S(1)}, u32[]{:S(2)}, u32[]{:S(2)}) collective-permute-start(bf16[512,768]{1,0:T(8,128)(2,1)S(1)} %collective-permute-done.13.refs_2_.refs_7_), channel_id=1, source_target_pairs={{0,16},{1,17},{2,18},{3,19},{4,20},{5,21},{6,22},{7,23},{8,24},{9,... | collective-permute-start | bytes 2359304 | tf_op jit(solution)/shard_map/ppermute | solution.py:41
  94.8 24.3 %collective-permute-start.20 = (bf16[512,768]{1,0:T(8,128)(2,1)S(1)}, bf16[512,768]{1,0:T(8,128)(2,1)S(1)}, u32[]{:S(2)}, u32[]{:S(2)}) collective-permute-start(bf16[512,768]{1,0:T(8,128)(2,1)S(1)} %collective-permute-done.13.refs_2_.refs_7_), channel_id=1, source_target_pairs={{0,8},{1,9},{2,10},{3,11},{4,12},{5,13},{6,14},{7,15},{8,0},{9,1},... | collective-permute-start | bytes 2359304 | tf_op jit(solution)/shard_map/ppermute | solution.py:41
  107.6 12.8 %copy-start.7 = (bf16[512,768]{1,0:T(8,128)(2,1)}, bf16[512,768]{1,0:T(8,128)(2,1)S(1)}, u32[]{:S(2)}) copy-start(bf16[512,768]{1,0:T(8,128)(2,1)S(1)} %collective-permute-done.18.refs_5_.refs_10_) | copy-start | bytes 2359300
  107.6 26.7 %collective-permute-start.14 = (bf16[1040,512]{1,0:T(8,128)(2,1)S(1)}, bf16[1040,512]{1,0:T(8,128)(2,1)}, u32[]{:S(2)}, u32[]{:S(2)}) collective-permute-start(bf16[1040,512]{1,0:T(8,128)(2,1)S(1)} %collective-permute-done.2.refs_1_), channel_id=1, source_target_pairs={{0,1},{1,2},{2,3},{3,0},{4,5},{5,6},{6,7},{7,4},{8,9},{9,10},{10,1... | collective-permute-start | bytes 3194888 | tf_op jit(solution)/shard_map/ppermute | solution.py:41
  107.6 8.6 %copy-start.5 = (bf16[512,768]{1,0:T(8,128)(2,1)}, bf16[512,768]{1,0:T(8,128)(2,1)S(1)}, u32[]{:S(2)}) copy-start(bf16[512,768]{1,0:T(8,128)(2,1)S(1)} %collective-permute-done.19.refs_4_.refs_6_) | copy-start | bytes 2359300
  107.6 26.7 %collective-permute-start.15 = (bf16[1040,512]{1,0:T(8,128)(2,1)S(1)}, bf16[1040,512]{1,0:T(8,128)(2,1)}, u32[]{:S(2)}, u32[]{:S(2)}) collective-permute-start(bf16[1040,512]{1,0:T(8,128)(2,1)S(1)} %collective-permute-done.8.refs_5_), channel_id=1, source_target_pairs={{0,3},{1,0},{2,1},{3,2},{4,7},{5,4},{6,5},{7,6},{8,11},{9,8},{10,9... | collective-permute-start | bytes 3194888 | tf_op jit(solution)/shard_map/ppermute | solution.py:41
  116.2 11.2 %collective-permute-start.21 = (bf16[512,768]{1,0:T(8,128)(2,1)S(1)}, bf16[512,768]{1,0:T(8,128)(2,1)S(1)}, u32[]{:S(2)}, u32[]{:S(2)}) collective-permute-start(bf16[512,768]{1,0:T(8,128)(2,1)S(1)} %collective-permute-done.16.refs_3_.refs_8_), channel_id=1, source_target_pairs={{0,8},{1,9},{2,10},{3,11},{4,12},{5,13},{6,14},{7,15},{8,0},{9,1},... | collective-permute-start | bytes 2359304 | tf_op jit(solution)/shard_map/ppermute | solution.py:41
  119.0 8.4 %collective-permute-start.22 = (bf16[512,768]{1,0:T(8,128)(2,1)S(1)}, bf16[512,768]{1,0:T(8,128)(2,1)S(1)}, u32[]{:S(2)}, u32[]{:S(2)}) collective-permute-start(bf16[512,768]{1,0:T(8,128)(2,1)S(1)} %collective-permute-done.17.refs_4_.refs_9_), channel_id=1, source_target_pairs={{0,8},{1,9},{2,10},{3,11},{4,12},{5,13},{6,14},{7,15},{8,0},{9,1},... | collective-permute-start | bytes 2359304 | tf_op jit(solution)/shard_map/ppermute | solution.py:41
  119.1 0.9 copy-start.9
  120.0 7.4 %collective-permute-start.23 = (bf16[512,768]{1,0:T(8,128)(2,1)S(1)}, bf16[512,768]{1,0:T(8,128)(2,1)S(1)}, u32[]{:S(2)}, u32[]{:S(2)}) collective-permute-start(bf16[512,768]{1,0:T(8,128)(2,1)S(1)} %collective-permute-done.18.refs_5_.refs_10_), channel_id=1, source_target_pairs={{0,8},{1,9},{2,10},{3,11},{4,12},{5,13},{6,14},{7,15},{8,0},{9,1},... | collective-permute-start | bytes 2359304 | tf_op jit(solution)/shard_map/ppermute | solution.py:41
  120.5 7.0 %copy-start.10 = (bf16[512,768]{1,0:T(8,128)(2,1)S(1)}, bf16[512,768]{1,0:T(8,128)(2,1)}, u32[]{:S(2)}) copy-start(bf16[512,768]{1,0:T(8,128)(2,1)} %copy-done.9) | copy-start | bytes 2359300
  126.5 0.9 copy-start.11
  127.4 6.9 %copy-start.4 = (bf16[512,768]{1,0:T(8,128)(2,1)S(1)}, bf16[512,768]{1,0:T(8,128)(2,1)}, u32[]{:S(2)}) copy-start(bf16[512,768]{1,0:T(8,128)(2,1)} %copy-done.3) | copy-start | bytes 2359300
  127.4 6.9 %copy-start.8 = (bf16[512,768]{1,0:T(8,128)(2,1)S(1)}, bf16[512,768]{1,0:T(8,128)(2,1)}, u32[]{:S(2)}) copy-start(bf16[512,768]{1,0:T(8,128)(2,1)} %copy-done.7) | copy-start | bytes 2359300
  127.4 6.9 %copy-start.12 = (bf16[512,768]{1,0:T(8,128)(2,1)S(1)}, bf16[512,768]{1,0:T(8,128)(2,1)}, u32[]{:S(2)}) copy-start(bf16[512,768]{1,0:T(8,128)(2,1)} %copy-done.11) | copy-start | bytes 2359300
  127.5 5.9 %copy-start.15 = (bf16[512,768]{1,0:T(8,128)(2,1)}, bf16[512,768]{1,0:T(8,128)(2,1)S(1)}, u32[]{:S(2)}) copy-start(bf16[512,768]{1,0:T(8,128)(2,1)S(1)} %collective-permute-done.23.refs_5_.refs_10_) | copy-start | bytes 2359300
  133.4 0.9 copy-start.13
  134.3 9.0 %copy-start.2 = (bf16[512,768]{1,0:T(8,128)(2,1)S(1)}, bf16[512,768]{1,0:T(8,128)(2,1)}, u32[]{:S(2)}) copy-start(bf16[512,768]{1,0:T(8,128)(2,1)} %copy-done.1) | copy-start | bytes 2359300
  134.3 9.0 %copy-start.6 = (bf16[512,768]{1,0:T(8,128)(2,1)S(1)}, bf16[512,768]{1,0:T(8,128)(2,1)}, u32[]{:S(2)}) copy-start(bf16[512,768]{1,0:T(8,128)(2,1)} %copy-done.5) | copy-start | bytes 2359300
  134.3 9.0 %copy-start.14 = (bf16[512,768]{1,0:T(8,128)(2,1)S(1)}, bf16[512,768]{1,0:T(8,128)(2,1)}, u32[]{:S(2)}) copy-start(bf16[512,768]{1,0:T(8,128)(2,1)} %copy-done.13) | copy-start | bytes 2359300
  134.3 9.0 %copy-start.16 = (bf16[512,768]{1,0:T(8,128)(2,1)S(1)}, bf16[512,768]{1,0:T(8,128)(2,1)}, u32[]{:S(2)}) copy-start(bf16[512,768]{1,0:T(8,128)(2,1)} %copy-done.15) | copy-start | bytes 2359300
  152.1 4.4 %collective-permute-start.26 = (f32[16,512]{1,0:T(8,128)S(1)}, f32[16,512]{1,0:T(8,128)S(1)}, u32[]{:S(2)}, u32[]{:S(2)}) collective-permute-start(f32[16,512]{1,0:T(8,128)S(1)} %pad_maximum_fusion.4), channel_id=1, source_target_pairs={{0,48},{1,49},{2,50},{3,51},{4,52},{5,53},{6,54},{7,55},{8,56},{9,... | collective-permute-start | bytes 98312 | tf_op jit(solution)/shard_map/ppermute | solution.py:41
  153.3 4.4 %collective-permute-start.25 = (f32[16,512]{1,0:T(8,128)S(1)}, f32[16,512]{1,0:T(8,128)S(1)}, u32[]{:S(2)}, u32[]{:S(2)}) collective-permute-start(f32[16,512]{1,0:T(8,128)S(1)} %pad_maximum_fusion.4), channel_id=1, source_target_pairs={{0,32},{1,33},{2,34},{3,35},{4,36},{5,37},{6,38},{7,39},{8,40},{9,... | collective-permute-start | bytes 98312 | tf_op jit(solution)/shard_map/ppermute | solution.py:41
  153.3 4.4 %collective-permute-start.24 = (f32[16,512]{1,0:T(8,128)S(1)}, f32[16,512]{1,0:T(8,128)S(1)}, u32[]{:S(2)}, u32[]{:S(2)}) collective-permute-start(f32[16,512]{1,0:T(8,128)S(1)} %pad_maximum_fusion.4), channel_id=1, source_target_pairs={{0,16},{1,17},{2,18},{3,19},{4,20},{5,21},{6,22},{7,23},{8,24},{9,... | collective-permute-start | bytes 98312 | tf_op jit(solution)/shard_map/ppermute | solution.py:41
  154.0 3.7 %copy-start.19 = (f32[4,16,512]{2,1,0:T(8,128)S(1)}, f32[4,16,512]{2,1,0:T(8,128)}, u32[]{:S(2)}) copy-start(f32[4,16,512]{2,1,0:T(8,128)} %pad_maximum_fusion.1) | copy-start | bytes 393220
  154.0 3.7 %copy-start.20 = (f32[3,16,512]{2,1,0:T(8,128)S(1)}, f32[3,16,512]{2,1,0:T(8,128)}, u32[]{:S(2)}) copy-start(f32[3,16,512]{2,1,0:T(8,128)} %pad_maximum_fusion.3) | copy-start | bytes 294916
  157.8 6.0 %collective-permute-start.27 = (f32[16,512]{1,0:T(8,128)S(1)}, f32[16,512]{1,0:T(8,128)S(1)}, u32[]{:S(2)}, u32[]{:S(2)}) collective-permute-start(f32[16,512]{1,0:T(8,128)S(1)} %get-tuple-element.125), channel_id=1, source_target_pairs={{0,8},{1,9},{2,10},{3,11},{4,12},{5,13},{6,14},{7,15},{8,0},{9,1},... | collective-permute-start | bytes 98312 | tf_op jit(solution)/shard_map/ppermute | solution.py:41
  159.8 4.0 %collective-permute-start.29 = (f32[16,512]{1,0:T(8,128)S(1)}, f32[16,512]{1,0:T(8,128)S(1)}, u32[]{:S(2)}, u32[]{:S(2)}) collective-permute-start(f32[16,512]{1,0:T(8,128)S(1)} %get-tuple-element.129), channel_id=1, source_target_pairs={{0,72},{1,73},{2,74},{3,75},{4,76},{5,77},{6,78},{7,79},{8,64},{9,... | collective-permute-start | bytes 98312 | tf_op jit(solution)/shard_map/ppermute | solution.py:41
  160.3 3.5 %collective-permute-start.28 = (f32[16,512]{1,0:T(8,128)S(1)}, f32[16,512]{1,0:T(8,128)S(1)}, u32[]{:S(2)}, u32[]{:S(2)}) collective-permute-start(f32[16,512]{1,0:T(8,128)S(1)} %get-tuple-element.129), channel_id=1, source_target_pairs={{0,64},{1,65},{2,66},{3,67},{4,68},{5,69},{6,70},{7,71},{8,72},{9,... | collective-permute-start | bytes 98312 | tf_op jit(solution)/shard_map/ppermute | solution.py:41
  161.2 2.6 %copy-start.17 = (f32[48,512]{1,0:T(8,128)S(1)}, f32[48,512]{1,0:T(8,128)}, u32[]{:S(2)}) copy-start(f32[48,512]{1,0:T(8,128)} %pad_maximum_fusion.2.fades) | copy-start | bytes 294916

commit v5 on v4

--- a/solution.py
+++ b/solution.py
@@ -77,56 +77,33 @@
     return jnp.where(rows >= steps, pltpu.roll(value, steps, 0), 0.0)
 
 
-def row_tiles(rows, body):
-    tile = (rows + HALO) // 5
-
-    def step(m, carry):
-        body(pl.ds(pl.multiple_of(m * tile, 16), tile))
-        return carry
-
-    lax.fori_loop(0, 5, step, 0)
-
-
-def copy_rows(rows, target, source):
-    def body(at):
-        target[at, :] = source[at, :]
-
-    row_tiles(rows, body)
-
-
-def first_half(rows, where, lhs, weights, acc):
-    def clear(at):
-        acc[at, :] = jnp.zeros((at.size, acc.shape[1]), F32)
-
-    row_tiles(rows, clear)
+def first_half(where, lhs, weights, acc):
+    acc[...] = jnp.zeros_like(acc)
     for k in range(4):
         slot = where[k]
 
         @pl.when(lax.rem(slot, 4) != 3)
         def _(k=k, slot=slot):
-            def body(at):
-                acc[at, :] += jnp.dot(lhs[slot, at, :], weights[k][...], preferred_element_type=F32)
-
-            row_tiles(rows, body)
-
-
-def begin_kernel(rows, where, *refs):
+            acc[...] += jnp.dot(lhs[slot], weights[k][...], preferred_element_type=F32)
+
+
+def begin_kernel(where, *refs):
     toks, weights, (lhs, acc) = refs[:6], refs[6:10], refs[10:]
     for n, s in enumerate((0, 1, 2, 4, 5, 6)):
-        copy_rows(rows, lhs.at[s], toks[n])
-    first_half(rows, where, lhs, weights, acc)
-
-
-def also_kernel(rows, where, *refs):
+        lhs[s] = toks[n][...]
+    first_half(where, lhs, weights, acc)
+
+
+def also_kernel(where, *refs):
     lhs, weights, acc = refs[0], refs[1:5], refs[5]
-    first_half(rows, where, lhs, weights, acc)
+    first_half(where, lhs, weights, acc)
 
 
 def begin(where, toks, weights, rows):
     vmem = pl.BlockSpec(memory_space=pltpu.VMEM)
     tall, width = rows + HALO, weights[0].shape[1]
     return pl.pallas_call(
-        functools.partial(begin_kernel, rows),
+        begin_kernel,
         out_shape=[
             jax.ShapeDtypeStruct((8, tall, BLOCK), jnp.bfloat16),
             jax.ShapeDtypeStruct((tall, width), F32),
@@ -144,7 +121,7 @@
     vmem = pl.BlockSpec(memory_space=pltpu.VMEM)
     tall, width = rows + HALO, weights[0].shape[1]
     return pl.pallas_call(
-        functools.partial(also_kernel, rows),
+        also_kernel,
         out_shape=jax.ShapeDtypeStruct((tall, width), F32),
         in_specs=[pl.BlockSpec(memory_space=pltpu.SMEM)] + [vmem] * 5,
         out_specs=vmem,
@@ -155,68 +132,52 @@
     )(where, lhs, *weights)
 
 
-def more_kernel(rows, where, *refs):
-    lhs, part, weights, acc = refs[0], refs[1], refs[2:6], refs[6]
-    copy_rows(rows, acc, part)
-    for k in range(4):
-        slot = where[4 + k]
-
-        @pl.when(lax.rem(slot, 4) != 3)
-        def _(k=k, slot=slot):
-            def body(at):
-                acc[at, :] += jnp.dot(lhs[slot, at, :], weights[k][...], preferred_element_type=F32)
-
-            row_tiles(rows, body)
-
-
-def more(where, lhs, part, weights, rows):
-    vmem = pl.BlockSpec(memory_space=pltpu.VMEM)
-    tall, width = rows + HALO, weights[0].shape[1]
-    return pl.pallas_call(
-        functools.partial(more_kernel, rows),
-        out_shape=jax.ShapeDtypeStruct((tall, width), F32),
-        in_specs=[pl.BlockSpec(memory_space=pltpu.SMEM)] + [vmem] * 6,
-        out_specs=vmem,
-        compiler_params=pltpu.CompilerParams(vmem_limit_bytes=26 << 20),
-        cost_estimate=pl.CostEstimate(
-            flops=2 * tall * 3 * BLOCK * width, bytes_accessed=12 << 20, transcendentals=0
-        ),
-    )(where, lhs, part, *weights)
-
-
 def project_kernel(rows, where, *refs):
-    near, far, part, *refs = refs
+    lhs, near, far, part, *refs = refs
     weights, refs = refs[:8], refs[8:]
-    prm, prod_ref, x1_ref, u_ref, end_ref, acc, proj = refs
+    prm, prod_ref, x1_ref, u_ref, end_ref, last, wfar, proj = refs
     seg_len = rows // SEG
     for k in range(8):
+        at = pl.ds(max(k - 3, 0) * BLOCK, BLOCK)
         for s, ref in ((3, near), (7, far)):
 
             @pl.when(where[k] == s)
-            def _(k=k, ref=ref):
-                def body(at):
-                    out = jnp.dot(ref[at, :], weights[k][...], preferred_element_type=F32)
-                    if k < 4:
-                        acc[at, :] = part[at, :] + out
-                        return
-                    out = (acc[at, :] + out).astype(jnp.bfloat16).astype(F32)
-                    for n in range(6):
-                        proj[n, at, :] = out[:, n * LANES:(n + 1) * LANES]
-
-                row_tiles(rows, body)
-
+            def _(k=k, ref=ref, at=at):
+                last[:, at] = ref[...]
+                if k < 4:
+                    wfar[...] = weights[k][...]
+
+        if k >= 4:
+
+            @pl.when(lax.rem(where[k], 4) != 3)
+            def _(k=k, at=at):
+                last[:, at] = lhs[where[k]]
+
+    for n in range(3):
+        cols = pl.ds(n * 2 * LANES, 2 * LANES)
+        right = jnp.concatenate([w[:, cols] for w in (wfar, *weights[4:])], axis=0)
+        out = part[:, cols] + jnp.dot(last[...], right, preferred_element_type=F32)
+        out = out.astype(jnp.bfloat16).astype(F32)
+        for q in range(2):
+            proj[2 * n + q] = out[:, q * LANES:(q + 1) * LANES]
+
+    top = lax.broadcasted_iota(jnp.int32, (SEG, LANES), 0) == 0
     for q in range(2):
         lanes = pl.ds(q * LANES, LANES)
         bcast = lambda r: jnp.broadcast_to(prm[pl.ds(r, 1), lanes], (SEG, LANES))
         decay = [bcast(k) for k in range(MODES)]
         taps = [[bcast(2 * MODES + 3 * j + g) for g in range(3)] for j in range(3)]
 
-        def load(g, at):
-            return proj[2 * g + q, pl.ds(at, SEG, stride=seg_len), :]
+        def load(g, i):
+            return proj[2 * g + q, pl.ds(pl.multiple_of(HALO + i * SEG, SEG), SEG), :]
+
+        def load_before(g, back):
+            halo = proj[2 * g + q, pl.ds(HALO - back, 1), :]
+            return jnp.where(top, halo, pltpu.roll(load(g, seg_len - back), 1, 0))
 
         def step(i, carry):
             before, last, states = carry
-            now = [load(g, HALO + i) for g in range(3)]
+            now = [load(g, i) for g in range(3)]
             feat = [
                 taps[0][g] * now[g] + taps[1][g] * last[g] + taps[2][g] * before[g]
                 for g in range(3)
@@ -228,7 +189,7 @@
             return (last, now, [decay[k] * states[k] + product for k in range(MODES)])
 
         zero = jnp.zeros((SEG, LANES), F32)
-        first = ([load(g, HALO - 2) for g in range(3)], [load(g, HALO - 1) for g in range(3)])
+        first = tuple([load_before(g, back) for g in range(3)] for back in (2, 1))
         _, _, states = lax.fori_loop(0, seg_len, step, (*first, [zero] * MODES), unroll=4)
         for k in range(MODES):
             rate = prm[pl.ds(48 + k, 1), lanes]
@@ -239,7 +200,7 @@
             end_ref[pl.ds(k, 1), lanes] = u[SEG - 1:]
 
 
-def project(where, near, far, part, weights, prm, rows):
+def project(where, lhs, near, far, part, weights, prm, rows):
     vmem = pl.BlockSpec(memory_space=pltpu.VMEM)
     wide, tall = 2 * LANES, rows + HALO
     return pl.pallas_call(
@@ -250,17 +211,18 @@
             jax.ShapeDtypeStruct((MODES * SEG, wide), F32),
             jax.ShapeDtypeStruct((MODES, wide), F32),
         ],
-        in_specs=[pl.BlockSpec(memory_space=pltpu.SMEM)] + [vmem] * 12,
+        in_specs=[pl.BlockSpec(memory_space=pltpu.SMEM)] + [vmem] * 13,
         out_specs=[vmem] * 4,
         scratch_shapes=[
-            pltpu.VMEM((tall, 3 * wide), F32),
+            pltpu.VMEM((tall, 5 * BLOCK), jnp.bfloat16),
+            pltpu.VMEM((BLOCK, 3 * wide), jnp.bfloat16),
             pltpu.VMEM((6, tall, LANES), F32),
         ],
         compiler_params=pltpu.CompilerParams(vmem_limit_bytes=26 << 20),
         cost_estimate=pl.CostEstimate(
-            flops=2 * tall * 4 * BLOCK * 3 * wide, bytes_accessed=12 << 20, transcendentals=0
+            flops=2 * tall * 5 * BLOCK * 3 * wide, bytes_accessed=12 << 20, transcendentals=0
         ),
-    )(where, near, far, part, *weights, prm)
+    )(where, lhs, near, far, part, *weights, prm)
 
 
 def read_kernel(rows, prod_ref, u_ref, prm, y_ref):
@@ -418,36 +380,37 @@
 
     w, tail = together((in_weight.reshape(BLOCK, 3 * wide), tokens[rows - HALO:]))
     b = transposed(w)
-    t = jnp.concatenate([send(tail, next_ctx), tokens], axis=0)
+    steps = tokens.reshape(SEG, rows // SEG, BLOCK).transpose(1, 0, 2).reshape(rows, BLOCK)
+    t = jnp.concatenate([send(tail, next_ctx), steps], axis=0)
     t, b, where, core_at, fades, behind, plane, chip, *prms = together(
         (t, b, where, core_at, fades, behind, plane, chip, *prms)
     )
-    ty = other_yhi(t)
-    tp_, tm = along_z(t, 1), along_z(t, -1)
+    tp_, tm, ty = along_z(t, 1), along_z(t, -1), other_yhi(t)
     bp, bm = along_x(b, 1), along_x(b, -1)
     t, b, tp_, tm, ty, bp, bm = together((t, b, tp_, tm, ty, bp, bm))
     typ, tym = along_z(ty, 1), along_z(ty, -1)
     cb, cbp, cbm = other_core(b), other_core(bp), other_core(bm)
     b, bp, cb, cbp, cbm = together((b, bp, cb, cbp, cbm))
     bf, a = along_x(bp, 1), other_ylo(b)
-    bf, a = together((bf, a))
-    ap, am, af = along_x(a, 1), along_x(a, -1), other_ylo(bf)
-    t, tp_, tm, ty, typ, tym, bf, a = together((t, tp_, tm, ty, typ, tym, bf, a))
+    t, b, tp_, tm, ty, bp, bm, typ, tym, bf, a, cb, cbp, cbm = together(
+        (t, b, tp_, tm, ty, bp, bm, typ, tym, bf, a, cb, cbp, cbm)
+    )
     tf, tyf = along_z(tp_, 1), along_z(tym, -1)
+    ap = along_x(a, 1)
     cbf, ca = other_core(bf), other_core(a)
+    bf, a, cbf, ca = together((bf, a, cbf, ca))
+    am, af = along_x(a, -1), other_ylo(bf)
     lhs, part = begin(where, [t, tp_, tm, ty, typ, tym], [b, bp, bm, bf], rows)
     part_too = also(where, lhs, [cb, cbp, cbm, cbf], rows)
-    ap, am, af, part_too = together((ap, am, af, part_too))
-    cap, cam, caf = other_core(ap), other_core(am), other_core(af)
+    lhs, part, part_too, ap, am, af, tf, tyf = together(
+        (lhs, part, part_too, ap, am, af, tf, tyf)
+    )
     mine = [b, bp, bm, bf, a, ap, am, af]
-    theirs = [cb, cbp, cbm, cbf, ca, cap, cam, caf]
-    part = more(where, lhs, part, mine[4:], rows)
-    part_too = more(where, lhs, part_too, theirs[4:], rows)
-    tf, tyf, part, part_too = together((tf, tyf, part, part_too))
+    theirs = [cb, cbp, cbm, cbf, ca] + [other_core(w) for w in (ap, am, af)]
 
     products, xs, us, ends = [], [], [], []
     for o, (weights, done) in enumerate(((mine, part), (theirs, part_too))):
-        product, x1, u, end = project(where, tf, tyf, done, weights, prms[o], rows)
+        product, x1, u, end = project(where, lhs, tf, tyf, done, weights, prms[o], rows)
         products.append(product)
         xs.append(x1)
         us.append(u)

time: 169 us -> 153 us (0.905)
  Pallas kernels: 51.7 us -> 33.3 us
  starting transfers between devices: 51.2 us -> 55.9 us
    pallas_call x4 -> x2, Pallas kernels: 24.3 us -> 8.04 us  [the longest x1 4.32 us: begin(): pl.pallas_call(begin_kernel, out_shape=[jax.ShapeDtypeStruct((8, tall, BL...]
    ppermute x30, starting transfers between devices: 51.2 us -> 55.9 us  [send(): return lax.ppermute(value, ('ctx', 'tp'), route(move))]
    unnamed x43 -> x7, local copies, waits for them, and re-layouts: 4.17 us -> 1.52 us
    pallas_call x2, Pallas kernels: 17.7 us -> 15.5 us  [project(): pl.pallas_call(functools.partial(project_kernel, rows), out_shape=[jax.Sh...]
  transfers between devices with their start and end apart: 30 -> 30, of which waited for: 11 -> 9; matrix products, arithmetic and copies ran while one was open for 2% -> 3% of each run, Pallas kernels for 17% -> 14%
where the time goes in v5:
time: 153 us
  starting transfers between devices  55.9 us (37%)
  waiting for transfers between devices  55.6 us (36%)
  Pallas kernels  33.3 us (22%)
  local copies, waits for them, and re-layouts  4.79 us (3%)
  other arithmetic  2.33 us (2%)
    ppermute x30, starting transfers between devices, send(): return lax.ppermute(value, ('ctx', 'tp'), route(move))  55.9 us
    ppermute x30, waiting for transfers between devices, send(): return lax.ppermute(value, ('ctx', 'tp'), route(move))  55.6 us
    pallas_call x2, Pallas kernels, project(): pl.pallas_call(functools.partial(project_kernel, rows), out_shape=[jax.Sh...  15.5 us
    pallas_call x2, Pallas kernels, read(): pl.pallas_call(functools.partial(read_kernel, rows), out_shape=jax.ShapeD...  5.19 us
    pallas_call x1, Pallas kernels, gate(): pl.pallas_call(functools.partial(gate_kernel, rows), out_shape=jax.ShapeD...  4.55 us
    pallas_call x1, Pallas kernels, begin(): pl.pallas_call(begin_kernel, out_shape=[jax.ShapeDtypeStruct((8, tall, BL...  4.32 us
    pallas_call x1, Pallas kernels, also(): pl.pallas_call(also_kernel, out_shape=jax.ShapeDtypeStruct((tall, width),...  3.72 us
  transfers between devices with their start and end apart: 30, of which 9 were waited for; matrix products, arithmetic and copies ran while one was open for 3% of the time, Pallas kernels for 14%

profile of v5, /device:TPU:1, one launch (start us, length us, event | category | flops | bytes accessed | tf_op | source)
XLA Modules:
  0.0 152.6 jit_solution(2494056724403570030)
XLA Ops:
  0.0 1.5 copy.9
  1.5 0.6 slice.24
  2.1 4.5 %collective-permute-start = (bf16[16,512]{1,0:T(8,128)(2,1)}, bf16[16,512]{1,0:T(8,128)(2,1)}, u32[]{:S(2)}, u32[]{:S(2)}) collective-permute-start(bf16[16,512]{1,0:T(8,128)(2,1)} %slice.24), channel_id=1, source_target_pairs={{0,8},{1,9},{2,10},{3,11},{4,12},{5,13},{6,14},{7,15},{8,16},{9,17... | collective-permute-start | bytes 49160 | tf_op jit(solution)/shard_map/ppermute | solution.py:41
  6.6 1.2 copy.11
  7.8 1.8 %collective-permute-start.1 = (bf16[512,768]{1,0:T(8,128)(2,1)}, bf16[512,768]{1,0:T(8,128)(2,1)S(1)}, u32[]{:S(2)}, u32[]{:S(2)}) collective-permute-start(bf16[512,768]{1,0:T(8,128)(2,1)} %copy.11), channel_id=1, source_target_pairs={{0,0},{1,16},{2,32},{3,48},{4,64},{5,80},{6,96},{7,112},{8,8},{9,2... | collective-permute-start | bytes 2359304 | tf_op jit(solution)/shard_map/ppermute | solution.py:41
  9.6 0.8 bitcast_multiply_fusion.7
  10.4 0.7 negate_exponential_fusion
  11.1 0.8 dynamic_slice.21
  12.2 0.6 copy.13
  12.8 0.1 stack.67.where
  12.9 0.8 pad_maximum_fusion.refs_0_
  13.7 19.4 %collective-permute-start.2 = (bf16[1040,512]{1,0:T(8,128)(2,1)S(1)}, bf16[1040,512]{1,0:T(8,128)(2,1)S(1)}, u32[]{:S(2)}, u32[]{:S(2)}) collective-permute-start(bf16[1040,512]{1,0:T(8,128)(2,1)S(1)} %pad_maximum_fusion.refs_0_), channel_id=1, source_target_pairs={{0,1},{1,2},{2,3},{3,0},{4,5},{5,6},{6,7},{7,4},{8,9},{9,10},{10,1... | collective-permute-start | bytes 3194888 | tf_op jit(solution)/shard_map/ppermute | solution.py:41
  33.1 3.3 %collective-permute-start.3 = (bf16[1040,512]{1,0:T(8,128)(2,1)S(1)}, bf16[1040,512]{1,0:T(8,128)(2,1)S(1)}, u32[]{:S(2)}, u32[]{:S(2)}) collective-permute-start(bf16[1040,512]{1,0:T(8,128)(2,1)S(1)} %pad_maximum_fusion.refs_0_), channel_id=1, source_target_pairs={{0,3},{1,0},{2,1},{3,2},{4,7},{5,4},{6,5},{7,6},{8,11},{9,8},{10,9... | collective-permute-start | bytes 3194888 | tf_op jit(solution)/shard_map/ppermute | solution.py:41
  36.4 3.8 %collective-permute-start.4 = (bf16[1040,512]{1,0:T(8,128)(2,1)S(1)}, bf16[1040,512]{1,0:T(8,128)(2,1)S(1)}, u32[]{:S(2)}, u32[]{:S(2)}) collective-permute-start(bf16[1040,512]{1,0:T(8,128)(2,1)S(1)} %pad_maximum_fusion.refs_0_), channel_id=1, source_target_pairs={{0,4},{1,5},{2,6},{3,7},{4,0},{5,1},{6,2},{7,3},{8,12},{9,13},{10,... | collective-permute-start | bytes 3194888 | tf_op jit(solution)/shard_map/ppermute | solution.py:41
  40.2 2.7 %collective-permute-start.6 = (bf16[512,768]{1,0:T(8,128)(2,1)S(1)}, bf16[512,768]{1,0:T(8,128)(2,1)S(1)}, u32[]{:S(2)}, u32[]{:S(2)}) collective-permute-start(bf16[512,768]{1,0:T(8,128)(2,1)S(1)} %collective-permute-done.1.refs_6_.refs_4_), channel_id=1, source_target_pairs={{0,48},{1,49},{2,50},{3,51},{4,52},{5,53},{6,54},{7,55},{8,56},{9,... | collective-permute-start | bytes 2359304 | tf_op jit(solution)/shard_map/ppermute | solution.py:41
  42.9 16.6 %collective-permute-done.5.refs_7_.refs_5_ = bf16[512,768]{1,0:T(8,128)(2,1)S(1)} collective-permute-done((bf16[512,768]{1,0:T(8,128)(2,1)S(1)}, bf16[512,768]{1,0:T(8,128)(2,1)S(1)}, u32[]{:S(2)}, u32[]{:S(2)}) %collective-permute-start.5) | collective-permute-done | bytes 786464 | tf_op jit(solution)/shard_map/ppermute | solution.py:41
  59.5 0.0 collective-permute-done.6.refs_8_.refs_6_
  59.5 0.4 collective-permute-done.2.refs_1_
  59.9 0.0 collective-permute-done.3.refs_2_
  59.9 3.5 %collective-permute-done.4.refs_3_ = bf16[1040,512]{1,0:T(8,128)(2,1)S(1)} collective-permute-done((bf16[1040,512]{1,0:T(8,128)(2,1)S(1)}, bf16[1040,512]{1,0:T(8,128)(2,1)S(1)}, u32[]{:S(2)}, u32[]{:S(2)}) %collective-permute-start.4) | collective-permute-done | bytes 1064992 | tf_op jit(solution)/shard_map/ppermute | solution.py:41
  63.4 1.2 collective-permute-start.7
  64.7 0.0 collective-permute-start.8
  64.7 0.5 collective-permute-start.9
  65.2 2.7 %collective-permute-start.11 = (bf16[1040,512]{1,0:T(8,128)(2,1)S(1)}, bf16[1040,512]{1,0:T(8,128)(2,1)S(1)}, u32[]{:S(2)}, u32[]{:S(2)}) collective-permute-start(bf16[1040,512]{1,0:T(8,128)(2,1)S(1)} %collective-permute-done.4.refs_3_), channel_id=1, source_target_pairs={{0,3},{1,0},{2,1},{3,2},{4,7},{5,4},{6,5},{7,6},{8,11},{9,8},{10,9... | collective-permute-start | bytes 3194888 | tf_op jit(solution)/shard_map/ppermute | solution.py:41
  67.9 0.0 collective-permute-done.7.refs_1_.refs_4_
  67.9 0.0 collective-permute-done.8.refs_2_.refs_5_
  67.9 1.0 collective-permute-done.9.refs_3_.refs_6_
  68.8 0.0 collective-permute-start.12
  68.8 0.9 collective-permute-start.13
  69.7 21.8 %collective-permute-done.10.refs_4_ = bf16[1040,512]{1,0:T(8,128)(2,1)S(1)} collective-permute-done((bf16[1040,512]{1,0:T(8,128)(2,1)S(1)}, bf16[1040,512]{1,0:T(8,128)(2,1)S(1)}, u32[]{:S(2)}, u32[]{:S(2)}) %collective-permute-start.10) | collective-permute-done | bytes 1064992 | tf_op jit(solution)/shard_map/ppermute | solution.py:41
  91.5 0.0 collective-permute-done.11.refs_5_
  91.5 0.0 collective-permute-done.12.refs_9_.refs_7_
  91.5 0.9 collective-permute-start.14
  92.4 0.1 collective-permute-start.15
  92.5 0.0 collective-permute-start.19
  92.5 2.7 %collective-permute-start.20 = (bf16[1040,512]{1,0:T(8,128)(2,1)S(1)}, bf16[1040,512]{1,0:T(8,128)(2,1)S(1)}, u32[]{:S(2)}, u32[]{:S(2)}) collective-permute-start(bf16[1040,512]{1,0:T(8,128)(2,1)S(1)} %collective-permute-done.11.refs_5_), channel_id=1, source_target_pairs={{0,3},{1,0},{2,1},{3,2},{4,7},{5,4},{6,5},{7,6},{8,11},{9,8},{10,9... | collective-permute-start | bytes 3194888 | tf_op jit(solution)/shard_map/ppermute | solution.py:41
  95.2 0.0 collective-permute-done.14.refs_4_.refs_7_
  95.2 0.3 collective-permute-done.15.refs_8_
  95.4 2.4 %collective-permute-start.17 = (bf16[512,768]{1,0:T(8,128)(2,1)S(1)}, bf16[512,768]{1,0:T(8,128)(2,1)S(1)}, u32[]{:S(2)}, u32[]{:S(2)}) collective-permute-start(bf16[512,768]{1,0:T(8,128)(2,1)S(1)} %collective-permute-done.13.refs_8_), channel_id=1, source_target_pairs={{0,48},{1,49},{2,50},{3,51},{4,52},{5,53},{6,54},{7,55},{8,56},{9,... | collective-permute-start | bytes 2359304 | tf_op jit(solution)/shard_map/ppermute | solution.py:41
  97.9 0.9 collective-permute-start.18
  98.7 4.3 %shard_map.64 = (bf16[8,1040,512]{2,1,0:T(8,128)(2,1)S(1)}, f32[1040,768]{1,0:T(8,128)S(1)}) custom-call(s32[9]{0:T(128)S(1)} %stack.67.where, bf16[1040,512]{1,0:T(8,128)(2,1)S(1)} %pad_maximum_fusion.refs_0_, bf16[1040,512]{1,0:T(8,128)(2,1)S(1)} %collective-permute-done.2.refs_1_, bf16[1040,512]{1,0:T(8,128)(2,1)S(1)} %collective-permute-done.3.refs_2_, ...), custom_call_target="tpu_custom_call" | custom-call | flops 2453667840 | bytes 12582912 | tf_op jit(solution)/shard_map/pallas_call | solution.py:105
  103.1 3.7 %shard_map.65.refs_3_ = f32[1040,768]{1,0:T(8,128)S(1)} custom-call(s32[9]{0:T(128)S(1)} %stack.67.where, bf16[8,1040,512]{2,1,0:T(8,128)(2,1)S(1)} %get-tuple-element.110.refs_0_, bf16[512,768]{1,0:T(8,128)(2,1)S(1)} %collective-permute-done.7.refs_1_.refs_4_, bf16[512,768]{1,0:T(8,128)(2,1)S(1)} %collective-permute-done.8.refs_2_.refs_5_, ...), custom_call_target="tpu_custom_call" | custom-call | flops 2453667840 | bytes 12582912 | tf_op jit(solution)/shard_map/pallas_call | solution.py:123
  106.8 7.7 %collective-permute-done.16.refs_9_ = bf16[512,768]{1,0:T(8,128)(2,1)S(1)} collective-permute-done((bf16[512,768]{1,0:T(8,128)(2,1)S(1)}, bf16[512,768]{1,0:T(8,128)(2,1)S(1)}, u32[]{:S(2)}, u32[]{:S(2)}) %collective-permute-start.16) | collective-permute-done | bytes 786464 | tf_op jit(solution)/shard_map/ppermute | solution.py:41
  114.4 3.9 %collective-permute-done.19.refs_1_ = bf16[1040,512]{1,0:T(8,128)(2,1)S(1)} collective-permute-done((bf16[1040,512]{1,0:T(8,128)(2,1)S(1)}, bf16[1040,512]{1,0:T(8,128)(2,1)S(1)}, u32[]{:S(2)}, u32[]{:S(2)}) %collective-permute-start.19) | collective-permute-done | bytes 1064992 | tf_op jit(solution)/shard_map/ppermute | solution.py:41
  118.4 0.0 collective-permute-done.17.refs_10_
  118.4 0.0 collective-permute-done.18.refs_11_
  118.4 1.3 collective-permute-start.21
  119.7 0.1 collective-permute-start.22
  119.8 0.4 collective-permute-start.23
  120.2 7.7 %shard_map.66 = (f32[1024,256]{1,0:T(8,128)S(1)}, f32[1024,256]{1,0:T(8,128)S(1)}, f32[128,256]{1,0:T(8,128)S(1)}, f32[16,256]{1,0:T(8,128)S(1)}) custom-call(s32[9]{0:T(128)S(1)} %stack.67.where, bf16[8,1040,512]{2,1,0:T(8,128)(2,1)S(1)} %get-tuple-element.110.refs_0_, bf16[1040,512]{1,0:T(8,128)(2,1)S(1)} %collective-permute-done.19.refs_1_, ...), custom_call_target="tpu_custom_call" | custom-call | flops 4089446400 | bytes 12582912 | tf_op jit(solution)/shard_map/pallas_call | solution.py:206
  127.9 0.0 collective-permute-done.23.refs_11_
  127.9 7.9 %shard_map.67 = (f32[1024,256]{1,0:T(8,128)S(1)}, f32[1024,256]{1,0:T(8,128)S(1)}, f32[128,256]{1,0:T(8,128)S(1)}, f32[16,256]{1,0:T(8,128)S(1)}) custom-call(s32[9]{0:T(128)S(1)} %stack.67.where, bf16[8,1040,512]{2,1,0:T(8,128)(2,1)S(1)} %get-tuple-element.110.refs_0_, bf16[1040,512]{1,0:T(8,128)(2,1)S(1)} %collective-permute-done.19.refs_1_, ...), custom_call_target="tpu_custom_call" | custom-call | flops 4089446400 | bytes 12582912 | tf_op jit(solution)/shard_map/pallas_call | solution.py:206
  135.9 0.1 collective-permute-start.24
  135.9 1.8 %collective-permute-start.25 = (f32[16,512]{1,0:T(8,128)S(1)}, f32[16,512]{1,0:T(8,128)S(1)}, u32[]{:S(2)}, u32[]{:S(2)}) collective-permute-start(f32[16,512]{1,0:T(8,128)S(1)} %pad_maximum_fusion.4), channel_id=1, source_target_pairs={{0,32},{1,33},{2,34},{3,35},{4,36},{5,37},{6,38},{7,39},{8,40},{9,... | collective-permute-start | bytes 98312 | tf_op jit(solution)/shard_map/ppermute | solution.py:41
  137.7 1.7 %collective-permute-start.26 = (f32[16,512]{1,0:T(8,128)S(1)}, f32[16,512]{1,0:T(8,128)S(1)}, u32[]{:S(2)}, u32[]{:S(2)}) collective-permute-start(f32[16,512]{1,0:T(8,128)S(1)} %pad_maximum_fusion.4), channel_id=1, source_target_pairs={{0,48},{1,49},{2,50},{3,51},{4,52},{5,53},{6,54},{7,55},{8,56},{9,... | collective-permute-start | bytes 98312 | tf_op jit(solution)/shard_map/ppermute | solution.py:41
  139.5 2.6 %shard_map.68.y0 = f32[1024,256]{1,0:T(8,128)S(1)} custom-call(f32[1024,256]{1,0:T(8,128)S(1)} %get-tuple-element.126.prod_ref, f32[128,256]{1,0:T(8,128)S(1)} %get-tuple-element.127.u_ref, f32[64,256]{1,0:T(8,128)S(1)} %get-tuple-element.117.refs_12_.prm.p0), custom_call_target="tpu_custom_call" | custom-call | flops 16777216 | bytes 12582912 | tf_op jit(solution)/shard_map/pallas_call | solution.py:255
  142.1 0.0 collective-permute-done.24
  142.1 0.0 collective-permute-done.25
  142.2 1.0 collective-permute-start.27
  143.2 1.4 collective-permute-start.28
  144.5 0.4 collective-permute-start.29
  144.9 2.6 %shard_map.69.y1 = f32[1024,256]{1,0:T(8,128)S(1)} custom-call(f32[1024,256]{1,0:T(8,128)S(1)} %get-tuple-element.129.prod_ref, f32[128,256]{1,0:T(8,128)S(1)} %get-tuple-element.130.u_ref, f32[64,256]{1,0:T(8,128)S(1)} %get-tuple-element.121.refs_12_.prm.p1), custom_call_target="tpu_custom_call" | custom-call | flops 16777216 | bytes 12582912 | tf_op jit(solution)/shard_map/pallas_call | solution.py:255
  147.5 0.4 collective-permute-done.29.cross
  147.9 4.6 %shard_map.70 = bf16[1024,512]{1,0:T(8,128)(2,1)} custom-call(s32[1]{0:T(128)} %bitcast.12.core_ref, f32[1024,256]{1,0:T(8,128)S(1)} %shard_map.68.y0, f32[1024,256]{1,0:T(8,128)S(1)} %shard_map.69.y1, f32[1024,256]{1,0:T(8,128)S(1)} %get-tuple-element.131.x0, f32[1024,256]{1,0:T(8,128)S(1)} %get-tuple-element.132.x1, ...), custom_call_target="tpu_custom_call" | custom-call | tf_op jit(solution)/shard_map/pallas_call | solution.py:322
  (29 shorter events, 0.2 us)
Async XLA Ops:
  0.0 11.0 %copy-start = (f32[3,3,4096]{2,1,0:T(4,128)S(1)}, f32[3,3,4096]{2,1,0:T(4,128)}, u32[]{:S(2)}) copy-start(f32[3,3,4096]{2,1,0:T(4,128)} %param.8) | copy-start | bytes 442372
  0.0 1.5 copy-start.1
  2.1 10.7 %collective-permute-start = (bf16[16,512]{1,0:T(8,128)(2,1)}, bf16[16,512]{1,0:T(8,128)(2,1)}, u32[]{:S(2)}, u32[]{:S(2)}) collective-permute-start(bf16[16,512]{1,0:T(8,128)(2,1)} %slice.24), channel_id=1, source_target_pairs={{0,8},{1,9},{2,10},{3,11},{4,12},{5,13},{6,14},{7,15},{8,16},{9,17... | collective-permute-start | bytes 49160 | tf_op jit(solution)/shard_map/ppermute | solution.py:41
  7.8 5.9 %collective-permute-start.1 = (bf16[512,768]{1,0:T(8,128)(2,1)}, bf16[512,768]{1,0:T(8,128)(2,1)S(1)}, u32[]{:S(2)}, u32[]{:S(2)}) collective-permute-start(bf16[512,768]{1,0:T(8,128)(2,1)} %copy.11), channel_id=1, source_target_pairs={{0,0},{1,16},{2,32},{3,48},{4,64},{5,80},{6,96},{7,112},{8,8},{9,2... | collective-permute-start | bytes 2359304 | tf_op jit(solution)/shard_map/ppermute | solution.py:41
  13.7 46.3 %collective-permute-start.2 = (bf16[1040,512]{1,0:T(8,128)(2,1)S(1)}, bf16[1040,512]{1,0:T(8,128)(2,1)S(1)}, u32[]{:S(2)}, u32[]{:S(2)}) collective-permute-start(bf16[1040,512]{1,0:T(8,128)(2,1)S(1)} %pad_maximum_fusion.refs_0_), channel_id=1, source_target_pairs={{0,1},{1,2},{2,3},{3,0},{4,5},{5,6},{6,7},{7,4},{8,9},{9,10},{10,1... | collective-permute-start | bytes 3194888 | tf_op jit(solution)/shard_map/ppermute | solution.py:41
  33.1 26.9 %collective-permute-start.3 = (bf16[1040,512]{1,0:T(8,128)(2,1)S(1)}, bf16[1040,512]{1,0:T(8,128)(2,1)S(1)}, u32[]{:S(2)}, u32[]{:S(2)}) collective-permute-start(bf16[1040,512]{1,0:T(8,128)(2,1)S(1)} %pad_maximum_fusion.refs_0_), channel_id=1, source_target_pairs={{0,3},{1,0},{2,1},{3,2},{4,7},{5,4},{6,5},{7,6},{8,11},{9,8},{10,9... | collective-permute-start | bytes 3194888 | tf_op jit(solution)/shard_map/ppermute | solution.py:41
  36.4 27.0 %collective-permute-start.4 = (bf16[1040,512]{1,0:T(8,128)(2,1)S(1)}, bf16[1040,512]{1,0:T(8,128)(2,1)S(1)}, u32[]{:S(2)}, u32[]{:S(2)}) collective-permute-start(bf16[1040,512]{1,0:T(8,128)(2,1)S(1)} %pad_maximum_fusion.refs_0_), channel_id=1, source_target_pairs={{0,4},{1,5},{2,6},{3,7},{4,0},{5,1},{6,2},{7,3},{8,12},{9,13},{10,... | collective-permute-start | bytes 3194888 | tf_op jit(solution)/shard_map/ppermute | solution.py:41
  40.2 19.3 %collective-permute-start.5 = (bf16[512,768]{1,0:T(8,128)(2,1)S(1)}, bf16[512,768]{1,0:T(8,128)(2,1)S(1)}, u32[]{:S(2)}, u32[]{:S(2)}) collective-permute-start(bf16[512,768]{1,0:T(8,128)(2,1)S(1)} %collective-permute-done.1.refs_6_.refs_4_), channel_id=1, source_target_pairs={{0,16},{1,17},{2,18},{3,19},{4,20},{5,21},{6,22},{7,23},{8,24},{9,... | collective-permute-start | bytes 2359304 | tf_op jit(solution)/shard_map/ppermute | solution.py:41
  40.2 19.3 %collective-permute-start.6 = (bf16[512,768]{1,0:T(8,128)(2,1)S(1)}, bf16[512,768]{1,0:T(8,128)(2,1)S(1)}, u32[]{:S(2)}, u32[]{:S(2)}) collective-permute-start(bf16[512,768]{1,0:T(8,128)(2,1)S(1)} %collective-permute-done.1.refs_6_.refs_4_), channel_id=1, source_target_pairs={{0,48},{1,49},{2,50},{3,51},{4,52},{5,53},{6,54},{7,55},{8,56},{9,... | collective-permute-start | bytes 2359304 | tf_op jit(solution)/shard_map/ppermute | solution.py:41
  63.4 4.4 %collective-permute-start.7 = (bf16[512,768]{1,0:T(8,128)(2,1)S(1)}, bf16[512,768]{1,0:T(8,128)(2,1)S(1)}, u32[]{:S(2)}, u32[]{:S(2)}) collective-permute-start(bf16[512,768]{1,0:T(8,128)(2,1)S(1)} %collective-permute-done.1.refs_6_.refs_4_), channel_id=1, source_target_pairs={{0,8},{1,9},{2,10},{3,11},{4,12},{5,13},{6,14},{7,15},{8,0},{9,1},... | collective-permute-start | bytes 2359304 | tf_op jit(solution)/shard_map/ppermute | solution.py:41
  64.7 3.2 %collective-permute-start.8 = (bf16[512,768]{1,0:T(8,128)(2,1)S(1)}, bf16[512,768]{1,0:T(8,128)(2,1)S(1)}, u32[]{:S(2)}, u32[]{:S(2)}) collective-permute-start(bf16[512,768]{1,0:T(8,128)(2,1)S(1)} %collective-permute-done.5.refs_7_.refs_5_), channel_id=1, source_target_pairs={{0,8},{1,9},{2,10},{3,11},{4,12},{5,13},{6,14},{7,15},{8,0},{9,1},... | collective-permute-start | bytes 2359304 | tf_op jit(solution)/shard_map/ppermute | solution.py:41
  64.7 4.2 %collective-permute-start.9 = (bf16[512,768]{1,0:T(8,128)(2,1)S(1)}, bf16[512,768]{1,0:T(8,128)(2,1)S(1)}, u32[]{:S(2)}, u32[]{:S(2)}) collective-permute-start(bf16[512,768]{1,0:T(8,128)(2,1)S(1)} %collective-permute-done.6.refs_8_.refs_6_), channel_id=1, source_target_pairs={{0,8},{1,9},{2,10},{3,11},{4,12},{5,13},{6,14},{7,15},{8,0},{9,1},... | collective-permute-start | bytes 2359304 | tf_op jit(solution)/shard_map/ppermute | solution.py:41
  65.2 26.4 %collective-permute-start.10 = (bf16[1040,512]{1,0:T(8,128)(2,1)S(1)}, bf16[1040,512]{1,0:T(8,128)(2,1)S(1)}, u32[]{:S(2)}, u32[]{:S(2)}) collective-permute-start(bf16[1040,512]{1,0:T(8,128)(2,1)S(1)} %collective-permute-done.4.refs_3_), channel_id=1, source_target_pairs={{0,1},{1,2},{2,3},{3,0},{4,5},{5,6},{6,7},{7,4},{8,9},{9,10},{10,1... | collective-permute-start | bytes 3194888 | tf_op jit(solution)/shard_map/ppermute | solution.py:41
  65.2 26.4 %collective-permute-start.11 = (bf16[1040,512]{1,0:T(8,128)(2,1)S(1)}, bf16[1040,512]{1,0:T(8,128)(2,1)S(1)}, u32[]{:S(2)}, u32[]{:S(2)}) collective-permute-start(bf16[1040,512]{1,0:T(8,128)(2,1)S(1)} %collective-permute-done.4.refs_3_), channel_id=1, source_target_pairs={{0,3},{1,0},{2,1},{3,2},{4,7},{5,4},{6,5},{7,6},{8,11},{9,8},{10,9... | collective-permute-start | bytes 3194888 | tf_op jit(solution)/shard_map/ppermute | solution.py:41
  68.8 22.7 %collective-permute-start.12 = (bf16[512,768]{1,0:T(8,128)(2,1)S(1)}, bf16[512,768]{1,0:T(8,128)(2,1)S(1)}, u32[]{:S(2)}, u32[]{:S(2)}) collective-permute-start(bf16[512,768]{1,0:T(8,128)(2,1)S(1)} %collective-permute-done.5.refs_7_.refs_5_), channel_id=1, source_target_pairs={{0,16},{1,17},{2,18},{3,19},{4,20},{5,21},{6,22},{7,23},{8,24},{9,... | collective-permute-start | bytes 2359304 | tf_op jit(solution)/shard_map/ppermute | solution.py:41
  68.8 22.7 %collective-permute-start.13 = (bf16[512,768]{1,0:T(8,128)(2,1)S(1)}, bf16[512,768]{1,0:T(8,128)(2,1)S(1)}, u32[]{:S(2)}, u32[]{:S(2)}) collective-permute-start(bf16[512,768]{1,0:T(8,128)(2,1)S(1)} %collective-permute-done.1.refs_6_.refs_4_), channel_id=1, source_target_pairs={{0,64},{1,65},{2,66},{3,67},{4,68},{5,69},{6,70},{7,71},{8,72},{9,... | collective-permute-start | bytes 2359304 | tf_op jit(solution)/shard_map/ppermute | solution.py:41
  91.5 3.6 %collective-permute-start.14 = (bf16[512,768]{1,0:T(8,128)(2,1)S(1)}, bf16[512,768]{1,0:T(8,128)(2,1)S(1)}, u32[]{:S(2)}, u32[]{:S(2)}) collective-permute-start(bf16[512,768]{1,0:T(8,128)(2,1)S(1)} %collective-permute-done.12.refs_9_.refs_7_), channel_id=1, source_target_pairs={{0,8},{1,9},{2,10},{3,11},{4,12},{5,13},{6,14},{7,15},{8,0},{9,1},... | collective-permute-start | bytes 2359304 | tf_op jit(solution)/shard_map/ppermute | solution.py:41
  92.4 3.0 %collective-permute-start.15 = (bf16[512,768]{1,0:T(8,128)(2,1)S(1)}, bf16[512,768]{1,0:T(8,128)(2,1)S(1)}, u32[]{:S(2)}, u32[]{:S(2)}) collective-permute-start(bf16[512,768]{1,0:T(8,128)(2,1)S(1)} %collective-permute-done.13.refs_8_), channel_id=1, source_target_pairs={{0,8},{1,9},{2,10},{3,11},{4,12},{5,13},{6,14},{7,15},{8,0},{9,1},... | collective-permute-start | bytes 2359304 | tf_op jit(solution)/shard_map/ppermute | solution.py:41
  92.5 25.9 %collective-permute-start.19 = (bf16[1040,512]{1,0:T(8,128)(2,1)S(1)}, bf16[1040,512]{1,0:T(8,128)(2,1)S(1)}, u32[]{:S(2)}, u32[]{:S(2)}) collective-permute-start(bf16[1040,512]{1,0:T(8,128)(2,1)S(1)} %collective-permute-done.2.refs_1_), channel_id=1, source_target_pairs={{0,1},{1,2},{2,3},{3,0},{4,5},{5,6},{6,7},{7,4},{8,9},{9,10},{10,1... | collective-permute-start | bytes 3194888 | tf_op jit(solution)/shard_map/ppermute | solution.py:41
  92.5 25.9 %collective-permute-start.20 = (bf16[1040,512]{1,0:T(8,128)(2,1)S(1)}, bf16[1040,512]{1,0:T(8,128)(2,1)S(1)}, u32[]{:S(2)}, u32[]{:S(2)}) collective-permute-start(bf16[1040,512]{1,0:T(8,128)(2,1)S(1)} %collective-permute-done.11.refs_5_), channel_id=1, source_target_pairs={{0,3},{1,0},{2,1},{3,2},{4,7},{5,4},{6,5},{7,6},{8,11},{9,8},{10,9... | collective-permute-start | bytes 3194888 | tf_op jit(solution)/shard_map/ppermute | solution.py:41
  95.2 19.3 %collective-permute-start.16 = (bf16[512,768]{1,0:T(8,128)(2,1)S(1)}, bf16[512,768]{1,0:T(8,128)(2,1)S(1)}, u32[]{:S(2)}, u32[]{:S(2)}) collective-permute-start(bf16[512,768]{1,0:T(8,128)(2,1)S(1)} %collective-permute-done.13.refs_8_), channel_id=1, source_target_pairs={{0,16},{1,17},{2,18},{3,19},{4,20},{5,21},{6,22},{7,23},{8,24},{9,... | collective-permute-start | bytes 2359304 | tf_op jit(solution)/shard_map/ppermute | solution.py:41
  95.4 22.9 %collective-permute-start.17 = (bf16[512,768]{1,0:T(8,128)(2,1)S(1)}, bf16[512,768]{1,0:T(8,128)(2,1)S(1)}, u32[]{:S(2)}, u32[]{:S(2)}) collective-permute-start(bf16[512,768]{1,0:T(8,128)(2,1)S(1)} %collective-permute-done.13.refs_8_), channel_id=1, source_target_pairs={{0,48},{1,49},{2,50},{3,51},{4,52},{5,53},{6,54},{7,55},{8,56},{9,... | collective-permute-start | bytes 2359304 | tf_op jit(solution)/shard_map/ppermute | solution.py:41
  97.9 20.5 %collective-permute-start.18 = (bf16[512,768]{1,0:T(8,128)(2,1)S(1)}, bf16[512,768]{1,0:T(8,128)(2,1)S(1)}, u32[]{:S(2)}, u32[]{:S(2)}) collective-permute-start(bf16[512,768]{1,0:T(8,128)(2,1)S(1)} %collective-permute-done.12.refs_9_.refs_7_), channel_id=1, source_target_pairs={{0,64},{1,65},{2,66},{3,67},{4,68},{5,69},{6,70},{7,71},{8,72},{9,... | collective-permute-start | bytes 2359304 | tf_op jit(solution)/shard_map/ppermute | solution.py:41
  118.4 9.5 %collective-permute-start.21 = (bf16[512,768]{1,0:T(8,128)(2,1)S(1)}, bf16[512,768]{1,0:T(8,128)(2,1)S(1)}, u32[]{:S(2)}, u32[]{:S(2)}) collective-permute-start(bf16[512,768]{1,0:T(8,128)(2,1)S(1)} %collective-permute-done.16.refs_9_), channel_id=1, source_target_pairs={{0,8},{1,9},{2,10},{3,11},{4,12},{5,13},{6,14},{7,15},{8,0},{9,1},... | collective-permute-start | bytes 2359304 | tf_op jit(solution)/shard_map/ppermute | solution.py:41
  119.7 8.2 %collective-permute-start.22 = (bf16[512,768]{1,0:T(8,128)(2,1)S(1)}, bf16[512,768]{1,0:T(8,128)(2,1)S(1)}, u32[]{:S(2)}, u32[]{:S(2)}) collective-permute-start(bf16[512,768]{1,0:T(8,128)(2,1)S(1)} %collective-permute-done.17.refs_10_), channel_id=1, source_target_pairs={{0,8},{1,9},{2,10},{3,11},{4,12},{5,13},{6,14},{7,15},{8,0},{9,1},... | collective-permute-start | bytes 2359304 | tf_op jit(solution)/shard_map/ppermute | solution.py:41
  119.8 8.1 %collective-permute-start.23 = (bf16[512,768]{1,0:T(8,128)(2,1)S(1)}, bf16[512,768]{1,0:T(8,128)(2,1)S(1)}, u32[]{:S(2)}, u32[]{:S(2)}) collective-permute-start(bf16[512,768]{1,0:T(8,128)(2,1)S(1)} %collective-permute-done.18.refs_11_), channel_id=1, source_target_pairs={{0,8},{1,9},{2,10},{3,11},{4,12},{5,13},{6,14},{7,15},{8,0},{9,1},... | collective-permute-start | bytes 2359304 | tf_op jit(solution)/shard_map/ppermute | solution.py:41
  135.9 6.2 %collective-permute-start.24 = (f32[16,512]{1,0:T(8,128)S(1)}, f32[16,512]{1,0:T(8,128)S(1)}, u32[]{:S(2)}, u32[]{:S(2)}) collective-permute-start(f32[16,512]{1,0:T(8,128)S(1)} %pad_maximum_fusion.4), channel_id=1, source_target_pairs={{0,16},{1,17},{2,18},{3,19},{4,20},{5,21},{6,22},{7,23},{8,24},{9,... | collective-permute-start | bytes 98312 | tf_op jit(solution)/shard_map/ppermute | solution.py:41
  135.9 6.2 %collective-permute-start.25 = (f32[16,512]{1,0:T(8,128)S(1)}, f32[16,512]{1,0:T(8,128)S(1)}, u32[]{:S(2)}, u32[]{:S(2)}) collective-permute-start(f32[16,512]{1,0:T(8,128)S(1)} %pad_maximum_fusion.4), channel_id=1, source_target_pairs={{0,32},{1,33},{2,34},{3,35},{4,36},{5,37},{6,38},{7,39},{8,40},{9,... | collective-permute-start | bytes 98312 | tf_op jit(solution)/shard_map/ppermute | solution.py:41
  137.7 4.4 %collective-permute-start.26 = (f32[16,512]{1,0:T(8,128)S(1)}, f32[16,512]{1,0:T(8,128)S(1)}, u32[]{:S(2)}, u32[]{:S(2)}) collective-permute-start(f32[16,512]{1,0:T(8,128)S(1)} %pad_maximum_fusion.4), channel_id=1, source_target_pairs={{0,48},{1,49},{2,50},{3,51},{4,52},{5,53},{6,54},{7,55},{8,56},{9,... | collective-permute-start | bytes 98312 | tf_op jit(solution)/shard_map/ppermute | solution.py:41
  139.5 2.6 %copy-start.2 = (f32[16,512]{1,0:T(8,128)S(1)}, f32[16,512]{1,0:T(8,128)}, u32[]{:S(2)}) copy-start(f32[16,512]{1,0:T(8,128)} %get-tuple-element.137) | copy-start | bytes 98308
  142.2 5.3 %collective-permute-start.27 = (f32[16,512]{1,0:T(8,128)S(1)}, f32[16,512]{1,0:T(8,128)S(1)}, u32[]{:S(2)}, u32[]{:S(2)}) collective-permute-start(f32[16,512]{1,0:T(8,128)S(1)} %get-tuple-element.141), channel_id=1, source_target_pairs={{0,8},{1,9},{2,10},{3,11},{4,12},{5,13},{6,14},{7,15},{8,0},{9,1},... | collective-permute-start | bytes 98312 | tf_op jit(solution)/shard_map/ppermute | solution.py:41
  143.2 4.3 %collective-permute-start.28 = (f32[16,512]{1,0:T(8,128)S(1)}, f32[16,512]{1,0:T(8,128)S(1)}, u32[]{:S(2)}, u32[]{:S(2)}) collective-permute-start(f32[16,512]{1,0:T(8,128)S(1)} %get-tuple-element.145), channel_id=1, source_target_pairs={{0,64},{1,65},{2,66},{3,67},{4,68},{5,69},{6,70},{7,71},{8,72},{9,... | collective-permute-start | bytes 98312 | tf_op jit(solution)/shard_map/ppermute | solution.py:41
  144.5 3.4 %collective-permute-start.29 = (f32[16,512]{1,0:T(8,128)S(1)}, f32[16,512]{1,0:T(8,128)S(1)}, u32[]{:S(2)}, u32[]{:S(2)}) collective-permute-start(f32[16,512]{1,0:T(8,128)S(1)} %get-tuple-element.145), channel_id=1, source_target_pairs={{0,72},{1,73},{2,74},{3,75},{4,76},{5,77},{6,78},{7,79},{8,64},{9,... | collective-permute-start | bytes 98312 | tf_op jit(solution)/shard_map/ppermute | solution.py:41

commit v6 on v5

--- a/solution.py
+++ b/solution.py
@@ -264,22 +264,11 @@
     )(prod, u, prm)
 
 
-def gate_kernel(rows, core_ref, y0, y1, x0, x1, p0, p1, near, sent, same, cross, fades,
-                out_ref, ybuf, xbuf, wide, sem):
+def gate_kernel(rows, core_ref, y0, y1, x0, x1, p0, p1, near, sent, same, cross, fades, out_ref, wide):
     seg_len = rows // SEG
     core = core_ref[0]
-    copies = []
-    for o, (y, x) in enumerate(((y0, x0), (y1, x1))):
-        copies.append(
-            (
-                pltpu.make_async_copy(y, ybuf.at[o], sem.at[2 * o]),
-                pltpu.make_async_copy(x, xbuf.at[o], sem.at[2 * o + 1]),
-            )
-        )
-        for copy in copies[o]:
-            copy.start()
     seg = lax.broadcasted_iota(jnp.int32, (SEG, LANES), 0).astype(F32) * seg_len
-    for o, prm in enumerate((p0, p1)):
+    for o, (y, x, prm) in enumerate(((y0, x0, p0), (y1, x1, p1))):
         base = lax.rem(core + o, 2) * (2 * LANES)
         for q in range(2):
             lanes = pl.ds(q * LANES, LANES)
@@ -297,17 +286,14 @@
                 start = jnp.exp(-rate * seg) * state[k:k + 1]
                 decay.append(d)
                 carried.append(prm[pl.ds(MODES + k, 1), lanes] * d * start)
-            if q == 0:
-                for copy in copies[o]:
-                    copy.wait()
 
             def step(i, carried):
                 terms = list(carried)
                 while len(terms) > 1:
                     terms = [a + b for a, b in zip(terms[::2], terms[1::2])]
                 at = pl.ds(pl.multiple_of(i * SEG, SEG), SEG)
-                wide[pl.ds(i, SEG, stride=seg_len), :] = xbuf[o, at, lanes] * (
-                    ybuf[o, at, lanes] + terms[0]
+                wide[pl.ds(i, SEG, stride=seg_len), :] = x[at, lanes] * (
+                    y[at, lanes] + terms[0]
                 )
                 return [c * d for c, d in zip(carried, decay)]
 
@@ -317,19 +303,12 @@
 
 def gate(core, ys, xs, prms, state, rows):
     vmem = pl.BlockSpec(memory_space=pltpu.VMEM)
-    anywhere = pl.BlockSpec(memory_space=pl.ANY)
-    wide = 2 * LANES
     return pl.pallas_call(
         functools.partial(gate_kernel, rows),
         out_shape=jax.ShapeDtypeStruct((rows, BLOCK), jnp.bfloat16),
-        in_specs=[pl.BlockSpec(memory_space=pltpu.SMEM)] + [anywhere] * 4 + [vmem] * 7,
+        in_specs=[pl.BlockSpec(memory_space=pltpu.SMEM)] + [vmem] * 11,
         out_specs=vmem,
-        scratch_shapes=[
-            pltpu.VMEM((2, rows, wide), F32),
-            pltpu.VMEM((2, rows, wide), F32),
-            pltpu.VMEM((rows, LANES), F32),
-            pltpu.SemaphoreType.DMA((4,)),
-        ],
+        scratch_shapes=[pltpu.VMEM((rows, LANES), F32)],
         compiler_params=pltpu.CompilerParams(vmem_limit_bytes=20 << 20),
     )(core, *ys, *xs, *prms, *state)
 
@@ -378,10 +357,11 @@
         n = (yl * 4 + x) * 2 + c + 1
         return None if n == 16 else (n // 8, (n // 2) % 4, n % 2, yh, z)
 
-    w, tail = together((in_weight.reshape(BLOCK, 3 * wide), tokens[rows - HALO:]))
+    w = in_weight.reshape(BLOCK, 3 * wide)
     b = transposed(w)
-    steps = tokens.reshape(SEG, rows // SEG, BLOCK).transpose(1, 0, 2).reshape(rows, BLOCK)
-    t = jnp.concatenate([send(tail, next_ctx), steps], axis=0)
+    shard_tokens, *prms = together((tokens, *prms))
+    steps = shard_tokens.reshape(SEG, rows // SEG, BLOCK).transpose(1, 0, 2).reshape(rows, BLOCK)
+    t = jnp.concatenate([send(shard_tokens[rows - HALO:], next_ctx), steps], axis=0)
     t, b, where, core_at, fades, behind, plane, chip, *prms = together(
         (t, b, where, core_at, fades, behind, plane, chip, *prms)
     )

time: 153 us -> 148 us (0.967)
  starting transfers between devices: 55.9 us -> 52.9 us
  waiting for transfers between devices: 55.6 us -> 53.5 us
    ppermute x30, starting transfers between devices: 55.9 us -> 52.9 us  [send(): return lax.ppermute(value, ('ctx', 'tp'), route(move))]
    ppermute x30, waiting for transfers between devices: 55.6 us -> 53.5 us  [send(): return lax.ppermute(value, ('ctx', 'tp'), route(move))]
  transfers between devices with their start and end apart: 30 -> 30, of which waited for: 9 -> 10; matrix products, arithmetic and copies ran while one was open for 3% -> 3% of each run, Pallas kernels for 14% -> 14%
where the time goes in v6:
time: 148 us
  waiting for transfers between devices  53.5 us (36%)
  starting transfers between devices  52.9 us (36%)
  Pallas kernels  33 us (22%)
  local copies, waits for them, and re-layouts  4.74 us (3%)
  other arithmetic  3.06 us (2%)
    ppermute x30, waiting for transfers between devices, send(): return lax.ppermute(value, ('ctx', 'tp'), route(move))  53.5 us
    ppermute x30, starting transfers between devices, send(): return lax.ppermute(value, ('ctx', 'tp'), route(move))  52.9 us
    pallas_call x2, Pallas kernels, project(): pl.pallas_call(functools.partial(project_kernel, rows), out_shape=[jax.Sh...  15.5 us
    pallas_call x2, Pallas kernels, read(): pl.pallas_call(functools.partial(read_kernel, rows), out_shape=jax.ShapeD...  5.19 us
    pallas_call x1, Pallas kernels, begin(): pl.pallas_call(begin_kernel, out_shape=[jax.ShapeDtypeStruct((8, tall, BL...  4.32 us
    pallas_call x1, Pallas kernels, gate(): pl.pallas_call(functools.partial(gate_kernel, rows), out_shape=jax.ShapeD...  4.19 us
    pallas_call x1, Pallas kernels, also(): pl.pallas_call(also_kernel, out_shape=jax.ShapeDtypeStruct((tall, width),...  3.72 us
  transfers between devices with their start and end apart: 30, of which 10 were waited for; matrix products, arithmetic and copies ran while one was open for 3% of the time, Pallas kernels for 14%

profile of v6, /device:TPU:1, one launch (start us, length us, event | category | flops | bytes accessed | tf_op | source)
XLA Modules:
  0.0 147.7 jit_solution(4502479279950125638)
XLA Ops:
  0.0 1.5 copy.10
  1.5 1.2 copy.11
  2.6 1.9 %collective-permute-start.1 = (bf16[512,768]{1,0:T(8,128)(2,1)}, bf16[512,768]{1,0:T(8,128)(2,1)S(1)}, u32[]{:S(2)}, u32[]{:S(2)}) collective-permute-start(bf16[512,768]{1,0:T(8,128)(2,1)} %copy.11), channel_id=1, source_target_pairs={{0,0},{1,16},{2,32},{3,48},{4,64},{5,80},{6,96},{7,112},{8,8},{9,2... | collective-permute-start | bytes 2359304 | tf_op jit(solution)/shard_map/ppermute | solution.py:41
  4.5 1.4 multiply_exponential_fusion
  5.9 0.8 exponential_bitcast_fusion.3
  6.8 0.8 dynamic_slice.21
  7.6 0.6 slice.24
  8.3 6.7 %collective-permute-start = (bf16[16,512]{1,0:T(8,128)(2,1)}, bf16[16,512]{1,0:T(8,128)(2,1)}, u32[]{:S(2)}, u32[]{:S(2)}) collective-permute-start(bf16[16,512]{1,0:T(8,128)(2,1)} %slice.24), channel_id=1, source_target_pairs={{0,8},{1,9},{2,10},{3,11},{4,12},{5,13},{6,14},{7,15},{8,16},{9,17... | collective-permute-start | bytes 49160 | tf_op jit(solution)/shard_map/ppermute | solution.py:41
  15.2 0.6 copy.13
  15.8 0.1 stack.67.where
  15.9 0.1 collective-permute-done
  16.0 0.8 pad_maximum_fusion.refs_0_
  16.8 0.0 collective-permute-done.1.refs_6_.refs_4_
  16.8 11.3 %collective-permute-start.2 = (bf16[1040,512]{1,0:T(8,128)(2,1)S(1)}, bf16[1040,512]{1,0:T(8,128)(2,1)S(1)}, u32[]{:S(2)}, u32[]{:S(2)}) collective-permute-start(bf16[1040,512]{1,0:T(8,128)(2,1)S(1)} %pad_maximum_fusion.refs_0_), channel_id=1, source_target_pairs={{0,1},{1,2},{2,3},{3,0},{4,5},{5,6},{6,7},{7,4},{8,9},{9,10},{10,1... | collective-permute-start | bytes 3194888 | tf_op jit(solution)/shard_map/ppermute | solution.py:41
  28.1 3.3 %collective-permute-start.3 = (bf16[1040,512]{1,0:T(8,128)(2,1)S(1)}, bf16[1040,512]{1,0:T(8,128)(2,1)S(1)}, u32[]{:S(2)}, u32[]{:S(2)}) collective-permute-start(bf16[1040,512]{1,0:T(8,128)(2,1)S(1)} %pad_maximum_fusion.refs_0_), channel_id=1, source_target_pairs={{0,3},{1,0},{2,1},{3,2},{4,7},{5,4},{6,5},{7,6},{8,11},{9,8},{10,9... | collective-permute-start | bytes 3194888 | tf_op jit(solution)/shard_map/ppermute | solution.py:41
  31.5 3.8 %collective-permute-start.4 = (bf16[1040,512]{1,0:T(8,128)(2,1)S(1)}, bf16[1040,512]{1,0:T(8,128)(2,1)S(1)}, u32[]{:S(2)}, u32[]{:S(2)}) collective-permute-start(bf16[1040,512]{1,0:T(8,128)(2,1)S(1)} %pad_maximum_fusion.refs_0_), channel_id=1, source_target_pairs={{0,4},{1,5},{2,6},{3,7},{4,0},{5,1},{6,2},{7,3},{8,12},{9,13},{10,... | collective-permute-start | bytes 3194888 | tf_op jit(solution)/shard_map/ppermute | solution.py:41
  35.3 2.7 %collective-permute-start.6 = (bf16[512,768]{1,0:T(8,128)(2,1)S(1)}, bf16[512,768]{1,0:T(8,128)(2,1)S(1)}, u32[]{:S(2)}, u32[]{:S(2)}) collective-permute-start(bf16[512,768]{1,0:T(8,128)(2,1)S(1)} %collective-permute-done.1.refs_6_.refs_4_), channel_id=1, source_target_pairs={{0,48},{1,49},{2,50},{3,51},{4,52},{5,53},{6,54},{7,55},{8,56},{9,... | collective-permute-start | bytes 2359304 | tf_op jit(solution)/shard_map/ppermute | solution.py:41
  37.9 15.5 %collective-permute-done.5.refs_7_.refs_5_ = bf16[512,768]{1,0:T(8,128)(2,1)S(1)} collective-permute-done((bf16[512,768]{1,0:T(8,128)(2,1)S(1)}, bf16[512,768]{1,0:T(8,128)(2,1)S(1)}, u32[]{:S(2)}, u32[]{:S(2)}) %collective-permute-start.5) | collective-permute-done | bytes 786464 | tf_op jit(solution)/shard_map/ppermute | solution.py:41
  53.4 0.0 collective-permute-done.6.refs_8_.refs_6_
  53.4 0.1 collective-permute-done.2.refs_1_
  53.5 0.0 collective-permute-done.3.refs_2_
  53.5 3.7 %collective-permute-done.4.refs_3_ = bf16[1040,512]{1,0:T(8,128)(2,1)S(1)} collective-permute-done((bf16[1040,512]{1,0:T(8,128)(2,1)S(1)}, bf16[1040,512]{1,0:T(8,128)(2,1)S(1)}, u32[]{:S(2)}, u32[]{:S(2)}) %collective-permute-start.4) | collective-permute-done | bytes 1064992 | tf_op jit(solution)/shard_map/ppermute | solution.py:41
  57.3 2.5 %collective-permute-start.7 = (bf16[512,768]{1,0:T(8,128)(2,1)S(1)}, bf16[512,768]{1,0:T(8,128)(2,1)S(1)}, u32[]{:S(2)}, u32[]{:S(2)}) collective-permute-start(bf16[512,768]{1,0:T(8,128)(2,1)S(1)} %collective-permute-done.1.refs_6_.refs_4_), channel_id=1, source_target_pairs={{0,8},{1,9},{2,10},{3,11},{4,12},{5,13},{6,14},{7,15},{8,0},{9,1},... | collective-permute-start | bytes 2359304 | tf_op jit(solution)/shard_map/ppermute | solution.py:41
  59.7 0.0 collective-permute-start.8
  59.7 0.5 collective-permute-start.9
  60.2 2.7 %collective-permute-start.11 = (bf16[1040,512]{1,0:T(8,128)(2,1)S(1)}, bf16[1040,512]{1,0:T(8,128)(2,1)S(1)}, u32[]{:S(2)}, u32[]{:S(2)}) collective-permute-start(bf16[1040,512]{1,0:T(8,128)(2,1)S(1)} %collective-permute-done.4.refs_3_), channel_id=1, source_target_pairs={{0,3},{1,0},{2,1},{3,2},{4,7},{5,4},{6,5},{7,6},{8,11},{9,8},{10,9... | collective-permute-start | bytes 3194888 | tf_op jit(solution)/shard_map/ppermute | solution.py:41
  62.9 0.0 collective-permute-done.7.refs_1_.refs_4_
  62.9 0.0 collective-permute-done.8.refs_2_.refs_5_
  62.9 1.0 collective-permute-done.9.refs_3_.refs_6_
  63.9 0.0 collective-permute-start.12
  63.9 1.3 collective-permute-start.13
  65.2 21.3 %collective-permute-done.10.refs_4_ = bf16[1040,512]{1,0:T(8,128)(2,1)S(1)} collective-permute-done((bf16[1040,512]{1,0:T(8,128)(2,1)S(1)}, bf16[1040,512]{1,0:T(8,128)(2,1)S(1)}, u32[]{:S(2)}, u32[]{:S(2)}) %collective-permute-start.10) | collective-permute-done | bytes 1064992 | tf_op jit(solution)/shard_map/ppermute | solution.py:41
  86.6 0.0 collective-permute-done.11.refs_5_
  86.6 0.9 collective-permute-start.14
  87.5 0.1 collective-permute-start.15
  87.6 0.0 collective-permute-start.19
  87.6 2.7 %collective-permute-start.20 = (bf16[1040,512]{1,0:T(8,128)(2,1)S(1)}, bf16[1040,512]{1,0:T(8,128)(2,1)S(1)}, u32[]{:S(2)}, u32[]{:S(2)}) collective-permute-start(bf16[1040,512]{1,0:T(8,128)(2,1)S(1)} %collective-permute-done.11.refs_5_), channel_id=1, source_target_pairs={{0,3},{1,0},{2,1},{3,2},{4,7},{5,4},{6,5},{7,6},{8,11},{9,8},{10,9... | collective-permute-start | bytes 3194888 | tf_op jit(solution)/shard_map/ppermute | solution.py:41
  90.2 0.0 collective-permute-start.16
  90.2 0.0 collective-permute-done.14.refs_4_.refs_7_
  90.2 0.3 collective-permute-done.15.refs_8_
  90.5 2.4 %collective-permute-start.17 = (bf16[512,768]{1,0:T(8,128)(2,1)S(1)}, bf16[512,768]{1,0:T(8,128)(2,1)S(1)}, u32[]{:S(2)}, u32[]{:S(2)}) collective-permute-start(bf16[512,768]{1,0:T(8,128)(2,1)S(1)} %collective-permute-done.13.refs_8_), channel_id=1, source_target_pairs={{0,48},{1,49},{2,50},{3,51},{4,52},{5,53},{6,54},{7,55},{8,56},{9,... | collective-permute-start | bytes 2359304 | tf_op jit(solution)/shard_map/ppermute | solution.py:41
  92.9 1.3 collective-permute-start.18
  94.3 4.3 %shard_map.64 = (bf16[8,1040,512]{2,1,0:T(8,128)(2,1)S(1)}, f32[1040,768]{1,0:T(8,128)S(1)}) custom-call(s32[9]{0:T(128)S(1)} %stack.67.where, bf16[1040,512]{1,0:T(8,128)(2,1)S(1)} %pad_maximum_fusion.refs_0_, bf16[1040,512]{1,0:T(8,128)(2,1)S(1)} %collective-permute-done.2.refs_1_, bf16[1040,512]{1,0:T(8,128)(2,1)S(1)} %collective-permute-done.3.refs_2_, ...), custom_call_target="tpu_custom_call" | custom-call | flops 2453667840 | bytes 12582912 | tf_op jit(solution)/shard_map/pallas_call | solution.py:105
  98.6 3.7 %shard_map.65.refs_3_ = f32[1040,768]{1,0:T(8,128)S(1)} custom-call(s32[9]{0:T(128)S(1)} %stack.67.where, bf16[8,1040,512]{2,1,0:T(8,128)(2,1)S(1)} %get-tuple-element.112.refs_0_, bf16[512,768]{1,0:T(8,128)(2,1)S(1)} %collective-permute-done.7.refs_1_.refs_4_, bf16[512,768]{1,0:T(8,128)(2,1)S(1)} %collective-permute-done.8.refs_2_.refs_5_, ...), custom_call_target="tpu_custom_call" | custom-call | flops 2453667840 | bytes 12582912 | tf_op jit(solution)/shard_map/pallas_call | solution.py:123
  102.3 7.2 %collective-permute-done.16.refs_9_ = bf16[512,768]{1,0:T(8,128)(2,1)S(1)} collective-permute-done((bf16[512,768]{1,0:T(8,128)(2,1)S(1)}, bf16[512,768]{1,0:T(8,128)(2,1)S(1)}, u32[]{:S(2)}, u32[]{:S(2)}) %collective-permute-start.16) | collective-permute-done | bytes 786464 | tf_op jit(solution)/shard_map/ppermute | solution.py:41
  109.5 3.9 %collective-permute-done.19.refs_1_ = bf16[1040,512]{1,0:T(8,128)(2,1)S(1)} collective-permute-done((bf16[1040,512]{1,0:T(8,128)(2,1)S(1)}, bf16[1040,512]{1,0:T(8,128)(2,1)S(1)}, u32[]{:S(2)}, u32[]{:S(2)}) %collective-permute-start.19) | collective-permute-done | bytes 1064992 | tf_op jit(solution)/shard_map/ppermute | solution.py:41
  113.4 0.0 collective-permute-done.20.refs_2_
  113.4 0.0 collective-permute-done.17.refs_10_
  113.5 0.0 collective-permute-done.18.refs_11_
  113.5 1.3 collective-permute-start.21
  114.8 0.1 collective-permute-start.22
  114.9 0.4 collective-permute-start.23
  115.3 7.7 %shard_map.66 = (f32[1024,256]{1,0:T(8,128)S(1)}, f32[1024,256]{1,0:T(8,128)S(1)}, f32[128,256]{1,0:T(8,128)S(1)}, f32[16,256]{1,0:T(8,128)S(1)}) custom-call(s32[9]{0:T(128)S(1)} %stack.67.where, bf16[8,1040,512]{2,1,0:T(8,128)(2,1)S(1)} %get-tuple-element.112.refs_0_, bf16[1040,512]{1,0:T(8,128)(2,1)S(1)} %collective-permute-done.19.refs_1_, ...), custom_call_target="tpu_custom_call" | custom-call | flops 4089446400 | bytes 12582912 | tf_op jit(solution)/shard_map/pallas_call | solution.py:206
  123.0 7.9 %shard_map.67 = (f32[1024,256]{1,0:T(8,128)S(1)}, f32[1024,256]{1,0:T(8,128)S(1)}, f32[128,256]{1,0:T(8,128)S(1)}, f32[16,256]{1,0:T(8,128)S(1)}) custom-call(s32[9]{0:T(128)S(1)} %stack.67.where, bf16[8,1040,512]{2,1,0:T(8,128)(2,1)S(1)} %get-tuple-element.112.refs_0_, bf16[1040,512]{1,0:T(8,128)(2,1)S(1)} %collective-permute-done.19.refs_1_, ...), custom_call_target="tpu_custom_call" | custom-call | flops 4089446400 | bytes 12582912 | tf_op jit(solution)/shard_map/pallas_call | solution.py:206
  130.9 0.1 collective-permute-start.24
  131.0 2.3 %collective-permute-start.25 = (f32[16,512]{1,0:T(8,128)S(1)}, f32[16,512]{1,0:T(8,128)S(1)}, u32[]{:S(2)}, u32[]{:S(2)}) collective-permute-start(f32[16,512]{1,0:T(8,128)S(1)} %pad_maximum_fusion.4), channel_id=1, source_target_pairs={{0,32},{1,33},{2,34},{3,35},{4,36},{5,37},{6,38},{7,39},{8,40},{9,... | collective-permute-start | bytes 98312 | tf_op jit(solution)/shard_map/ppermute | solution.py:41
  133.3 1.8 %collective-permute-start.26 = (f32[16,512]{1,0:T(8,128)S(1)}, f32[16,512]{1,0:T(8,128)S(1)}, u32[]{:S(2)}, u32[]{:S(2)}) collective-permute-start(f32[16,512]{1,0:T(8,128)S(1)} %pad_maximum_fusion.4), channel_id=1, source_target_pairs={{0,48},{1,49},{2,50},{3,51},{4,52},{5,53},{6,54},{7,55},{8,56},{9,... | collective-permute-start | bytes 98312 | tf_op jit(solution)/shard_map/ppermute | solution.py:41
  135.1 2.6 %shard_map.68.y0 = f32[1024,256]{1,0:T(8,128)S(1)} custom-call(f32[1024,256]{1,0:T(8,128)S(1)} %get-tuple-element.128.prod_ref, f32[128,256]{1,0:T(8,128)S(1)} %get-tuple-element.129.u_ref, f32[64,256]{1,0:T(8,128)S(1)} %get-tuple-element.119.refs_12_.prm.p0), custom_call_target="tpu_custom_call" | custom-call | flops 16777216 | bytes 12582912 | tf_op jit(solution)/shard_map/pallas_call | solution.py:255
  137.8 1.0 collective-permute-start.27
  138.8 1.4 collective-permute-start.28
  140.1 0.4 collective-permute-start.29
  140.5 2.6 %shard_map.69.y1 = f32[1024,256]{1,0:T(8,128)S(1)} custom-call(f32[1024,256]{1,0:T(8,128)S(1)} %get-tuple-element.131.prod_ref, f32[128,256]{1,0:T(8,128)S(1)} %get-tuple-element.132.u_ref, f32[64,256]{1,0:T(8,128)S(1)} %get-tuple-element.123.refs_12_.prm.p1), custom_call_target="tpu_custom_call" | custom-call | flops 16777216 | bytes 12582912 | tf_op jit(solution)/shard_map/pallas_call | solution.py:255
  143.1 0.4 collective-permute-done.29.cross
  143.5 4.2 %shard_map.70 = bf16[1024,512]{1,0:T(8,128)(2,1)} custom-call(s32[1]{0:T(128)} %bitcast.15.core_ref, f32[1024,256]{1,0:T(8,128)S(1)} %shard_map.68.y0, f32[1024,256]{1,0:T(8,128)S(1)} %shard_map.69.y1, f32[1024,256]{1,0:T(8,128)S(1)} %get-tuple-element.133.x0, f32[1024,256]{1,0:T(8,128)S(1)} %get-tuple-element.134.x1, ...), custom_call_target="tpu_custom_call" | custom-call | tf_op jit(solution)/shard_map/pallas_call | solution.py:306
  (29 shorter events, 0.2 us)
Async XLA Ops:
  0.0 6.7 %copy-start = (f32[3,3,4096]{2,1,0:T(4,128)S(1)}, f32[3,3,4096]{2,1,0:T(4,128)}, u32[]{:S(2)}) copy-start(f32[3,3,4096]{2,1,0:T(4,128)} %param.8) | copy-start | bytes 442372
  2.6 5.0 %copy-start.1 = (bf16[1024,512]{1,0:T(8,128)(2,1)S(1)}, bf16[1024,512]{1,0:T(8,128)(2,1)}, u32[]{:S(2)}) copy-start(bf16[1024,512]{1,0:T(8,128)(2,1)} %param.6) | copy-start | bytes 3145732
  2.6 14.2 %collective-permute-start.1 = (bf16[512,768]{1,0:T(8,128)(2,1)}, bf16[512,768]{1,0:T(8,128)(2,1)S(1)}, u32[]{:S(2)}, u32[]{:S(2)}) collective-permute-start(bf16[512,768]{1,0:T(8,128)(2,1)} %copy.11), channel_id=1, source_target_pairs={{0,0},{1,16},{2,32},{3,48},{4,64},{5,80},{6,96},{7,112},{8,8},{9,2... | collective-permute-start | bytes 2359304 | tf_op jit(solution)/shard_map/ppermute | solution.py:41
  8.3 7.7 %collective-permute-start = (bf16[16,512]{1,0:T(8,128)(2,1)}, bf16[16,512]{1,0:T(8,128)(2,1)}, u32[]{:S(2)}, u32[]{:S(2)}) collective-permute-start(bf16[16,512]{1,0:T(8,128)(2,1)} %slice.24), channel_id=1, source_target_pairs={{0,8},{1,9},{2,10},{3,11},{4,12},{5,13},{6,14},{7,15},{8,16},{9,17... | collective-permute-start | bytes 49160 | tf_op jit(solution)/shard_map/ppermute | solution.py:41
  16.8 36.8 %collective-permute-start.2 = (bf16[1040,512]{1,0:T(8,128)(2,1)S(1)}, bf16[1040,512]{1,0:T(8,128)(2,1)S(1)}, u32[]{:S(2)}, u32[]{:S(2)}) collective-permute-start(bf16[1040,512]{1,0:T(8,128)(2,1)S(1)} %pad_maximum_fusion.refs_0_), channel_id=1, source_target_pairs={{0,1},{1,2},{2,3},{3,0},{4,5},{5,6},{6,7},{7,4},{8,9},{9,10},{10,1... | collective-permute-start | bytes 3194888 | tf_op jit(solution)/shard_map/ppermute | solution.py:41
  28.1 25.4 %collective-permute-start.3 = (bf16[1040,512]{1,0:T(8,128)(2,1)S(1)}, bf16[1040,512]{1,0:T(8,128)(2,1)S(1)}, u32[]{:S(2)}, u32[]{:S(2)}) collective-permute-start(bf16[1040,512]{1,0:T(8,128)(2,1)S(1)} %pad_maximum_fusion.refs_0_), channel_id=1, source_target_pairs={{0,3},{1,0},{2,1},{3,2},{4,7},{5,4},{6,5},{7,6},{8,11},{9,8},{10,9... | collective-permute-start | bytes 3194888 | tf_op jit(solution)/shard_map/ppermute | solution.py:41
  31.5 25.8 %collective-permute-start.4 = (bf16[1040,512]{1,0:T(8,128)(2,1)S(1)}, bf16[1040,512]{1,0:T(8,128)(2,1)S(1)}, u32[]{:S(2)}, u32[]{:S(2)}) collective-permute-start(bf16[1040,512]{1,0:T(8,128)(2,1)S(1)} %pad_maximum_fusion.refs_0_), channel_id=1, source_target_pairs={{0,4},{1,5},{2,6},{3,7},{4,0},{5,1},{6,2},{7,3},{8,12},{9,13},{10,... | collective-permute-start | bytes 3194888 | tf_op jit(solution)/shard_map/ppermute | solution.py:41
  35.3 18.1 %collective-permute-start.5 = (bf16[512,768]{1,0:T(8,128)(2,1)S(1)}, bf16[512,768]{1,0:T(8,128)(2,1)S(1)}, u32[]{:S(2)}, u32[]{:S(2)}) collective-permute-start(bf16[512,768]{1,0:T(8,128)(2,1)S(1)} %collective-permute-done.1.refs_6_.refs_4_), channel_id=1, source_target_pairs={{0,16},{1,17},{2,18},{3,19},{4,20},{5,21},{6,22},{7,23},{8,24},{9,... | collective-permute-start | bytes 2359304 | tf_op jit(solution)/shard_map/ppermute | solution.py:41
  35.3 18.1 %collective-permute-start.6 = (bf16[512,768]{1,0:T(8,128)(2,1)S(1)}, bf16[512,768]{1,0:T(8,128)(2,1)S(1)}, u32[]{:S(2)}, u32[]{:S(2)}) collective-permute-start(bf16[512,768]{1,0:T(8,128)(2,1)S(1)} %collective-permute-done.1.refs_6_.refs_4_), channel_id=1, source_target_pairs={{0,48},{1,49},{2,50},{3,51},{4,52},{5,53},{6,54},{7,55},{8,56},{9,... | collective-permute-start | bytes 2359304 | tf_op jit(solution)/shard_map/ppermute | solution.py:41
  57.3 5.7 %collective-permute-start.7 = (bf16[512,768]{1,0:T(8,128)(2,1)S(1)}, bf16[512,768]{1,0:T(8,128)(2,1)S(1)}, u32[]{:S(2)}, u32[]{:S(2)}) collective-permute-start(bf16[512,768]{1,0:T(8,128)(2,1)S(1)} %collective-permute-done.1.refs_6_.refs_4_), channel_id=1, source_target_pairs={{0,8},{1,9},{2,10},{3,11},{4,12},{5,13},{6,14},{7,15},{8,0},{9,1},... | collective-permute-start | bytes 2359304 | tf_op jit(solution)/shard_map/ppermute | solution.py:41
  59.7 3.2 %collective-permute-start.8 = (bf16[512,768]{1,0:T(8,128)(2,1)S(1)}, bf16[512,768]{1,0:T(8,128)(2,1)S(1)}, u32[]{:S(2)}, u32[]{:S(2)}) collective-permute-start(bf16[512,768]{1,0:T(8,128)(2,1)S(1)} %collective-permute-done.5.refs_7_.refs_5_), channel_id=1, source_target_pairs={{0,8},{1,9},{2,10},{3,11},{4,12},{5,13},{6,14},{7,15},{8,0},{9,1},... | collective-permute-start | bytes 2359304 | tf_op jit(solution)/shard_map/ppermute | solution.py:41
  59.7 4.2 %collective-permute-start.9 = (bf16[512,768]{1,0:T(8,128)(2,1)S(1)}, bf16[512,768]{1,0:T(8,128)(2,1)S(1)}, u32[]{:S(2)}, u32[]{:S(2)}) collective-permute-start(bf16[512,768]{1,0:T(8,128)(2,1)S(1)} %collective-permute-done.6.refs_8_.refs_6_), channel_id=1, source_target_pairs={{0,8},{1,9},{2,10},{3,11},{4,12},{5,13},{6,14},{7,15},{8,0},{9,1},... | collective-permute-start | bytes 2359304 | tf_op jit(solution)/shard_map/ppermute | solution.py:41
  60.2 26.4 %collective-permute-start.10 = (bf16[1040,512]{1,0:T(8,128)(2,1)S(1)}, bf16[1040,512]{1,0:T(8,128)(2,1)S(1)}, u32[]{:S(2)}, u32[]{:S(2)}) collective-permute-start(bf16[1040,512]{1,0:T(8,128)(2,1)S(1)} %collective-permute-done.4.refs_3_), channel_id=1, source_target_pairs={{0,1},{1,2},{2,3},{3,0},{4,5},{5,6},{6,7},{7,4},{8,9},{9,10},{10,1... | collective-permute-start | bytes 3194888 | tf_op jit(solution)/shard_map/ppermute | solution.py:41
  60.2 26.4 %collective-permute-start.11 = (bf16[1040,512]{1,0:T(8,128)(2,1)S(1)}, bf16[1040,512]{1,0:T(8,128)(2,1)S(1)}, u32[]{:S(2)}, u32[]{:S(2)}) collective-permute-start(bf16[1040,512]{1,0:T(8,128)(2,1)S(1)} %collective-permute-done.4.refs_3_), channel_id=1, source_target_pairs={{0,3},{1,0},{2,1},{3,2},{4,7},{5,4},{6,5},{7,6},{8,11},{9,8},{10,9... | collective-permute-start | bytes 3194888 | tf_op jit(solution)/shard_map/ppermute | solution.py:41
  63.9 22.7 %collective-permute-start.12 = (bf16[512,768]{1,0:T(8,128)(2,1)S(1)}, bf16[512,768]{1,0:T(8,128)(2,1)S(1)}, u32[]{:S(2)}, u32[]{:S(2)}) collective-permute-start(bf16[512,768]{1,0:T(8,128)(2,1)S(1)} %collective-permute-done.5.refs_7_.refs_5_), channel_id=1, source_target_pairs={{0,16},{1,17},{2,18},{3,19},{4,20},{5,21},{6,22},{7,23},{8,24},{9,... | collective-permute-start | bytes 2359304 | tf_op jit(solution)/shard_map/ppermute | solution.py:41
  63.9 22.7 %collective-permute-start.13 = (bf16[512,768]{1,0:T(8,128)(2,1)S(1)}, bf16[512,768]{1,0:T(8,128)(2,1)S(1)}, u32[]{:S(2)}, u32[]{:S(2)}) collective-permute-start(bf16[512,768]{1,0:T(8,128)(2,1)S(1)} %collective-permute-done.1.refs_6_.refs_4_), channel_id=1, source_target_pairs={{0,64},{1,65},{2,66},{3,67},{4,68},{5,69},{6,70},{7,71},{8,72},{9,... | collective-permute-start | bytes 2359304 | tf_op jit(solution)/shard_map/ppermute | solution.py:41
  86.6 3.6 %collective-permute-start.14 = (bf16[512,768]{1,0:T(8,128)(2,1)S(1)}, bf16[512,768]{1,0:T(8,128)(2,1)S(1)}, u32[]{:S(2)}, u32[]{:S(2)}) collective-permute-start(bf16[512,768]{1,0:T(8,128)(2,1)S(1)} %collective-permute-done.12.refs_9_.refs_7_), channel_id=1, source_target_pairs={{0,8},{1,9},{2,10},{3,11},{4,12},{5,13},{6,14},{7,15},{8,0},{9,1},... | collective-permute-start | bytes 2359304 | tf_op jit(solution)/shard_map/ppermute | solution.py:41
  87.5 3.0 %collective-permute-start.15 = (bf16[512,768]{1,0:T(8,128)(2,1)S(1)}, bf16[512,768]{1,0:T(8,128)(2,1)S(1)}, u32[]{:S(2)}, u32[]{:S(2)}) collective-permute-start(bf16[512,768]{1,0:T(8,128)(2,1)S(1)} %collective-permute-done.13.refs_8_), channel_id=1, source_target_pairs={{0,8},{1,9},{2,10},{3,11},{4,12},{5,13},{6,14},{7,15},{8,0},{9,1},... | collective-permute-start | bytes 2359304 | tf_op jit(solution)/shard_map/ppermute | solution.py:41
  87.6 25.9 %collective-permute-start.19 = (bf16[1040,512]{1,0:T(8,128)(2,1)S(1)}, bf16[1040,512]{1,0:T(8,128)(2,1)S(1)}, u32[]{:S(2)}, u32[]{:S(2)}) collective-permute-start(bf16[1040,512]{1,0:T(8,128)(2,1)S(1)} %collective-permute-done.2.refs_1_), channel_id=1, source_target_pairs={{0,1},{1,2},{2,3},{3,0},{4,5},{5,6},{6,7},{7,4},{8,9},{9,10},{10,1... | collective-permute-start | bytes 3194888 | tf_op jit(solution)/shard_map/ppermute | solution.py:41
  87.6 25.9 %collective-permute-start.20 = (bf16[1040,512]{1,0:T(8,128)(2,1)S(1)}, bf16[1040,512]{1,0:T(8,128)(2,1)S(1)}, u32[]{:S(2)}, u32[]{:S(2)}) collective-permute-start(bf16[1040,512]{1,0:T(8,128)(2,1)S(1)} %collective-permute-done.11.refs_5_), channel_id=1, source_target_pairs={{0,3},{1,0},{2,1},{3,2},{4,7},{5,4},{6,5},{7,6},{8,11},{9,8},{10,9... | collective-permute-start | bytes 3194888 | tf_op jit(solution)/shard_map/ppermute | solution.py:41
  90.2 19.3 %collective-permute-start.16 = (bf16[512,768]{1,0:T(8,128)(2,1)S(1)}, bf16[512,768]{1,0:T(8,128)(2,1)S(1)}, u32[]{:S(2)}, u32[]{:S(2)}) collective-permute-start(bf16[512,768]{1,0:T(8,128)(2,1)S(1)} %collective-permute-done.13.refs_8_), channel_id=1, source_target_pairs={{0,16},{1,17},{2,18},{3,19},{4,20},{5,21},{6,22},{7,23},{8,24},{9,... | collective-permute-start | bytes 2359304 | tf_op jit(solution)/shard_map/ppermute | solution.py:41
  90.5 22.9 %collective-permute-start.17 = (bf16[512,768]{1,0:T(8,128)(2,1)S(1)}, bf16[512,768]{1,0:T(8,128)(2,1)S(1)}, u32[]{:S(2)}, u32[]{:S(2)}) collective-permute-start(bf16[512,768]{1,0:T(8,128)(2,1)S(1)} %collective-permute-done.13.refs_8_), channel_id=1, source_target_pairs={{0,48},{1,49},{2,50},{3,51},{4,52},{5,53},{6,54},{7,55},{8,56},{9,... | collective-permute-start | bytes 2359304 | tf_op jit(solution)/shard_map/ppermute | solution.py:41
  92.9 20.5 %collective-permute-start.18 = (bf16[512,768]{1,0:T(8,128)(2,1)S(1)}, bf16[512,768]{1,0:T(8,128)(2,1)S(1)}, u32[]{:S(2)}, u32[]{:S(2)}) collective-permute-start(bf16[512,768]{1,0:T(8,128)(2,1)S(1)} %collective-permute-done.12.refs_9_.refs_7_), channel_id=1, source_target_pairs={{0,64},{1,65},{2,66},{3,67},{4,68},{5,69},{6,70},{7,71},{8,72},{9,... | collective-permute-start | bytes 2359304 | tf_op jit(solution)/shard_map/ppermute | solution.py:41
  113.5 9.5 %collective-permute-start.21 = (bf16[512,768]{1,0:T(8,128)(2,1)S(1)}, bf16[512,768]{1,0:T(8,128)(2,1)S(1)}, u32[]{:S(2)}, u32[]{:S(2)}) collective-permute-start(bf16[512,768]{1,0:T(8,128)(2,1)S(1)} %collective-permute-done.16.refs_9_), channel_id=1, source_target_pairs={{0,8},{1,9},{2,10},{3,11},{4,12},{5,13},{6,14},{7,15},{8,0},{9,1},... | collective-permute-start | bytes 2359304 | tf_op jit(solution)/shard_map/ppermute | solution.py:41
  114.8 8.2 %collective-permute-start.22 = (bf16[512,768]{1,0:T(8,128)(2,1)S(1)}, bf16[512,768]{1,0:T(8,128)(2,1)S(1)}, u32[]{:S(2)}, u32[]{:S(2)}) collective-permute-start(bf16[512,768]{1,0:T(8,128)(2,1)S(1)} %collective-permute-done.17.refs_10_), channel_id=1, source_target_pairs={{0,8},{1,9},{2,10},{3,11},{4,12},{5,13},{6,14},{7,15},{8,0},{9,1},... | collective-permute-start | bytes 2359304 | tf_op jit(solution)/shard_map/ppermute | solution.py:41
  114.9 8.1 %collective-permute-start.23 = (bf16[512,768]{1,0:T(8,128)(2,1)S(1)}, bf16[512,768]{1,0:T(8,128)(2,1)S(1)}, u32[]{:S(2)}, u32[]{:S(2)}) collective-permute-start(bf16[512,768]{1,0:T(8,128)(2,1)S(1)} %collective-permute-done.18.refs_11_), channel_id=1, source_target_pairs={{0,8},{1,9},{2,10},{3,11},{4,12},{5,13},{6,14},{7,15},{8,0},{9,1},... | collective-permute-start | bytes 2359304 | tf_op jit(solution)/shard_map/ppermute | solution.py:41
  130.9 6.8 %collective-permute-start.24 = (f32[16,512]{1,0:T(8,128)S(1)}, f32[16,512]{1,0:T(8,128)S(1)}, u32[]{:S(2)}, u32[]{:S(2)}) collective-permute-start(f32[16,512]{1,0:T(8,128)S(1)} %pad_maximum_fusion.4), channel_id=1, source_target_pairs={{0,16},{1,17},{2,18},{3,19},{4,20},{5,21},{6,22},{7,23},{8,24},{9,... | collective-permute-start | bytes 98312 | tf_op jit(solution)/shard_map/ppermute | solution.py:41
  131.0 6.7 %collective-permute-start.25 = (f32[16,512]{1,0:T(8,128)S(1)}, f32[16,512]{1,0:T(8,128)S(1)}, u32[]{:S(2)}, u32[]{:S(2)}) collective-permute-start(f32[16,512]{1,0:T(8,128)S(1)} %pad_maximum_fusion.4), channel_id=1, source_target_pairs={{0,32},{1,33},{2,34},{3,35},{4,36},{5,37},{6,38},{7,39},{8,40},{9,... | collective-permute-start | bytes 98312 | tf_op jit(solution)/shard_map/ppermute | solution.py:41
  133.3 4.4 %collective-permute-start.26 = (f32[16,512]{1,0:T(8,128)S(1)}, f32[16,512]{1,0:T(8,128)S(1)}, u32[]{:S(2)}, u32[]{:S(2)}) collective-permute-start(f32[16,512]{1,0:T(8,128)S(1)} %pad_maximum_fusion.4), channel_id=1, source_target_pairs={{0,48},{1,49},{2,50},{3,51},{4,52},{5,53},{6,54},{7,55},{8,56},{9,... | collective-permute-start | bytes 98312 | tf_op jit(solution)/shard_map/ppermute | solution.py:41
  135.1 2.6 %copy-start.2 = (f32[16,512]{1,0:T(8,128)S(1)}, f32[16,512]{1,0:T(8,128)}, u32[]{:S(2)}) copy-start(f32[16,512]{1,0:T(8,128)} %get-tuple-element.139) | copy-start | bytes 98308
  137.8 5.3 %collective-permute-start.27 = (f32[16,512]{1,0:T(8,128)S(1)}, f32[16,512]{1,0:T(8,128)S(1)}, u32[]{:S(2)}, u32[]{:S(2)}) collective-permute-start(f32[16,512]{1,0:T(8,128)S(1)} %get-tuple-element.143), channel_id=1, source_target_pairs={{0,8},{1,9},{2,10},{3,11},{4,12},{5,13},{6,14},{7,15},{8,0},{9,1},... | collective-permute-start | bytes 98312 | tf_op jit(solution)/shard_map/ppermute | solution.py:41
  138.8 4.3 %collective-permute-start.28 = (f32[16,512]{1,0:T(8,128)S(1)}, f32[16,512]{1,0:T(8,128)S(1)}, u32[]{:S(2)}, u32[]{:S(2)}) collective-permute-start(f32[16,512]{1,0:T(8,128)S(1)} %get-tuple-element.147), channel_id=1, source_target_pairs={{0,64},{1,65},{2,66},{3,67},{4,68},{5,69},{6,70},{7,71},{8,72},{9,... | collective-permute-start | bytes 98312 | tf_op jit(solution)/shard_map/ppermute | solution.py:41
  140.1 3.4 %collective-permute-start.29 = (f32[16,512]{1,0:T(8,128)S(1)}, f32[16,512]{1,0:T(8,128)S(1)}, u32[]{:S(2)}, u32[]{:S(2)}) collective-permute-start(f32[16,512]{1,0:T(8,128)S(1)} %get-tuple-element.147), channel_id=1, source_target_pairs={{0,72},{1,73},{2,74},{3,75},{4,76},{5,77},{6,78},{7,79},{8,64},{9,... | collective-permute-start | bytes 98312 | tf_op jit(solution)/shard_map/ppermute | solution.py:41

commit v7 on v6

--- a/solution.py
+++ b/solution.py
@@ -264,7 +264,7 @@
     )(prod, u, prm)
 
 
-def gate_kernel(rows, core_ref, y0, y1, x0, x1, p0, p1, near, sent, same, cross, fades, out_ref, wide):
+def gate_kernel(rows, core_ref, y0, y1, x0, x1, p0, p1, local, up, two, down, first, scale, out_ref, wide):
     seg_len = rows // SEG
     core = core_ref[0]
     seg = lax.broadcasted_iota(jnp.int32, (SEG, LANES), 0).astype(F32) * seg_len
@@ -273,12 +273,8 @@
         for q in range(2):
             lanes = pl.ds(q * LANES, LANES)
             to = pl.ds(pl.multiple_of(base + q * LANES, LANES), LANES)
-            shard, straight, across = (
-                fades[pl.ds(n * MODES, MODES), to] for n in range(3)
-            )
-            state = (
-                shard * near[:, to] + sent[:, to] + straight * same[:, to] + across * cross[:, to]
-            )
+            state = local[:, to] + up[:, to] + two[:, to] + down[:, to]
+            state = scale[:, to] * state + first[:, to]
             decay, carried = [], []
             for k in range(MODES):
                 d = jnp.broadcast_to(prm[pl.ds(k, 1), lanes], (SEG, LANES))
@@ -306,7 +302,7 @@
     return pl.pallas_call(
         functools.partial(gate_kernel, rows),
         out_shape=jax.ShapeDtypeStruct((rows, BLOCK), jnp.bfloat16),
-        in_specs=[pl.BlockSpec(memory_space=pltpu.SMEM)] + [vmem] * 11,
+        in_specs=[pl.BlockSpec(memory_space=pltpu.SMEM)] + [vmem] * 12,
         out_specs=vmem,
         scratch_shapes=[pltpu.VMEM((rows, LANES), F32)],
         compiler_params=pltpu.CompilerParams(vmem_limit_bytes=20 << 20),
@@ -334,14 +330,13 @@
         return jnp.exp(-rates * jnp.asarray(steps).astype(F32))
 
     shard = fade(rows)
-    behind = [jnp.where(x >= m, fade(2 * rows * (m - 1)), 0.0) for m in (1, 2, 3)]
-    plane = [fade(2 * rows * (3 - (x - m) % 4)) for m in range(4)]
-    chip = fade(2 * rows)
-    lower = jnp.where(y_lo == 1, fade(2 * rows * x), 0.0)
-    straight = lower * shard
-    across = lower * jnp.where(core == 0, 1.0, shard * shard)
-    fades = jnp.concatenate([shard, straight, across], axis=0)
-    behind, plane = jnp.stack(behind), jnp.stack(plane)
+    scale = jnp.where(core == 0, 1.0, shard)
+    own, lower = [], []
+    for m in range(4):
+        to = (x + m) % 4
+        own.append(jnp.where(to > x, fade(2 * rows * jnp.maximum(to - x - 1, 0)), 0.0))
+        lower.append(jnp.where(y_lo == 1, fade(2 * rows * (to + 3 - x)), 0.0))
+    own, lower = jnp.stack(own), jnp.stack(lower)
 
     slots = []
     for of_y in (y_lo, 1 - y_lo):
@@ -357,13 +352,13 @@
         n = (yl * 4 + x) * 2 + c + 1
         return None if n == 16 else (n // 8, (n // 2) % 4, n % 2, yh, z)
 
-    w = in_weight.reshape(BLOCK, 3 * wide)
+    w = jnp.concatenate([in_weight[:, g] for g in range(3)], axis=1)
     b = transposed(w)
     shard_tokens, *prms = together((tokens, *prms))
     steps = shard_tokens.reshape(SEG, rows // SEG, BLOCK).transpose(1, 0, 2).reshape(rows, BLOCK)
     t = jnp.concatenate([send(shard_tokens[rows - HALO:], next_ctx), steps], axis=0)
-    t, b, where, core_at, fades, behind, plane, chip, *prms = together(
-        (t, b, where, core_at, fades, behind, plane, chip, *prms)
+    t, b, where, core_at, shard, scale, own, lower, *prms = together(
+        (t, b, where, core_at, shard, scale, own, lower, *prms)
     )
     tp_, tm, ty = along_z(t, 1), along_z(t, -1), other_yhi(t)
     bp, bm = along_x(b, 1), along_x(b, -1)
@@ -400,16 +395,19 @@
         [jnp.where(core == 0, ends[0], ends[1]), jnp.where(core == 0, ends[1], ends[0])], axis=1
     )
     total, products[0] = together((total, products[0]))
-    came = [total] + [along_x(total, m) for m in (1, 2, 3)]
+    came = [total, other_core(total), other_ylo(total), other_ylo_and_core(total)]
     y0 = read(products[0], us[0], prms[0], rows)
     came, products[1], y0 = together((came, products[1], y0))
-    total = came[0]
-    near = behind[0] * came[1] + behind[1] * came[2] + behind[2] * came[3]
-    whole = plane[0] * came[0] + plane[1] * came[1] + plane[2] * came[2] + plane[3] * came[3]
-    sent = other_core(jnp.where(core == 0, chip * near + total, near))
-    same, cross = other_ylo(whole), other_ylo_and_core(whole)
+
+    def chip_end(mine, other):
+        return shard * jnp.where(core == 0, mine, other) + jnp.where(core == 0, other, mine)
+
+    here, there = chip_end(*came[:2]), chip_end(*came[2:])
+    ends = [own[m] * here + lower[m] * there for m in range(4)]
+    state = ends[:1] + [along_x(ends[m], m) for m in (1, 2, 3)]
+    first = jnp.where(core == 0, 0.0, came[1])
     y1 = read(products[1], us[1], prms[1], rows)
-    return gate(core_at, [y0, y1], xs, prms, [near, sent, same, cross, fades], rows)
+    return gate(core_at, [y0, y1], xs, prms, [*state, first, scale], rows)
 
 
 def solution(mesh):

time: 148 us -> 147 us (level)
  no operation moved by 1% of the time
where the time goes in v7:
time: 147 us
  waiting for transfers between devices  53.8 us (37%)
  starting transfers between devices  52.7 us (36%)
  Pallas kernels  33 us (22%)
  other arithmetic  3.38 us (2%)
  local copies, waits for them, and re-layouts  3.34 us (2%)
    ppermute x30, waiting for transfers between devices, send(): return lax.ppermute(value, ('ctx', 'tp'), route(move))  53.8 us
    ppermute x30, starting transfers between devices, send(): return lax.ppermute(value, ('ctx', 'tp'), route(move))  52.7 us
    pallas_call x2, Pallas kernels, project(): pl.pallas_call(functools.partial(project_kernel, rows), out_shape=[jax.Sh...  15.5 us
    pallas_call x2, Pallas kernels, read(): pl.pallas_call(functools.partial(read_kernel, rows), out_shape=jax.ShapeD...  5.19 us
    pallas_call x1, Pallas kernels, begin(): pl.pallas_call(begin_kernel, out_shape=[jax.ShapeDtypeStruct((8, tall, BL...  4.32 us
    pallas_call x1, Pallas kernels, gate(): pl.pallas_call(functools.partial(gate_kernel, rows), out_shape=jax.ShapeD...  4.21 us
    pallas_call x1, Pallas kernels, also(): pl.pallas_call(also_kernel, out_shape=jax.ShapeDtypeStruct((tall, width),...  3.72 us
  transfers between devices with their start and end apart: 30, of which 10 were waited for; matrix products, arithmetic and copies ran while one was open for 3% of the time, Pallas kernels for 14%

profile of v7, /device:TPU:1, one launch (start us, length us, event | category | flops | bytes accessed | tf_op | source)
XLA Modules:
  0.0 146.9 jit_solution(4512649538687659535)
XLA Ops:
  0.0 1.2 slice_bitcast_fusion.2
  1.2 0.0 copy-start.1
  1.2 0.9 pad_maximum_fusion.1
  2.1 1.8 %collective-permute-start.1 = (bf16[512,768]{1,0:T(8,128)(2,1)}, bf16[512,768]{1,0:T(8,128)(2,1)S(1)}, u32[]{:S(2)}, u32[]{:S(2)}) collective-permute-start(bf16[512,768]{1,0:T(8,128)(2,1)} %pad_maximum_fusion.1), channel_id=1, source_target_pairs={{0,0},{1,16},{2,32},{3,48},{4,64},{5,80},{6,96},{7,112},{8,8},{9,2... | collective-permute-start | bytes 2359304 | tf_op jit(solution)/shard_map/ppermute | solution.py:41
  3.9 0.8 select_bitcast_fusion.3
  4.9 0.8 dynamic_slice.21
  5.6 0.8 select_bitcast_fusion.2
  6.5 0.6 slice.36
  7.2 6.6 %collective-permute-start = (bf16[16,512]{1,0:T(8,128)(2,1)}, bf16[16,512]{1,0:T(8,128)(2,1)}, u32[]{:S(2)}, u32[]{:S(2)}) collective-permute-start(bf16[16,512]{1,0:T(8,128)(2,1)} %slice.36), channel_id=1, source_target_pairs={{0,8},{1,9},{2,10},{3,11},{4,12},{5,13},{6,14},{7,15},{8,16},{9,17... | collective-permute-start | bytes 49160 | tf_op jit(solution)/shard_map/ppermute | solution.py:41
  14.0 0.6 copy.9
  14.6 0.1 stack.70.where
  14.7 0.1 collective-permute-done
  14.8 0.8 pad_maximum_fusion.refs_0_
  15.6 11.9 %collective-permute-start.2 = (bf16[1040,512]{1,0:T(8,128)(2,1)S(1)}, bf16[1040,512]{1,0:T(8,128)(2,1)S(1)}, u32[]{:S(2)}, u32[]{:S(2)}) collective-permute-start(bf16[1040,512]{1,0:T(8,128)(2,1)S(1)} %pad_maximum_fusion.refs_0_), channel_id=1, source_target_pairs={{0,1},{1,2},{2,3},{3,0},{4,5},{5,6},{6,7},{7,4},{8,9},{9,10},{10,1... | collective-permute-start | bytes 3194888 | tf_op jit(solution)/shard_map/ppermute | solution.py:41
  27.5 3.3 %collective-permute-start.3 = (bf16[1040,512]{1,0:T(8,128)(2,1)S(1)}, bf16[1040,512]{1,0:T(8,128)(2,1)S(1)}, u32[]{:S(2)}, u32[]{:S(2)}) collective-permute-start(bf16[1040,512]{1,0:T(8,128)(2,1)S(1)} %pad_maximum_fusion.refs_0_), channel_id=1, source_target_pairs={{0,3},{1,0},{2,1},{3,2},{4,7},{5,4},{6,5},{7,6},{8,11},{9,8},{10,9... | collective-permute-start | bytes 3194888 | tf_op jit(solution)/shard_map/ppermute | solution.py:41
  30.9 3.8 %collective-permute-start.4 = (bf16[1040,512]{1,0:T(8,128)(2,1)S(1)}, bf16[1040,512]{1,0:T(8,128)(2,1)S(1)}, u32[]{:S(2)}, u32[]{:S(2)}) collective-permute-start(bf16[1040,512]{1,0:T(8,128)(2,1)S(1)} %pad_maximum_fusion.refs_0_), channel_id=1, source_target_pairs={{0,4},{1,5},{2,6},{3,7},{4,0},{5,1},{6,2},{7,3},{8,12},{9,13},{10,... | collective-permute-start | bytes 3194888 | tf_op jit(solution)/shard_map/ppermute | solution.py:41
  34.7 0.0 collective-permute-start.5
  34.7 2.7 %collective-permute-start.6 = (bf16[512,768]{1,0:T(8,128)(2,1)S(1)}, bf16[512,768]{1,0:T(8,128)(2,1)S(1)}, u32[]{:S(2)}, u32[]{:S(2)}) collective-permute-start(bf16[512,768]{1,0:T(8,128)(2,1)S(1)} %collective-permute-done.1.refs_6_.refs_4_), channel_id=1, source_target_pairs={{0,48},{1,49},{2,50},{3,51},{4,52},{5,53},{6,54},{7,55},{8,56},{9,... | collective-permute-start | bytes 2359304 | tf_op jit(solution)/shard_map/ppermute | solution.py:41
  37.3 15.5 %collective-permute-done.5.refs_7_.refs_5_ = bf16[512,768]{1,0:T(8,128)(2,1)S(1)} collective-permute-done((bf16[512,768]{1,0:T(8,128)(2,1)S(1)}, bf16[512,768]{1,0:T(8,128)(2,1)S(1)}, u32[]{:S(2)}, u32[]{:S(2)}) %collective-permute-start.5) | collective-permute-done | bytes 786464 | tf_op jit(solution)/shard_map/ppermute | solution.py:41
  52.8 0.0 collective-permute-done.6.refs_8_.refs_6_
  52.8 0.1 collective-permute-done.2.refs_1_
  52.9 0.0 collective-permute-done.3.refs_2_
  53.0 3.7 %collective-permute-done.4.refs_3_ = bf16[1040,512]{1,0:T(8,128)(2,1)S(1)} collective-permute-done((bf16[1040,512]{1,0:T(8,128)(2,1)S(1)}, bf16[1040,512]{1,0:T(8,128)(2,1)S(1)}, u32[]{:S(2)}, u32[]{:S(2)}) %collective-permute-start.4) | collective-permute-done | bytes 1064992 | tf_op jit(solution)/shard_map/ppermute | solution.py:41
  56.7 2.5 %collective-permute-start.7 = (bf16[512,768]{1,0:T(8,128)(2,1)S(1)}, bf16[512,768]{1,0:T(8,128)(2,1)S(1)}, u32[]{:S(2)}, u32[]{:S(2)}) collective-permute-start(bf16[512,768]{1,0:T(8,128)(2,1)S(1)} %collective-permute-done.1.refs_6_.refs_4_), channel_id=1, source_target_pairs={{0,8},{1,9},{2,10},{3,11},{4,12},{5,13},{6,14},{7,15},{8,0},{9,1},... | collective-permute-start | bytes 2359304 | tf_op jit(solution)/shard_map/ppermute | solution.py:41
  59.1 0.0 collective-permute-start.8
  59.1 0.5 collective-permute-start.9
  59.6 2.7 %collective-permute-start.11 = (bf16[1040,512]{1,0:T(8,128)(2,1)S(1)}, bf16[1040,512]{1,0:T(8,128)(2,1)S(1)}, u32[]{:S(2)}, u32[]{:S(2)}) collective-permute-start(bf16[1040,512]{1,0:T(8,128)(2,1)S(1)} %collective-permute-done.4.refs_3_), channel_id=1, source_target_pairs={{0,3},{1,0},{2,1},{3,2},{4,7},{5,4},{6,5},{7,6},{8,11},{9,8},{10,9... | collective-permute-start | bytes 3194888 | tf_op jit(solution)/shard_map/ppermute | solution.py:41
  62.3 0.0 collective-permute-done.7.refs_1_.refs_4_
  62.3 0.0 collective-permute-done.8.refs_2_.refs_5_
  62.3 1.0 collective-permute-done.9.refs_3_.refs_6_
  63.3 0.0 collective-permute-start.12
  63.3 1.3 collective-permute-start.13
  64.6 21.3 %collective-permute-done.10.refs_4_ = bf16[1040,512]{1,0:T(8,128)(2,1)S(1)} collective-permute-done((bf16[1040,512]{1,0:T(8,128)(2,1)S(1)}, bf16[1040,512]{1,0:T(8,128)(2,1)S(1)}, u32[]{:S(2)}, u32[]{:S(2)}) %collective-permute-start.10) | collective-permute-done | bytes 1064992 | tf_op jit(solution)/shard_map/ppermute | solution.py:41
  86.0 0.0 collective-permute-done.11.refs_5_
  86.0 0.9 collective-permute-start.14
  86.9 0.1 collective-permute-start.15
  87.0 0.0 collective-permute-start.19
  87.0 2.7 %collective-permute-start.20 = (bf16[1040,512]{1,0:T(8,128)(2,1)S(1)}, bf16[1040,512]{1,0:T(8,128)(2,1)S(1)}, u32[]{:S(2)}, u32[]{:S(2)}) collective-permute-start(bf16[1040,512]{1,0:T(8,128)(2,1)S(1)} %collective-permute-done.11.refs_5_), channel_id=1, source_target_pairs={{0,3},{1,0},{2,1},{3,2},{4,7},{5,4},{6,5},{7,6},{8,11},{9,8},{10,9... | collective-permute-start | bytes 3194888 | tf_op jit(solution)/shard_map/ppermute | solution.py:41
  89.6 0.0 collective-permute-start.16
  89.6 0.0 collective-permute-done.14.refs_4_.refs_7_
  89.6 0.3 collective-permute-done.15.refs_8_
  89.9 2.4 %collective-permute-start.17 = (bf16[512,768]{1,0:T(8,128)(2,1)S(1)}, bf16[512,768]{1,0:T(8,128)(2,1)S(1)}, u32[]{:S(2)}, u32[]{:S(2)}) collective-permute-start(bf16[512,768]{1,0:T(8,128)(2,1)S(1)} %collective-permute-done.13.refs_8_), channel_id=1, source_target_pairs={{0,48},{1,49},{2,50},{3,51},{4,52},{5,53},{6,54},{7,55},{8,56},{9,... | collective-permute-start | bytes 2359304 | tf_op jit(solution)/shard_map/ppermute | solution.py:41
  92.3 1.3 collective-permute-start.18
  93.7 4.3 %shard_map.64 = (bf16[8,1040,512]{2,1,0:T(8,128)(2,1)S(1)}, f32[1040,768]{1,0:T(8,128)S(1)}) custom-call(s32[9]{0:T(128)S(1)} %stack.70.where, bf16[1040,512]{1,0:T(8,128)(2,1)S(1)} %pad_maximum_fusion.refs_0_, bf16[1040,512]{1,0:T(8,128)(2,1)S(1)} %collective-permute-done.2.refs_1_, bf16[1040,512]{1,0:T(8,128)(2,1)S(1)} %collective-permute-done.3.refs_2_, ...), custom_call_target="tpu_custom_call" | custom-call | flops 2453667840 | bytes 12582912 | tf_op jit(solution)/shard_map/pallas_call | solution.py:105
  98.0 3.7 %shard_map.65.refs_3_ = f32[1040,768]{1,0:T(8,128)S(1)} custom-call(s32[9]{0:T(128)S(1)} %stack.70.where, bf16[8,1040,512]{2,1,0:T(8,128)(2,1)S(1)} %get-tuple-element.112.refs_0_, bf16[512,768]{1,0:T(8,128)(2,1)S(1)} %collective-permute-done.7.refs_1_.refs_4_, bf16[512,768]{1,0:T(8,128)(2,1)S(1)} %collective-permute-done.8.refs_2_.refs_5_, ...), custom_call_target="tpu_custom_call" | custom-call | flops 2453667840 | bytes 12582912 | tf_op jit(solution)/shard_map/pallas_call | solution.py:123
  101.7 7.2 %collective-permute-done.16.refs_9_ = bf16[512,768]{1,0:T(8,128)(2,1)S(1)} collective-permute-done((bf16[512,768]{1,0:T(8,128)(2,1)S(1)}, bf16[512,768]{1,0:T(8,128)(2,1)S(1)}, u32[]{:S(2)}, u32[]{:S(2)}) %collective-permute-start.16) | collective-permute-done | bytes 786464 | tf_op jit(solution)/shard_map/ppermute | solution.py:41
  108.9 3.9 %collective-permute-done.19.refs_1_ = bf16[1040,512]{1,0:T(8,128)(2,1)S(1)} collective-permute-done((bf16[1040,512]{1,0:T(8,128)(2,1)S(1)}, bf16[1040,512]{1,0:T(8,128)(2,1)S(1)}, u32[]{:S(2)}, u32[]{:S(2)}) %collective-permute-start.19) | collective-permute-done | bytes 1064992 | tf_op jit(solution)/shard_map/ppermute | solution.py:41
  112.8 0.0 collective-permute-done.20.refs_2_
  112.9 0.0 collective-permute-done.17.refs_10_
  112.9 1.3 collective-permute-start.21
  114.2 0.1 collective-permute-start.22
  114.3 0.4 collective-permute-start.23
  114.7 7.7 %shard_map.66 = (f32[1024,256]{1,0:T(8,128)S(1)}, f32[1024,256]{1,0:T(8,128)S(1)}, f32[128,256]{1,0:T(8,128)S(1)}, f32[16,256]{1,0:T(8,128)S(1)}) custom-call(s32[9]{0:T(128)S(1)} %stack.70.where, bf16[8,1040,512]{2,1,0:T(8,128)(2,1)S(1)} %get-tuple-element.112.refs_0_, bf16[1040,512]{1,0:T(8,128)(2,1)S(1)} %collective-permute-done.19.refs_1_, ...), custom_call_target="tpu_custom_call" | custom-call | flops 4089446400 | bytes 12582912 | tf_op jit(solution)/shard_map/pallas_call | solution.py:206
  122.4 7.9 %shard_map.67 = (f32[1024,256]{1,0:T(8,128)S(1)}, f32[1024,256]{1,0:T(8,128)S(1)}, f32[128,256]{1,0:T(8,128)S(1)}, f32[16,256]{1,0:T(8,128)S(1)}) custom-call(s32[9]{0:T(128)S(1)} %stack.70.where, bf16[8,1040,512]{2,1,0:T(8,128)(2,1)S(1)} %get-tuple-element.112.refs_0_, bf16[1040,512]{1,0:T(8,128)(2,1)S(1)} %collective-permute-done.19.refs_1_, ...), custom_call_target="tpu_custom_call" | custom-call | flops 4089446400 | bytes 12582912 | tf_op jit(solution)/shard_map/pallas_call | solution.py:206
  130.3 0.2 collective-permute-start.24
  130.5 1.3 collective-permute-start.25
  131.8 0.7 collective-permute-start.26
  132.5 2.6 %shard_map.68.y0 = f32[1024,256]{1,0:T(8,128)S(1)} custom-call(f32[1024,256]{1,0:T(8,128)S(1)} %get-tuple-element.128.prod_ref, f32[128,256]{1,0:T(8,128)S(1)} %get-tuple-element.129.u_ref, f32[64,256]{1,0:T(8,128)S(1)} %get-tuple-element.119.refs_12_.prm.p0), custom_call_target="tpu_custom_call" | custom-call | flops 16777216 | bytes 12582912 | tf_op jit(solution)/shard_map/pallas_call | solution.py:255
  135.2 0.7 collective-permute-done.26
  135.9 0.1 collective-permute-start.27
  136.0 2.3 %collective-permute-start.28 = (f32[16,512]{1,0:T(8,128)S(1)}, f32[16,512]{1,0:T(8,128)S(1)}, u32[]{:S(2)}, u32[]{:S(2)}) collective-permute-start(f32[16,512]{1,0:T(8,128)S(1)} %get-tuple-element.151), channel_id=1, source_target_pairs={{0,32},{1,33},{2,34},{3,35},{4,36},{5,37},{6,38},{7,39},{8,40},{9,... | collective-permute-start | bytes 98312 | tf_op jit(solution)/shard_map/ppermute | solution.py:41
  138.2 1.8 %collective-permute-start.29 = (f32[16,512]{1,0:T(8,128)S(1)}, f32[16,512]{1,0:T(8,128)S(1)}, u32[]{:S(2)}, u32[]{:S(2)}) collective-permute-start(f32[16,512]{1,0:T(8,128)S(1)} %get-tuple-element.143), channel_id=1, source_target_pairs={{0,48},{1,49},{2,50},{3,51},{4,52},{5,53},{6,54},{7,55},{8,56},{9,... | collective-permute-start | bytes 98312 | tf_op jit(solution)/shard_map/ppermute | solution.py:41
  140.0 2.6 %shard_map.69.y1 = f32[1024,256]{1,0:T(8,128)S(1)} custom-call(f32[1024,256]{1,0:T(8,128)S(1)} %get-tuple-element.131.prod_ref, f32[128,256]{1,0:T(8,128)S(1)} %get-tuple-element.132.u_ref, f32[64,256]{1,0:T(8,128)S(1)} %get-tuple-element.123.refs_12_.prm.p1), custom_call_target="tpu_custom_call" | custom-call | flops 16777216 | bytes 12582912 | tf_op jit(solution)/shard_map/pallas_call | solution.py:255
  142.6 4.2 %shard_map.70 = bf16[1024,512]{1,0:T(8,128)(2,1)} custom-call(s32[1]{0:T(128)} %bitcast.17.core_ref, f32[1024,256]{1,0:T(8,128)S(1)} %shard_map.68.y0, f32[1024,256]{1,0:T(8,128)S(1)} %shard_map.69.y1, f32[1024,256]{1,0:T(8,128)S(1)} %get-tuple-element.133.x0, f32[1024,256]{1,0:T(8,128)S(1)} %get-tuple-element.134.x1, ...), custom_call_target="tpu_custom_call" | custom-call | tf_op jit(solution)/shard_map/pallas_call | solution.py:302
  (26 shorter events, 0.2 us)
Async XLA Ops:
  0.0 4.7 %copy-start = (f32[3,3,4096]{2,1,0:T(4,128)S(1)}, f32[3,3,4096]{2,1,0:T(4,128)}, u32[]{:S(2)}) copy-start(f32[3,3,4096]{2,1,0:T(4,128)} %param.8) | copy-start | bytes 442372
  1.2 5.3 %copy-start.1 = (bf16[1024,512]{1,0:T(8,128)(2,1)S(1)}, bf16[1024,512]{1,0:T(8,128)(2,1)}, u32[]{:S(2)}) copy-start(bf16[1024,512]{1,0:T(8,128)(2,1)} %param.6) | copy-start | bytes 3145732
  2.1 13.5 %collective-permute-start.1 = (bf16[512,768]{1,0:T(8,128)(2,1)}, bf16[512,768]{1,0:T(8,128)(2,1)S(1)}, u32[]{:S(2)}, u32[]{:S(2)}) collective-permute-start(bf16[512,768]{1,0:T(8,128)(2,1)} %pad_maximum_fusion.1), channel_id=1, source_target_pairs={{0,0},{1,16},{2,32},{3,48},{4,64},{5,80},{6,96},{7,112},{8,8},{9,2... | collective-permute-start | bytes 2359304 | tf_op jit(solution)/shard_map/ppermute | solution.py:41
  7.2 7.7 %collective-permute-start = (bf16[16,512]{1,0:T(8,128)(2,1)}, bf16[16,512]{1,0:T(8,128)(2,1)}, u32[]{:S(2)}, u32[]{:S(2)}) collective-permute-start(bf16[16,512]{1,0:T(8,128)(2,1)} %slice.36), channel_id=1, source_target_pairs={{0,8},{1,9},{2,10},{3,11},{4,12},{5,13},{6,14},{7,15},{8,16},{9,17... | collective-permute-start | bytes 49160 | tf_op jit(solution)/shard_map/ppermute | solution.py:41
  15.6 37.3 %collective-permute-start.2 = (bf16[1040,512]{1,0:T(8,128)(2,1)S(1)}, bf16[1040,512]{1,0:T(8,128)(2,1)S(1)}, u32[]{:S(2)}, u32[]{:S(2)}) collective-permute-start(bf16[1040,512]{1,0:T(8,128)(2,1)S(1)} %pad_maximum_fusion.refs_0_), channel_id=1, source_target_pairs={{0,1},{1,2},{2,3},{3,0},{4,5},{5,6},{6,7},{7,4},{8,9},{9,10},{10,1... | collective-permute-start | bytes 3194888 | tf_op jit(solution)/shard_map/ppermute | solution.py:41
  27.5 25.4 %collective-permute-start.3 = (bf16[1040,512]{1,0:T(8,128)(2,1)S(1)}, bf16[1040,512]{1,0:T(8,128)(2,1)S(1)}, u32[]{:S(2)}, u32[]{:S(2)}) collective-permute-start(bf16[1040,512]{1,0:T(8,128)(2,1)S(1)} %pad_maximum_fusion.refs_0_), channel_id=1, source_target_pairs={{0,3},{1,0},{2,1},{3,2},{4,7},{5,4},{6,5},{7,6},{8,11},{9,8},{10,9... | collective-permute-start | bytes 3194888 | tf_op jit(solution)/shard_map/ppermute | solution.py:41
  30.9 25.8 %collective-permute-start.4 = (bf16[1040,512]{1,0:T(8,128)(2,1)S(1)}, bf16[1040,512]{1,0:T(8,128)(2,1)S(1)}, u32[]{:S(2)}, u32[]{:S(2)}) collective-permute-start(bf16[1040,512]{1,0:T(8,128)(2,1)S(1)} %pad_maximum_fusion.refs_0_), channel_id=1, source_target_pairs={{0,4},{1,5},{2,6},{3,7},{4,0},{5,1},{6,2},{7,3},{8,12},{9,13},{10,... | collective-permute-start | bytes 3194888 | tf_op jit(solution)/shard_map/ppermute | solution.py:41
  34.7 18.1 %collective-permute-start.5 = (bf16[512,768]{1,0:T(8,128)(2,1)S(1)}, bf16[512,768]{1,0:T(8,128)(2,1)S(1)}, u32[]{:S(2)}, u32[]{:S(2)}) collective-permute-start(bf16[512,768]{1,0:T(8,128)(2,1)S(1)} %collective-permute-done.1.refs_6_.refs_4_), channel_id=1, source_target_pairs={{0,16},{1,17},{2,18},{3,19},{4,20},{5,21},{6,22},{7,23},{8,24},{9,... | collective-permute-start | bytes 2359304 | tf_op jit(solution)/shard_map/ppermute | solution.py:41
  34.7 18.1 %collective-permute-start.6 = (bf16[512,768]{1,0:T(8,128)(2,1)S(1)}, bf16[512,768]{1,0:T(8,128)(2,1)S(1)}, u32[]{:S(2)}, u32[]{:S(2)}) collective-permute-start(bf16[512,768]{1,0:T(8,128)(2,1)S(1)} %collective-permute-done.1.refs_6_.refs_4_), channel_id=1, source_target_pairs={{0,48},{1,49},{2,50},{3,51},{4,52},{5,53},{6,54},{7,55},{8,56},{9,... | collective-permute-start | bytes 2359304 | tf_op jit(solution)/shard_map/ppermute | solution.py:41
  56.7 5.7 %collective-permute-start.7 = (bf16[512,768]{1,0:T(8,128)(2,1)S(1)}, bf16[512,768]{1,0:T(8,128)(2,1)S(1)}, u32[]{:S(2)}, u32[]{:S(2)}) collective-permute-start(bf16[512,768]{1,0:T(8,128)(2,1)S(1)} %collective-permute-done.1.refs_6_.refs_4_), channel_id=1, source_target_pairs={{0,8},{1,9},{2,10},{3,11},{4,12},{5,13},{6,14},{7,15},{8,0},{9,1},... | collective-permute-start | bytes 2359304 | tf_op jit(solution)/shard_map/ppermute | solution.py:41
  59.1 3.2 %collective-permute-start.8 = (bf16[512,768]{1,0:T(8,128)(2,1)S(1)}, bf16[512,768]{1,0:T(8,128)(2,1)S(1)}, u32[]{:S(2)}, u32[]{:S(2)}) collective-permute-start(bf16[512,768]{1,0:T(8,128)(2,1)S(1)} %collective-permute-done.5.refs_7_.refs_5_), channel_id=1, source_target_pairs={{0,8},{1,9},{2,10},{3,11},{4,12},{5,13},{6,14},{7,15},{8,0},{9,1},... | collective-permute-start | bytes 2359304 | tf_op jit(solution)/shard_map/ppermute | solution.py:41
  59.1 4.2 %collective-permute-start.9 = (bf16[512,768]{1,0:T(8,128)(2,1)S(1)}, bf16[512,768]{1,0:T(8,128)(2,1)S(1)}, u32[]{:S(2)}, u32[]{:S(2)}) collective-permute-start(bf16[512,768]{1,0:T(8,128)(2,1)S(1)} %collective-permute-done.6.refs_8_.refs_6_), channel_id=1, source_target_pairs={{0,8},{1,9},{2,10},{3,11},{4,12},{5,13},{6,14},{7,15},{8,0},{9,1},... | collective-permute-start | bytes 2359304 | tf_op jit(solution)/shard_map/ppermute | solution.py:41
  59.6 26.4 %collective-permute-start.10 = (bf16[1040,512]{1,0:T(8,128)(2,1)S(1)}, bf16[1040,512]{1,0:T(8,128)(2,1)S(1)}, u32[]{:S(2)}, u32[]{:S(2)}) collective-permute-start(bf16[1040,512]{1,0:T(8,128)(2,1)S(1)} %collective-permute-done.4.refs_3_), channel_id=1, source_target_pairs={{0,1},{1,2},{2,3},{3,0},{4,5},{5,6},{6,7},{7,4},{8,9},{9,10},{10,1... | collective-permute-start | bytes 3194888 | tf_op jit(solution)/shard_map/ppermute | solution.py:41
  59.6 26.4 %collective-permute-start.11 = (bf16[1040,512]{1,0:T(8,128)(2,1)S(1)}, bf16[1040,512]{1,0:T(8,128)(2,1)S(1)}, u32[]{:S(2)}, u32[]{:S(2)}) collective-permute-start(bf16[1040,512]{1,0:T(8,128)(2,1)S(1)} %collective-permute-done.4.refs_3_), channel_id=1, source_target_pairs={{0,3},{1,0},{2,1},{3,2},{4,7},{5,4},{6,5},{7,6},{8,11},{9,8},{10,9... | collective-permute-start | bytes 3194888 | tf_op jit(solution)/shard_map/ppermute | solution.py:41
  63.3 22.7 %collective-permute-start.12 = (bf16[512,768]{1,0:T(8,128)(2,1)S(1)}, bf16[512,768]{1,0:T(8,128)(2,1)S(1)}, u32[]{:S(2)}, u32[]{:S(2)}) collective-permute-start(bf16[512,768]{1,0:T(8,128)(2,1)S(1)} %collective-permute-done.5.refs_7_.refs_5_), channel_id=1, source_target_pairs={{0,16},{1,17},{2,18},{3,19},{4,20},{5,21},{6,22},{7,23},{8,24},{9,... | collective-permute-start | bytes 2359304 | tf_op jit(solution)/shard_map/ppermute | solution.py:41
  63.3 22.7 %collective-permute-start.13 = (bf16[512,768]{1,0:T(8,128)(2,1)S(1)}, bf16[512,768]{1,0:T(8,128)(2,1)S(1)}, u32[]{:S(2)}, u32[]{:S(2)}) collective-permute-start(bf16[512,768]{1,0:T(8,128)(2,1)S(1)} %collective-permute-done.1.refs_6_.refs_4_), channel_id=1, source_target_pairs={{0,64},{1,65},{2,66},{3,67},{4,68},{5,69},{6,70},{7,71},{8,72},{9,... | collective-permute-start | bytes 2359304 | tf_op jit(solution)/shard_map/ppermute | solution.py:41
  86.0 3.6 %collective-permute-start.14 = (bf16[512,768]{1,0:T(8,128)(2,1)S(1)}, bf16[512,768]{1,0:T(8,128)(2,1)S(1)}, u32[]{:S(2)}, u32[]{:S(2)}) collective-permute-start(bf16[512,768]{1,0:T(8,128)(2,1)S(1)} %collective-permute-done.12.refs_9_.refs_7_), channel_id=1, source_target_pairs={{0,8},{1,9},{2,10},{3,11},{4,12},{5,13},{6,14},{7,15},{8,0},{9,1},... | collective-permute-start | bytes 2359304 | tf_op jit(solution)/shard_map/ppermute | solution.py:41
  86.9 3.0 %collective-permute-start.15 = (bf16[512,768]{1,0:T(8,128)(2,1)S(1)}, bf16[512,768]{1,0:T(8,128)(2,1)S(1)}, u32[]{:S(2)}, u32[]{:S(2)}) collective-permute-start(bf16[512,768]{1,0:T(8,128)(2,1)S(1)} %collective-permute-done.13.refs_8_), channel_id=1, source_target_pairs={{0,8},{1,9},{2,10},{3,11},{4,12},{5,13},{6,14},{7,15},{8,0},{9,1},... | collective-permute-start | bytes 2359304 | tf_op jit(solution)/shard_map/ppermute | solution.py:41
  87.0 25.9 %collective-permute-start.19 = (bf16[1040,512]{1,0:T(8,128)(2,1)S(1)}, bf16[1040,512]{1,0:T(8,128)(2,1)S(1)}, u32[]{:S(2)}, u32[]{:S(2)}) collective-permute-start(bf16[1040,512]{1,0:T(8,128)(2,1)S(1)} %collective-permute-done.2.refs_1_), channel_id=1, source_target_pairs={{0,1},{1,2},{2,3},{3,0},{4,5},{5,6},{6,7},{7,4},{8,9},{9,10},{10,1... | collective-permute-start | bytes 3194888 | tf_op jit(solution)/shard_map/ppermute | solution.py:41
  87.0 25.9 %collective-permute-start.20 = (bf16[1040,512]{1,0:T(8,128)(2,1)S(1)}, bf16[1040,512]{1,0:T(8,128)(2,1)S(1)}, u32[]{:S(2)}, u32[]{:S(2)}) collective-permute-start(bf16[1040,512]{1,0:T(8,128)(2,1)S(1)} %collective-permute-done.11.refs_5_), channel_id=1, source_target_pairs={{0,3},{1,0},{2,1},{3,2},{4,7},{5,4},{6,5},{7,6},{8,11},{9,8},{10,9... | collective-permute-start | bytes 3194888 | tf_op jit(solution)/shard_map/ppermute | solution.py:41
  89.6 19.3 %collective-permute-start.16 = (bf16[512,768]{1,0:T(8,128)(2,1)S(1)}, bf16[512,768]{1,0:T(8,128)(2,1)S(1)}, u32[]{:S(2)}, u32[]{:S(2)}) collective-permute-start(bf16[512,768]{1,0:T(8,128)(2,1)S(1)} %collective-permute-done.13.refs_8_), channel_id=1, source_target_pairs={{0,16},{1,17},{2,18},{3,19},{4,20},{5,21},{6,22},{7,23},{8,24},{9,... | collective-permute-start | bytes 2359304 | tf_op jit(solution)/shard_map/ppermute | solution.py:41
  89.9 22.9 %collective-permute-start.17 = (bf16[512,768]{1,0:T(8,128)(2,1)S(1)}, bf16[512,768]{1,0:T(8,128)(2,1)S(1)}, u32[]{:S(2)}, u32[]{:S(2)}) collective-permute-start(bf16[512,768]{1,0:T(8,128)(2,1)S(1)} %collective-permute-done.13.refs_8_), channel_id=1, source_target_pairs={{0,48},{1,49},{2,50},{3,51},{4,52},{5,53},{6,54},{7,55},{8,56},{9,... | collective-permute-start | bytes 2359304 | tf_op jit(solution)/shard_map/ppermute | solution.py:41
  92.3 20.5 %collective-permute-start.18 = (bf16[512,768]{1,0:T(8,128)(2,1)S(1)}, bf16[512,768]{1,0:T(8,128)(2,1)S(1)}, u32[]{:S(2)}, u32[]{:S(2)}) collective-permute-start(bf16[512,768]{1,0:T(8,128)(2,1)S(1)} %collective-permute-done.12.refs_9_.refs_7_), channel_id=1, source_target_pairs={{0,64},{1,65},{2,66},{3,67},{4,68},{5,69},{6,70},{7,71},{8,72},{9,... | collective-permute-start | bytes 2359304 | tf_op jit(solution)/shard_map/ppermute | solution.py:41
  112.9 9.5 %collective-permute-start.21 = (bf16[512,768]{1,0:T(8,128)(2,1)S(1)}, bf16[512,768]{1,0:T(8,128)(2,1)S(1)}, u32[]{:S(2)}, u32[]{:S(2)}) collective-permute-start(bf16[512,768]{1,0:T(8,128)(2,1)S(1)} %collective-permute-done.16.refs_9_), channel_id=1, source_target_pairs={{0,8},{1,9},{2,10},{3,11},{4,12},{5,13},{6,14},{7,15},{8,0},{9,1},... | collective-permute-start | bytes 2359304 | tf_op jit(solution)/shard_map/ppermute | solution.py:41
  114.2 8.2 %collective-permute-start.22 = (bf16[512,768]{1,0:T(8,128)(2,1)S(1)}, bf16[512,768]{1,0:T(8,128)(2,1)S(1)}, u32[]{:S(2)}, u32[]{:S(2)}) collective-permute-start(bf16[512,768]{1,0:T(8,128)(2,1)S(1)} %collective-permute-done.17.refs_10_), channel_id=1, source_target_pairs={{0,8},{1,9},{2,10},{3,11},{4,12},{5,13},{6,14},{7,15},{8,0},{9,1},... | collective-permute-start | bytes 2359304 | tf_op jit(solution)/shard_map/ppermute | solution.py:41
  114.3 8.1 %collective-permute-start.23 = (bf16[512,768]{1,0:T(8,128)(2,1)S(1)}, bf16[512,768]{1,0:T(8,128)(2,1)S(1)}, u32[]{:S(2)}, u32[]{:S(2)}) collective-permute-start(bf16[512,768]{1,0:T(8,128)(2,1)S(1)} %collective-permute-done.18.refs_11_), channel_id=1, source_target_pairs={{0,8},{1,9},{2,10},{3,11},{4,12},{5,13},{6,14},{7,15},{8,0},{9,1},... | collective-permute-start | bytes 2359304 | tf_op jit(solution)/shard_map/ppermute | solution.py:41
  130.3 4.8 %collective-permute-start.24 = (f32[16,512]{1,0:T(8,128)S(1)}, f32[16,512]{1,0:T(8,128)S(1)}, u32[]{:S(2)}, u32[]{:S(2)}) collective-permute-start(f32[16,512]{1,0:T(8,128)S(1)} %pad_maximum_fusion.4), channel_id=1, source_target_pairs={{0,8},{1,9},{2,10},{3,11},{4,12},{5,13},{6,14},{7,15},{8,0},{9,1},... | collective-permute-start | bytes 98312 | tf_op jit(solution)/shard_map/ppermute | solution.py:41
  130.5 4.7 %collective-permute-start.25 = (f32[16,512]{1,0:T(8,128)S(1)}, f32[16,512]{1,0:T(8,128)S(1)}, u32[]{:S(2)}, u32[]{:S(2)}) collective-permute-start(f32[16,512]{1,0:T(8,128)S(1)} %pad_maximum_fusion.4), channel_id=1, source_target_pairs={{0,64},{1,65},{2,66},{3,67},{4,68},{5,69},{6,70},{7,71},{8,72},{9,... | collective-permute-start | bytes 98312 | tf_op jit(solution)/shard_map/ppermute | solution.py:41
  131.8 4.0 %collective-permute-start.26 = (f32[16,512]{1,0:T(8,128)S(1)}, f32[16,512]{1,0:T(8,128)S(1)}, u32[]{:S(2)}, u32[]{:S(2)}) collective-permute-start(f32[16,512]{1,0:T(8,128)S(1)} %pad_maximum_fusion.4), channel_id=1, source_target_pairs={{0,72},{1,73},{2,74},{3,75},{4,76},{5,77},{6,78},{7,79},{8,64},{9,... | collective-permute-start | bytes 98312 | tf_op jit(solution)/shard_map/ppermute | solution.py:41
  135.9 6.7 %collective-permute-start.27 = (f32[16,512]{1,0:T(8,128)S(1)}, f32[16,512]{1,0:T(8,128)S(1)}, u32[]{:S(2)}, u32[]{:S(2)}) collective-permute-start(f32[16,512]{1,0:T(8,128)S(1)} %get-tuple-element.152), channel_id=1, source_target_pairs={{0,16},{1,17},{2,18},{3,19},{4,20},{5,21},{6,22},{7,23},{8,24},{9,... | collective-permute-start | bytes 98312 | tf_op jit(solution)/shard_map/ppermute | solution.py:41
  136.0 6.7 %collective-permute-start.28 = (f32[16,512]{1,0:T(8,128)S(1)}, f32[16,512]{1,0:T(8,128)S(1)}, u32[]{:S(2)}, u32[]{:S(2)}) collective-permute-start(f32[16,512]{1,0:T(8,128)S(1)} %get-tuple-element.151), channel_id=1, source_target_pairs={{0,32},{1,33},{2,34},{3,35},{4,36},{5,37},{6,38},{7,39},{8,40},{9,... | collective-permute-start | bytes 98312 | tf_op jit(solution)/shard_map/ppermute | solution.py:41
  138.2 4.4 %collective-permute-start.29 = (f32[16,512]{1,0:T(8,128)S(1)}, f32[16,512]{1,0:T(8,128)S(1)}, u32[]{:S(2)}, u32[]{:S(2)}) collective-permute-start(f32[16,512]{1,0:T(8,128)S(1)} %get-tuple-element.143), channel_id=1, source_target_pairs={{0,48},{1,49},{2,50},{3,51},{4,52},{5,53},{6,54},{7,55},{8,56},{9,... | collective-permute-start | bytes 98312 | tf_op jit(solution)/shard_map/ppermute | solution.py:41

commit v8 on v7

--- a/solution.py
+++ b/solution.py
@@ -132,22 +132,57 @@
     )(where, lhs, *weights)
 
 
-def project_kernel(rows, where, *refs):
+def more_kernel(where, lhs, part, *refs):
+    weights, acc = refs[:4], refs[4]
+    is_near = [lax.rem(where[4 + k], 4) != 3 for k in range(4)]
+
+    def product(k):
+        return jnp.dot(lhs[where[4 + k]], weights[k][...], preferred_element_type=F32)
+
+    def start(k):
+        acc[...] = part[...] + product(k)
+
+    def add(k):
+        acc[...] += product(k)
+
+    pl.when(is_near[0])(functools.partial(start, 0))
+    pl.when(jnp.logical_not(is_near[0]))(functools.partial(start, 1))
+    pl.when(jnp.logical_and(is_near[0], is_near[1]))(functools.partial(add, 1))
+    pl.when(is_near[2])(functools.partial(add, 2))
+    pl.when(is_near[3])(functools.partial(add, 3))
+
+
+def more(where, lhs, part, weights, rows):
+    vmem = pl.BlockSpec(memory_space=pltpu.VMEM)
+    tall, width = rows + HALO, weights[0].shape[1]
+    return pl.pallas_call(
+        more_kernel,
+        out_shape=jax.ShapeDtypeStruct((tall, width), F32),
+        in_specs=[pl.BlockSpec(memory_space=pltpu.SMEM)] + [vmem] * 6,
+        out_specs=vmem,
+        compiler_params=pltpu.CompilerParams(vmem_limit_bytes=26 << 20),
+        cost_estimate=pl.CostEstimate(
+            flops=2 * tall * 3 * BLOCK * width, bytes_accessed=12 << 20, transcendentals=0
+        ),
+    )(where, lhs, part, *weights)
+
+
+def project_kernel(rows, few, where, *refs):
     lhs, near, far, part, *refs = refs
     weights, refs = refs[:8], refs[8:]
-    prm, prod_ref, x1_ref, u_ref, end_ref, last, wfar, proj = refs
+    prm, prod_ref, x1_ref, u_ref, end_ref, last, late, proj = refs
     seg_len = rows // SEG
     for k in range(8):
-        at = pl.ds(max(k - 3, 0) * BLOCK, BLOCK)
+        at = pl.ds((k // 4 if few else max(k - 3, 0)) * BLOCK, BLOCK)
         for s, ref in ((3, near), (7, far)):
 
             @pl.when(where[k] == s)
             def _(k=k, ref=ref, at=at):
                 last[:, at] = ref[...]
-                if k < 4:
-                    wfar[...] = weights[k][...]
-
-        if k >= 4:
+                if few or k < 4:
+                    late[at, :] = weights[k][...]
+
+        if k >= 4 and not few:
 
             @pl.when(lax.rem(where[k], 4) != 3)
             def _(k=k, at=at):
@@ -155,7 +190,7 @@
 
     for n in range(3):
         cols = pl.ds(n * 2 * LANES, 2 * LANES)
-        right = jnp.concatenate([w[:, cols] for w in (wfar, *weights[4:])], axis=0)
+        right = jnp.concatenate([w[:, cols] for w in ((late,) if few else (late, *weights[4:]))], axis=0)
         out = part[:, cols] + jnp.dot(last[...], right, preferred_element_type=F32)
         out = out.astype(jnp.bfloat16).astype(F32)
         for q in range(2):
@@ -200,11 +235,11 @@
             end_ref[pl.ds(k, 1), lanes] = u[SEG - 1:]
 
 
-def project(where, lhs, near, far, part, weights, prm, rows):
+def project(few, where, lhs, near, far, part, weights, prm, rows):
     vmem = pl.BlockSpec(memory_space=pltpu.VMEM)
     wide, tall = 2 * LANES, rows + HALO
     return pl.pallas_call(
-        functools.partial(project_kernel, rows),
+        functools.partial(project_kernel, rows, few),
         out_shape=[
             jax.ShapeDtypeStruct((rows, wide), F32),
             jax.ShapeDtypeStruct((rows, wide), F32),
@@ -214,8 +249,8 @@
         in_specs=[pl.BlockSpec(memory_space=pltpu.SMEM)] + [vmem] * 13,
         out_specs=[vmem] * 4,
         scratch_shapes=[
-            pltpu.VMEM((tall, 5 * BLOCK), jnp.bfloat16),
-            pltpu.VMEM((BLOCK, 3 * wide), jnp.bfloat16),
+            pltpu.VMEM((tall, (2 if few else 5) * BLOCK), jnp.bfloat16),
+            pltpu.VMEM(((2 if few else 1) * BLOCK, 3 * wide), jnp.bfloat16),
             pltpu.VMEM((6, tall, LANES), F32),
         ],
         compiler_params=pltpu.CompilerParams(vmem_limit_bytes=26 << 20),
@@ -293,7 +328,7 @@
                 )
                 return [c * d for c, d in zip(carried, decay)]
 
-            lax.fori_loop(0, seg_len, step, carried, unroll=4)
+            lax.fori_loop(0, seg_len, step, carried, unroll=8)
             out_ref[:, to] = wide[...].astype(out_ref.dtype)
 
 
@@ -377,6 +412,7 @@
     am, af = along_x(a, -1), other_ylo(bf)
     lhs, part = begin(where, [t, tp_, tm, ty, typ, tym], [b, bp, bm, bf], rows)
     part_too = also(where, lhs, [cb, cbp, cbm, cbf], rows)
+    part = more(where, lhs, part, [a, ap, am, af], rows)
     lhs, part, part_too, ap, am, af, tf, tyf = together(
         (lhs, part, part_too, ap, am, af, tf, tyf)
     )
@@ -385,7 +421,7 @@
 
     products, xs, us, ends = [], [], [], []
     for o, (weights, done) in enumerate(((mine, part), (theirs, part_too))):
-        product, x1, u, end = project(where, lhs, tf, tyf, done, weights, prms[o], rows)
+        product, x1, u, end = project(o == 0, where, lhs, tf, tyf, done, weights, prms[o], rows)
         products.append(product)
         xs.append(x1)
         us.append(u)

time: 147 us -> 145 us (0.986)
  waiting for transfers between devices: 53.8 us -> 50.8 us
    ppermute x30, waiting for transfers between devices: 53.8 us -> 50.8 us  [send(): return lax.ppermute(value, ('ctx', 'tp'), route(move))]
    pallas_call x2 -> x3, Pallas kernels: 15.5 us -> 16.4 us  [the longest x2 12.9 us: project(): pl.pallas_call(functools.partial(project_kernel, rows, few), out_shape=[j...]
  transfers between devices with their start and end apart: 30 -> 30, of which waited for: 10 -> 10; matrix products, arithmetic and copies ran while one was open for 3% -> 3% of each run, Pallas kernels for 14% -> 15%
where the time goes in v8:
time: 145 us; the launch traced here: 144 us
  starting transfers between devices  52.7 us (36%)
  waiting for transfers between devices  50.8 us (35%)
  Pallas kernels  33.6 us (23%)
  other arithmetic  3.38 us (2%)
  local copies, waits for them, and re-layouts  3.34 us (2%)
    ppermute x30, starting transfers between devices, send(): return lax.ppermute(value, ('ctx', 'tp'), route(move))  52.7 us
    ppermute x30, waiting for transfers between devices, send(): return lax.ppermute(value, ('ctx', 'tp'), route(move))  50.8 us
    pallas_call x2, Pallas kernels, project(): pl.pallas_call(functools.partial(project_kernel, rows, few), out_shape=[j...  12.9 us
    pallas_call x2, Pallas kernels, read(): pl.pallas_call(functools.partial(read_kernel, rows), out_shape=jax.ShapeD...  5.19 us
    pallas_call x1, Pallas kernels, begin(): pl.pallas_call(begin_kernel, out_shape=[jax.ShapeDtypeStruct((8, tall, BL...  4.32 us
    pallas_call x1, Pallas kernels, gate(): pl.pallas_call(functools.partial(gate_kernel, rows), out_shape=jax.ShapeD...  3.96 us
    pallas_call x1, Pallas kernels, also(): pl.pallas_call(also_kernel, out_shape=jax.ShapeDtypeStruct((tall, width),...  3.72 us
    pallas_call x1, Pallas kernels, more(): pl.pallas_call(more_kernel, out_shape=jax.ShapeDtypeStruct((tall, width),...  3.54 us
  transfers between devices with their start and end apart: 30, of which 10 were waited for; matrix products, arithmetic and copies ran while one was open for 3% of the time, Pallas kernels for 15%

profile of v8, /device:TPU:1, one launch (start us, length us, event | category | flops | bytes accessed | tf_op | source)
XLA Modules:
  0.0 144.5 jit_solution(15474795600668152303)
XLA Ops:
  0.0 1.2 slice_bitcast_fusion.2
  1.2 0.0 copy-start.1
  1.2 0.9 pad_maximum_fusion.1
  2.1 1.8 %collective-permute-start.1 = (bf16[512,768]{1,0:T(8,128)(2,1)}, bf16[512,768]{1,0:T(8,128)(2,1)S(1)}, u32[]{:S(2)}, u32[]{:S(2)}) collective-permute-start(bf16[512,768]{1,0:T(8,128)(2,1)} %pad_maximum_fusion.1), channel_id=1, source_target_pairs={{0,0},{1,16},{2,32},{3,48},{4,64},{5,80},{6,96},{7,112},{8,8},{9,2... | collective-permute-start | bytes 2359304 | tf_op jit(solution)/shard_map/ppermute | solution.py:41
  3.9 0.8 select_bitcast_fusion.3
  4.9 0.8 dynamic_slice.21
  5.6 0.8 select_bitcast_fusion.2
  6.5 0.6 slice.36
  7.2 6.6 %collective-permute-start = (bf16[16,512]{1,0:T(8,128)(2,1)}, bf16[16,512]{1,0:T(8,128)(2,1)}, u32[]{:S(2)}, u32[]{:S(2)}) collective-permute-start(bf16[16,512]{1,0:T(8,128)(2,1)} %slice.36), channel_id=1, source_target_pairs={{0,8},{1,9},{2,10},{3,11},{4,12},{5,13},{6,14},{7,15},{8,16},{9,17... | collective-permute-start | bytes 49160 | tf_op jit(solution)/shard_map/ppermute | solution.py:41
  14.0 0.6 copy.9
  14.6 0.1 stack.70.where
  14.7 0.1 collective-permute-done
  14.8 0.8 pad_maximum_fusion.refs_0_
  15.6 0.0 collective-permute-done.1.refs_6_.refs_4_
  15.6 11.9 %collective-permute-start.2 = (bf16[1040,512]{1,0:T(8,128)(2,1)S(1)}, bf16[1040,512]{1,0:T(8,128)(2,1)S(1)}, u32[]{:S(2)}, u32[]{:S(2)}) collective-permute-start(bf16[1040,512]{1,0:T(8,128)(2,1)S(1)} %pad_maximum_fusion.refs_0_), channel_id=1, source_target_pairs={{0,1},{1,2},{2,3},{3,0},{4,5},{5,6},{6,7},{7,4},{8,9},{9,10},{10,1... | collective-permute-start | bytes 3194888 | tf_op jit(solution)/shard_map/ppermute | solution.py:41
  27.5 3.3 %collective-permute-start.3 = (bf16[1040,512]{1,0:T(8,128)(2,1)S(1)}, bf16[1040,512]{1,0:T(8,128)(2,1)S(1)}, u32[]{:S(2)}, u32[]{:S(2)}) collective-permute-start(bf16[1040,512]{1,0:T(8,128)(2,1)S(1)} %pad_maximum_fusion.refs_0_), channel_id=1, source_target_pairs={{0,3},{1,0},{2,1},{3,2},{4,7},{5,4},{6,5},{7,6},{8,11},{9,8},{10,9... | collective-permute-start | bytes 3194888 | tf_op jit(solution)/shard_map/ppermute | solution.py:41
  30.9 3.8 %collective-permute-start.4 = (bf16[1040,512]{1,0:T(8,128)(2,1)S(1)}, bf16[1040,512]{1,0:T(8,128)(2,1)S(1)}, u32[]{:S(2)}, u32[]{:S(2)}) collective-permute-start(bf16[1040,512]{1,0:T(8,128)(2,1)S(1)} %pad_maximum_fusion.refs_0_), channel_id=1, source_target_pairs={{0,4},{1,5},{2,6},{3,7},{4,0},{5,1},{6,2},{7,3},{8,12},{9,13},{10,... | collective-permute-start | bytes 3194888 | tf_op jit(solution)/shard_map/ppermute | solution.py:41
  34.7 2.7 %collective-permute-start.6 = (bf16[512,768]{1,0:T(8,128)(2,1)S(1)}, bf16[512,768]{1,0:T(8,128)(2,1)S(1)}, u32[]{:S(2)}, u32[]{:S(2)}) collective-permute-start(bf16[512,768]{1,0:T(8,128)(2,1)S(1)} %collective-permute-done.1.refs_6_.refs_4_), channel_id=1, source_target_pairs={{0,48},{1,49},{2,50},{3,51},{4,52},{5,53},{6,54},{7,55},{8,56},{9,... | collective-permute-start | bytes 2359304 | tf_op jit(solution)/shard_map/ppermute | solution.py:41
  37.3 15.5 %collective-permute-done.5.refs_7_.refs_5_ = bf16[512,768]{1,0:T(8,128)(2,1)S(1)} collective-permute-done((bf16[512,768]{1,0:T(8,128)(2,1)S(1)}, bf16[512,768]{1,0:T(8,128)(2,1)S(1)}, u32[]{:S(2)}, u32[]{:S(2)}) %collective-permute-start.5) | collective-permute-done | bytes 786464 | tf_op jit(solution)/shard_map/ppermute | solution.py:41
  52.8 0.0 collective-permute-done.6.refs_8_.refs_6_
  52.8 0.1 collective-permute-done.2.refs_1_
  52.9 0.0 collective-permute-done.3.refs_2_
  53.0 3.7 %collective-permute-done.4.refs_3_ = bf16[1040,512]{1,0:T(8,128)(2,1)S(1)} collective-permute-done((bf16[1040,512]{1,0:T(8,128)(2,1)S(1)}, bf16[1040,512]{1,0:T(8,128)(2,1)S(1)}, u32[]{:S(2)}, u32[]{:S(2)}) %collective-permute-start.4) | collective-permute-done | bytes 1064992 | tf_op jit(solution)/shard_map/ppermute | solution.py:41
  56.7 2.5 %collective-permute-start.7 = (bf16[512,768]{1,0:T(8,128)(2,1)S(1)}, bf16[512,768]{1,0:T(8,128)(2,1)S(1)}, u32[]{:S(2)}, u32[]{:S(2)}) collective-permute-start(bf16[512,768]{1,0:T(8,128)(2,1)S(1)} %collective-permute-done.1.refs_6_.refs_4_), channel_id=1, source_target_pairs={{0,8},{1,9},{2,10},{3,11},{4,12},{5,13},{6,14},{7,15},{8,0},{9,1},... | collective-permute-start | bytes 2359304 | tf_op jit(solution)/shard_map/ppermute | solution.py:41
  59.1 0.0 collective-permute-start.8
  59.1 0.5 collective-permute-start.9
  59.6 0.0 collective-permute-start.10
  59.6 2.7 %collective-permute-start.11 = (bf16[1040,512]{1,0:T(8,128)(2,1)S(1)}, bf16[1040,512]{1,0:T(8,128)(2,1)S(1)}, u32[]{:S(2)}, u32[]{:S(2)}) collective-permute-start(bf16[1040,512]{1,0:T(8,128)(2,1)S(1)} %collective-permute-done.4.refs_3_), channel_id=1, source_target_pairs={{0,3},{1,0},{2,1},{3,2},{4,7},{5,4},{6,5},{7,6},{8,11},{9,8},{10,9... | collective-permute-start | bytes 3194888 | tf_op jit(solution)/shard_map/ppermute | solution.py:41
  62.3 0.0 collective-permute-done.7.refs_1_.refs_4_
  62.3 0.0 collective-permute-done.8.refs_2_.refs_5_
  62.3 1.0 collective-permute-done.9.refs_3_.refs_6_
  63.3 1.3 collective-permute-start.13
  64.6 21.3 %collective-permute-done.10.refs_4_ = bf16[1040,512]{1,0:T(8,128)(2,1)S(1)} collective-permute-done((bf16[1040,512]{1,0:T(8,128)(2,1)S(1)}, bf16[1040,512]{1,0:T(8,128)(2,1)S(1)}, u32[]{:S(2)}, u32[]{:S(2)}) %collective-permute-start.10) | collective-permute-done | bytes 1064992 | tf_op jit(solution)/shard_map/ppermute | solution.py:41
  86.0 0.0 collective-permute-done.11.refs_5_
  86.0 0.0 collective-permute-done.12.refs_9_.refs_7_
  86.0 0.0 collective-permute-done.13.refs_0_.refs_8_
  86.0 0.9 collective-permute-start.14
  86.9 0.1 collective-permute-start.15
  87.0 0.0 collective-permute-start.19
  87.0 2.7 %collective-permute-start.20 = (bf16[1040,512]{1,0:T(8,128)(2,1)S(1)}, bf16[1040,512]{1,0:T(8,128)(2,1)S(1)}, u32[]{:S(2)}, u32[]{:S(2)}) collective-permute-start(bf16[1040,512]{1,0:T(8,128)(2,1)S(1)} %collective-permute-done.11.refs_5_), channel_id=1, source_target_pairs={{0,3},{1,0},{2,1},{3,2},{4,7},{5,4},{6,5},{7,6},{8,11},{9,8},{10,9... | collective-permute-start | bytes 3194888 | tf_op jit(solution)/shard_map/ppermute | solution.py:41
  89.6 0.3 collective-permute-done.15.refs_8_
  89.9 2.4 %collective-permute-start.17 = (bf16[512,768]{1,0:T(8,128)(2,1)S(1)}, bf16[512,768]{1,0:T(8,128)(2,1)S(1)}, u32[]{:S(2)}, u32[]{:S(2)}) collective-permute-start(bf16[512,768]{1,0:T(8,128)(2,1)S(1)} %collective-permute-done.13.refs_0_.refs_8_), channel_id=1, source_target_pairs={{0,48},{1,49},{2,50},{3,51},{4,52},{5,53},{6,54},{7,55},{8,56},{9,... | collective-permute-start | bytes 2359304 | tf_op jit(solution)/shard_map/ppermute | solution.py:41
  92.3 1.3 collective-permute-start.18
  93.7 4.3 %shard_map.64 = (bf16[8,1040,512]{2,1,0:T(8,128)(2,1)S(1)}, f32[1040,768]{1,0:T(8,128)S(1)}) custom-call(s32[9]{0:T(128)S(1)} %stack.70.where, bf16[1040,512]{1,0:T(8,128)(2,1)S(1)} %pad_maximum_fusion.refs_0_, bf16[1040,512]{1,0:T(8,128)(2,1)S(1)} %collective-permute-done.2.refs_1_, bf16[1040,512]{1,0:T(8,128)(2,1)S(1)} %collective-permute-done.3.refs_2_, ...), custom_call_target="tpu_custom_call" | custom-call | flops 2453667840 | bytes 12582912 | tf_op jit(solution)/shard_map/pallas_call | solution.py:105
  98.0 3.7 %shard_map.66.refs_3_ = f32[1040,768]{1,0:T(8,128)S(1)} custom-call(s32[9]{0:T(128)S(1)} %stack.70.where, bf16[8,1040,512]{2,1,0:T(8,128)(2,1)S(1)} %get-tuple-element.112.lhs.refs_0_, bf16[512,768]{1,0:T(8,128)(2,1)S(1)} %collective-permute-done.7.refs_1_.refs_4_, bf16[512,768]{1,0:T(8,128)(2,1)S(1)} %collective-permute-done.8.refs_2_.refs_5_, ...), custom_call_target="tpu_custom_call" | custom-call | flops 2453667840 | bytes 12582912 | tf_op jit(solution)/shard_map/pallas_call | solution.py:123
  101.7 7.2 %collective-permute-done.16.refs_1_.refs_9_ = bf16[512,768]{1,0:T(8,128)(2,1)S(1)} collective-permute-done((bf16[512,768]{1,0:T(8,128)(2,1)S(1)}, bf16[512,768]{1,0:T(8,128)(2,1)S(1)}, u32[]{:S(2)}, u32[]{:S(2)}) %collective-permute-start.16) | collective-permute-done | bytes 786464 | tf_op jit(solution)/shard_map/ppermute | solution.py:41
  108.9 0.0 collective-permute-done.17.refs_2_.refs_10_
  108.9 0.9 collective-permute-done.18.refs_3_.refs_11_
  109.8 3.5 %shard_map.65.refs_3_ = f32[1040,768]{1,0:T(8,128)S(1)} custom-call(s32[9]{0:T(128)S(1)} %stack.70.where, bf16[8,1040,512]{2,1,0:T(8,128)(2,1)S(1)} %get-tuple-element.112.lhs.refs_0_, f32[1040,768]{1,0:T(8,128)S(1)} %get-tuple-element.106.part, bf16[512,768]{1,0:T(8,128)(2,1)S(1)} %collective-permute-done.13.refs_0_.refs_8_, ...), custom_call_target="tpu_custom_call" | custom-call | flops 2453667840 | bytes 12582912 | tf_op jit(solution)/shard_map/pallas_call | solution.py:158
  113.4 2.5 %collective-permute-start.21 = (bf16[512,768]{1,0:T(8,128)(2,1)S(1)}, bf16[512,768]{1,0:T(8,128)(2,1)S(1)}, u32[]{:S(2)}, u32[]{:S(2)}) collective-permute-start(bf16[512,768]{1,0:T(8,128)(2,1)S(1)} %collective-permute-done.16.refs_1_.refs_9_), channel_id=1, source_target_pairs={{0,8},{1,9},{2,10},{3,11},{4,12},{5,13},{6,14},{7,15},{8,0},{9,1},... | collective-permute-start | bytes 2359304 | tf_op jit(solution)/shard_map/ppermute | solution.py:41
  115.9 0.1 collective-permute-start.22
  116.0 0.4 collective-permute-start.23
  116.4 5.0 %shard_map.67 = (f32[1024,256]{1,0:T(8,128)S(1)}, f32[1024,256]{1,0:T(8,128)S(1)}, f32[128,256]{1,0:T(8,128)S(1)}, f32[16,256]{1,0:T(8,128)S(1)}) custom-call(s32[9]{0:T(128)S(1)} %stack.70.where, bf16[8,1040,512]{2,1,0:T(8,128)(2,1)S(1)} %get-tuple-element.112.lhs.refs_0_, bf16[1040,512]{1,0:T(8,128)(2,1)S(1)} %collective-permute-done.19.refs_1_, ...), custom_call_target="tpu_custom_call" | custom-call | flops 4089446400 | bytes 12582912 | tf_op jit(solution)/shard_map/pallas_call | solution.py:241
  121.5 7.9 %shard_map.68 = (f32[1024,256]{1,0:T(8,128)S(1)}, f32[1024,256]{1,0:T(8,128)S(1)}, f32[128,256]{1,0:T(8,128)S(1)}, f32[16,256]{1,0:T(8,128)S(1)}) custom-call(s32[9]{0:T(128)S(1)} %stack.70.where, bf16[8,1040,512]{2,1,0:T(8,128)(2,1)S(1)} %get-tuple-element.112.lhs.refs_0_, bf16[1040,512]{1,0:T(8,128)(2,1)S(1)} %collective-permute-done.19.refs_1_, ...), custom_call_target="tpu_custom_call" | custom-call | flops 4089446400 | bytes 12582912 | tf_op jit(solution)/shard_map/pallas_call | solution.py:241
  129.4 0.2 collective-permute-start.24
  129.6 1.3 collective-permute-start.25
  130.9 0.7 collective-permute-start.26
  131.6 2.6 %shard_map.69.y0 = f32[1024,256]{1,0:T(8,128)S(1)} custom-call(f32[1024,256]{1,0:T(8,128)S(1)} %get-tuple-element.128.prod_ref, f32[128,256]{1,0:T(8,128)S(1)} %get-tuple-element.129.u_ref, f32[64,256]{1,0:T(8,128)S(1)} %get-tuple-element.119.refs_12_.prm.p0), custom_call_target="tpu_custom_call" | custom-call | flops 16777216 | bytes 12582912 | tf_op jit(solution)/shard_map/pallas_call | solution.py:290
  134.2 0.7 collective-permute-done.26
  134.9 0.1 collective-permute-start.27
  135.0 2.4 %collective-permute-start.28 = (f32[16,512]{1,0:T(8,128)S(1)}, f32[16,512]{1,0:T(8,128)S(1)}, u32[]{:S(2)}, u32[]{:S(2)}) collective-permute-start(f32[16,512]{1,0:T(8,128)S(1)} %get-tuple-element.151), channel_id=1, source_target_pairs={{0,32},{1,33},{2,34},{3,35},{4,36},{5,37},{6,38},{7,39},{8,40},{9,... | collective-permute-start | bytes 98312 | tf_op jit(solution)/shard_map/ppermute | solution.py:41
  137.4 0.5 collective-permute-start.29
  137.9 2.6 %shard_map.70.y1 = f32[1024,256]{1,0:T(8,128)S(1)} custom-call(f32[1024,256]{1,0:T(8,128)S(1)} %get-tuple-element.131.prod_ref, f32[128,256]{1,0:T(8,128)S(1)} %get-tuple-element.132.u_ref, f32[64,256]{1,0:T(8,128)S(1)} %get-tuple-element.123.refs_12_.prm.p1), custom_call_target="tpu_custom_call" | custom-call | flops 16777216 | bytes 12582912 | tf_op jit(solution)/shard_map/pallas_call | solution.py:290
  140.5 4.0 %shard_map.71 = bf16[1024,512]{1,0:T(8,128)(2,1)} custom-call(s32[1]{0:T(128)} %bitcast.17.core_ref, f32[1024,256]{1,0:T(8,128)S(1)} %shard_map.69.y0, f32[1024,256]{1,0:T(8,128)S(1)} %shard_map.70.y1, f32[1024,256]{1,0:T(8,128)S(1)} %get-tuple-element.133.x0, f32[1024,256]{1,0:T(8,128)S(1)} %get-tuple-element.134.x1, ...), custom_call_target="tpu_custom_call" | custom-call | tf_op jit(solution)/shard_map/pallas_call | solution.py:337
  (27 shorter events, 0.2 us)
Async XLA Ops:
  0.0 4.7 %copy-start = (f32[3,3,4096]{2,1,0:T(4,128)S(1)}, f32[3,3,4096]{2,1,0:T(4,128)}, u32[]{:S(2)}) copy-start(f32[3,3,4096]{2,1,0:T(4,128)} %param.8) | copy-start | bytes 442372
  1.2 5.3 %copy-start.1 = (bf16[1024,512]{1,0:T(8,128)(2,1)S(1)}, bf16[1024,512]{1,0:T(8,128)(2,1)}, u32[]{:S(2)}) copy-start(bf16[1024,512]{1,0:T(8,128)(2,1)} %param.6) | copy-start | bytes 3145732
  2.1 13.5 %collective-permute-start.1 = (bf16[512,768]{1,0:T(8,128)(2,1)}, bf16[512,768]{1,0:T(8,128)(2,1)S(1)}, u32[]{:S(2)}, u32[]{:S(2)}) collective-permute-start(bf16[512,768]{1,0:T(8,128)(2,1)} %pad_maximum_fusion.1), channel_id=1, source_target_pairs={{0,0},{1,16},{2,32},{3,48},{4,64},{5,80},{6,96},{7,112},{8,8},{9,2... | collective-permute-start | bytes 2359304 | tf_op jit(solution)/shard_map/ppermute | solution.py:41
  7.2 7.7 %collective-permute-start = (bf16[16,512]{1,0:T(8,128)(2,1)}, bf16[16,512]{1,0:T(8,128)(2,1)}, u32[]{:S(2)}, u32[]{:S(2)}) collective-permute-start(bf16[16,512]{1,0:T(8,128)(2,1)} %slice.36), channel_id=1, source_target_pairs={{0,8},{1,9},{2,10},{3,11},{4,12},{5,13},{6,14},{7,15},{8,16},{9,17... | collective-permute-start | bytes 49160 | tf_op jit(solution)/shard_map/ppermute | solution.py:41
  15.6 37.3 %collective-permute-start.2 = (bf16[1040,512]{1,0:T(8,128)(2,1)S(1)}, bf16[1040,512]{1,0:T(8,128)(2,1)S(1)}, u32[]{:S(2)}, u32[]{:S(2)}) collective-permute-start(bf16[1040,512]{1,0:T(8,128)(2,1)S(1)} %pad_maximum_fusion.refs_0_), channel_id=1, source_target_pairs={{0,1},{1,2},{2,3},{3,0},{4,5},{5,6},{6,7},{7,4},{8,9},{9,10},{10,1... | collective-permute-start | bytes 3194888 | tf_op jit(solution)/shard_map/ppermute | solution.py:41
  27.5 25.4 %collective-permute-start.3 = (bf16[1040,512]{1,0:T(8,128)(2,1)S(1)}, bf16[1040,512]{1,0:T(8,128)(2,1)S(1)}, u32[]{:S(2)}, u32[]{:S(2)}) collective-permute-start(bf16[1040,512]{1,0:T(8,128)(2,1)S(1)} %pad_maximum_fusion.refs_0_), channel_id=1, source_target_pairs={{0,3},{1,0},{2,1},{3,2},{4,7},{5,4},{6,5},{7,6},{8,11},{9,8},{10,9... | collective-permute-start | bytes 3194888 | tf_op jit(solution)/shard_map/ppermute | solution.py:41
  30.9 25.8 %collective-permute-start.4 = (bf16[1040,512]{1,0:T(8,128)(2,1)S(1)}, bf16[1040,512]{1,0:T(8,128)(2,1)S(1)}, u32[]{:S(2)}, u32[]{:S(2)}) collective-permute-start(bf16[1040,512]{1,0:T(8,128)(2,1)S(1)} %pad_maximum_fusion.refs_0_), channel_id=1, source_target_pairs={{0,4},{1,5},{2,6},{3,7},{4,0},{5,1},{6,2},{7,3},{8,12},{9,13},{10,... | collective-permute-start | bytes 3194888 | tf_op jit(solution)/shard_map/ppermute | solution.py:41
  34.7 18.1 %collective-permute-start.5 = (bf16[512,768]{1,0:T(8,128)(2,1)S(1)}, bf16[512,768]{1,0:T(8,128)(2,1)S(1)}, u32[]{:S(2)}, u32[]{:S(2)}) collective-permute-start(bf16[512,768]{1,0:T(8,128)(2,1)S(1)} %collective-permute-done.1.refs_6_.refs_4_), channel_id=1, source_target_pairs={{0,16},{1,17},{2,18},{3,19},{4,20},{5,21},{6,22},{7,23},{8,24},{9,... | collective-permute-start | bytes 2359304 | tf_op jit(solution)/shard_map/ppermute | solution.py:41
  34.7 18.1 %collective-permute-start.6 = (bf16[512,768]{1,0:T(8,128)(2,1)S(1)}, bf16[512,768]{1,0:T(8,128)(2,1)S(1)}, u32[]{:S(2)}, u32[]{:S(2)}) collective-permute-start(bf16[512,768]{1,0:T(8,128)(2,1)S(1)} %collective-permute-done.1.refs_6_.refs_4_), channel_id=1, source_target_pairs={{0,48},{1,49},{2,50},{3,51},{4,52},{5,53},{6,54},{7,55},{8,56},{9,... | collective-permute-start | bytes 2359304 | tf_op jit(solution)/shard_map/ppermute | solution.py:41
  56.7 5.7 %collective-permute-start.7 = (bf16[512,768]{1,0:T(8,128)(2,1)S(1)}, bf16[512,768]{1,0:T(8,128)(2,1)S(1)}, u32[]{:S(2)}, u32[]{:S(2)}) collective-permute-start(bf16[512,768]{1,0:T(8,128)(2,1)S(1)} %collective-permute-done.1.refs_6_.refs_4_), channel_id=1, source_target_pairs={{0,8},{1,9},{2,10},{3,11},{4,12},{5,13},{6,14},{7,15},{8,0},{9,1},... | collective-permute-start | bytes 2359304 | tf_op jit(solution)/shard_map/ppermute | solution.py:41
  59.1 3.2 %collective-permute-start.8 = (bf16[512,768]{1,0:T(8,128)(2,1)S(1)}, bf16[512,768]{1,0:T(8,128)(2,1)S(1)}, u32[]{:S(2)}, u32[]{:S(2)}) collective-permute-start(bf16[512,768]{1,0:T(8,128)(2,1)S(1)} %collective-permute-done.5.refs_7_.refs_5_), channel_id=1, source_target_pairs={{0,8},{1,9},{2,10},{3,11},{4,12},{5,13},{6,14},{7,15},{8,0},{9,1},... | collective-permute-start | bytes 2359304 | tf_op jit(solution)/shard_map/ppermute | solution.py:41
  59.1 4.2 %collective-permute-start.9 = (bf16[512,768]{1,0:T(8,128)(2,1)S(1)}, bf16[512,768]{1,0:T(8,128)(2,1)S(1)}, u32[]{:S(2)}, u32[]{:S(2)}) collective-permute-start(bf16[512,768]{1,0:T(8,128)(2,1)S(1)} %collective-permute-done.6.refs_8_.refs_6_), channel_id=1, source_target_pairs={{0,8},{1,9},{2,10},{3,11},{4,12},{5,13},{6,14},{7,15},{8,0},{9,1},... | collective-permute-start | bytes 2359304 | tf_op jit(solution)/shard_map/ppermute | solution.py:41
  59.6 26.4 %collective-permute-start.10 = (bf16[1040,512]{1,0:T(8,128)(2,1)S(1)}, bf16[1040,512]{1,0:T(8,128)(2,1)S(1)}, u32[]{:S(2)}, u32[]{:S(2)}) collective-permute-start(bf16[1040,512]{1,0:T(8,128)(2,1)S(1)} %collective-permute-done.4.refs_3_), channel_id=1, source_target_pairs={{0,1},{1,2},{2,3},{3,0},{4,5},{5,6},{6,7},{7,4},{8,9},{9,10},{10,1... | collective-permute-start | bytes 3194888 | tf_op jit(solution)/shard_map/ppermute | solution.py:41
  59.6 26.4 %collective-permute-start.11 = (bf16[1040,512]{1,0:T(8,128)(2,1)S(1)}, bf16[1040,512]{1,0:T(8,128)(2,1)S(1)}, u32[]{:S(2)}, u32[]{:S(2)}) collective-permute-start(bf16[1040,512]{1,0:T(8,128)(2,1)S(1)} %collective-permute-done.4.refs_3_), channel_id=1, source_target_pairs={{0,3},{1,0},{2,1},{3,2},{4,7},{5,4},{6,5},{7,6},{8,11},{9,8},{10,9... | collective-permute-start | bytes 3194888 | tf_op jit(solution)/shard_map/ppermute | solution.py:41
  63.3 22.7 %collective-permute-start.12 = (bf16[512,768]{1,0:T(8,128)(2,1)S(1)}, bf16[512,768]{1,0:T(8,128)(2,1)S(1)}, u32[]{:S(2)}, u32[]{:S(2)}) collective-permute-start(bf16[512,768]{1,0:T(8,128)(2,1)S(1)} %collective-permute-done.5.refs_7_.refs_5_), channel_id=1, source_target_pairs={{0,16},{1,17},{2,18},{3,19},{4,20},{5,21},{6,22},{7,23},{8,24},{9,... | collective-permute-start | bytes 2359304 | tf_op jit(solution)/shard_map/ppermute | solution.py:41
  63.3 22.7 %collective-permute-start.13 = (bf16[512,768]{1,0:T(8,128)(2,1)S(1)}, bf16[512,768]{1,0:T(8,128)(2,1)S(1)}, u32[]{:S(2)}, u32[]{:S(2)}) collective-permute-start(bf16[512,768]{1,0:T(8,128)(2,1)S(1)} %collective-permute-done.1.refs_6_.refs_4_), channel_id=1, source_target_pairs={{0,64},{1,65},{2,66},{3,67},{4,68},{5,69},{6,70},{7,71},{8,72},{9,... | collective-permute-start | bytes 2359304 | tf_op jit(solution)/shard_map/ppermute | solution.py:41
  86.0 3.6 %collective-permute-start.14 = (bf16[512,768]{1,0:T(8,128)(2,1)S(1)}, bf16[512,768]{1,0:T(8,128)(2,1)S(1)}, u32[]{:S(2)}, u32[]{:S(2)}) collective-permute-start(bf16[512,768]{1,0:T(8,128)(2,1)S(1)} %collective-permute-done.12.refs_9_.refs_7_), channel_id=1, source_target_pairs={{0,8},{1,9},{2,10},{3,11},{4,12},{5,13},{6,14},{7,15},{8,0},{9,1},... | collective-permute-start | bytes 2359304 | tf_op jit(solution)/shard_map/ppermute | solution.py:41
  86.9 3.0 %collective-permute-start.15 = (bf16[512,768]{1,0:T(8,128)(2,1)S(1)}, bf16[512,768]{1,0:T(8,128)(2,1)S(1)}, u32[]{:S(2)}, u32[]{:S(2)}) collective-permute-start(bf16[512,768]{1,0:T(8,128)(2,1)S(1)} %collective-permute-done.13.refs_0_.refs_8_), channel_id=1, source_target_pairs={{0,8},{1,9},{2,10},{3,11},{4,12},{5,13},{6,14},{7,15},{8,0},{9,1},... | collective-permute-start | bytes 2359304 | tf_op jit(solution)/shard_map/ppermute | solution.py:41
  87.0 26.4 %collective-permute-start.19 = (bf16[1040,512]{1,0:T(8,128)(2,1)S(1)}, bf16[1040,512]{1,0:T(8,128)(2,1)S(1)}, u32[]{:S(2)}, u32[]{:S(2)}) collective-permute-start(bf16[1040,512]{1,0:T(8,128)(2,1)S(1)} %collective-permute-done.2.refs_1_), channel_id=1, source_target_pairs={{0,1},{1,2},{2,3},{3,0},{4,5},{5,6},{6,7},{7,4},{8,9},{9,10},{10,1... | collective-permute-start | bytes 3194888 | tf_op jit(solution)/shard_map/ppermute | solution.py:41
  87.0 26.4 %collective-permute-start.20 = (bf16[1040,512]{1,0:T(8,128)(2,1)S(1)}, bf16[1040,512]{1,0:T(8,128)(2,1)S(1)}, u32[]{:S(2)}, u32[]{:S(2)}) collective-permute-start(bf16[1040,512]{1,0:T(8,128)(2,1)S(1)} %collective-permute-done.11.refs_5_), channel_id=1, source_target_pairs={{0,3},{1,0},{2,1},{3,2},{4,7},{5,4},{6,5},{7,6},{8,11},{9,8},{10,9... | collective-permute-start | bytes 3194888 | tf_op jit(solution)/shard_map/ppermute | solution.py:41
  89.6 19.3 %collective-permute-start.16 = (bf16[512,768]{1,0:T(8,128)(2,1)S(1)}, bf16[512,768]{1,0:T(8,128)(2,1)S(1)}, u32[]{:S(2)}, u32[]{:S(2)}) collective-permute-start(bf16[512,768]{1,0:T(8,128)(2,1)S(1)} %collective-permute-done.13.refs_0_.refs_8_), channel_id=1, source_target_pairs={{0,16},{1,17},{2,18},{3,19},{4,20},{5,21},{6,22},{7,23},{8,24},{9,... | collective-permute-start | bytes 2359304 | tf_op jit(solution)/shard_map/ppermute | solution.py:41
  89.9 19.0 %collective-permute-start.17 = (bf16[512,768]{1,0:T(8,128)(2,1)S(1)}, bf16[512,768]{1,0:T(8,128)(2,1)S(1)}, u32[]{:S(2)}, u32[]{:S(2)}) collective-permute-start(bf16[512,768]{1,0:T(8,128)(2,1)S(1)} %collective-permute-done.13.refs_0_.refs_8_), channel_id=1, source_target_pairs={{0,48},{1,49},{2,50},{3,51},{4,52},{5,53},{6,54},{7,55},{8,56},{9,... | collective-permute-start | bytes 2359304 | tf_op jit(solution)/shard_map/ppermute | solution.py:41
  92.3 17.5 %collective-permute-start.18 = (bf16[512,768]{1,0:T(8,128)(2,1)S(1)}, bf16[512,768]{1,0:T(8,128)(2,1)S(1)}, u32[]{:S(2)}, u32[]{:S(2)}) collective-permute-start(bf16[512,768]{1,0:T(8,128)(2,1)S(1)} %collective-permute-done.12.refs_9_.refs_7_), channel_id=1, source_target_pairs={{0,64},{1,65},{2,66},{3,67},{4,68},{5,69},{6,70},{7,71},{8,72},{9,... | collective-permute-start | bytes 2359304 | tf_op jit(solution)/shard_map/ppermute | solution.py:41
  113.4 8.1 %collective-permute-start.21 = (bf16[512,768]{1,0:T(8,128)(2,1)S(1)}, bf16[512,768]{1,0:T(8,128)(2,1)S(1)}, u32[]{:S(2)}, u32[]{:S(2)}) collective-permute-start(bf16[512,768]{1,0:T(8,128)(2,1)S(1)} %collective-permute-done.16.refs_1_.refs_9_), channel_id=1, source_target_pairs={{0,8},{1,9},{2,10},{3,11},{4,12},{5,13},{6,14},{7,15},{8,0},{9,1},... | collective-permute-start | bytes 2359304 | tf_op jit(solution)/shard_map/ppermute | solution.py:41
  115.9 5.5 %collective-permute-start.22 = (bf16[512,768]{1,0:T(8,128)(2,1)S(1)}, bf16[512,768]{1,0:T(8,128)(2,1)S(1)}, u32[]{:S(2)}, u32[]{:S(2)}) collective-permute-start(bf16[512,768]{1,0:T(8,128)(2,1)S(1)} %collective-permute-done.17.refs_2_.refs_10_), channel_id=1, source_target_pairs={{0,8},{1,9},{2,10},{3,11},{4,12},{5,13},{6,14},{7,15},{8,0},{9,1},... | collective-permute-start | bytes 2359304 | tf_op jit(solution)/shard_map/ppermute | solution.py:41
  116.0 5.4 %collective-permute-start.23 = (bf16[512,768]{1,0:T(8,128)(2,1)S(1)}, bf16[512,768]{1,0:T(8,128)(2,1)S(1)}, u32[]{:S(2)}, u32[]{:S(2)}) collective-permute-start(bf16[512,768]{1,0:T(8,128)(2,1)S(1)} %collective-permute-done.18.refs_3_.refs_11_), channel_id=1, source_target_pairs={{0,8},{1,9},{2,10},{3,11},{4,12},{5,13},{6,14},{7,15},{8,0},{9,1},... | collective-permute-start | bytes 2359304 | tf_op jit(solution)/shard_map/ppermute | solution.py:41
  129.4 4.8 %collective-permute-start.24 = (f32[16,512]{1,0:T(8,128)S(1)}, f32[16,512]{1,0:T(8,128)S(1)}, u32[]{:S(2)}, u32[]{:S(2)}) collective-permute-start(f32[16,512]{1,0:T(8,128)S(1)} %pad_maximum_fusion.4), channel_id=1, source_target_pairs={{0,8},{1,9},{2,10},{3,11},{4,12},{5,13},{6,14},{7,15},{8,0},{9,1},... | collective-permute-start | bytes 98312 | tf_op jit(solution)/shard_map/ppermute | solution.py:41
  129.6 4.7 %collective-permute-start.25 = (f32[16,512]{1,0:T(8,128)S(1)}, f32[16,512]{1,0:T(8,128)S(1)}, u32[]{:S(2)}, u32[]{:S(2)}) collective-permute-start(f32[16,512]{1,0:T(8,128)S(1)} %pad_maximum_fusion.4), channel_id=1, source_target_pairs={{0,64},{1,65},{2,66},{3,67},{4,68},{5,69},{6,70},{7,71},{8,72},{9,... | collective-permute-start | bytes 98312 | tf_op jit(solution)/shard_map/ppermute | solution.py:41
  130.9 4.0 %collective-permute-start.26 = (f32[16,512]{1,0:T(8,128)S(1)}, f32[16,512]{1,0:T(8,128)S(1)}, u32[]{:S(2)}, u32[]{:S(2)}) collective-permute-start(f32[16,512]{1,0:T(8,128)S(1)} %pad_maximum_fusion.4), channel_id=1, source_target_pairs={{0,72},{1,73},{2,74},{3,75},{4,76},{5,77},{6,78},{7,79},{8,64},{9,... | collective-permute-start | bytes 98312 | tf_op jit(solution)/shard_map/ppermute | solution.py:41
  134.9 5.5 %collective-permute-start.27 = (f32[16,512]{1,0:T(8,128)S(1)}, f32[16,512]{1,0:T(8,128)S(1)}, u32[]{:S(2)}, u32[]{:S(2)}) collective-permute-start(f32[16,512]{1,0:T(8,128)S(1)} %get-tuple-element.152), channel_id=1, source_target_pairs={{0,16},{1,17},{2,18},{3,19},{4,20},{5,21},{6,22},{7,23},{8,24},{9,... | collective-permute-start | bytes 98312 | tf_op jit(solution)/shard_map/ppermute | solution.py:41
  135.0 5.5 %collective-permute-start.28 = (f32[16,512]{1,0:T(8,128)S(1)}, f32[16,512]{1,0:T(8,128)S(1)}, u32[]{:S(2)}, u32[]{:S(2)}) collective-permute-start(f32[16,512]{1,0:T(8,128)S(1)} %get-tuple-element.151), channel_id=1, source_target_pairs={{0,32},{1,33},{2,34},{3,35},{4,36},{5,37},{6,38},{7,39},{8,40},{9,... | collective-permute-start | bytes 98312 | tf_op jit(solution)/shard_map/ppermute | solution.py:41
  137.4 3.1 %collective-permute-start.29 = (f32[16,512]{1,0:T(8,128)S(1)}, f32[16,512]{1,0:T(8,128)S(1)}, u32[]{:S(2)}, u32[]{:S(2)}) collective-permute-start(f32[16,512]{1,0:T(8,128)S(1)} %get-tuple-element.143), channel_id=1, source_target_pairs={{0,48},{1,49},{2,50},{3,51},{4,52},{5,53},{6,54},{7,55},{8,56},{9,... | collective-permute-start | bytes 98312 | tf_op jit(solution)/shard_map/ppermute | solution.py:41

commit v9 on v8

--- a/solution.py
+++ b/solution.py
@@ -77,6 +77,10 @@
     return jnp.where(rows >= steps, pltpu.roll(value, steps, 0), 0.0)
 
 
+def side_by_side(weight):
+    return jnp.concatenate([weight[g] for g in range(3)], axis=1)
+
+
 def first_half(where, lhs, weights, acc):
     acc[...] = jnp.zeros_like(acc)
     for k in range(4):
@@ -84,7 +88,7 @@
 
         @pl.when(lax.rem(slot, 4) != 3)
         def _(k=k, slot=slot):
-            acc[...] += jnp.dot(lhs[slot], weights[k][...], preferred_element_type=F32)
+            acc[...] += jnp.dot(lhs[slot], side_by_side(weights[k]), preferred_element_type=F32)
 
 
 def begin_kernel(where, *refs):
@@ -101,7 +105,7 @@
 
 def begin(where, toks, weights, rows):
     vmem = pl.BlockSpec(memory_space=pltpu.VMEM)
-    tall, width = rows + HALO, weights[0].shape[1]
+    tall, width = rows + HALO, 3 * weights[0].shape[2]
     return pl.pallas_call(
         begin_kernel,
         out_shape=[
@@ -119,7 +123,7 @@
 
 def also(where, lhs, weights, rows):
     vmem = pl.BlockSpec(memory_space=pltpu.VMEM)
-    tall, width = rows + HALO, weights[0].shape[1]
+    tall, width = rows + HALO, 3 * weights[0].shape[2]
     return pl.pallas_call(
         also_kernel,
         out_shape=jax.ShapeDtypeStruct((tall, width), F32),
@@ -137,7 +141,7 @@
     is_near = [lax.rem(where[4 + k], 4) != 3 for k in range(4)]
 
     def product(k):
-        return jnp.dot(lhs[where[4 + k]], weights[k][...], preferred_element_type=F32)
+        return jnp.dot(lhs[where[4 + k]], side_by_side(weights[k]), preferred_element_type=F32)
 
     def start(k):
         acc[...] = part[...] + product(k)
@@ -154,7 +158,7 @@
 
 def more(where, lhs, part, weights, rows):
     vmem = pl.BlockSpec(memory_space=pltpu.VMEM)
-    tall, width = rows + HALO, weights[0].shape[1]
+    tall, width = rows + HALO, 3 * weights[0].shape[2]
     return pl.pallas_call(
         more_kernel,
         out_shape=jax.ShapeDtypeStruct((tall, width), F32),
@@ -180,7 +184,7 @@
             def _(k=k, ref=ref, at=at):
                 last[:, at] = ref[...]
                 if few or k < 4:
-                    late[at, :] = weights[k][...]
+                    late[at, :] = side_by_side(weights[k])
 
         if k >= 4 and not few:
 
@@ -190,7 +194,7 @@
 
     for n in range(3):
         cols = pl.ds(n * 2 * LANES, 2 * LANES)
-        right = jnp.concatenate([w[:, cols] for w in ((late,) if few else (late, *weights[4:]))], axis=0)
+        right = jnp.concatenate([late[:, cols]] + [w[n] for w in ([] if few else weights[4:])], axis=0)
         out = part[:, cols] + jnp.dot(last[...], right, preferred_element_type=F32)
         out = out.astype(jnp.bfloat16).astype(F32)
         for q in range(2):
@@ -387,7 +391,7 @@
         n = (yl * 4 + x) * 2 + c + 1
         return None if n == 16 else (n // 8, (n // 2) % 4, n % 2, yh, z)
 
-    w = jnp.concatenate([in_weight[:, g] for g in range(3)], axis=1)
+    w = in_weight.transpose(1, 0, 2)
     b = transposed(w)
     shard_tokens, *prms = together((tokens, *prms))
     steps = shard_tokens.reshape(SEG, rows // SEG, BLOCK).transpose(1, 0, 2).reshape(rows, BLOCK)

time: 145 us -> 143 us (0.986)
  no operation moved by 1% of the time
where the time goes in v9:
time: 143 us; the launch traced here: 142 us
  starting transfers between devices  52.8 us (37%)
  waiting for transfers between devices  50.8 us (36%)
  Pallas kernels  33.6 us (23%)
  other arithmetic  2.45 us (2%)
  local copies, waits for them, and re-layouts  2.14 us (1%)
    ppermute x30, starting transfers between devices, send(): return lax.ppermute(value, ('ctx', 'tp'), route(move))  52.8 us
    ppermute x30, waiting for transfers between devices, send(): return lax.ppermute(value, ('ctx', 'tp'), route(move))  50.8 us
    pallas_call x2, Pallas kernels, project(): pl.pallas_call(functools.partial(project_kernel, rows, few), out_shape=[j...  12.9 us
    pallas_call x2, Pallas kernels, read(): pl.pallas_call(functools.partial(read_kernel, rows), out_shape=jax.ShapeD...  5.19 us
    pallas_call x1, Pallas kernels, begin(): pl.pallas_call(begin_kernel, out_shape=[jax.ShapeDtypeStruct((8, tall, BL...  4.14 us
    pallas_call x1, Pallas kernels, gate(): pl.pallas_call(functools.partial(gate_kernel, rows), out_shape=jax.ShapeD...  3.96 us
    pallas_call x1, Pallas kernels, also(): pl.pallas_call(also_kernel, out_shape=jax.ShapeDtypeStruct((tall, width),...  3.9 us
    pallas_call x1, Pallas kernels, more(): pl.pallas_call(more_kernel, out_shape=jax.ShapeDtypeStruct((tall, width),...  3.54 us
  transfers between devices with their start and end apart: 30, of which 10 were waited for; matrix products, arithmetic and copies ran while one was open for 3% of the time, Pallas kernels for 15%

profile of v9, /device:TPU:1, one launch (start us, length us, event | category | flops | bytes accessed | tf_op | source)
XLA Modules:
  0.0 142.4 jit_solution(10586202820073389331)
XLA Ops:
  0.0 1.9 %collective-permute-start.1 = (bf16[3,512,256]{2,1,0:T(8,128)(2,1)}, bf16[3,512,256]{2,1,0:T(8,128)(2,1)S(1)}, u32[]{:S(2)}, u32[]{:S(2)}) collective-permute-start(bf16[3,512,256]{2,1,0:T(8,128)(2,1)} %bitcast.73), channel_id=1, source_target_pairs={{0,0},{1,16},{2,32},{3,48},{4,64},{5,80},{6,96},{7,112},{8,8},{9,2... | collective-permute-start | bytes 2359304 | tf_op jit(solution)/shard_map/ppermute | solution.py:41
  1.9 0.8 select_bitcast_fusion.3
  2.9 0.8 dynamic_slice.21
  3.6 0.8 select_bitcast_fusion.2
  4.5 0.6 slice.27
  5.1 6.6 %collective-permute-start = (bf16[16,512]{1,0:T(8,128)(2,1)}, bf16[16,512]{1,0:T(8,128)(2,1)}, u32[]{:S(2)}, u32[]{:S(2)}) collective-permute-start(bf16[16,512]{1,0:T(8,128)(2,1)} %slice.27), channel_id=1, source_target_pairs={{0,8},{1,9},{2,10},{3,11},{4,12},{5,13},{6,14},{7,15},{8,16},{9,17... | collective-permute-start | bytes 49160 | tf_op jit(solution)/shard_map/ppermute | solution.py:41
  12.0 0.6 copy.9
  12.6 0.1 stack.70.where
  12.7 0.1 collective-permute-done
  12.8 0.8 pad_maximum_fusion.refs_0_
  13.6 0.0 collective-permute-done.1.refs_6_.refs_4_
  13.6 11.9 %collective-permute-start.2 = (bf16[1040,512]{1,0:T(8,128)(2,1)S(1)}, bf16[1040,512]{1,0:T(8,128)(2,1)S(1)}, u32[]{:S(2)}, u32[]{:S(2)}) collective-permute-start(bf16[1040,512]{1,0:T(8,128)(2,1)S(1)} %pad_maximum_fusion.refs_0_), channel_id=1, source_target_pairs={{0,1},{1,2},{2,3},{3,0},{4,5},{5,6},{6,7},{7,4},{8,9},{9,10},{10,1... | collective-permute-start | bytes 3194888 | tf_op jit(solution)/shard_map/ppermute | solution.py:41
  25.5 3.3 %collective-permute-start.3 = (bf16[1040,512]{1,0:T(8,128)(2,1)S(1)}, bf16[1040,512]{1,0:T(8,128)(2,1)S(1)}, u32[]{:S(2)}, u32[]{:S(2)}) collective-permute-start(bf16[1040,512]{1,0:T(8,128)(2,1)S(1)} %pad_maximum_fusion.refs_0_), channel_id=1, source_target_pairs={{0,3},{1,0},{2,1},{3,2},{4,7},{5,4},{6,5},{7,6},{8,11},{9,8},{10,9... | collective-permute-start | bytes 3194888 | tf_op jit(solution)/shard_map/ppermute | solution.py:41
  28.8 3.8 %collective-permute-start.4 = (bf16[1040,512]{1,0:T(8,128)(2,1)S(1)}, bf16[1040,512]{1,0:T(8,128)(2,1)S(1)}, u32[]{:S(2)}, u32[]{:S(2)}) collective-permute-start(bf16[1040,512]{1,0:T(8,128)(2,1)S(1)} %pad_maximum_fusion.refs_0_), channel_id=1, source_target_pairs={{0,4},{1,5},{2,6},{3,7},{4,0},{5,1},{6,2},{7,3},{8,12},{9,13},{10,... | collective-permute-start | bytes 3194888 | tf_op jit(solution)/shard_map/ppermute | solution.py:41
  32.7 0.0 collective-permute-start.5
  32.7 2.7 %collective-permute-start.6 = (bf16[3,512,256]{2,1,0:T(8,128)(2,1)S(1)}, bf16[3,512,256]{2,1,0:T(8,128)(2,1)S(1)}, u32[]{:S(2)}, u32[]{:S(2)}) collective-permute-start(bf16[3,512,256]{2,1,0:T(8,128)(2,1)S(1)} %collective-permute-done.1.refs_6_.refs_4_), channel_id=1, source_target_pairs={{0,48},{1,49},{2,50},{3,51},{4,52},{5,53},{6,54},{7,55},{8,56},{9,... | collective-permute-start | bytes 2359304 | tf_op jit(solution)/shard_map/ppermute | solution.py:41
  35.3 15.5 %collective-permute-done.5.refs_7_.refs_5_ = bf16[3,512,256]{2,1,0:T(8,128)(2,1)S(1)} collective-permute-done((bf16[3,512,256]{2,1,0:T(8,128)(2,1)S(1)}, bf16[3,512,256]{2,1,0:T(8,128)(2,1)S(1)}, u32[]{:S(2)}, u32[]{:S(2)}) %collective-permute-start.5) | collective-permute-done | bytes 786464 | tf_op jit(solution)/shard_map/ppermute | solution.py:41
  50.8 0.0 collective-permute-done.6.refs_8_.refs_6_
  50.8 0.1 collective-permute-done.2.refs_1_
  50.9 0.0 collective-permute-done.3.refs_2_
  50.9 3.7 %collective-permute-done.4.refs_3_ = bf16[1040,512]{1,0:T(8,128)(2,1)S(1)} collective-permute-done((bf16[1040,512]{1,0:T(8,128)(2,1)S(1)}, bf16[1040,512]{1,0:T(8,128)(2,1)S(1)}, u32[]{:S(2)}, u32[]{:S(2)}) %collective-permute-start.4) | collective-permute-done | bytes 1064992 | tf_op jit(solution)/shard_map/ppermute | solution.py:41
  54.7 2.5 %collective-permute-start.7 = (bf16[3,512,256]{2,1,0:T(8,128)(2,1)S(1)}, bf16[3,512,256]{2,1,0:T(8,128)(2,1)S(1)}, u32[]{:S(2)}, u32[]{:S(2)}) collective-permute-start(bf16[3,512,256]{2,1,0:T(8,128)(2,1)S(1)} %collective-permute-done.1.refs_6_.refs_4_), channel_id=1, source_target_pairs={{0,8},{1,9},{2,10},{3,11},{4,12},{5,13},{6,14},{7,15},{8,0},{9,1},... | collective-permute-start | bytes 2359304 | tf_op jit(solution)/shard_map/ppermute | solution.py:41
  57.1 0.0 collective-permute-start.8
  57.1 0.5 collective-permute-start.9
  57.6 0.0 collective-permute-start.10
  57.6 2.7 %collective-permute-start.11 = (bf16[1040,512]{1,0:T(8,128)(2,1)S(1)}, bf16[1040,512]{1,0:T(8,128)(2,1)S(1)}, u32[]{:S(2)}, u32[]{:S(2)}) collective-permute-start(bf16[1040,512]{1,0:T(8,128)(2,1)S(1)} %collective-permute-done.4.refs_3_), channel_id=1, source_target_pairs={{0,3},{1,0},{2,1},{3,2},{4,7},{5,4},{6,5},{7,6},{8,11},{9,8},{10,9... | collective-permute-start | bytes 3194888 | tf_op jit(solution)/shard_map/ppermute | solution.py:41
  60.3 0.0 collective-permute-done.7.refs_1_.refs_4_
  60.3 1.0 collective-permute-done.9.refs_3_.refs_6_
  61.3 1.3 collective-permute-start.13
  62.6 21.3 %collective-permute-done.10.refs_4_ = bf16[1040,512]{1,0:T(8,128)(2,1)S(1)} collective-permute-done((bf16[1040,512]{1,0:T(8,128)(2,1)S(1)}, bf16[1040,512]{1,0:T(8,128)(2,1)S(1)}, u32[]{:S(2)}, u32[]{:S(2)}) %collective-permute-start.10) | collective-permute-done | bytes 1064992 | tf_op jit(solution)/shard_map/ppermute | solution.py:41
  84.0 0.0 collective-permute-done.12.refs_9_.refs_7_
  84.0 0.0 collective-permute-done.13.refs_0_.refs_8_
  84.0 0.9 collective-permute-start.14
  84.9 0.1 collective-permute-start.15
  85.0 2.7 %collective-permute-start.20 = (bf16[1040,512]{1,0:T(8,128)(2,1)S(1)}, bf16[1040,512]{1,0:T(8,128)(2,1)S(1)}, u32[]{:S(2)}, u32[]{:S(2)}) collective-permute-start(bf16[1040,512]{1,0:T(8,128)(2,1)S(1)} %collective-permute-done.11.refs_5_), channel_id=1, source_target_pairs={{0,3},{1,0},{2,1},{3,2},{4,7},{5,4},{6,5},{7,6},{8,11},{9,8},{10,9... | collective-permute-start | bytes 3194888 | tf_op jit(solution)/shard_map/ppermute | solution.py:41
  87.6 0.0 collective-permute-start.16
  87.6 0.3 collective-permute-done.15.refs_8_
  87.9 2.4 %collective-permute-start.17 = (bf16[3,512,256]{2,1,0:T(8,128)(2,1)S(1)}, bf16[3,512,256]{2,1,0:T(8,128)(2,1)S(1)}, u32[]{:S(2)}, u32[]{:S(2)}) collective-permute-start(bf16[3,512,256]{2,1,0:T(8,128)(2,1)S(1)} %collective-permute-done.13.refs_0_.refs_8_), channel_id=1, source_target_pairs={{0,48},{1,49},{2,50},{3,51},{4,52},{5,53},{6,54},{7,55},{8,56},{9,... | collective-permute-start | bytes 2359304 | tf_op jit(solution)/shard_map/ppermute | solution.py:41
  90.3 1.3 collective-permute-start.18
  91.7 4.1 %shard_map.64 = (bf16[8,1040,512]{2,1,0:T(8,128)(2,1)S(1)}, f32[1040,768]{1,0:T(8,128)S(1)}) custom-call(s32[9]{0:T(128)S(1)} %stack.70.where, bf16[1040,512]{1,0:T(8,128)(2,1)S(1)} %pad_maximum_fusion.refs_0_, bf16[1040,512]{1,0:T(8,128)(2,1)S(1)} %collective-permute-done.2.refs_1_, bf16[1040,512]{1,0:T(8,128)(2,1)S(1)} %collective-permute-done.3.refs_2_, ...), custom_call_target="tpu_custom_call" | custom-call | flops 2453667840 | bytes 12582912 | tf_op jit(solution)/shard_map/pallas_call | solution.py:109
  95.8 3.9 %shard_map.66.refs_3_ = f32[1040,768]{1,0:T(8,128)S(1)} custom-call(s32[9]{0:T(128)S(1)} %stack.70.where, bf16[8,1040,512]{2,1,0:T(8,128)(2,1)S(1)} %get-tuple-element.112.lhs.refs_0_, bf16[3,512,256]{2,1,0:T(8,128)(2,1)S(1)} %collective-permute-done.7.refs_1_.refs_4_, bf16[3,512,256]{2,1,0:T(8,128)(2,1)S(1)} %collective-permute-done.8.refs_2_.refs_5_, ...), custom_call_target="tpu_custom_call" | custom-call | flops 2453667840 | bytes 12582912 | tf_op jit(solution)/shard_map/pallas_call | solution.py:127
  99.7 7.2 %collective-permute-done.16.refs_1_.refs_9_ = bf16[3,512,256]{2,1,0:T(8,128)(2,1)S(1)} collective-permute-done((bf16[3,512,256]{2,1,0:T(8,128)(2,1)S(1)}, bf16[3,512,256]{2,1,0:T(8,128)(2,1)S(1)}, u32[]{:S(2)}, u32[]{:S(2)}) %collective-permute-start.16) | collective-permute-done | bytes 786464 | tf_op jit(solution)/shard_map/ppermute | solution.py:41
  106.9 0.9 collective-permute-done.18.refs_3_.refs_11_
  107.8 3.5 %shard_map.65.refs_3_ = f32[1040,768]{1,0:T(8,128)S(1)} custom-call(s32[9]{0:T(128)S(1)} %stack.70.where, bf16[8,1040,512]{2,1,0:T(8,128)(2,1)S(1)} %get-tuple-element.112.lhs.refs_0_, f32[1040,768]{1,0:T(8,128)S(1)} %get-tuple-element.106.part, bf16[3,512,256]{2,1,0:T(8,128)(2,1)S(1)} %collective-permute-done.13.refs_0_.refs_8_, ...), custom_call_target="tpu_custom_call" | custom-call | flops 2453667840 | bytes 12582912 | tf_op jit(solution)/shard_map/pallas_call | solution.py:162
  111.4 0.0 collective-permute-done.20.refs_2_
  111.4 2.5 %collective-permute-start.21 = (bf16[3,512,256]{2,1,0:T(8,128)(2,1)S(1)}, bf16[3,512,256]{2,1,0:T(8,128)(2,1)S(1)}, u32[]{:S(2)}, u32[]{:S(2)}) collective-permute-start(bf16[3,512,256]{2,1,0:T(8,128)(2,1)S(1)} %collective-permute-done.16.refs_1_.refs_9_), channel_id=1, source_target_pairs={{0,8},{1,9},{2,10},{3,11},{4,12},{5,13},{6,14},{7,15},{8,0},{9,1},... | collective-permute-start | bytes 2359304 | tf_op jit(solution)/shard_map/ppermute | solution.py:41
  113.9 0.1 collective-permute-start.22
  114.0 0.4 collective-permute-start.23
  114.4 5.0 %shard_map.67 = (f32[1024,256]{1,0:T(8,128)S(1)}, f32[1024,256]{1,0:T(8,128)S(1)}, f32[128,256]{1,0:T(8,128)S(1)}, f32[16,256]{1,0:T(8,128)S(1)}) custom-call(s32[9]{0:T(128)S(1)} %stack.70.where, bf16[8,1040,512]{2,1,0:T(8,128)(2,1)S(1)} %get-tuple-element.112.lhs.refs_0_, bf16[1040,512]{1,0:T(8,128)(2,1)S(1)} %collective-permute-done.19.refs_1_, ...), custom_call_target="tpu_custom_call" | custom-call | flops 4089446400 | bytes 12582912 | tf_op jit(solution)/shard_map/pallas_call | solution.py:245
  119.4 0.0 collective-permute-done.21.refs_9_
  119.5 7.9 %shard_map.68 = (f32[1024,256]{1,0:T(8,128)S(1)}, f32[1024,256]{1,0:T(8,128)S(1)}, f32[128,256]{1,0:T(8,128)S(1)}, f32[16,256]{1,0:T(8,128)S(1)}) custom-call(s32[9]{0:T(128)S(1)} %stack.70.where, bf16[8,1040,512]{2,1,0:T(8,128)(2,1)S(1)} %get-tuple-element.112.lhs.refs_0_, bf16[1040,512]{1,0:T(8,128)(2,1)S(1)} %collective-permute-done.19.refs_1_, ...), custom_call_target="tpu_custom_call" | custom-call | flops 4089446400 | bytes 12582912 | tf_op jit(solution)/shard_map/pallas_call | solution.py:245
  127.4 0.2 collective-permute-start.24
  127.6 1.3 collective-permute-start.25
  128.9 0.7 collective-permute-start.26
  129.6 2.6 %shard_map.69.y0 = f32[1024,256]{1,0:T(8,128)S(1)} custom-call(f32[1024,256]{1,0:T(8,128)S(1)} %get-tuple-element.128.prod_ref, f32[128,256]{1,0:T(8,128)S(1)} %get-tuple-element.129.u_ref, f32[64,256]{1,0:T(8,128)S(1)} %get-tuple-element.119.refs_12_.prm.p0), custom_call_target="tpu_custom_call" | custom-call | flops 16777216 | bytes 12582912 | tf_op jit(solution)/shard_map/pallas_call | solution.py:294
  132.2 0.0 collective-permute-done.24
  132.2 0.6 collective-permute-done.26
  132.9 0.1 collective-permute-start.27
  133.0 2.4 %collective-permute-start.28 = (f32[16,512]{1,0:T(8,128)S(1)}, f32[16,512]{1,0:T(8,128)S(1)}, u32[]{:S(2)}, u32[]{:S(2)}) collective-permute-start(f32[16,512]{1,0:T(8,128)S(1)} %get-tuple-element.148), channel_id=1, source_target_pairs={{0,32},{1,33},{2,34},{3,35},{4,36},{5,37},{6,38},{7,39},{8,40},{9,... | collective-permute-start | bytes 98312 | tf_op jit(solution)/shard_map/ppermute | solution.py:41
  135.4 0.5 collective-permute-start.29
  135.9 2.6 %shard_map.70.y1 = f32[1024,256]{1,0:T(8,128)S(1)} custom-call(f32[1024,256]{1,0:T(8,128)S(1)} %get-tuple-element.131.prod_ref, f32[128,256]{1,0:T(8,128)S(1)} %get-tuple-element.132.u_ref, f32[64,256]{1,0:T(8,128)S(1)} %get-tuple-element.123.refs_12_.prm.p1), custom_call_target="tpu_custom_call" | custom-call | flops 16777216 | bytes 12582912 | tf_op jit(solution)/shard_map/pallas_call | solution.py:294
  138.5 0.0 collective-permute-done.28.two
  138.5 0.0 collective-permute-done.29.down
  138.5 4.0 %shard_map.71 = bf16[1024,512]{1,0:T(8,128)(2,1)} custom-call(s32[1]{0:T(128)} %bitcast.15.core_ref, f32[1024,256]{1,0:T(8,128)S(1)} %shard_map.69.y0, f32[1024,256]{1,0:T(8,128)S(1)} %shard_map.70.y1, f32[1024,256]{1,0:T(8,128)S(1)} %get-tuple-element.133.x0, f32[1024,256]{1,0:T(8,128)S(1)} %get-tuple-element.134.x1, ...), custom_call_target="tpu_custom_call" | custom-call | tf_op jit(solution)/shard_map/pallas_call | solution.py:341
  (25 shorter events, 0.2 us)
Async XLA Ops:
  0.0 2.7 %copy-start = (f32[3,3,4096]{2,1,0:T(4,128)S(1)}, f32[3,3,4096]{2,1,0:T(4,128)}, u32[]{:S(2)}) copy-start(f32[3,3,4096]{2,1,0:T(4,128)} %param.8) | copy-start | bytes 442372
  0.0 4.5 %copy-start.1 = (bf16[1024,512]{1,0:T(8,128)(2,1)S(1)}, bf16[1024,512]{1,0:T(8,128)(2,1)}, u32[]{:S(2)}) copy-start(bf16[1024,512]{1,0:T(8,128)(2,1)} %param.6) | copy-start | bytes 3145732
  0.0 13.6 %collective-permute-start.1 = (bf16[3,512,256]{2,1,0:T(8,128)(2,1)}, bf16[3,512,256]{2,1,0:T(8,128)(2,1)S(1)}, u32[]{:S(2)}, u32[]{:S(2)}) collective-permute-start(bf16[3,512,256]{2,1,0:T(8,128)(2,1)} %bitcast.73), channel_id=1, source_target_pairs={{0,0},{1,16},{2,32},{3,48},{4,64},{5,80},{6,96},{7,112},{8,8},{9,2... | collective-permute-start | bytes 2359304 | tf_op jit(solution)/shard_map/ppermute | solution.py:41
  5.1 7.7 %collective-permute-start = (bf16[16,512]{1,0:T(8,128)(2,1)}, bf16[16,512]{1,0:T(8,128)(2,1)}, u32[]{:S(2)}, u32[]{:S(2)}) collective-permute-start(bf16[16,512]{1,0:T(8,128)(2,1)} %slice.27), channel_id=1, source_target_pairs={{0,8},{1,9},{2,10},{3,11},{4,12},{5,13},{6,14},{7,15},{8,16},{9,17... | collective-permute-start | bytes 49160 | tf_op jit(solution)/shard_map/ppermute | solution.py:41
  13.6 37.3 %collective-permute-start.2 = (bf16[1040,512]{1,0:T(8,128)(2,1)S(1)}, bf16[1040,512]{1,0:T(8,128)(2,1)S(1)}, u32[]{:S(2)}, u32[]{:S(2)}) collective-permute-start(bf16[1040,512]{1,0:T(8,128)(2,1)S(1)} %pad_maximum_fusion.refs_0_), channel_id=1, source_target_pairs={{0,1},{1,2},{2,3},{3,0},{4,5},{5,6},{6,7},{7,4},{8,9},{9,10},{10,1... | collective-permute-start | bytes 3194888 | tf_op jit(solution)/shard_map/ppermute | solution.py:41
  25.5 25.4 %collective-permute-start.3 = (bf16[1040,512]{1,0:T(8,128)(2,1)S(1)}, bf16[1040,512]{1,0:T(8,128)(2,1)S(1)}, u32[]{:S(2)}, u32[]{:S(2)}) collective-permute-start(bf16[1040,512]{1,0:T(8,128)(2,1)S(1)} %pad_maximum_fusion.refs_0_), channel_id=1, source_target_pairs={{0,3},{1,0},{2,1},{3,2},{4,7},{5,4},{6,5},{7,6},{8,11},{9,8},{10,9... | collective-permute-start | bytes 3194888 | tf_op jit(solution)/shard_map/ppermute | solution.py:41
  28.8 25.8 %collective-permute-start.4 = (bf16[1040,512]{1,0:T(8,128)(2,1)S(1)}, bf16[1040,512]{1,0:T(8,128)(2,1)S(1)}, u32[]{:S(2)}, u32[]{:S(2)}) collective-permute-start(bf16[1040,512]{1,0:T(8,128)(2,1)S(1)} %pad_maximum_fusion.refs_0_), channel_id=1, source_target_pairs={{0,4},{1,5},{2,6},{3,7},{4,0},{5,1},{6,2},{7,3},{8,12},{9,13},{10,... | collective-permute-start | bytes 3194888 | tf_op jit(solution)/shard_map/ppermute | solution.py:41
  32.7 18.1 %collective-permute-start.5 = (bf16[3,512,256]{2,1,0:T(8,128)(2,1)S(1)}, bf16[3,512,256]{2,1,0:T(8,128)(2,1)S(1)}, u32[]{:S(2)}, u32[]{:S(2)}) collective-permute-start(bf16[3,512,256]{2,1,0:T(8,128)(2,1)S(1)} %collective-permute-done.1.refs_6_.refs_4_), channel_id=1, source_target_pairs={{0,16},{1,17},{2,18},{3,19},{4,20},{5,21},{6,22},{7,23},{8,24},{9,... | collective-permute-start | bytes 2359304 | tf_op jit(solution)/shard_map/ppermute | solution.py:41
  32.7 18.1 %collective-permute-start.6 = (bf16[3,512,256]{2,1,0:T(8,128)(2,1)S(1)}, bf16[3,512,256]{2,1,0:T(8,128)(2,1)S(1)}, u32[]{:S(2)}, u32[]{:S(2)}) collective-permute-start(bf16[3,512,256]{2,1,0:T(8,128)(2,1)S(1)} %collective-permute-done.1.refs_6_.refs_4_), channel_id=1, source_target_pairs={{0,48},{1,49},{2,50},{3,51},{4,52},{5,53},{6,54},{7,55},{8,56},{9,... | collective-permute-start | bytes 2359304 | tf_op jit(solution)/shard_map/ppermute | solution.py:41
  54.7 5.7 %collective-permute-start.7 = (bf16[3,512,256]{2,1,0:T(8,128)(2,1)S(1)}, bf16[3,512,256]{2,1,0:T(8,128)(2,1)S(1)}, u32[]{:S(2)}, u32[]{:S(2)}) collective-permute-start(bf16[3,512,256]{2,1,0:T(8,128)(2,1)S(1)} %collective-permute-done.1.refs_6_.refs_4_), channel_id=1, source_target_pairs={{0,8},{1,9},{2,10},{3,11},{4,12},{5,13},{6,14},{7,15},{8,0},{9,1},... | collective-permute-start | bytes 2359304 | tf_op jit(solution)/shard_map/ppermute | solution.py:41
  57.1 3.2 %collective-permute-start.8 = (bf16[3,512,256]{2,1,0:T(8,128)(2,1)S(1)}, bf16[3,512,256]{2,1,0:T(8,128)(2,1)S(1)}, u32[]{:S(2)}, u32[]{:S(2)}) collective-permute-start(bf16[3,512,256]{2,1,0:T(8,128)(2,1)S(1)} %collective-permute-done.5.refs_7_.refs_5_), channel_id=1, source_target_pairs={{0,8},{1,9},{2,10},{3,11},{4,12},{5,13},{6,14},{7,15},{8,0},{9,1},... | collective-permute-start | bytes 2359304 | tf_op jit(solution)/shard_map/ppermute | solution.py:41
  57.1 4.2 %collective-permute-start.9 = (bf16[3,512,256]{2,1,0:T(8,128)(2,1)S(1)}, bf16[3,512,256]{2,1,0:T(8,128)(2,1)S(1)}, u32[]{:S(2)}, u32[]{:S(2)}) collective-permute-start(bf16[3,512,256]{2,1,0:T(8,128)(2,1)S(1)} %collective-permute-done.6.refs_8_.refs_6_), channel_id=1, source_target_pairs={{0,8},{1,9},{2,10},{3,11},{4,12},{5,13},{6,14},{7,15},{8,0},{9,1},... | collective-permute-start | bytes 2359304 | tf_op jit(solution)/shard_map/ppermute | solution.py:41
  57.6 26.4 %collective-permute-start.10 = (bf16[1040,512]{1,0:T(8,128)(2,1)S(1)}, bf16[1040,512]{1,0:T(8,128)(2,1)S(1)}, u32[]{:S(2)}, u32[]{:S(2)}) collective-permute-start(bf16[1040,512]{1,0:T(8,128)(2,1)S(1)} %collective-permute-done.4.refs_3_), channel_id=1, source_target_pairs={{0,1},{1,2},{2,3},{3,0},{4,5},{5,6},{6,7},{7,4},{8,9},{9,10},{10,1... | collective-permute-start | bytes 3194888 | tf_op jit(solution)/shard_map/ppermute | solution.py:41
  57.6 26.4 %collective-permute-start.11 = (bf16[1040,512]{1,0:T(8,128)(2,1)S(1)}, bf16[1040,512]{1,0:T(8,128)(2,1)S(1)}, u32[]{:S(2)}, u32[]{:S(2)}) collective-permute-start(bf16[1040,512]{1,0:T(8,128)(2,1)S(1)} %collective-permute-done.4.refs_3_), channel_id=1, source_target_pairs={{0,3},{1,0},{2,1},{3,2},{4,7},{5,4},{6,5},{7,6},{8,11},{9,8},{10,9... | collective-permute-start | bytes 3194888 | tf_op jit(solution)/shard_map/ppermute | solution.py:41
  61.3 22.7 %collective-permute-start.12 = (bf16[3,512,256]{2,1,0:T(8,128)(2,1)S(1)}, bf16[3,512,256]{2,1,0:T(8,128)(2,1)S(1)}, u32[]{:S(2)}, u32[]{:S(2)}) collective-permute-start(bf16[3,512,256]{2,1,0:T(8,128)(2,1)S(1)} %collective-permute-done.5.refs_7_.refs_5_), channel_id=1, source_target_pairs={{0,16},{1,17},{2,18},{3,19},{4,20},{5,21},{6,22},{7,23},{8,24},{9,... | collective-permute-start | bytes 2359304 | tf_op jit(solution)/shard_map/ppermute | solution.py:41
  61.3 22.7 %collective-permute-start.13 = (bf16[3,512,256]{2,1,0:T(8,128)(2,1)S(1)}, bf16[3,512,256]{2,1,0:T(8,128)(2,1)S(1)}, u32[]{:S(2)}, u32[]{:S(2)}) collective-permute-start(bf16[3,512,256]{2,1,0:T(8,128)(2,1)S(1)} %collective-permute-done.1.refs_6_.refs_4_), channel_id=1, source_target_pairs={{0,64},{1,65},{2,66},{3,67},{4,68},{5,69},{6,70},{7,71},{8,72},{9,... | collective-permute-start | bytes 2359304 | tf_op jit(solution)/shard_map/ppermute | solution.py:41
  84.0 3.6 %collective-permute-start.14 = (bf16[3,512,256]{2,1,0:T(8,128)(2,1)S(1)}, bf16[3,512,256]{2,1,0:T(8,128)(2,1)S(1)}, u32[]{:S(2)}, u32[]{:S(2)}) collective-permute-start(bf16[3,512,256]{2,1,0:T(8,128)(2,1)S(1)} %collective-permute-done.12.refs_9_.refs_7_), channel_id=1, source_target_pairs={{0,8},{1,9},{2,10},{3,11},{4,12},{5,13},{6,14},{7,15},{8,0},{9,1},... | collective-permute-start | bytes 2359304 | tf_op jit(solution)/shard_map/ppermute | solution.py:41
  84.9 3.0 %collective-permute-start.15 = (bf16[3,512,256]{2,1,0:T(8,128)(2,1)S(1)}, bf16[3,512,256]{2,1,0:T(8,128)(2,1)S(1)}, u32[]{:S(2)}, u32[]{:S(2)}) collective-permute-start(bf16[3,512,256]{2,1,0:T(8,128)(2,1)S(1)} %collective-permute-done.13.refs_0_.refs_8_), channel_id=1, source_target_pairs={{0,8},{1,9},{2,10},{3,11},{4,12},{5,13},{6,14},{7,15},{8,0},{9,1},... | collective-permute-start | bytes 2359304 | tf_op jit(solution)/shard_map/ppermute | solution.py:41
  85.0 26.4 %collective-permute-start.19 = (bf16[1040,512]{1,0:T(8,128)(2,1)S(1)}, bf16[1040,512]{1,0:T(8,128)(2,1)S(1)}, u32[]{:S(2)}, u32[]{:S(2)}) collective-permute-start(bf16[1040,512]{1,0:T(8,128)(2,1)S(1)} %collective-permute-done.2.refs_1_), channel_id=1, source_target_pairs={{0,1},{1,2},{2,3},{3,0},{4,5},{5,6},{6,7},{7,4},{8,9},{9,10},{10,1... | collective-permute-start | bytes 3194888 | tf_op jit(solution)/shard_map/ppermute | solution.py:41
  85.0 26.4 %collective-permute-start.20 = (bf16[1040,512]{1,0:T(8,128)(2,1)S(1)}, bf16[1040,512]{1,0:T(8,128)(2,1)S(1)}, u32[]{:S(2)}, u32[]{:S(2)}) collective-permute-start(bf16[1040,512]{1,0:T(8,128)(2,1)S(1)} %collective-permute-done.11.refs_5_), channel_id=1, source_target_pairs={{0,3},{1,0},{2,1},{3,2},{4,7},{5,4},{6,5},{7,6},{8,11},{9,8},{10,9... | collective-permute-start | bytes 3194888 | tf_op jit(solution)/shard_map/ppermute | solution.py:41
  87.6 19.3 %collective-permute-start.16 = (bf16[3,512,256]{2,1,0:T(8,128)(2,1)S(1)}, bf16[3,512,256]{2,1,0:T(8,128)(2,1)S(1)}, u32[]{:S(2)}, u32[]{:S(2)}) collective-permute-start(bf16[3,512,256]{2,1,0:T(8,128)(2,1)S(1)} %collective-permute-done.13.refs_0_.refs_8_), channel_id=1, source_target_pairs={{0,16},{1,17},{2,18},{3,19},{4,20},{5,21},{6,22},{7,23},{8,24},{9,... | collective-permute-start | bytes 2359304 | tf_op jit(solution)/shard_map/ppermute | solution.py:41
  87.9 19.0 %collective-permute-start.17 = (bf16[3,512,256]{2,1,0:T(8,128)(2,1)S(1)}, bf16[3,512,256]{2,1,0:T(8,128)(2,1)S(1)}, u32[]{:S(2)}, u32[]{:S(2)}) collective-permute-start(bf16[3,512,256]{2,1,0:T(8,128)(2,1)S(1)} %collective-permute-done.13.refs_0_.refs_8_), channel_id=1, source_target_pairs={{0,48},{1,49},{2,50},{3,51},{4,52},{5,53},{6,54},{7,55},{8,56},{9,... | collective-permute-start | bytes 2359304 | tf_op jit(solution)/shard_map/ppermute | solution.py:41
  90.3 17.5 %collective-permute-start.18 = (bf16[3,512,256]{2,1,0:T(8,128)(2,1)S(1)}, bf16[3,512,256]{2,1,0:T(8,128)(2,1)S(1)}, u32[]{:S(2)}, u32[]{:S(2)}) collective-permute-start(bf16[3,512,256]{2,1,0:T(8,128)(2,1)S(1)} %collective-permute-done.12.refs_9_.refs_7_), channel_id=1, source_target_pairs={{0,64},{1,65},{2,66},{3,67},{4,68},{5,69},{6,70},{7,71},{8,72},{9,... | collective-permute-start | bytes 2359304 | tf_op jit(solution)/shard_map/ppermute | solution.py:41
  111.4 8.1 %collective-permute-start.21 = (bf16[3,512,256]{2,1,0:T(8,128)(2,1)S(1)}, bf16[3,512,256]{2,1,0:T(8,128)(2,1)S(1)}, u32[]{:S(2)}, u32[]{:S(2)}) collective-permute-start(bf16[3,512,256]{2,1,0:T(8,128)(2,1)S(1)} %collective-permute-done.16.refs_1_.refs_9_), channel_id=1, source_target_pairs={{0,8},{1,9},{2,10},{3,11},{4,12},{5,13},{6,14},{7,15},{8,0},{9,1},... | collective-permute-start | bytes 2359304 | tf_op jit(solution)/shard_map/ppermute | solution.py:41
  113.9 5.5 %collective-permute-start.22 = (bf16[3,512,256]{2,1,0:T(8,128)(2,1)S(1)}, bf16[3,512,256]{2,1,0:T(8,128)(2,1)S(1)}, u32[]{:S(2)}, u32[]{:S(2)}) collective-permute-start(bf16[3,512,256]{2,1,0:T(8,128)(2,1)S(1)} %collective-permute-done.17.refs_2_.refs_10_), channel_id=1, source_target_pairs={{0,8},{1,9},{2,10},{3,11},{4,12},{5,13},{6,14},{7,15},{8,0},{9,1},... | collective-permute-start | bytes 2359304 | tf_op jit(solution)/shard_map/ppermute | solution.py:41
  114.0 5.4 %collective-permute-start.23 = (bf16[3,512,256]{2,1,0:T(8,128)(2,1)S(1)}, bf16[3,512,256]{2,1,0:T(8,128)(2,1)S(1)}, u32[]{:S(2)}, u32[]{:S(2)}) collective-permute-start(bf16[3,512,256]{2,1,0:T(8,128)(2,1)S(1)} %collective-permute-done.18.refs_3_.refs_11_), channel_id=1, source_target_pairs={{0,8},{1,9},{2,10},{3,11},{4,12},{5,13},{6,14},{7,15},{8,0},{9,1},... | collective-permute-start | bytes 2359304 | tf_op jit(solution)/shard_map/ppermute | solution.py:41
  127.4 4.8 %collective-permute-start.24 = (f32[16,512]{1,0:T(8,128)S(1)}, f32[16,512]{1,0:T(8,128)S(1)}, u32[]{:S(2)}, u32[]{:S(2)}) collective-permute-start(f32[16,512]{1,0:T(8,128)S(1)} %pad_maximum_fusion.3), channel_id=1, source_target_pairs={{0,8},{1,9},{2,10},{3,11},{4,12},{5,13},{6,14},{7,15},{8,0},{9,1},... | collective-permute-start | bytes 98312 | tf_op jit(solution)/shard_map/ppermute | solution.py:41
  127.6 4.7 %collective-permute-start.25 = (f32[16,512]{1,0:T(8,128)S(1)}, f32[16,512]{1,0:T(8,128)S(1)}, u32[]{:S(2)}, u32[]{:S(2)}) collective-permute-start(f32[16,512]{1,0:T(8,128)S(1)} %pad_maximum_fusion.3), channel_id=1, source_target_pairs={{0,64},{1,65},{2,66},{3,67},{4,68},{5,69},{6,70},{7,71},{8,72},{9,... | collective-permute-start | bytes 98312 | tf_op jit(solution)/shard_map/ppermute | solution.py:41
  128.9 4.0 %collective-permute-start.26 = (f32[16,512]{1,0:T(8,128)S(1)}, f32[16,512]{1,0:T(8,128)S(1)}, u32[]{:S(2)}, u32[]{:S(2)}) collective-permute-start(f32[16,512]{1,0:T(8,128)S(1)} %pad_maximum_fusion.3), channel_id=1, source_target_pairs={{0,72},{1,73},{2,74},{3,75},{4,76},{5,77},{6,78},{7,79},{8,64},{9,... | collective-permute-start | bytes 98312 | tf_op jit(solution)/shard_map/ppermute | solution.py:41
  132.9 5.5 %collective-permute-start.27 = (f32[16,512]{1,0:T(8,128)S(1)}, f32[16,512]{1,0:T(8,128)S(1)}, u32[]{:S(2)}, u32[]{:S(2)}) collective-permute-start(f32[16,512]{1,0:T(8,128)S(1)} %get-tuple-element.149), channel_id=1, source_target_pairs={{0,16},{1,17},{2,18},{3,19},{4,20},{5,21},{6,22},{7,23},{8,24},{9,... | collective-permute-start | bytes 98312 | tf_op jit(solution)/shard_map/ppermute | solution.py:41
  133.0 5.5 %collective-permute-start.28 = (f32[16,512]{1,0:T(8,128)S(1)}, f32[16,512]{1,0:T(8,128)S(1)}, u32[]{:S(2)}, u32[]{:S(2)}) collective-permute-start(f32[16,512]{1,0:T(8,128)S(1)} %get-tuple-element.148), channel_id=1, source_target_pairs={{0,32},{1,33},{2,34},{3,35},{4,36},{5,37},{6,38},{7,39},{8,40},{9,... | collective-permute-start | bytes 98312 | tf_op jit(solution)/shard_map/ppermute | solution.py:41
  135.4 3.1 %collective-permute-start.29 = (f32[16,512]{1,0:T(8,128)S(1)}, f32[16,512]{1,0:T(8,128)S(1)}, u32[]{:S(2)}, u32[]{:S(2)}) collective-permute-start(f32[16,512]{1,0:T(8,128)S(1)} %get-tuple-element.143), channel_id=1, source_target_pairs={{0,48},{1,49},{2,50},{3,51},{4,52},{5,53},{6,54},{7,55},{8,56},{9,... | collective-permute-start | bytes 98312 | tf_op jit(solution)/shard_map/ppermute | solution.py:41

commit v10 on v9

--- a/solution.py
+++ b/solution.py
@@ -399,9 +399,10 @@
     t, b, where, core_at, shard, scale, own, lower, *prms = together(
         (t, b, where, core_at, shard, scale, own, lower, *prms)
     )
-    tp_, tm, ty = along_z(t, 1), along_z(t, -1), other_yhi(t)
+    ty = other_yhi(t)
+    tp_, tm = along_z(t, 1), along_z(t, -1)
     bp, bm = along_x(b, 1), along_x(b, -1)
-    t, b, tp_, tm, ty, bp, bm = together((t, b, tp_, tm, ty, bp, bm))
+    ty, t, b, tp_, tm, bp, bm = together((ty, t, b, tp_, tm, bp, bm))
     typ, tym = along_z(ty, 1), along_z(ty, -1)
     cb, cbp, cbm = other_core(b), other_core(bp), other_core(bm)
     b, bp, cb, cbp, cbm = together((b, bp, cb, cbp, cbm))

time: 143 us -> 142 us (level)
  starting transfers between devices: 52.8 us -> 50.2 us
  waiting for transfers between devices: 50.8 us -> 52.9 us
    ppermute x30, starting transfers between devices: 52.8 us -> 50.2 us  [send(): return lax.ppermute(value, ('ctx', 'tp'), route(move))]
    ppermute x30, waiting for transfers between devices: 50.8 us -> 52.9 us  [send(): return lax.ppermute(value, ('ctx', 'tp'), route(move))]
  transfers between devices with their start and end apart: 30 -> 30, of which waited for: 10 -> 8; matrix products, arithmetic and copies ran while one was open for 3% -> 3% of each run, Pallas kernels for 15% -> 15%
where the time goes in v10:
time: 142 us
  waiting for transfers between devices  52.9 us (37%)
  starting transfers between devices  50.2 us (35%)
  Pallas kernels  33.6 us (24%)
  other arithmetic  2.45 us (2%)
  local copies, waits for them, and re-layouts  2.14 us (2%)
    ppermute x30, waiting for transfers between devices, send(): return lax.ppermute(value, ('ctx', 'tp'), route(move))  52.9 us
    ppermute x30, starting transfers between devices, send(): return lax.ppermute(value, ('ctx', 'tp'), route(move))  50.2 us
    pallas_call x2, Pallas kernels, project(): pl.pallas_call(functools.partial(project_kernel, rows, few), out_shape=[j...  12.9 us
    pallas_call x2, Pallas kernels, read(): pl.pallas_call(functools.partial(read_kernel, rows), out_shape=jax.ShapeD...  5.19 us
    pallas_call x1, Pallas kernels, begin(): pl.pallas_call(begin_kernel, out_shape=[jax.ShapeDtypeStruct((8, tall, BL...  4.14 us
    pallas_call x1, Pallas kernels, gate(): pl.pallas_call(functools.partial(gate_kernel, rows), out_shape=jax.ShapeD...  3.96 us
    pallas_call x1, Pallas kernels, also(): pl.pallas_call(also_kernel, out_shape=jax.ShapeDtypeStruct((tall, width),...  3.9 us
    pallas_call x1, Pallas kernels, more(): pl.pallas_call(more_kernel, out_shape=jax.ShapeDtypeStruct((tall, width),...  3.54 us
  transfers between devices with their start and end apart: 30, of which 8 were waited for; matrix products, arithmetic and copies ran while one was open for 3% of the time, Pallas kernels for 15%

profile of v10, /device:TPU:1, one launch (start us, length us, event | category | flops | bytes accessed | tf_op | source)
XLA Modules:
  0.0 141.8 jit_solution(13123324329134625037)
XLA Ops:
  0.0 1.9 %collective-permute-start.1 = (bf16[3,512,256]{2,1,0:T(8,128)(2,1)}, bf16[3,512,256]{2,1,0:T(8,128)(2,1)S(1)}, u32[]{:S(2)}, u32[]{:S(2)}) collective-permute-start(bf16[3,512,256]{2,1,0:T(8,128)(2,1)} %bitcast.73), channel_id=1, source_target_pairs={{0,0},{1,16},{2,32},{3,48},{4,64},{5,80},{6,96},{7,112},{8,8},{9,2... | collective-permute-start | bytes 2359304 | tf_op jit(solution)/shard_map/ppermute | solution.py:41
  1.9 0.8 select_bitcast_fusion.3
  2.9 0.8 dynamic_slice.21
  3.6 0.8 select_bitcast_fusion.2
  4.5 0.6 slice.27
  5.1 6.6 %collective-permute-start = (bf16[16,512]{1,0:T(8,128)(2,1)}, bf16[16,512]{1,0:T(8,128)(2,1)}, u32[]{:S(2)}, u32[]{:S(2)}) collective-permute-start(bf16[16,512]{1,0:T(8,128)(2,1)} %slice.27), channel_id=1, source_target_pairs={{0,8},{1,9},{2,10},{3,11},{4,12},{5,13},{6,14},{7,15},{8,16},{9,17... | collective-permute-start | bytes 49160 | tf_op jit(solution)/shard_map/ppermute | solution.py:41
  12.0 0.6 copy.9
  12.6 0.1 stack.70.where
  12.7 0.1 collective-permute-done
  12.8 0.8 pad_maximum_fusion.refs_0_
  13.6 0.0 collective-permute-done.1.refs_6_.refs_4_
  13.6 10.8 %collective-permute-start.2 = (bf16[1040,512]{1,0:T(8,128)(2,1)S(1)}, bf16[1040,512]{1,0:T(8,128)(2,1)S(1)}, u32[]{:S(2)}, u32[]{:S(2)}) collective-permute-start(bf16[1040,512]{1,0:T(8,128)(2,1)S(1)} %pad_maximum_fusion.refs_0_), channel_id=1, source_target_pairs={{0,4},{1,5},{2,6},{3,7},{4,0},{5,1},{6,2},{7,3},{8,12},{9,13},{10,... | collective-permute-start | bytes 3194888 | tf_op jit(solution)/shard_map/ppermute | solution.py:41
  24.4 4.9 %collective-permute-start.3 = (bf16[1040,512]{1,0:T(8,128)(2,1)S(1)}, bf16[1040,512]{1,0:T(8,128)(2,1)S(1)}, u32[]{:S(2)}, u32[]{:S(2)}) collective-permute-start(bf16[1040,512]{1,0:T(8,128)(2,1)S(1)} %pad_maximum_fusion.refs_0_), channel_id=1, source_target_pairs={{0,1},{1,2},{2,3},{3,0},{4,5},{5,6},{6,7},{7,4},{8,9},{9,10},{10,1... | collective-permute-start | bytes 3194888 | tf_op jit(solution)/shard_map/ppermute | solution.py:41
  29.3 3.3 %collective-permute-start.4 = (bf16[1040,512]{1,0:T(8,128)(2,1)S(1)}, bf16[1040,512]{1,0:T(8,128)(2,1)S(1)}, u32[]{:S(2)}, u32[]{:S(2)}) collective-permute-start(bf16[1040,512]{1,0:T(8,128)(2,1)S(1)} %pad_maximum_fusion.refs_0_), channel_id=1, source_target_pairs={{0,3},{1,0},{2,1},{3,2},{4,7},{5,4},{6,5},{7,6},{8,11},{9,8},{10,9... | collective-permute-start | bytes 3194888 | tf_op jit(solution)/shard_map/ppermute | solution.py:41
  32.7 0.0 collective-permute-start.5
  32.7 2.7 %collective-permute-start.6 = (bf16[3,512,256]{2,1,0:T(8,128)(2,1)S(1)}, bf16[3,512,256]{2,1,0:T(8,128)(2,1)S(1)}, u32[]{:S(2)}, u32[]{:S(2)}) collective-permute-start(bf16[3,512,256]{2,1,0:T(8,128)(2,1)S(1)} %collective-permute-done.1.refs_6_.refs_4_), channel_id=1, source_target_pairs={{0,48},{1,49},{2,50},{3,51},{4,52},{5,53},{6,54},{7,55},{8,56},{9,... | collective-permute-start | bytes 2359304 | tf_op jit(solution)/shard_map/ppermute | solution.py:41
  35.3 15.5 %collective-permute-done.5.refs_7_.refs_5_ = bf16[3,512,256]{2,1,0:T(8,128)(2,1)S(1)} collective-permute-done((bf16[3,512,256]{2,1,0:T(8,128)(2,1)S(1)}, bf16[3,512,256]{2,1,0:T(8,128)(2,1)S(1)}, u32[]{:S(2)}, u32[]{:S(2)}) %collective-permute-start.5) | collective-permute-done | bytes 786464 | tf_op jit(solution)/shard_map/ppermute | solution.py:41
  50.8 0.0 collective-permute-done.6.refs_8_.refs_6_
  50.8 0.0 collective-permute-done.2.refs_3_
  50.8 3.8 %collective-permute-done.3.refs_1_ = bf16[1040,512]{1,0:T(8,128)(2,1)S(1)} collective-permute-done((bf16[1040,512]{1,0:T(8,128)(2,1)S(1)}, bf16[1040,512]{1,0:T(8,128)(2,1)S(1)}, u32[]{:S(2)}, u32[]{:S(2)}) %collective-permute-start.3) | collective-permute-done | bytes 1064992 | tf_op jit(solution)/shard_map/ppermute | solution.py:41
  54.6 0.0 collective-permute-done.4.refs_2_
  54.6 2.5 %collective-permute-start.7 = (bf16[3,512,256]{2,1,0:T(8,128)(2,1)S(1)}, bf16[3,512,256]{2,1,0:T(8,128)(2,1)S(1)}, u32[]{:S(2)}, u32[]{:S(2)}) collective-permute-start(bf16[3,512,256]{2,1,0:T(8,128)(2,1)S(1)} %collective-permute-done.1.refs_6_.refs_4_), channel_id=1, source_target_pairs={{0,8},{1,9},{2,10},{3,11},{4,12},{5,13},{6,14},{7,15},{8,0},{9,1},... | collective-permute-start | bytes 2359304 | tf_op jit(solution)/shard_map/ppermute | solution.py:41
  57.1 0.0 collective-permute-start.8
  57.1 0.5 collective-permute-start.9
  57.6 0.9 collective-permute-start.10
  58.5 1.8 %collective-permute-start.11 = (bf16[1040,512]{1,0:T(8,128)(2,1)S(1)}, bf16[1040,512]{1,0:T(8,128)(2,1)S(1)}, u32[]{:S(2)}, u32[]{:S(2)}) collective-permute-start(bf16[1040,512]{1,0:T(8,128)(2,1)S(1)} %collective-permute-done.2.refs_3_), channel_id=1, source_target_pairs={{0,3},{1,0},{2,1},{3,2},{4,7},{5,4},{6,5},{7,6},{8,11},{9,8},{10,9... | collective-permute-start | bytes 3194888 | tf_op jit(solution)/shard_map/ppermute | solution.py:41
  60.3 0.0 collective-permute-done.7.refs_1_.refs_4_
  60.3 0.0 collective-permute-done.8.refs_2_.refs_5_
  60.3 1.0 collective-permute-done.9.refs_3_.refs_6_
  61.3 22.7 %collective-permute-done.10.refs_4_ = bf16[1040,512]{1,0:T(8,128)(2,1)S(1)} collective-permute-done((bf16[1040,512]{1,0:T(8,128)(2,1)S(1)}, bf16[1040,512]{1,0:T(8,128)(2,1)S(1)}, u32[]{:S(2)}, u32[]{:S(2)}) %collective-permute-start.10) | collective-permute-done | bytes 1064992 | tf_op jit(solution)/shard_map/ppermute | solution.py:41
  84.0 0.0 collective-permute-done.11.refs_5_
  84.0 0.0 collective-permute-done.12.refs_9_.refs_7_
  84.0 0.0 collective-permute-done.13.refs_0_.refs_8_
  84.0 0.9 collective-permute-start.14
  84.9 0.1 collective-permute-start.15
  85.0 1.0 collective-permute-start.19
  86.0 1.7 %collective-permute-start.20 = (bf16[1040,512]{1,0:T(8,128)(2,1)S(1)}, bf16[1040,512]{1,0:T(8,128)(2,1)S(1)}, u32[]{:S(2)}, u32[]{:S(2)}) collective-permute-start(bf16[1040,512]{1,0:T(8,128)(2,1)S(1)} %collective-permute-done.11.refs_5_), channel_id=1, source_target_pairs={{0,3},{1,0},{2,1},{3,2},{4,7},{5,4},{6,5},{7,6},{8,11},{9,8},{10,9... | collective-permute-start | bytes 3194888 | tf_op jit(solution)/shard_map/ppermute | solution.py:41
  87.6 0.3 collective-permute-done.15.refs_8_
  87.9 2.4 %collective-permute-start.17 = (bf16[3,512,256]{2,1,0:T(8,128)(2,1)S(1)}, bf16[3,512,256]{2,1,0:T(8,128)(2,1)S(1)}, u32[]{:S(2)}, u32[]{:S(2)}) collective-permute-start(bf16[3,512,256]{2,1,0:T(8,128)(2,1)S(1)} %collective-permute-done.13.refs_0_.refs_8_), channel_id=1, source_target_pairs={{0,48},{1,49},{2,50},{3,51},{4,52},{5,53},{6,54},{7,55},{8,56},{9,... | collective-permute-start | bytes 2359304 | tf_op jit(solution)/shard_map/ppermute | solution.py:41
  90.3 4.1 %shard_map.64 = (bf16[8,1040,512]{2,1,0:T(8,128)(2,1)S(1)}, f32[1040,768]{1,0:T(8,128)S(1)}) custom-call(s32[9]{0:T(128)S(1)} %stack.70.where, bf16[1040,512]{1,0:T(8,128)(2,1)S(1)} %pad_maximum_fusion.refs_0_, bf16[1040,512]{1,0:T(8,128)(2,1)S(1)} %collective-permute-done.3.refs_1_, bf16[1040,512]{1,0:T(8,128)(2,1)S(1)} %collective-permute-done.4.refs_2_, ...), custom_call_target="tpu_custom_call" | custom-call | flops 2453667840 | bytes 12582912 | tf_op jit(solution)/shard_map/pallas_call | solution.py:109
  94.5 3.9 %shard_map.66.refs_3_ = f32[1040,768]{1,0:T(8,128)S(1)} custom-call(s32[9]{0:T(128)S(1)} %stack.70.where, bf16[8,1040,512]{2,1,0:T(8,128)(2,1)S(1)} %get-tuple-element.112.lhs.refs_0_, bf16[3,512,256]{2,1,0:T(8,128)(2,1)S(1)} %collective-permute-done.7.refs_1_.refs_4_, bf16[3,512,256]{2,1,0:T(8,128)(2,1)S(1)} %collective-permute-done.8.refs_2_.refs_5_, ...), custom_call_target="tpu_custom_call" | custom-call | flops 2453667840 | bytes 12582912 | tf_op jit(solution)/shard_map/pallas_call | solution.py:127
  98.4 8.5 %collective-permute-done.16.refs_1_.refs_9_ = bf16[3,512,256]{2,1,0:T(8,128)(2,1)S(1)} collective-permute-done((bf16[3,512,256]{2,1,0:T(8,128)(2,1)S(1)}, bf16[3,512,256]{2,1,0:T(8,128)(2,1)S(1)}, u32[]{:S(2)}, u32[]{:S(2)}) %collective-permute-start.16) | collective-permute-done | bytes 786464 | tf_op jit(solution)/shard_map/ppermute | solution.py:41
  106.9 0.0 collective-permute-done.17.refs_2_.refs_10_
  106.9 0.9 collective-permute-done.18.refs_3_.refs_11_
  107.8 3.5 %shard_map.65.refs_3_ = f32[1040,768]{1,0:T(8,128)S(1)} custom-call(s32[9]{0:T(128)S(1)} %stack.70.where, bf16[8,1040,512]{2,1,0:T(8,128)(2,1)S(1)} %get-tuple-element.112.lhs.refs_0_, f32[1040,768]{1,0:T(8,128)S(1)} %get-tuple-element.106.part, bf16[3,512,256]{2,1,0:T(8,128)(2,1)S(1)} %collective-permute-done.13.refs_0_.refs_8_, ...), custom_call_target="tpu_custom_call" | custom-call | flops 2453667840 | bytes 12582912 | tf_op jit(solution)/shard_map/pallas_call | solution.py:162
  111.4 0.0 collective-permute-done.20.refs_2_
  111.4 2.5 %collective-permute-start.21 = (bf16[3,512,256]{2,1,0:T(8,128)(2,1)S(1)}, bf16[3,512,256]{2,1,0:T(8,128)(2,1)S(1)}, u32[]{:S(2)}, u32[]{:S(2)}) collective-permute-start(bf16[3,512,256]{2,1,0:T(8,128)(2,1)S(1)} %collective-permute-done.16.refs_1_.refs_9_), channel_id=1, source_target_pairs={{0,8},{1,9},{2,10},{3,11},{4,12},{5,13},{6,14},{7,15},{8,0},{9,1},... | collective-permute-start | bytes 2359304 | tf_op jit(solution)/shard_map/ppermute | solution.py:41
  113.9 0.1 collective-permute-start.22
  114.0 0.4 collective-permute-start.23
  114.4 5.0 %shard_map.67 = (f32[1024,256]{1,0:T(8,128)S(1)}, f32[1024,256]{1,0:T(8,128)S(1)}, f32[128,256]{1,0:T(8,128)S(1)}, f32[16,256]{1,0:T(8,128)S(1)}) custom-call(s32[9]{0:T(128)S(1)} %stack.70.where, bf16[8,1040,512]{2,1,0:T(8,128)(2,1)S(1)} %get-tuple-element.112.lhs.refs_0_, bf16[1040,512]{1,0:T(8,128)(2,1)S(1)} %collective-permute-done.19.refs_1_, ...), custom_call_target="tpu_custom_call" | custom-call | flops 4089446400 | bytes 12582912 | tf_op jit(solution)/shard_map/pallas_call | solution.py:245
  119.4 0.0 collective-permute-done.22.refs_10_
  119.5 0.0 collective-permute-done.23.refs_11_
  119.5 7.9 %shard_map.68 = (f32[1024,256]{1,0:T(8,128)S(1)}, f32[1024,256]{1,0:T(8,128)S(1)}, f32[128,256]{1,0:T(8,128)S(1)}, f32[16,256]{1,0:T(8,128)S(1)}) custom-call(s32[9]{0:T(128)S(1)} %stack.70.where, bf16[8,1040,512]{2,1,0:T(8,128)(2,1)S(1)} %get-tuple-element.112.lhs.refs_0_, bf16[1040,512]{1,0:T(8,128)(2,1)S(1)} %collective-permute-done.19.refs_1_, ...), custom_call_target="tpu_custom_call" | custom-call | flops 4089446400 | bytes 12582912 | tf_op jit(solution)/shard_map/pallas_call | solution.py:245
  127.4 0.2 collective-permute-start.24
  127.6 0.0 collective-permute-start.25
  127.6 2.0 %collective-permute-start.26 = (f32[16,512]{1,0:T(8,128)S(1)}, f32[16,512]{1,0:T(8,128)S(1)}, u32[]{:S(2)}, u32[]{:S(2)}) collective-permute-start(f32[16,512]{1,0:T(8,128)S(1)} %pad_maximum_fusion.3), channel_id=1, source_target_pairs={{0,72},{1,73},{2,74},{3,75},{4,76},{5,77},{6,78},{7,79},{8,64},{9,... | collective-permute-start | bytes 98312 | tf_op jit(solution)/shard_map/ppermute | solution.py:41
  129.6 2.6 %shard_map.69.y0 = f32[1024,256]{1,0:T(8,128)S(1)} custom-call(f32[1024,256]{1,0:T(8,128)S(1)} %get-tuple-element.128.prod_ref, f32[128,256]{1,0:T(8,128)S(1)} %get-tuple-element.129.u_ref, f32[64,256]{1,0:T(8,128)S(1)} %get-tuple-element.119.refs_12_.prm.p0), custom_call_target="tpu_custom_call" | custom-call | flops 16777216 | bytes 12582912 | tf_op jit(solution)/shard_map/pallas_call | solution.py:294
  132.2 0.0 collective-permute-done.25
  132.3 0.1 collective-permute-start.27
  132.4 2.4 %collective-permute-start.28 = (f32[16,512]{1,0:T(8,128)S(1)}, f32[16,512]{1,0:T(8,128)S(1)}, u32[]{:S(2)}, u32[]{:S(2)}) collective-permute-start(f32[16,512]{1,0:T(8,128)S(1)} %get-tuple-element.148), channel_id=1, source_target_pairs={{0,32},{1,33},{2,34},{3,35},{4,36},{5,37},{6,38},{7,39},{8,40},{9,... | collective-permute-start | bytes 98312 | tf_op jit(solution)/shard_map/ppermute | solution.py:41
  134.8 0.5 collective-permute-start.29
  135.2 2.6 %shard_map.70.y1 = f32[1024,256]{1,0:T(8,128)S(1)} custom-call(f32[1024,256]{1,0:T(8,128)S(1)} %get-tuple-element.131.prod_ref, f32[128,256]{1,0:T(8,128)S(1)} %get-tuple-element.132.u_ref, f32[64,256]{1,0:T(8,128)S(1)} %get-tuple-element.123.refs_12_.prm.p1), custom_call_target="tpu_custom_call" | custom-call | flops 16777216 | bytes 12582912 | tf_op jit(solution)/shard_map/pallas_call | solution.py:294
  137.8 0.0 collective-permute-done.27.up
  137.9 4.0 %shard_map.71 = bf16[1024,512]{1,0:T(8,128)(2,1)} custom-call(s32[1]{0:T(128)} %bitcast.15.core_ref, f32[1024,256]{1,0:T(8,128)S(1)} %shard_map.69.y0, f32[1024,256]{1,0:T(8,128)S(1)} %shard_map.70.y1, f32[1024,256]{1,0:T(8,128)S(1)} %get-tuple-element.133.x0, f32[1024,256]{1,0:T(8,128)S(1)} %get-tuple-element.134.x1, ...), custom_call_target="tpu_custom_call" | custom-call | tf_op jit(solution)/shard_map/pallas_call | solution.py:341
  (25 shorter events, 0.2 us)
Async XLA Ops:
  0.0 2.7 %copy-start = (f32[3,3,4096]{2,1,0:T(4,128)S(1)}, f32[3,3,4096]{2,1,0:T(4,128)}, u32[]{:S(2)}) copy-start(f32[3,3,4096]{2,1,0:T(4,128)} %param.8) | copy-start | bytes 442372
  0.0 4.5 %copy-start.1 = (bf16[1024,512]{1,0:T(8,128)(2,1)S(1)}, bf16[1024,512]{1,0:T(8,128)(2,1)}, u32[]{:S(2)}) copy-start(bf16[1024,512]{1,0:T(8,128)(2,1)} %param.6) | copy-start | bytes 3145732
  0.0 13.6 %collective-permute-start.1 = (bf16[3,512,256]{2,1,0:T(8,128)(2,1)}, bf16[3,512,256]{2,1,0:T(8,128)(2,1)S(1)}, u32[]{:S(2)}, u32[]{:S(2)}) collective-permute-start(bf16[3,512,256]{2,1,0:T(8,128)(2,1)} %bitcast.73), channel_id=1, source_target_pairs={{0,0},{1,16},{2,32},{3,48},{4,64},{5,80},{6,96},{7,112},{8,8},{9,2... | collective-permute-start | bytes 2359304 | tf_op jit(solution)/shard_map/ppermute | solution.py:41
  5.1 7.7 %collective-permute-start = (bf16[16,512]{1,0:T(8,128)(2,1)}, bf16[16,512]{1,0:T(8,128)(2,1)}, u32[]{:S(2)}, u32[]{:S(2)}) collective-permute-start(bf16[16,512]{1,0:T(8,128)(2,1)} %slice.27), channel_id=1, source_target_pairs={{0,8},{1,9},{2,10},{3,11},{4,12},{5,13},{6,14},{7,15},{8,16},{9,17... | collective-permute-start | bytes 49160 | tf_op jit(solution)/shard_map/ppermute | solution.py:41
  13.6 37.2 %collective-permute-start.2 = (bf16[1040,512]{1,0:T(8,128)(2,1)S(1)}, bf16[1040,512]{1,0:T(8,128)(2,1)S(1)}, u32[]{:S(2)}, u32[]{:S(2)}) collective-permute-start(bf16[1040,512]{1,0:T(8,128)(2,1)S(1)} %pad_maximum_fusion.refs_0_), channel_id=1, source_target_pairs={{0,4},{1,5},{2,6},{3,7},{4,0},{5,1},{6,2},{7,3},{8,12},{9,13},{10,... | collective-permute-start | bytes 3194888 | tf_op jit(solution)/shard_map/ppermute | solution.py:41
  24.4 30.3 %collective-permute-start.3 = (bf16[1040,512]{1,0:T(8,128)(2,1)S(1)}, bf16[1040,512]{1,0:T(8,128)(2,1)S(1)}, u32[]{:S(2)}, u32[]{:S(2)}) collective-permute-start(bf16[1040,512]{1,0:T(8,128)(2,1)S(1)} %pad_maximum_fusion.refs_0_), channel_id=1, source_target_pairs={{0,1},{1,2},{2,3},{3,0},{4,5},{5,6},{6,7},{7,4},{8,9},{9,10},{10,1... | collective-permute-start | bytes 3194888 | tf_op jit(solution)/shard_map/ppermute | solution.py:41
  29.3 25.3 %collective-permute-start.4 = (bf16[1040,512]{1,0:T(8,128)(2,1)S(1)}, bf16[1040,512]{1,0:T(8,128)(2,1)S(1)}, u32[]{:S(2)}, u32[]{:S(2)}) collective-permute-start(bf16[1040,512]{1,0:T(8,128)(2,1)S(1)} %pad_maximum_fusion.refs_0_), channel_id=1, source_target_pairs={{0,3},{1,0},{2,1},{3,2},{4,7},{5,4},{6,5},{7,6},{8,11},{9,8},{10,9... | collective-permute-start | bytes 3194888 | tf_op jit(solution)/shard_map/ppermute | solution.py:41
  32.7 18.1 %collective-permute-start.5 = (bf16[3,512,256]{2,1,0:T(8,128)(2,1)S(1)}, bf16[3,512,256]{2,1,0:T(8,128)(2,1)S(1)}, u32[]{:S(2)}, u32[]{:S(2)}) collective-permute-start(bf16[3,512,256]{2,1,0:T(8,128)(2,1)S(1)} %collective-permute-done.1.refs_6_.refs_4_), channel_id=1, source_target_pairs={{0,16},{1,17},{2,18},{3,19},{4,20},{5,21},{6,22},{7,23},{8,24},{9,... | collective-permute-start | bytes 2359304 | tf_op jit(solution)/shard_map/ppermute | solution.py:41
  32.7 18.1 %collective-permute-start.6 = (bf16[3,512,256]{2,1,0:T(8,128)(2,1)S(1)}, bf16[3,512,256]{2,1,0:T(8,128)(2,1)S(1)}, u32[]{:S(2)}, u32[]{:S(2)}) collective-permute-start(bf16[3,512,256]{2,1,0:T(8,128)(2,1)S(1)} %collective-permute-done.1.refs_6_.refs_4_), channel_id=1, source_target_pairs={{0,48},{1,49},{2,50},{3,51},{4,52},{5,53},{6,54},{7,55},{8,56},{9,... | collective-permute-start | bytes 2359304 | tf_op jit(solution)/shard_map/ppermute | solution.py:41
  54.6 5.7 %collective-permute-start.7 = (bf16[3,512,256]{2,1,0:T(8,128)(2,1)S(1)}, bf16[3,512,256]{2,1,0:T(8,128)(2,1)S(1)}, u32[]{:S(2)}, u32[]{:S(2)}) collective-permute-start(bf16[3,512,256]{2,1,0:T(8,128)(2,1)S(1)} %collective-permute-done.1.refs_6_.refs_4_), channel_id=1, source_target_pairs={{0,8},{1,9},{2,10},{3,11},{4,12},{5,13},{6,14},{7,15},{8,0},{9,1},... | collective-permute-start | bytes 2359304 | tf_op jit(solution)/shard_map/ppermute | solution.py:41
  57.1 3.2 %collective-permute-start.8 = (bf16[3,512,256]{2,1,0:T(8,128)(2,1)S(1)}, bf16[3,512,256]{2,1,0:T(8,128)(2,1)S(1)}, u32[]{:S(2)}, u32[]{:S(2)}) collective-permute-start(bf16[3,512,256]{2,1,0:T(8,128)(2,1)S(1)} %collective-permute-done.5.refs_7_.refs_5_), channel_id=1, source_target_pairs={{0,8},{1,9},{2,10},{3,11},{4,12},{5,13},{6,14},{7,15},{8,0},{9,1},... | collective-permute-start | bytes 2359304 | tf_op jit(solution)/shard_map/ppermute | solution.py:41
  57.1 4.2 %collective-permute-start.9 = (bf16[3,512,256]{2,1,0:T(8,128)(2,1)S(1)}, bf16[3,512,256]{2,1,0:T(8,128)(2,1)S(1)}, u32[]{:S(2)}, u32[]{:S(2)}) collective-permute-start(bf16[3,512,256]{2,1,0:T(8,128)(2,1)S(1)} %collective-permute-done.6.refs_8_.refs_6_), channel_id=1, source_target_pairs={{0,8},{1,9},{2,10},{3,11},{4,12},{5,13},{6,14},{7,15},{8,0},{9,1},... | collective-permute-start | bytes 2359304 | tf_op jit(solution)/shard_map/ppermute | solution.py:41
  57.6 26.4 %collective-permute-start.10 = (bf16[1040,512]{1,0:T(8,128)(2,1)S(1)}, bf16[1040,512]{1,0:T(8,128)(2,1)S(1)}, u32[]{:S(2)}, u32[]{:S(2)}) collective-permute-start(bf16[1040,512]{1,0:T(8,128)(2,1)S(1)} %collective-permute-done.2.refs_3_), channel_id=1, source_target_pairs={{0,1},{1,2},{2,3},{3,0},{4,5},{5,6},{6,7},{7,4},{8,9},{9,10},{10,1... | collective-permute-start | bytes 3194888 | tf_op jit(solution)/shard_map/ppermute | solution.py:41
  58.5 25.5 %collective-permute-start.11 = (bf16[1040,512]{1,0:T(8,128)(2,1)S(1)}, bf16[1040,512]{1,0:T(8,128)(2,1)S(1)}, u32[]{:S(2)}, u32[]{:S(2)}) collective-permute-start(bf16[1040,512]{1,0:T(8,128)(2,1)S(1)} %collective-permute-done.2.refs_3_), channel_id=1, source_target_pairs={{0,3},{1,0},{2,1},{3,2},{4,7},{5,4},{6,5},{7,6},{8,11},{9,8},{10,9... | collective-permute-start | bytes 3194888 | tf_op jit(solution)/shard_map/ppermute | solution.py:41
  61.3 22.7 %collective-permute-start.12 = (bf16[3,512,256]{2,1,0:T(8,128)(2,1)S(1)}, bf16[3,512,256]{2,1,0:T(8,128)(2,1)S(1)}, u32[]{:S(2)}, u32[]{:S(2)}) collective-permute-start(bf16[3,512,256]{2,1,0:T(8,128)(2,1)S(1)} %collective-permute-done.5.refs_7_.refs_5_), channel_id=1, source_target_pairs={{0,16},{1,17},{2,18},{3,19},{4,20},{5,21},{6,22},{7,23},{8,24},{9,... | collective-permute-start | bytes 2359304 | tf_op jit(solution)/shard_map/ppermute | solution.py:41
  61.3 22.7 %collective-permute-start.13 = (bf16[3,512,256]{2,1,0:T(8,128)(2,1)S(1)}, bf16[3,512,256]{2,1,0:T(8,128)(2,1)S(1)}, u32[]{:S(2)}, u32[]{:S(2)}) collective-permute-start(bf16[3,512,256]{2,1,0:T(8,128)(2,1)S(1)} %collective-permute-done.1.refs_6_.refs_4_), channel_id=1, source_target_pairs={{0,64},{1,65},{2,66},{3,67},{4,68},{5,69},{6,70},{7,71},{8,72},{9,... | collective-permute-start | bytes 2359304 | tf_op jit(solution)/shard_map/ppermute | solution.py:41
  84.0 3.6 %collective-permute-start.14 = (bf16[3,512,256]{2,1,0:T(8,128)(2,1)S(1)}, bf16[3,512,256]{2,1,0:T(8,128)(2,1)S(1)}, u32[]{:S(2)}, u32[]{:S(2)}) collective-permute-start(bf16[3,512,256]{2,1,0:T(8,128)(2,1)S(1)} %collective-permute-done.12.refs_9_.refs_7_), channel_id=1, source_target_pairs={{0,8},{1,9},{2,10},{3,11},{4,12},{5,13},{6,14},{7,15},{8,0},{9,1},... | collective-permute-start | bytes 2359304 | tf_op jit(solution)/shard_map/ppermute | solution.py:41
  84.9 3.0 %collective-permute-start.15 = (bf16[3,512,256]{2,1,0:T(8,128)(2,1)S(1)}, bf16[3,512,256]{2,1,0:T(8,128)(2,1)S(1)}, u32[]{:S(2)}, u32[]{:S(2)}) collective-permute-start(bf16[3,512,256]{2,1,0:T(8,128)(2,1)S(1)} %collective-permute-done.13.refs_0_.refs_8_), channel_id=1, source_target_pairs={{0,8},{1,9},{2,10},{3,11},{4,12},{5,13},{6,14},{7,15},{8,0},{9,1},... | collective-permute-start | bytes 2359304 | tf_op jit(solution)/shard_map/ppermute | solution.py:41
  85.0 26.4 %collective-permute-start.19 = (bf16[1040,512]{1,0:T(8,128)(2,1)S(1)}, bf16[1040,512]{1,0:T(8,128)(2,1)S(1)}, u32[]{:S(2)}, u32[]{:S(2)}) collective-permute-start(bf16[1040,512]{1,0:T(8,128)(2,1)S(1)} %collective-permute-done.3.refs_1_), channel_id=1, source_target_pairs={{0,1},{1,2},{2,3},{3,0},{4,5},{5,6},{6,7},{7,4},{8,9},{9,10},{10,1... | collective-permute-start | bytes 3194888 | tf_op jit(solution)/shard_map/ppermute | solution.py:41
  86.0 25.4 %collective-permute-start.20 = (bf16[1040,512]{1,0:T(8,128)(2,1)S(1)}, bf16[1040,512]{1,0:T(8,128)(2,1)S(1)}, u32[]{:S(2)}, u32[]{:S(2)}) collective-permute-start(bf16[1040,512]{1,0:T(8,128)(2,1)S(1)} %collective-permute-done.11.refs_5_), channel_id=1, source_target_pairs={{0,3},{1,0},{2,1},{3,2},{4,7},{5,4},{6,5},{7,6},{8,11},{9,8},{10,9... | collective-permute-start | bytes 3194888 | tf_op jit(solution)/shard_map/ppermute | solution.py:41
  87.6 19.3 %collective-permute-start.16 = (bf16[3,512,256]{2,1,0:T(8,128)(2,1)S(1)}, bf16[3,512,256]{2,1,0:T(8,128)(2,1)S(1)}, u32[]{:S(2)}, u32[]{:S(2)}) collective-permute-start(bf16[3,512,256]{2,1,0:T(8,128)(2,1)S(1)} %collective-permute-done.13.refs_0_.refs_8_), channel_id=1, source_target_pairs={{0,16},{1,17},{2,18},{3,19},{4,20},{5,21},{6,22},{7,23},{8,24},{9,... | collective-permute-start | bytes 2359304 | tf_op jit(solution)/shard_map/ppermute | solution.py:41
  87.9 19.0 %collective-permute-start.17 = (bf16[3,512,256]{2,1,0:T(8,128)(2,1)S(1)}, bf16[3,512,256]{2,1,0:T(8,128)(2,1)S(1)}, u32[]{:S(2)}, u32[]{:S(2)}) collective-permute-start(bf16[3,512,256]{2,1,0:T(8,128)(2,1)S(1)} %collective-permute-done.13.refs_0_.refs_8_), channel_id=1, source_target_pairs={{0,48},{1,49},{2,50},{3,51},{4,52},{5,53},{6,54},{7,55},{8,56},{9,... | collective-permute-start | bytes 2359304 | tf_op jit(solution)/shard_map/ppermute | solution.py:41
  90.3 17.5 %collective-permute-start.18 = (bf16[3,512,256]{2,1,0:T(8,128)(2,1)S(1)}, bf16[3,512,256]{2,1,0:T(8,128)(2,1)S(1)}, u32[]{:S(2)}, u32[]{:S(2)}) collective-permute-start(bf16[3,512,256]{2,1,0:T(8,128)(2,1)S(1)} %collective-permute-done.12.refs_9_.refs_7_), channel_id=1, source_target_pairs={{0,64},{1,65},{2,66},{3,67},{4,68},{5,69},{6,70},{7,71},{8,72},{9,... | collective-permute-start | bytes 2359304 | tf_op jit(solution)/shard_map/ppermute | solution.py:41
  111.4 8.1 %collective-permute-start.21 = (bf16[3,512,256]{2,1,0:T(8,128)(2,1)S(1)}, bf16[3,512,256]{2,1,0:T(8,128)(2,1)S(1)}, u32[]{:S(2)}, u32[]{:S(2)}) collective-permute-start(bf16[3,512,256]{2,1,0:T(8,128)(2,1)S(1)} %collective-permute-done.16.refs_1_.refs_9_), channel_id=1, source_target_pairs={{0,8},{1,9},{2,10},{3,11},{4,12},{5,13},{6,14},{7,15},{8,0},{9,1},... | collective-permute-start | bytes 2359304 | tf_op jit(solution)/shard_map/ppermute | solution.py:41
  113.9 5.5 %collective-permute-start.22 = (bf16[3,512,256]{2,1,0:T(8,128)(2,1)S(1)}, bf16[3,512,256]{2,1,0:T(8,128)(2,1)S(1)}, u32[]{:S(2)}, u32[]{:S(2)}) collective-permute-start(bf16[3,512,256]{2,1,0:T(8,128)(2,1)S(1)} %collective-permute-done.17.refs_2_.refs_10_), channel_id=1, source_target_pairs={{0,8},{1,9},{2,10},{3,11},{4,12},{5,13},{6,14},{7,15},{8,0},{9,1},... | collective-permute-start | bytes 2359304 | tf_op jit(solution)/shard_map/ppermute | solution.py:41
  114.0 5.4 %collective-permute-start.23 = (bf16[3,512,256]{2,1,0:T(8,128)(2,1)S(1)}, bf16[3,512,256]{2,1,0:T(8,128)(2,1)S(1)}, u32[]{:S(2)}, u32[]{:S(2)}) collective-permute-start(bf16[3,512,256]{2,1,0:T(8,128)(2,1)S(1)} %collective-permute-done.18.refs_3_.refs_11_), channel_id=1, source_target_pairs={{0,8},{1,9},{2,10},{3,11},{4,12},{5,13},{6,14},{7,15},{8,0},{9,1},... | collective-permute-start | bytes 2359304 | tf_op jit(solution)/shard_map/ppermute | solution.py:41
  127.4 4.8 %collective-permute-start.24 = (f32[16,512]{1,0:T(8,128)S(1)}, f32[16,512]{1,0:T(8,128)S(1)}, u32[]{:S(2)}, u32[]{:S(2)}) collective-permute-start(f32[16,512]{1,0:T(8,128)S(1)} %pad_maximum_fusion.3), channel_id=1, source_target_pairs={{0,8},{1,9},{2,10},{3,11},{4,12},{5,13},{6,14},{7,15},{8,0},{9,1},... | collective-permute-start | bytes 98312 | tf_op jit(solution)/shard_map/ppermute | solution.py:41
  127.6 4.7 %collective-permute-start.25 = (f32[16,512]{1,0:T(8,128)S(1)}, f32[16,512]{1,0:T(8,128)S(1)}, u32[]{:S(2)}, u32[]{:S(2)}) collective-permute-start(f32[16,512]{1,0:T(8,128)S(1)} %pad_maximum_fusion.3), channel_id=1, source_target_pairs={{0,64},{1,65},{2,66},{3,67},{4,68},{5,69},{6,70},{7,71},{8,72},{9,... | collective-permute-start | bytes 98312 | tf_op jit(solution)/shard_map/ppermute | solution.py:41
  127.6 4.7 %collective-permute-start.26 = (f32[16,512]{1,0:T(8,128)S(1)}, f32[16,512]{1,0:T(8,128)S(1)}, u32[]{:S(2)}, u32[]{:S(2)}) collective-permute-start(f32[16,512]{1,0:T(8,128)S(1)} %pad_maximum_fusion.3), channel_id=1, source_target_pairs={{0,72},{1,73},{2,74},{3,75},{4,76},{5,77},{6,78},{7,79},{8,64},{9,... | collective-permute-start | bytes 98312 | tf_op jit(solution)/shard_map/ppermute | solution.py:41
  132.3 5.5 %collective-permute-start.27 = (f32[16,512]{1,0:T(8,128)S(1)}, f32[16,512]{1,0:T(8,128)S(1)}, u32[]{:S(2)}, u32[]{:S(2)}) collective-permute-start(f32[16,512]{1,0:T(8,128)S(1)} %get-tuple-element.149), channel_id=1, source_target_pairs={{0,16},{1,17},{2,18},{3,19},{4,20},{5,21},{6,22},{7,23},{8,24},{9,... | collective-permute-start | bytes 98312 | tf_op jit(solution)/shard_map/ppermute | solution.py:41
  132.4 5.5 %collective-permute-start.28 = (f32[16,512]{1,0:T(8,128)S(1)}, f32[16,512]{1,0:T(8,128)S(1)}, u32[]{:S(2)}, u32[]{:S(2)}) collective-permute-start(f32[16,512]{1,0:T(8,128)S(1)} %get-tuple-element.148), channel_id=1, source_target_pairs={{0,32},{1,33},{2,34},{3,35},{4,36},{5,37},{6,38},{7,39},{8,40},{9,... | collective-permute-start | bytes 98312 | tf_op jit(solution)/shard_map/ppermute | solution.py:41
  134.8 3.1 %collective-permute-start.29 = (f32[16,512]{1,0:T(8,128)S(1)}, f32[16,512]{1,0:T(8,128)S(1)}, u32[]{:S(2)}, u32[]{:S(2)}) collective-permute-start(f32[16,512]{1,0:T(8,128)S(1)} %get-tuple-element.143), channel_id=1, source_target_pairs={{0,48},{1,49},{2,50},{3,51},{4,52},{5,53},{6,54},{7,55},{8,56},{9,... | collective-permute-start | bytes 98312 | tf_op jit(solution)/shard_map/ppermute | solution.py:41

commit v11 on v10

--- a/solution.py
+++ b/solution.py
@@ -229,7 +229,7 @@
 
         zero = jnp.zeros((SEG, LANES), F32)
         first = tuple([load_before(g, back) for g in range(3)] for back in (2, 1))
-        _, _, states = lax.fori_loop(0, seg_len, step, (*first, [zero] * MODES), unroll=4)
+        _, _, states = lax.fori_loop(0, seg_len, step, (*first, [zero] * MODES), unroll=8)
         for k in range(MODES):
             rate = prm[pl.ds(48 + k, 1), lanes]
             u = states[k]
@@ -286,7 +286,7 @@
             return states
 
         start = [shift_down(u_ref[pl.ds(k * SEG, SEG), lanes], 1) for k in range(MODES)]
-        lax.fori_loop(0, seg_len, step, start, unroll=4)
+        lax.fori_loop(0, seg_len, step, start, unroll=8)
 
 
 def read(prod, u, prm, rows):

time: 142 us -> 142 us (level)
  transfers between devices with their start and end apart: 30 -> 30, of which waited for: 8 -> 9; matrix products, arithmetic and copies ran while one was open for 3% -> 3% of each run, Pallas kernels for 15% -> 15%
where the time goes in v11:
time: 142 us; the launch traced here: 141 us
  waiting for transfers between devices  53.1 us (37%)
  starting transfers between devices  50.1 us (35%)
  Pallas kernels  32.9 us (23%)
  other arithmetic  2.45 us (2%)
  local copies, waits for them, and re-layouts  2.14 us (2%)
    ppermute x30, waiting for transfers between devices, send(): return lax.ppermute(value, ('ctx', 'tp'), route(move))  53.1 us
    ppermute x30, starting transfers between devices, send(): return lax.ppermute(value, ('ctx', 'tp'), route(move))  50.1 us
    pallas_call x2, Pallas kernels, project(): pl.pallas_call(functools.partial(project_kernel, rows, few), out_shape=[j...  12.5 us
    pallas_call x2, Pallas kernels, read(): pl.pallas_call(functools.partial(read_kernel, rows), out_shape=jax.ShapeD...  4.83 us
    pallas_call x1, Pallas kernels, begin(): pl.pallas_call(begin_kernel, out_shape=[jax.ShapeDtypeStruct((8, tall, BL...  4.14 us
    pallas_call x1, Pallas kernels, gate(): pl.pallas_call(functools.partial(gate_kernel, rows), out_shape=jax.ShapeD...  3.95 us
    pallas_call x1, Pallas kernels, also(): pl.pallas_call(also_kernel, out_shape=jax.ShapeDtypeStruct((tall, width),...  3.9 us
    pallas_call x1, Pallas kernels, more(): pl.pallas_call(more_kernel, out_shape=jax.ShapeDtypeStruct((tall, width),...  3.54 us
  transfers between devices with their start and end apart: 30, of which 9 were waited for; matrix products, arithmetic and copies ran while one was open for 3% of the time, Pallas kernels for 15%

profile of v11, /device:TPU:1, one launch (start us, length us, event | category | flops | bytes accessed | tf_op | source)
XLA Modules:
  0.0 141.3 jit_solution(9300892722167058868)
XLA Ops:
  0.0 1.9 %collective-permute-start.1 = (bf16[3,512,256]{2,1,0:T(8,128)(2,1)}, bf16[3,512,256]{2,1,0:T(8,128)(2,1)S(1)}, u32[]{:S(2)}, u32[]{:S(2)}) collective-permute-start(bf16[3,512,256]{2,1,0:T(8,128)(2,1)} %bitcast.73), channel_id=1, source_target_pairs={{0,0},{1,16},{2,32},{3,48},{4,64},{5,80},{6,96},{7,112},{8,8},{9,2... | collective-permute-start | bytes 2359304 | tf_op jit(solution)/shard_map/ppermute | solution.py:41
  1.9 0.8 select_bitcast_fusion.3
  2.9 0.8 dynamic_slice.21
  3.6 0.8 select_bitcast_fusion.2
  4.5 0.6 slice.27
  5.1 6.6 %collective-permute-start = (bf16[16,512]{1,0:T(8,128)(2,1)}, bf16[16,512]{1,0:T(8,128)(2,1)}, u32[]{:S(2)}, u32[]{:S(2)}) collective-permute-start(bf16[16,512]{1,0:T(8,128)(2,1)} %slice.27), channel_id=1, source_target_pairs={{0,8},{1,9},{2,10},{3,11},{4,12},{5,13},{6,14},{7,15},{8,16},{9,17... | collective-permute-start | bytes 49160 | tf_op jit(solution)/shard_map/ppermute | solution.py:41
  12.0 0.6 copy.9
  12.6 0.1 stack.70.where
  12.7 0.1 collective-permute-done
  12.8 0.8 pad_maximum_fusion.refs_0_
  13.6 10.8 %collective-permute-start.2 = (bf16[1040,512]{1,0:T(8,128)(2,1)S(1)}, bf16[1040,512]{1,0:T(8,128)(2,1)S(1)}, u32[]{:S(2)}, u32[]{:S(2)}) collective-permute-start(bf16[1040,512]{1,0:T(8,128)(2,1)S(1)} %pad_maximum_fusion.refs_0_), channel_id=1, source_target_pairs={{0,4},{1,5},{2,6},{3,7},{4,0},{5,1},{6,2},{7,3},{8,12},{9,13},{10,... | collective-permute-start | bytes 3194888 | tf_op jit(solution)/shard_map/ppermute | solution.py:41
  24.4 4.9 %collective-permute-start.3 = (bf16[1040,512]{1,0:T(8,128)(2,1)S(1)}, bf16[1040,512]{1,0:T(8,128)(2,1)S(1)}, u32[]{:S(2)}, u32[]{:S(2)}) collective-permute-start(bf16[1040,512]{1,0:T(8,128)(2,1)S(1)} %pad_maximum_fusion.refs_0_), channel_id=1, source_target_pairs={{0,1},{1,2},{2,3},{3,0},{4,5},{5,6},{6,7},{7,4},{8,9},{9,10},{10,1... | collective-permute-start | bytes 3194888 | tf_op jit(solution)/shard_map/ppermute | solution.py:41
  29.3 3.3 %collective-permute-start.4 = (bf16[1040,512]{1,0:T(8,128)(2,1)S(1)}, bf16[1040,512]{1,0:T(8,128)(2,1)S(1)}, u32[]{:S(2)}, u32[]{:S(2)}) collective-permute-start(bf16[1040,512]{1,0:T(8,128)(2,1)S(1)} %pad_maximum_fusion.refs_0_), channel_id=1, source_target_pairs={{0,3},{1,0},{2,1},{3,2},{4,7},{5,4},{6,5},{7,6},{8,11},{9,8},{10,9... | collective-permute-start | bytes 3194888 | tf_op jit(solution)/shard_map/ppermute | solution.py:41
  32.7 2.7 %collective-permute-start.6 = (bf16[3,512,256]{2,1,0:T(8,128)(2,1)S(1)}, bf16[3,512,256]{2,1,0:T(8,128)(2,1)S(1)}, u32[]{:S(2)}, u32[]{:S(2)}) collective-permute-start(bf16[3,512,256]{2,1,0:T(8,128)(2,1)S(1)} %collective-permute-done.1.refs_6_.refs_4_), channel_id=1, source_target_pairs={{0,48},{1,49},{2,50},{3,51},{4,52},{5,53},{6,54},{7,55},{8,56},{9,... | collective-permute-start | bytes 2359304 | tf_op jit(solution)/shard_map/ppermute | solution.py:41
  35.3 15.5 %collective-permute-done.5.refs_7_.refs_5_ = bf16[3,512,256]{2,1,0:T(8,128)(2,1)S(1)} collective-permute-done((bf16[3,512,256]{2,1,0:T(8,128)(2,1)S(1)}, bf16[3,512,256]{2,1,0:T(8,128)(2,1)S(1)}, u32[]{:S(2)}, u32[]{:S(2)}) %collective-permute-start.5) | collective-permute-done | bytes 786464 | tf_op jit(solution)/shard_map/ppermute | solution.py:41
  50.8 0.0 collective-permute-done.6.refs_8_.refs_6_
  50.8 0.0 collective-permute-done.2.refs_3_
  50.8 3.8 %collective-permute-done.3.refs_1_ = bf16[1040,512]{1,0:T(8,128)(2,1)S(1)} collective-permute-done((bf16[1040,512]{1,0:T(8,128)(2,1)S(1)}, bf16[1040,512]{1,0:T(8,128)(2,1)S(1)}, u32[]{:S(2)}, u32[]{:S(2)}) %collective-permute-start.3) | collective-permute-done | bytes 1064992 | tf_op jit(solution)/shard_map/ppermute | solution.py:41
  54.6 0.0 collective-permute-done.4.refs_2_
  54.6 2.5 %collective-permute-start.7 = (bf16[3,512,256]{2,1,0:T(8,128)(2,1)S(1)}, bf16[3,512,256]{2,1,0:T(8,128)(2,1)S(1)}, u32[]{:S(2)}, u32[]{:S(2)}) collective-permute-start(bf16[3,512,256]{2,1,0:T(8,128)(2,1)S(1)} %collective-permute-done.1.refs_6_.refs_4_), channel_id=1, source_target_pairs={{0,8},{1,9},{2,10},{3,11},{4,12},{5,13},{6,14},{7,15},{8,0},{9,1},... | collective-permute-start | bytes 2359304 | tf_op jit(solution)/shard_map/ppermute | solution.py:41
  57.1 0.0 collective-permute-start.8
  57.1 0.5 collective-permute-start.9
  57.6 0.9 collective-permute-start.10
  58.5 1.8 %collective-permute-start.11 = (bf16[1040,512]{1,0:T(8,128)(2,1)S(1)}, bf16[1040,512]{1,0:T(8,128)(2,1)S(1)}, u32[]{:S(2)}, u32[]{:S(2)}) collective-permute-start(bf16[1040,512]{1,0:T(8,128)(2,1)S(1)} %collective-permute-done.2.refs_3_), channel_id=1, source_target_pairs={{0,3},{1,0},{2,1},{3,2},{4,7},{5,4},{6,5},{7,6},{8,11},{9,8},{10,9... | collective-permute-start | bytes 3194888 | tf_op jit(solution)/shard_map/ppermute | solution.py:41
  60.3 0.0 collective-permute-done.7.refs_1_.refs_4_
  60.3 1.0 collective-permute-done.9.refs_3_.refs_6_
  61.3 0.0 collective-permute-start.12
  61.3 0.0 collective-permute-start.13
  61.3 22.7 %collective-permute-done.10.refs_4_ = bf16[1040,512]{1,0:T(8,128)(2,1)S(1)} collective-permute-done((bf16[1040,512]{1,0:T(8,128)(2,1)S(1)}, bf16[1040,512]{1,0:T(8,128)(2,1)S(1)}, u32[]{:S(2)}, u32[]{:S(2)}) %collective-permute-start.10) | collective-permute-done | bytes 1064992 | tf_op jit(solution)/shard_map/ppermute | solution.py:41
  84.0 0.9 collective-permute-start.14
  84.9 0.1 collective-permute-start.15
  85.0 1.0 collective-permute-start.19
  86.0 1.7 %collective-permute-start.20 = (bf16[1040,512]{1,0:T(8,128)(2,1)S(1)}, bf16[1040,512]{1,0:T(8,128)(2,1)S(1)}, u32[]{:S(2)}, u32[]{:S(2)}) collective-permute-start(bf16[1040,512]{1,0:T(8,128)(2,1)S(1)} %collective-permute-done.11.refs_5_), channel_id=1, source_target_pairs={{0,3},{1,0},{2,1},{3,2},{4,7},{5,4},{6,5},{7,6},{8,11},{9,8},{10,9... | collective-permute-start | bytes 3194888 | tf_op jit(solution)/shard_map/ppermute | solution.py:41
  87.6 0.0 collective-permute-start.16
  87.6 0.0 collective-permute-done.14.refs_4_.refs_7_
  87.6 0.3 collective-permute-done.15.refs_8_
  87.9 2.4 %collective-permute-start.17 = (bf16[3,512,256]{2,1,0:T(8,128)(2,1)S(1)}, bf16[3,512,256]{2,1,0:T(8,128)(2,1)S(1)}, u32[]{:S(2)}, u32[]{:S(2)}) collective-permute-start(bf16[3,512,256]{2,1,0:T(8,128)(2,1)S(1)} %collective-permute-done.13.refs_0_.refs_8_), channel_id=1, source_target_pairs={{0,48},{1,49},{2,50},{3,51},{4,52},{5,53},{6,54},{7,55},{8,56},{9,... | collective-permute-start | bytes 2359304 | tf_op jit(solution)/shard_map/ppermute | solution.py:41
  90.3 0.0 collective-permute-start.18
  90.3 4.1 %shard_map.64 = (bf16[8,1040,512]{2,1,0:T(8,128)(2,1)S(1)}, f32[1040,768]{1,0:T(8,128)S(1)}) custom-call(s32[9]{0:T(128)S(1)} %stack.70.where, bf16[1040,512]{1,0:T(8,128)(2,1)S(1)} %pad_maximum_fusion.refs_0_, bf16[1040,512]{1,0:T(8,128)(2,1)S(1)} %collective-permute-done.3.refs_1_, bf16[1040,512]{1,0:T(8,128)(2,1)S(1)} %collective-permute-done.4.refs_2_, ...), custom_call_target="tpu_custom_call" | custom-call | flops 2453667840 | bytes 12582912 | tf_op jit(solution)/shard_map/pallas_call | solution.py:109
  94.5 3.9 %shard_map.66.refs_3_ = f32[1040,768]{1,0:T(8,128)S(1)} custom-call(s32[9]{0:T(128)S(1)} %stack.70.where, bf16[8,1040,512]{2,1,0:T(8,128)(2,1)S(1)} %get-tuple-element.112.lhs.refs_0_, bf16[3,512,256]{2,1,0:T(8,128)(2,1)S(1)} %collective-permute-done.7.refs_1_.refs_4_, bf16[3,512,256]{2,1,0:T(8,128)(2,1)S(1)} %collective-permute-done.8.refs_2_.refs_5_, ...), custom_call_target="tpu_custom_call" | custom-call | flops 2453667840 | bytes 12582912 | tf_op jit(solution)/shard_map/pallas_call | solution.py:127
  98.4 8.5 %collective-permute-done.16.refs_1_.refs_9_ = bf16[3,512,256]{2,1,0:T(8,128)(2,1)S(1)} collective-permute-done((bf16[3,512,256]{2,1,0:T(8,128)(2,1)S(1)}, bf16[3,512,256]{2,1,0:T(8,128)(2,1)S(1)}, u32[]{:S(2)}, u32[]{:S(2)}) %collective-permute-start.16) | collective-permute-done | bytes 786464 | tf_op jit(solution)/shard_map/ppermute | solution.py:41
  106.9 0.0 collective-permute-done.17.refs_2_.refs_10_
  106.9 0.9 collective-permute-done.18.refs_3_.refs_11_
  107.8 3.5 %shard_map.65.refs_3_ = f32[1040,768]{1,0:T(8,128)S(1)} custom-call(s32[9]{0:T(128)S(1)} %stack.70.where, bf16[8,1040,512]{2,1,0:T(8,128)(2,1)S(1)} %get-tuple-element.112.lhs.refs_0_, f32[1040,768]{1,0:T(8,128)S(1)} %get-tuple-element.106.part, bf16[3,512,256]{2,1,0:T(8,128)(2,1)S(1)} %collective-permute-done.13.refs_0_.refs_8_, ...), custom_call_target="tpu_custom_call" | custom-call | flops 2453667840 | bytes 12582912 | tf_op jit(solution)/shard_map/pallas_call | solution.py:162
  111.4 0.0 collective-permute-done.19.refs_1_
  111.4 2.5 %collective-permute-start.21 = (bf16[3,512,256]{2,1,0:T(8,128)(2,1)S(1)}, bf16[3,512,256]{2,1,0:T(8,128)(2,1)S(1)}, u32[]{:S(2)}, u32[]{:S(2)}) collective-permute-start(bf16[3,512,256]{2,1,0:T(8,128)(2,1)S(1)} %collective-permute-done.16.refs_1_.refs_9_), channel_id=1, source_target_pairs={{0,8},{1,9},{2,10},{3,11},{4,12},{5,13},{6,14},{7,15},{8,0},{9,1},... | collective-permute-start | bytes 2359304 | tf_op jit(solution)/shard_map/ppermute | solution.py:41
  113.9 0.1 collective-permute-start.22
  114.0 0.4 collective-permute-start.23
  114.4 4.8 %shard_map.67 = (f32[1024,256]{1,0:T(8,128)S(1)}, f32[1024,256]{1,0:T(8,128)S(1)}, f32[128,256]{1,0:T(8,128)S(1)}, f32[16,256]{1,0:T(8,128)S(1)}) custom-call(s32[9]{0:T(128)S(1)} %stack.70.where, bf16[8,1040,512]{2,1,0:T(8,128)(2,1)S(1)} %get-tuple-element.112.lhs.refs_0_, bf16[1040,512]{1,0:T(8,128)(2,1)S(1)} %collective-permute-done.19.refs_1_, ...), custom_call_target="tpu_custom_call" | custom-call | flops 4089446400 | bytes 12582912 | tf_op jit(solution)/shard_map/pallas_call | solution.py:245
  119.2 0.0 collective-permute-done.21.refs_9_
  119.2 0.0 collective-permute-done.23.refs_11_
  119.3 7.7 %shard_map.68 = (f32[1024,256]{1,0:T(8,128)S(1)}, f32[1024,256]{1,0:T(8,128)S(1)}, f32[128,256]{1,0:T(8,128)S(1)}, f32[16,256]{1,0:T(8,128)S(1)}) custom-call(s32[9]{0:T(128)S(1)} %stack.70.where, bf16[8,1040,512]{2,1,0:T(8,128)(2,1)S(1)} %get-tuple-element.112.lhs.refs_0_, bf16[1040,512]{1,0:T(8,128)(2,1)S(1)} %collective-permute-done.19.refs_1_, ...), custom_call_target="tpu_custom_call" | custom-call | flops 4089446400 | bytes 12582912 | tf_op jit(solution)/shard_map/pallas_call | solution.py:245
  127.0 0.2 collective-permute-start.24
  127.2 0.0 collective-permute-start.25
  127.2 2.0 %collective-permute-start.26 = (f32[16,512]{1,0:T(8,128)S(1)}, f32[16,512]{1,0:T(8,128)S(1)}, u32[]{:S(2)}, u32[]{:S(2)}) collective-permute-start(f32[16,512]{1,0:T(8,128)S(1)} %pad_maximum_fusion.3), channel_id=1, source_target_pairs={{0,72},{1,73},{2,74},{3,75},{4,76},{5,77},{6,78},{7,79},{8,64},{9,... | collective-permute-start | bytes 98312 | tf_op jit(solution)/shard_map/ppermute | solution.py:41
  129.2 2.4 %shard_map.69.y0 = f32[1024,256]{1,0:T(8,128)S(1)} custom-call(f32[1024,256]{1,0:T(8,128)S(1)} %get-tuple-element.128.prod_ref, f32[128,256]{1,0:T(8,128)S(1)} %get-tuple-element.129.u_ref, f32[64,256]{1,0:T(8,128)S(1)} %get-tuple-element.119.refs_12_.prm.p0), custom_call_target="tpu_custom_call" | custom-call | flops 16777216 | bytes 12582912 | tf_op jit(solution)/shard_map/pallas_call | solution.py:294
  131.7 0.0 collective-permute-done.25
  131.7 0.0 collective-permute-done.26
  131.8 0.1 collective-permute-start.27
  131.8 2.4 %collective-permute-start.28 = (f32[16,512]{1,0:T(8,128)S(1)}, f32[16,512]{1,0:T(8,128)S(1)}, u32[]{:S(2)}, u32[]{:S(2)}) collective-permute-start(f32[16,512]{1,0:T(8,128)S(1)} %get-tuple-element.148), channel_id=1, source_target_pairs={{0,32},{1,33},{2,34},{3,35},{4,36},{5,37},{6,38},{7,39},{8,40},{9,... | collective-permute-start | bytes 98312 | tf_op jit(solution)/shard_map/ppermute | solution.py:41
  134.2 0.4 collective-permute-start.29
  134.7 2.4 %shard_map.70.y1 = f32[1024,256]{1,0:T(8,128)S(1)} custom-call(f32[1024,256]{1,0:T(8,128)S(1)} %get-tuple-element.131.prod_ref, f32[128,256]{1,0:T(8,128)S(1)} %get-tuple-element.132.u_ref, f32[64,256]{1,0:T(8,128)S(1)} %get-tuple-element.123.refs_12_.prm.p1), custom_call_target="tpu_custom_call" | custom-call | flops 16777216 | bytes 12582912 | tf_op jit(solution)/shard_map/pallas_call | solution.py:294
  137.1 0.2 collective-permute-done.29.down
  137.4 4.0 %shard_map.71 = bf16[1024,512]{1,0:T(8,128)(2,1)} custom-call(s32[1]{0:T(128)} %bitcast.15.core_ref, f32[1024,256]{1,0:T(8,128)S(1)} %shard_map.69.y0, f32[1024,256]{1,0:T(8,128)S(1)} %shard_map.70.y1, f32[1024,256]{1,0:T(8,128)S(1)} %get-tuple-element.133.x0, f32[1024,256]{1,0:T(8,128)S(1)} %get-tuple-element.134.x1, ...), custom_call_target="tpu_custom_call" | custom-call | tf_op jit(solution)/shard_map/pallas_call | solution.py:341
  (25 shorter events, 0.2 us)
Async XLA Ops:
  0.0 2.7 %copy-start = (f32[3,3,4096]{2,1,0:T(4,128)S(1)}, f32[3,3,4096]{2,1,0:T(4,128)}, u32[]{:S(2)}) copy-start(f32[3,3,4096]{2,1,0:T(4,128)} %param.8) | copy-start | bytes 442372
  0.0 4.5 %copy-start.1 = (bf16[1024,512]{1,0:T(8,128)(2,1)S(1)}, bf16[1024,512]{1,0:T(8,128)(2,1)}, u32[]{:S(2)}) copy-start(bf16[1024,512]{1,0:T(8,128)(2,1)} %param.6) | copy-start | bytes 3145732
  0.0 13.6 %collective-permute-start.1 = (bf16[3,512,256]{2,1,0:T(8,128)(2,1)}, bf16[3,512,256]{2,1,0:T(8,128)(2,1)S(1)}, u32[]{:S(2)}, u32[]{:S(2)}) collective-permute-start(bf16[3,512,256]{2,1,0:T(8,128)(2,1)} %bitcast.73), channel_id=1, source_target_pairs={{0,0},{1,16},{2,32},{3,48},{4,64},{5,80},{6,96},{7,112},{8,8},{9,2... | collective-permute-start | bytes 2359304 | tf_op jit(solution)/shard_map/ppermute | solution.py:41
  5.1 7.7 %collective-permute-start = (bf16[16,512]{1,0:T(8,128)(2,1)}, bf16[16,512]{1,0:T(8,128)(2,1)}, u32[]{:S(2)}, u32[]{:S(2)}) collective-permute-start(bf16[16,512]{1,0:T(8,128)(2,1)} %slice.27), channel_id=1, source_target_pairs={{0,8},{1,9},{2,10},{3,11},{4,12},{5,13},{6,14},{7,15},{8,16},{9,17... | collective-permute-start | bytes 49160 | tf_op jit(solution)/shard_map/ppermute | solution.py:41
  13.6 37.2 %collective-permute-start.2 = (bf16[1040,512]{1,0:T(8,128)(2,1)S(1)}, bf16[1040,512]{1,0:T(8,128)(2,1)S(1)}, u32[]{:S(2)}, u32[]{:S(2)}) collective-permute-start(bf16[1040,512]{1,0:T(8,128)(2,1)S(1)} %pad_maximum_fusion.refs_0_), channel_id=1, source_target_pairs={{0,4},{1,5},{2,6},{3,7},{4,0},{5,1},{6,2},{7,3},{8,12},{9,13},{10,... | collective-permute-start | bytes 3194888 | tf_op jit(solution)/shard_map/ppermute | solution.py:41
  24.4 30.3 %collective-permute-start.3 = (bf16[1040,512]{1,0:T(8,128)(2,1)S(1)}, bf16[1040,512]{1,0:T(8,128)(2,1)S(1)}, u32[]{:S(2)}, u32[]{:S(2)}) collective-permute-start(bf16[1040,512]{1,0:T(8,128)(2,1)S(1)} %pad_maximum_fusion.refs_0_), channel_id=1, source_target_pairs={{0,1},{1,2},{2,3},{3,0},{4,5},{5,6},{6,7},{7,4},{8,9},{9,10},{10,1... | collective-permute-start | bytes 3194888 | tf_op jit(solution)/shard_map/ppermute | solution.py:41
  29.3 25.3 %collective-permute-start.4 = (bf16[1040,512]{1,0:T(8,128)(2,1)S(1)}, bf16[1040,512]{1,0:T(8,128)(2,1)S(1)}, u32[]{:S(2)}, u32[]{:S(2)}) collective-permute-start(bf16[1040,512]{1,0:T(8,128)(2,1)S(1)} %pad_maximum_fusion.refs_0_), channel_id=1, source_target_pairs={{0,3},{1,0},{2,1},{3,2},{4,7},{5,4},{6,5},{7,6},{8,11},{9,8},{10,9... | collective-permute-start | bytes 3194888 | tf_op jit(solution)/shard_map/ppermute | solution.py:41
  32.7 18.1 %collective-permute-start.5 = (bf16[3,512,256]{2,1,0:T(8,128)(2,1)S(1)}, bf16[3,512,256]{2,1,0:T(8,128)(2,1)S(1)}, u32[]{:S(2)}, u32[]{:S(2)}) collective-permute-start(bf16[3,512,256]{2,1,0:T(8,128)(2,1)S(1)} %collective-permute-done.1.refs_6_.refs_4_), channel_id=1, source_target_pairs={{0,16},{1,17},{2,18},{3,19},{4,20},{5,21},{6,22},{7,23},{8,24},{9,... | collective-permute-start | bytes 2359304 | tf_op jit(solution)/shard_map/ppermute | solution.py:41
  32.7 18.1 %collective-permute-start.6 = (bf16[3,512,256]{2,1,0:T(8,128)(2,1)S(1)}, bf16[3,512,256]{2,1,0:T(8,128)(2,1)S(1)}, u32[]{:S(2)}, u32[]{:S(2)}) collective-permute-start(bf16[3,512,256]{2,1,0:T(8,128)(2,1)S(1)} %collective-permute-done.1.refs_6_.refs_4_), channel_id=1, source_target_pairs={{0,48},{1,49},{2,50},{3,51},{4,52},{5,53},{6,54},{7,55},{8,56},{9,... | collective-permute-start | bytes 2359304 | tf_op jit(solution)/shard_map/ppermute | solution.py:41
  54.6 5.7 %collective-permute-start.7 = (bf16[3,512,256]{2,1,0:T(8,128)(2,1)S(1)}, bf16[3,512,256]{2,1,0:T(8,128)(2,1)S(1)}, u32[]{:S(2)}, u32[]{:S(2)}) collective-permute-start(bf16[3,512,256]{2,1,0:T(8,128)(2,1)S(1)} %collective-permute-done.1.refs_6_.refs_4_), channel_id=1, source_target_pairs={{0,8},{1,9},{2,10},{3,11},{4,12},{5,13},{6,14},{7,15},{8,0},{9,1},... | collective-permute-start | bytes 2359304 | tf_op jit(solution)/shard_map/ppermute | solution.py:41
  57.1 3.2 %collective-permute-start.8 = (bf16[3,512,256]{2,1,0:T(8,128)(2,1)S(1)}, bf16[3,512,256]{2,1,0:T(8,128)(2,1)S(1)}, u32[]{:S(2)}, u32[]{:S(2)}) collective-permute-start(bf16[3,512,256]{2,1,0:T(8,128)(2,1)S(1)} %collective-permute-done.5.refs_7_.refs_5_), channel_id=1, source_target_pairs={{0,8},{1,9},{2,10},{3,11},{4,12},{5,13},{6,14},{7,15},{8,0},{9,1},... | collective-permute-start | bytes 2359304 | tf_op jit(solution)/shard_map/ppermute | solution.py:41
  57.1 4.2 %collective-permute-start.9 = (bf16[3,512,256]{2,1,0:T(8,128)(2,1)S(1)}, bf16[3,512,256]{2,1,0:T(8,128)(2,1)S(1)}, u32[]{:S(2)}, u32[]{:S(2)}) collective-permute-start(bf16[3,512,256]{2,1,0:T(8,128)(2,1)S(1)} %collective-permute-done.6.refs_8_.refs_6_), channel_id=1, source_target_pairs={{0,8},{1,9},{2,10},{3,11},{4,12},{5,13},{6,14},{7,15},{8,0},{9,1},... | collective-permute-start | bytes 2359304 | tf_op jit(solution)/shard_map/ppermute | solution.py:41
  57.6 26.4 %collective-permute-start.10 = (bf16[1040,512]{1,0:T(8,128)(2,1)S(1)}, bf16[1040,512]{1,0:T(8,128)(2,1)S(1)}, u32[]{:S(2)}, u32[]{:S(2)}) collective-permute-start(bf16[1040,512]{1,0:T(8,128)(2,1)S(1)} %collective-permute-done.2.refs_3_), channel_id=1, source_target_pairs={{0,1},{1,2},{2,3},{3,0},{4,5},{5,6},{6,7},{7,4},{8,9},{9,10},{10,1... | collective-permute-start | bytes 3194888 | tf_op jit(solution)/shard_map/ppermute | solution.py:41
  58.5 25.5 %collective-permute-start.11 = (bf16[1040,512]{1,0:T(8,128)(2,1)S(1)}, bf16[1040,512]{1,0:T(8,128)(2,1)S(1)}, u32[]{:S(2)}, u32[]{:S(2)}) collective-permute-start(bf16[1040,512]{1,0:T(8,128)(2,1)S(1)} %collective-permute-done.2.refs_3_), channel_id=1, source_target_pairs={{0,3},{1,0},{2,1},{3,2},{4,7},{5,4},{6,5},{7,6},{8,11},{9,8},{10,9... | collective-permute-start | bytes 3194888 | tf_op jit(solution)/shard_map/ppermute | solution.py:41
  61.3 22.7 %collective-permute-start.12 = (bf16[3,512,256]{2,1,0:T(8,128)(2,1)S(1)}, bf16[3,512,256]{2,1,0:T(8,128)(2,1)S(1)}, u32[]{:S(2)}, u32[]{:S(2)}) collective-permute-start(bf16[3,512,256]{2,1,0:T(8,128)(2,1)S(1)} %collective-permute-done.5.refs_7_.refs_5_), channel_id=1, source_target_pairs={{0,16},{1,17},{2,18},{3,19},{4,20},{5,21},{6,22},{7,23},{8,24},{9,... | collective-permute-start | bytes 2359304 | tf_op jit(solution)/shard_map/ppermute | solution.py:41
  61.3 22.7 %collective-permute-start.13 = (bf16[3,512,256]{2,1,0:T(8,128)(2,1)S(1)}, bf16[3,512,256]{2,1,0:T(8,128)(2,1)S(1)}, u32[]{:S(2)}, u32[]{:S(2)}) collective-permute-start(bf16[3,512,256]{2,1,0:T(8,128)(2,1)S(1)} %collective-permute-done.1.refs_6_.refs_4_), channel_id=1, source_target_pairs={{0,64},{1,65},{2,66},{3,67},{4,68},{5,69},{6,70},{7,71},{8,72},{9,... | collective-permute-start | bytes 2359304 | tf_op jit(solution)/shard_map/ppermute | solution.py:41
  84.0 3.6 %collective-permute-start.14 = (bf16[3,512,256]{2,1,0:T(8,128)(2,1)S(1)}, bf16[3,512,256]{2,1,0:T(8,128)(2,1)S(1)}, u32[]{:S(2)}, u32[]{:S(2)}) collective-permute-start(bf16[3,512,256]{2,1,0:T(8,128)(2,1)S(1)} %collective-permute-done.12.refs_9_.refs_7_), channel_id=1, source_target_pairs={{0,8},{1,9},{2,10},{3,11},{4,12},{5,13},{6,14},{7,15},{8,0},{9,1},... | collective-permute-start | bytes 2359304 | tf_op jit(solution)/shard_map/ppermute | solution.py:41
  84.9 3.0 %collective-permute-start.15 = (bf16[3,512,256]{2,1,0:T(8,128)(2,1)S(1)}, bf16[3,512,256]{2,1,0:T(8,128)(2,1)S(1)}, u32[]{:S(2)}, u32[]{:S(2)}) collective-permute-start(bf16[3,512,256]{2,1,0:T(8,128)(2,1)S(1)} %collective-permute-done.13.refs_0_.refs_8_), channel_id=1, source_target_pairs={{0,8},{1,9},{2,10},{3,11},{4,12},{5,13},{6,14},{7,15},{8,0},{9,1},... | collective-permute-start | bytes 2359304 | tf_op jit(solution)/shard_map/ppermute | solution.py:41
  85.0 26.4 %collective-permute-start.19 = (bf16[1040,512]{1,0:T(8,128)(2,1)S(1)}, bf16[1040,512]{1,0:T(8,128)(2,1)S(1)}, u32[]{:S(2)}, u32[]{:S(2)}) collective-permute-start(bf16[1040,512]{1,0:T(8,128)(2,1)S(1)} %collective-permute-done.3.refs_1_), channel_id=1, source_target_pairs={{0,1},{1,2},{2,3},{3,0},{4,5},{5,6},{6,7},{7,4},{8,9},{9,10},{10,1... | collective-permute-start | bytes 3194888 | tf_op jit(solution)/shard_map/ppermute | solution.py:41
  86.0 25.4 %collective-permute-start.20 = (bf16[1040,512]{1,0:T(8,128)(2,1)S(1)}, bf16[1040,512]{1,0:T(8,128)(2,1)S(1)}, u32[]{:S(2)}, u32[]{:S(2)}) collective-permute-start(bf16[1040,512]{1,0:T(8,128)(2,1)S(1)} %collective-permute-done.11.refs_5_), channel_id=1, source_target_pairs={{0,3},{1,0},{2,1},{3,2},{4,7},{5,4},{6,5},{7,6},{8,11},{9,8},{10,9... | collective-permute-start | bytes 3194888 | tf_op jit(solution)/shard_map/ppermute | solution.py:41
  87.6 19.3 %collective-permute-start.16 = (bf16[3,512,256]{2,1,0:T(8,128)(2,1)S(1)}, bf16[3,512,256]{2,1,0:T(8,128)(2,1)S(1)}, u32[]{:S(2)}, u32[]{:S(2)}) collective-permute-start(bf16[3,512,256]{2,1,0:T(8,128)(2,1)S(1)} %collective-permute-done.13.refs_0_.refs_8_), channel_id=1, source_target_pairs={{0,16},{1,17},{2,18},{3,19},{4,20},{5,21},{6,22},{7,23},{8,24},{9,... | collective-permute-start | bytes 2359304 | tf_op jit(solution)/shard_map/ppermute | solution.py:41
  87.9 19.0 %collective-permute-start.17 = (bf16[3,512,256]{2,1,0:T(8,128)(2,1)S(1)}, bf16[3,512,256]{2,1,0:T(8,128)(2,1)S(1)}, u32[]{:S(2)}, u32[]{:S(2)}) collective-permute-start(bf16[3,512,256]{2,1,0:T(8,128)(2,1)S(1)} %collective-permute-done.13.refs_0_.refs_8_), channel_id=1, source_target_pairs={{0,48},{1,49},{2,50},{3,51},{4,52},{5,53},{6,54},{7,55},{8,56},{9,... | collective-permute-start | bytes 2359304 | tf_op jit(solution)/shard_map/ppermute | solution.py:41
  90.3 17.5 %collective-permute-start.18 = (bf16[3,512,256]{2,1,0:T(8,128)(2,1)S(1)}, bf16[3,512,256]{2,1,0:T(8,128)(2,1)S(1)}, u32[]{:S(2)}, u32[]{:S(2)}) collective-permute-start(bf16[3,512,256]{2,1,0:T(8,128)(2,1)S(1)} %collective-permute-done.12.refs_9_.refs_7_), channel_id=1, source_target_pairs={{0,64},{1,65},{2,66},{3,67},{4,68},{5,69},{6,70},{7,71},{8,72},{9,... | collective-permute-start | bytes 2359304 | tf_op jit(solution)/shard_map/ppermute | solution.py:41
  111.4 7.9 %collective-permute-start.21 = (bf16[3,512,256]{2,1,0:T(8,128)(2,1)S(1)}, bf16[3,512,256]{2,1,0:T(8,128)(2,1)S(1)}, u32[]{:S(2)}, u32[]{:S(2)}) collective-permute-start(bf16[3,512,256]{2,1,0:T(8,128)(2,1)S(1)} %collective-permute-done.16.refs_1_.refs_9_), channel_id=1, source_target_pairs={{0,8},{1,9},{2,10},{3,11},{4,12},{5,13},{6,14},{7,15},{8,0},{9,1},... | collective-permute-start | bytes 2359304 | tf_op jit(solution)/shard_map/ppermute | solution.py:41
  113.9 5.3 %collective-permute-start.22 = (bf16[3,512,256]{2,1,0:T(8,128)(2,1)S(1)}, bf16[3,512,256]{2,1,0:T(8,128)(2,1)S(1)}, u32[]{:S(2)}, u32[]{:S(2)}) collective-permute-start(bf16[3,512,256]{2,1,0:T(8,128)(2,1)S(1)} %collective-permute-done.17.refs_2_.refs_10_), channel_id=1, source_target_pairs={{0,8},{1,9},{2,10},{3,11},{4,12},{5,13},{6,14},{7,15},{8,0},{9,1},... | collective-permute-start | bytes 2359304 | tf_op jit(solution)/shard_map/ppermute | solution.py:41
  114.0 5.2 %collective-permute-start.23 = (bf16[3,512,256]{2,1,0:T(8,128)(2,1)S(1)}, bf16[3,512,256]{2,1,0:T(8,128)(2,1)S(1)}, u32[]{:S(2)}, u32[]{:S(2)}) collective-permute-start(bf16[3,512,256]{2,1,0:T(8,128)(2,1)S(1)} %collective-permute-done.18.refs_3_.refs_11_), channel_id=1, source_target_pairs={{0,8},{1,9},{2,10},{3,11},{4,12},{5,13},{6,14},{7,15},{8,0},{9,1},... | collective-permute-start | bytes 2359304 | tf_op jit(solution)/shard_map/ppermute | solution.py:41
  127.0 4.6 %collective-permute-start.24 = (f32[16,512]{1,0:T(8,128)S(1)}, f32[16,512]{1,0:T(8,128)S(1)}, u32[]{:S(2)}, u32[]{:S(2)}) collective-permute-start(f32[16,512]{1,0:T(8,128)S(1)} %pad_maximum_fusion.3), channel_id=1, source_target_pairs={{0,8},{1,9},{2,10},{3,11},{4,12},{5,13},{6,14},{7,15},{8,0},{9,1},... | collective-permute-start | bytes 98312 | tf_op jit(solution)/shard_map/ppermute | solution.py:41
  127.2 4.5 %collective-permute-start.25 = (f32[16,512]{1,0:T(8,128)S(1)}, f32[16,512]{1,0:T(8,128)S(1)}, u32[]{:S(2)}, u32[]{:S(2)}) collective-permute-start(f32[16,512]{1,0:T(8,128)S(1)} %pad_maximum_fusion.3), channel_id=1, source_target_pairs={{0,64},{1,65},{2,66},{3,67},{4,68},{5,69},{6,70},{7,71},{8,72},{9,... | collective-permute-start | bytes 98312 | tf_op jit(solution)/shard_map/ppermute | solution.py:41
  127.2 4.5 %collective-permute-start.26 = (f32[16,512]{1,0:T(8,128)S(1)}, f32[16,512]{1,0:T(8,128)S(1)}, u32[]{:S(2)}, u32[]{:S(2)}) collective-permute-start(f32[16,512]{1,0:T(8,128)S(1)} %pad_maximum_fusion.3), channel_id=1, source_target_pairs={{0,72},{1,73},{2,74},{3,75},{4,76},{5,77},{6,78},{7,79},{8,64},{9,... | collective-permute-start | bytes 98312 | tf_op jit(solution)/shard_map/ppermute | solution.py:41
  131.8 5.3 %collective-permute-start.27 = (f32[16,512]{1,0:T(8,128)S(1)}, f32[16,512]{1,0:T(8,128)S(1)}, u32[]{:S(2)}, u32[]{:S(2)}) collective-permute-start(f32[16,512]{1,0:T(8,128)S(1)} %get-tuple-element.149), channel_id=1, source_target_pairs={{0,16},{1,17},{2,18},{3,19},{4,20},{5,21},{6,22},{7,23},{8,24},{9,... | collective-permute-start | bytes 98312 | tf_op jit(solution)/shard_map/ppermute | solution.py:41
  131.8 5.3 %collective-permute-start.28 = (f32[16,512]{1,0:T(8,128)S(1)}, f32[16,512]{1,0:T(8,128)S(1)}, u32[]{:S(2)}, u32[]{:S(2)}) collective-permute-start(f32[16,512]{1,0:T(8,128)S(1)} %get-tuple-element.148), channel_id=1, source_target_pairs={{0,32},{1,33},{2,34},{3,35},{4,36},{5,37},{6,38},{7,39},{8,40},{9,... | collective-permute-start | bytes 98312 | tf_op jit(solution)/shard_map/ppermute | solution.py:41
  134.2 3.1 %collective-permute-start.29 = (f32[16,512]{1,0:T(8,128)S(1)}, f32[16,512]{1,0:T(8,128)S(1)}, u32[]{:S(2)}, u32[]{:S(2)}) collective-permute-start(f32[16,512]{1,0:T(8,128)S(1)} %get-tuple-element.143), channel_id=1, source_target_pairs={{0,48},{1,49},{2,50},{3,51},{4,52},{5,53},{6,54},{7,55},{8,56},{9,... | collective-permute-start | bytes 98312 | tf_op jit(solution)/shard_map/ppermute | solution.py:41
